TPU v7x, 32 devices: a whole 2x2x4 slice. The times are simulated.
32 devices in a mesh: wide: 8 (over z, x), tp: 4 (over y, core).
Axes of the slice: x: 2, y: 2, z: 4, core: 2. Of those that a mesh axis runs over, the one named last changes fastest.
Arguments:
- maps: bfloat16 [64, 4, 32, 32, 256], P(('wide', 'tp')), may hold values from -6 to 6
- roi_image: int32 [8192], P(('wide', 'tp')), may hold values from 0 to 1
- roi_level: int32 [8192], P(('wide', 'tp')), may hold values from 0 to 3
- roi_corner: int32 [8192, 2], P(('wide', 'tp')), may hold values from 0 to 16
- roi_weights: bfloat16 [8192, 2, 7, 16], P(('wide', 'tp')), may hold values from 0.049804688 to 0.5
- crowd: int32 [8192], P(('wide', 'tp')), may hold values from 0 to 1
- labels: int32 [8192], P(('wide', 'tp')), may hold values from 0 to 80
- box_targets: bfloat16 [8192, 4], P(('wide', 'tp')), may hold values from -5 to 5
- w_first: float32 [12544, 1024], P('wide', 'tp'), may hold values from -0.0546875 to 0.0546875
- m_first: float32 [12544, 1024], P('wide', 'tp'), may hold values from -0.0009765625 to 0.0009765625
- v_first: float32 [12544, 1024], P('wide', 'tp'), may hold values from 1.5869141e-10 to 2.4414062e-09
- w_second: float32 [1024, 1024], P('tp', 'wide'), may hold values from -0.1875 to 0.1875
- m_second: float32 [1024, 1024], P('tp', 'wide'), may hold values from -0.0009765625 to 0.0009765625
- v_second: float32 [1024, 1024], P('tp', 'wide'), may hold values from 1.5869141e-10 to 2.4414062e-09
- w_heads: float32 [1024, 401], P(('wide', 'tp')), may hold values from -0.375 to 0.375
- m_heads: float32 [1024, 401], P(('wide', 'tp')), may hold values from -0.0009765625 to 0.0009765625
- v_heads: float32 [1024, 401], P(('wide', 'tp')), may hold values from 1.5869141e-10 to 2.4414062e-09
- biases: float32 [2449], replicated, may hold values from -3 to 3
- bias_m: float32 [2449], replicated, may hold values from -0.0009765625 to 0.0009765625
- bias_v: float32 [2449], replicated, may hold values from 1.5869141e-10 to 2.4414062e-09
Outputs:
- loss_total: float32 [], replicated
- roi_count: float32 [], replicated
- first_new: float32 [12544, 1024], P('wide', 'tp')
- first_moment: float32 [12544, 1024], P('wide', 'tp')
- first_second: float32 [12544, 1024], P('wide', 'tp')
- second_new: float32 [1024, 1024], P('tp', 'wide')
- second_moment: float32 [1024, 1024], P('tp', 'wide')
- second_second: float32 [1024, 1024], P('tp', 'wide')
- heads_new: float32 [1024, 401], P(('wide', 'tp'))
- heads_moment: float32 [1024, 401], P(('wide', 'tp'))
- heads_second: float32 [1024, 401], P(('wide', 'tp'))
- biases_new: float32 [2449], replicated
- biases_moment: float32 [2449], replicated
- biases_second: float32 [2449], replicated
All inputs are finite; a program needn't handle non-finite values.
Results may differ from a plain program's by a relative error of at most 0.019.
Values may be sent and summed in bfloat16 or wider, within the bound.
No kernel may reach another device: no remote copies, remote signals or barrier semaphores. Data moves between devices by JAX's collectives and lax.ppermute only.
A program may use at most 192 MiB of HBM per device.

v0:
```python
import jax
import jax.numpy as jnp
from jax import lax
from jax.sharding import PartitionSpec as P

HID = 1024
CLS = 81
WIN = 16
MICRO = 4
STEP = 10
BOX = 320
HEAD = 401


highest = lax.Precision.HIGHEST
rate_first = 0.02
rate_second = 0.06
rate_heads = 0.06
rate_biases = 0.3
decay_one = 0.9
decay_two = 0.999
epsilon = 1e-08
weight_decay = 0.1


def window_crops(maps, image, level, corner, weights):
    channels = maps.shape[4]

    def single_window(img, lev, row_at, col_at):
        zero = jnp.zeros((), jnp.int32)
        return lax.dynamic_slice(
            maps, (img, lev, row_at, col_at, zero), (1, 1, WIN, WIN, channels)
        )[0, 0]

    windows = jax.vmap(single_window)(image, level, corner[:, 0], corner[:, 1])
    partial_rows = jnp.einsum(
        "rau,ruvc->ravc", weights[:, 0], windows, preferred_element_type=jnp.float32
    )
    pooled = jnp.einsum(
        "rbv,ravc->rabc", weights[:, 1].astype(jnp.float32), partial_rows, precision=highest
    )
    return pooled.reshape(pooled.shape[0], -1).astype(jnp.bfloat16)


def head_terms(outputs, tags, roi_count):
    logits = outputs[:, :CLS]
    boxes = outputs[:, CLS:].reshape(-1, CLS - 1, 4)
    targets = tags[:, :4].astype(jnp.float32)
    label_ids = tags[:, 4].astype(jnp.int32)
    valid_rows = 1.0 - tags[:, 5].astype(jnp.float32)
    classes = jnp.arange(CLS, dtype=jnp.int32)
    onehot = (label_ids[:, None] == classes[None, :]).astype(jnp.float32)
    row_max = jnp.max(logits, axis=1, keepdims=True)
    shifted = jnp.exp(logits - row_max)
    exp_total = jnp.sum(shifted, axis=1, keepdims=True)
    log_total = jnp.log(exp_total[:, 0]) + row_max[:, 0]
    cross_entropy = log_total - jnp.sum(onehot * logits, axis=1)
    foreground = valid_rows * (label_ids > 0).astype(jnp.float32)
    class_select = onehot[:, 1:]
    box_error = jnp.sum(class_select[:, :, None] * boxes, axis=1) - targets
    magnitude = jnp.abs(box_error)
    smooth_loss = jnp.sum(
        jnp.where(magnitude < 1.0, 0.5 * box_error * box_error, magnitude - 0.5), axis=1
    )
    row_loss = valid_rows * cross_entropy + foreground * smooth_loss
    grad_logits = (shifted / exp_total - onehot) * (valid_rows / roi_count)[:, None]
    grad_boxes = class_select[:, :, None] * jnp.clip(box_error, -1.0, 1.0)[:, None, :]
    grad_boxes = grad_boxes * (foreground / roi_count)[:, None, None]
    grad_out = jnp.concatenate([grad_logits, grad_boxes.reshape(-1, BOX)], axis=1)
    return (row_loss, grad_out.astype(jnp.bfloat16))


def adam_update(weight, grad, first, second, rate):
    first_new = decay_one * first + (1.0 - decay_one) * grad
    second_new = decay_two * second + (1.0 - decay_two) * grad * grad
    first_hat = first_new / (1.0 - decay_one**STEP)
    second_hat = second_new / (1.0 - decay_two**STEP)
    weight_new = weight - rate * (
        first_hat / (jnp.sqrt(second_hat) + epsilon) + weight_decay * weight
    )
    return (weight_new, first_new, second_new)


def shards(
    maps,
    roi_image,
    roi_level,
    roi_corner,
    roi_weights,
    crowd,
    labels,
    box_targets,
    w_first,
    m_first,
    v_first,
    w_second,
    m_second,
    v_second,
    w_heads,
    m_heads,
    v_heads,
    biases,
    bias_m,
    bias_v,
):
    tp_size = lax.axis_size("tp")
    tp_index = lax.axis_index("tp")
    unit_share = HID // tp_size
    first_rows, second_cols = (
        lax.all_gather(w_first.astype(jnp.bfloat16), "wide", axis=0, tiled=True),
        lax.all_gather(w_second.astype(jnp.bfloat16), "wide", axis=1, tiled=True),
    )
    head_matrix = lax.all_gather(w_heads.astype(jnp.bfloat16), ("wide", "tp"), axis=0, tiled=True)
    first_bias = biases[:HID]
    second_bias = biases[HID : 2 * HID]
    head_bias = biases[2 * HID :]
    bias_local = lax.dynamic_slice_in_dim(first_bias, tp_index * unit_share, unit_share, 0)
    unit_groups = second_cols.shape[0] // unit_share
    roi_count = lax.psum(jnp.sum(1.0 - crowd.astype(jnp.float32)), ("wide", "tp"))
    rows_micro = crowd.shape[0] // MICRO
    tags_all = jnp.concatenate(
        [box_targets, labels[:, None].astype(jnp.bfloat16), crowd[:, None].astype(jnp.bfloat16)],
        axis=1,
    )
    weights_grouped = second_cols.reshape(unit_groups, unit_share, HID)
    grad_first = jnp.zeros(first_rows.shape, jnp.float32)
    grad_second = jnp.zeros(weights_grouped.shape, jnp.float32)
    grad_heads = jnp.zeros(head_matrix.shape, jnp.float32)
    grad_first_bias = jnp.zeros((first_rows.shape[1],), jnp.float32)
    grad_second_bias = jnp.zeros((HID,), jnp.float32)
    grad_head_bias = jnp.zeros((HEAD,), jnp.float32)
    loss_sum = jnp.zeros((), jnp.float32)
    for micro_index in range(MICRO):
        begin = micro_index * rows_micro
        crops = window_crops(
            maps,
            roi_image[begin : begin + rows_micro],
            roi_level[begin : begin + rows_micro],
            roi_corner[begin : begin + rows_micro],
            roi_weights[begin : begin + rows_micro],
        )
        tags = tags_all[begin : begin + rows_micro]
        crops, tags = (
            lax.all_gather(crops, "tp", axis=0, tiled=True),
            lax.all_gather(tags, "tp", axis=0, tiled=True),
        )
        own_start = tp_index * rows_micro
        row_total = crops.shape[0]
        pre_first = jnp.dot(crops, first_rows, preferred_element_type=jnp.float32) + bias_local
        hidden_first, gelu_first = jax.vjp(jax.nn.gelu, pre_first)
        hidden_first = hidden_first.astype(jnp.bfloat16)
        grouped = hidden_first.reshape(row_total, unit_groups, unit_share)
        parts = jnp.einsum(
            "rgk,gkh->rgh", grouped, weights_grouped, preferred_element_type=jnp.float32
        )
        summed = lax.psum(parts[:, 0].astype(jnp.bfloat16), "tp").astype(jnp.float32)
        pre_second = summed + second_bias
        hidden_second, gelu_second = jax.vjp(jax.nn.gelu, pre_second)
        hidden_second = hidden_second.astype(jnp.bfloat16)
        outputs = (
            jnp.dot(hidden_second, head_matrix, preferred_element_type=jnp.float32) + head_bias
        )
        row_loss, grad_out = head_terms(outputs, tags, roi_count)
        grad_hidden_second = jnp.einsum(
            "rh,kh->rk", grad_out, head_matrix, preferred_element_type=jnp.float32
        )
        grad_pre_second = gelu_second(grad_hidden_second)[0].astype(jnp.bfloat16)
        own_hidden = lax.dynamic_slice_in_dim(hidden_second, own_start, rows_micro, 0)
        own_grad_out = lax.dynamic_slice_in_dim(grad_out, own_start, rows_micro, 0)
        own_grad_second = lax.dynamic_slice_in_dim(grad_pre_second, own_start, rows_micro, 0)
        grad_heads = grad_heads + jnp.einsum(
            "rk,rh->kh", own_hidden, own_grad_out, preferred_element_type=jnp.float32
        )
        grad_head_bias = grad_head_bias + jnp.sum(own_grad_out.astype(jnp.float32), axis=0)
        grad_second_bias = grad_second_bias + jnp.sum(own_grad_second.astype(jnp.float32), axis=0)
        loss_sum = loss_sum + jnp.sum(lax.dynamic_slice_in_dim(row_loss, own_start, rows_micro, 0))
        grad_hidden_first = jnp.einsum(
            "rh,gkh->rgk", grad_pre_second, weights_grouped, preferred_element_type=jnp.float32
        ).reshape(row_total, -1)
        grad_second = grad_second + jnp.einsum(
            "rgk,rh->gkh", grouped, grad_pre_second, preferred_element_type=jnp.float32
        )
        grad_pre_first = gelu_first(grad_hidden_first)[0].astype(jnp.bfloat16)
        grad_first = grad_first + jnp.einsum(
            "rf,rk->fk", crops, grad_pre_first, preferred_element_type=jnp.float32
        )
        grad_first_bias = grad_first_bias + jnp.sum(grad_pre_first.astype(jnp.float32), axis=0)
    grad_second = grad_second.reshape(-1, HID)
    first_bias_full = lax.dynamic_update_slice_in_dim(
        jnp.zeros((HID,), jnp.float32), grad_first_bias, tp_index * unit_share, 0
    )
    grad_first, grad_second = (
        lax.psum_scatter(
            grad_first.astype(jnp.bfloat16), "wide", scatter_dimension=0, tiled=True
        ).astype(jnp.float32),
        lax.psum_scatter(
            grad_second.astype(jnp.bfloat16), "wide", scatter_dimension=1, tiled=True
        ).astype(jnp.float32),
    )
    grad_heads = lax.psum_scatter(grad_heads, ("wide", "tp"), scatter_dimension=0, tiled=True)
    bias_grad = jnp.concatenate([first_bias_full, grad_second_bias, grad_head_bias])
    loss_total, bias_grad = lax.psum((loss_sum, bias_grad), ("wide", "tp"))
    first_out = adam_update(w_first, grad_first, m_first, v_first, rate_first)
    second_out = adam_update(w_second, grad_second, m_second, v_second, rate_second)
    heads_out = adam_update(w_heads, grad_heads, m_heads, v_heads, rate_heads)
    bias_out = adam_update(biases, bias_grad, bias_m, bias_v, rate_biases)
    return (
        loss_total,
        roi_count,
        first_out[0],
        first_out[1],
        first_out[2],
        second_out[0],
        second_out[1],
        second_out[2],
        heads_out[0],
        heads_out[1],
        heads_out[2],
        bias_out[0],
        bias_out[1],
        bias_out[2],
    )


def solution(mesh):
    return jax.shard_map(
        shards,
        mesh=mesh,
        in_specs=(
            P(("wide", "tp"), None, None, None, None),
            P(("wide", "tp")),
            P(("wide", "tp")),
            P(("wide", "tp"), None),
            P(("wide", "tp"), None, None, None),
            P(("wide", "tp")),
            P(("wide", "tp")),
            P(("wide", "tp"), None),
            P("wide", "tp"),
            P("wide", "tp"),
            P("wide", "tp"),
            P("tp", "wide"),
            P("tp", "wide"),
            P("tp", "wide"),
            P(("wide", "tp"), None),
            P(("wide", "tp"), None),
            P(("wide", "tp"), None),
            P(),
            P(),
            P(),
        ),
        out_specs=(
            P(),
            P(),
            P("wide", "tp"),
            P("wide", "tp"),
            P("wide", "tp"),
            P("tp", "wide"),
            P("tp", "wide"),
            P("tp", "wide"),
            P(("wide", "tp"), None),
            P(("wide", "tp"), None),
            P(("wide", "tp"), None),
            P(),
            P(),
            P(),
        ),
        check_vma=False,
    )
```

profile of v0, /device:TPU:0, one launch (start us, length us, event | category | flops | bytes accessed | tf_op | source)
XLA Modules:
  0.0 839.5 jit_solution(13341429466751522030)
XLA Ops:
  9.0 8.1 copy.55
  17.9 20.6 %gather_fusion.3 = bf16[64,16,16,256]{3,0,2,1:T(8,128)(2,1)} fusion(bf16[2,4,32,32,256]{4,1,0,3,2:T(4,128)(2,1)} %copy.55, s32[64]{0:T(128)S(1)} %get-tuple-element.82), kind=kCustom, calls=%fused_computation.3 | custom fusion | bytes 16778496 | tf_op jit(solution)/shard_map/vmap()/gather | solution.py:31
  38.6 19.2 %fusion.26 = f32[64,7,16,256]{3,1,2,0:T(8,128)S(1)} fusion(bf16[64,16,16,256]{3,0,2,1:T(8,128)(2,1)} %gather_fusion.3, bf16[64,1,7,16]{3,2,0,1:T(8,128)(2,1)S(1)} %copy.94), kind=kOutput, calls=%fused_computation.27 | convolution fusion | flops 58720256 | bytes 15742976 | tf_op jit(solution)/shard_map/rau,ruvc->ravc/dot_general | solution.py:36
  57.7 4.8 convert_bitcast_fusion
  62.5 2.6 convert_element_type.331
  67.2 20.9 %gather_fusion.2 = bf16[64,16,16,256]{3,0,2,1:T(8,128)(2,1)} fusion(bf16[2,4,32,32,256]{4,1,0,3,2:T(4,128)(2,1)} %copy.55, s32[64]{0:T(128)S(1)} %get-tuple-element.85), kind=kCustom, calls=%fused_computation.2 | custom fusion | bytes 16778496 | tf_op jit(solution)/shard_map/vmap()/gather | solution.py:31
  88.3 19.1 %fusion.23 = f32[64,7,16,256]{3,1,2,0:T(8,128)S(1)} fusion(bf16[64,16,16,256]{3,0,2,1:T(8,128)(2,1)} %gather_fusion.2, bf16[64,1,7,16]{3,2,0,1:T(8,128)(2,1)S(1)} %copy.92), kind=kOutput, calls=%fused_computation.26 | convolution fusion | flops 58720256 | bytes 15742976 | tf_op jit(solution)/shard_map/rau,ruvc->ravc/dot_general | solution.py:36
  107.4 4.8 convert_bitcast_fusion.1
  112.2 2.6 convert_element_type.320
  115.1 20.5 %gather_fusion.1 = bf16[64,16,16,256]{3,0,2,1:T(8,128)(2,1)} fusion(bf16[2,4,32,32,256]{4,1,0,3,2:T(4,128)(2,1)} %copy.55, s32[64]{0:T(128)S(1)} %get-tuple-element.84), kind=kCustom, calls=%fused_computation.1 | custom fusion | bytes 16778496 | tf_op jit(solution)/shard_map/vmap()/gather | solution.py:31
  135.7 19.1 %fusion.20 = f32[64,7,16,256]{3,1,2,0:T(8,128)S(1)} fusion(bf16[64,16,16,256]{3,0,2,1:T(8,128)(2,1)} %gather_fusion.1, bf16[64,1,7,16]{3,2,0,1:T(8,128)(2,1)S(1)} %copy.90), kind=kOutput, calls=%fused_computation.25 | convolution fusion | flops 58720256 | bytes 15742976 | tf_op jit(solution)/shard_map/rau,ruvc->ravc/dot_general | solution.py:36
  154.9 4.8 convert_bitcast_fusion.2
  159.6 2.6 convert_element_type.309
  162.5 20.7 %gather_fusion = bf16[64,16,16,256]{3,0,2,1:T(8,128)(2,1)} fusion(bf16[2,4,32,32,256]{4,1,0,3,2:T(4,128)(2,1)} %copy.55, s32[64]{0:T(128)S(1)} %get-tuple-element.83), kind=kCustom, calls=%fused_computation | custom fusion | bytes 16778496 | tf_op jit(solution)/shard_map/vmap()/gather | solution.py:31
  183.3 19.1 %fusion.17 = f32[64,7,16,256]{3,1,2,0:T(8,128)S(1)} fusion(bf16[64,16,16,256]{3,0,2,1:T(8,128)(2,1)} %gather_fusion, bf16[64,1,7,16]{3,2,0,1:T(8,128)(2,1)S(1)} %copy.88), kind=kOutput, calls=%fused_computation.24 | convolution fusion | flops 58720256 | bytes 15742976 | tf_op jit(solution)/shard_map/rau,ruvc->ravc/dot_general | solution.py:36
  202.4 4.8 convert_bitcast_fusion.3
  207.2 2.6 convert_element_type.295
  210.6 42.2 %psum.54 = f32[]{:T(128)} all-reduce(f32[]{:T(128)} %subtract_reduce_fusion), channel_id=1, replica_groups=mesh['wide'=8,'tp'=4] {'wide','tp'}, use_global_device_ids=true, to_apply=%region_30.31 | all-reduce | flops 1 | bytes 8 | tf_op jit(solution)/shard_map/psum | solution.py:119
  253.0 5.6 all-gather.1
  258.7 5.4 all-gather
  265.5 5.2 all-gather.2
  270.7 5.3 all-gather.3
  278.1 27.6 %all_gather.36 = bf16[256,1024]{1,0:T(8,128)(2,1)S(1)} all-gather(bf16[256,128]{1,0:T(8,128)(2,1)S(1)} %convert_element_type.298), channel_id=1, replica_groups=mesh['wide'=8,'tp'=4] {'wide'}, dimensions={1}, use_global_device_ids=true | all-gather | bytes 589824 | tf_op jit(solution)/shard_map/all_gather | solution.py:111
  305.7 6.6 convolution_add_fusion.10
  314.2 6.6 convolution_add_fusion.11
  322.6 8.1 convolution_add_fusion.12
  332.6 32.4 %all-gather.10.cloned.1.call-done = bf16[256,12544]{1,0:T(8,128)(2,1)} async-done(((bf16[64,12544]{1,0:T(8,128)(2,1)}), bf16[256,12544]{1,0:T(8,128)(2,1)}) %all-gather.10.cloned.1.call-update) | async-done | bytes 6422544 | tf_op jit(solution)/shard_map/all_gather | solution.py:144
  365.0 6.6 convolution_add_fusion.13
  377.2 44.2 %all_gather.37 = bf16[1024,401]{1,0:T(8,128)(2,1)S(1)} all-gather(bf16[32,401]{1,0:T(8,128)(2,1)S(1)} %convert_element_type.302), channel_id=1, replica_groups=mesh['wide'=8,'tp'=4] {'wide','tp'}, dimensions={0}, use_global_device_ids=true | all-gather | bytes 846912 | tf_op jit(solution)/shard_map/all_gather | solution.py:113
  421.5 12.8 %all-reduce.4.cloned.1.call-done = (bf16[256,1024]{1,0:T(8,128)(2,1)}, bf16[256,1024]{1,0:T(8,128)(2,1)}, bf16[256,1024]{1,0:T(8,128)(2,1)}, bf16[256,1024]{1,0:T(8,128)(2,1)}) async-done(((bf16[256,1024]{1,0:T(8,128)(2,1)}, bf16[256,1024]{1,0:T(8,128)(2,1)}, bf16[256,1024]{1,0:T(8,128)(2,1)}, bf16[256,1024]{1,0:T(8,128)(2,1)}), (bf16[256,1024]{1,0:T(8,128)(2,1)}, bf16[256,1024]{1,0:T(8,128)(2,1)}, ...) | async-done | bytes 2097168 | tf_op jit(solution)/shard_map/psum | solution.py:156
  434.2 3.1 multiply_convert_fusion
  459.8 1.9 select_divide_fusion.3
  462.7 2.1 fusion.46
  464.8 3.0 fusion.127
  470.1 1.9 fusion.125
  491.8 2.8 convert_reduce_fusion.6
  500.4 1.9 select_divide_fusion
  509.7 2.1 convert_reduce_fusion.5
  511.8 2.6 convert_reduce_fusion.4
  514.4 4.2 add_add_fusion
  518.7 4.9 fusion.232
  523.7 6.7 convolution_add_fusion.2
  530.3 8.5 %convolution_add_fusion.1 = f32[12544,256]{1,0:T(8,128)S(1)} fusion(f32[12544,256]{1,0:T(8,128)} %convolution_add_fusion.2, bf16[256,12544]{1,0:T(8,128)(2,1)} %all-gather.16.cloned.1.call-done, bf16[256,256]{1,0:T(8,128)(2,1)S(1)} %get-tuple-element.45), kind=kOutput, calls=%fused_computation.6 | convolution fusion | flops 1647378432 | bytes 32243712 | tf_op jit(solution)/shard_map/rf,rk->fk/dot_general | solution.py:184
  538.8 7.6 fusion
  563.4 39.3 %all-reduce = (f32[]{:T(128)}, f32[2449]{0:T(1024)S(1)}) all-reduce(f32[]{:T(128)S(6)} %add.445, f32[2449]{0:T(1024)S(1)} %pad_maximum_fusion.16), channel_id=1, replica_groups=mesh['wide'=8,'tp'=4] {'wide','tp'}, use_global_device_ids=true, to_apply=%region_28.29 | all-reduce | flops 2450 | bytes 19600 | tf_op jit(solution)/shard_map/psum | solution.py:202
  606.8 101.2 %reduce-scatter.8.cloned.1.call-done = f32[32,401]{1,0:T(8,128)} async-done(((f32[1024,401]{1,0:T(8,128)}), f32[32,401]{1,0:T(8,128)}) %reduce-scatter.8.cloned.1.call-update) | async-done | bytes 51344 | tf_op jit(solution)/shard_map/reduce_scatter | solution.py:200
  709.7 118.2 %reduce-scatter.6.cloned.1.call-done = bf16[1568,256]{1,0:T(8,128)(2,1)} async-done(((bf16[12544,256]{1,0:T(8,128)(2,1)}), bf16[1568,256]{1,0:T(8,128)(2,1)}) %reduce-scatter.6.cloned.1.call-update) | async-done | bytes 802832 | tf_op jit(solution)/shard_map/reduce_scatter | solution.py:193
  827.8 4.7 multiply_subtract_fusion
  (314 shorter events, 99.2 us)
Async XLA Ops:
  7.2 298.5 %all-gather.18.cloned.1.call-start = ((), (), s32[]{:S(2)}) async-start(), calls=%async_computation.7 | async-start | bytes 8028160 | tf_op jit(solution)/shard_map/all_gather | solution.py:144
  38.6 19.2 %copy-start.23 = (bf16[64,1,7,16]{3,2,0,1:T(8,128)(2,1)S(1)}, bf16[64,1,7,16]{3,2,0,1:T(8,128)(2,1)}, u32[]{:S(2)}) copy-start(bf16[64,1,7,16]{3,2,0,1:T(8,128)(2,1)} %copy.95) | copy-start | bytes 43012
  65.2 240.5 %all-gather.12.cloned.1.call-start = ((), (), s32[]{:S(2)}) async-start(), calls=%async_computation.4 | async-start | bytes 7225344 | tf_op jit(solution)/shard_map/all_gather | solution.py:110
  66.3 247.9 %all-gather.16.cloned.1.call-start = ((), (), s32[]{:S(2)}) async-start(), calls=%async_computation.6 | async-start | bytes 8028160 | tf_op jit(solution)/shard_map/all_gather | solution.py:144
  67.2 20.9 %copy-start.36 = (bf16[64,1,7,16]{0,3,2,1:T(8,128)(2,1)S(1)}, bf16[64,1,7,16]{0,3,2,1:T(8,128)(2,1)}, u32[]{:S(2)}) copy-start(bf16[64,1,7,16]{0,3,2,1:T(8,128)(2,1)} %get-tuple-element.50) | copy-start | bytes 43012
  114.9 207.8 %all-gather.14.cloned.1.call-start = ((), (), s32[]{:S(2)}) async-start(), calls=%async_computation.5 | async-start | bytes 8028160 | tf_op jit(solution)/shard_map/all_gather | solution.py:144
  162.3 202.7 %all-gather.10.cloned.1.call-start = ((), (), s32[]{:S(2)}) async-start(), calls=%async_computation.3 | async-start | bytes 8028160 | tf_op jit(solution)/shard_map/all_gather | solution.py:144
  202.4 50.4 %copy-start.27 = (f32[256,128]{1,0:T(8,128)S(1)}, f32[256,128]{1,0:T(8,128)}, u32[]{:S(2)}) copy-start(f32[256,128]{1,0:T(8,128)} %param.31) | copy-start | bytes 393220
  202.4 50.4 %copy-start.32 = (f32[32,401]{1,0:T(8,128)S(1)}, f32[32,401]{1,0:T(8,128)}, u32[]{:S(2)}) copy-start(f32[32,401]{1,0:T(8,128)} %param.34) | copy-start | bytes 153988
  202.4 50.5 %copy-start.38 = (f32[2449]{0:T(1024)S(1)}, f32[2449]{0:T(1024)}, u32[]{:S(2)}) copy-start(f32[2449]{0:T(1024)} %param.37) | copy-start | bytes 29392
  202.4 50.5 %copy-start.78 = (s32[256]{0:T(256)S(1)}, s32[256]{0:T(256)}, u32[]{:S(2)}) copy-start(s32[256]{0:T(256)} %param.26) | copy-start | bytes 3076
  202.4 50.5 %copy-start.75 = (bf16[256,4]{0,1:T(4,128)(2,1)S(1)}, bf16[256,4]{0,1:T(4,128)(2,1)}, u32[]{:S(2)}) copy-start(bf16[256,4]{0,1:T(4,128)(2,1)} %param.27) | copy-start | bytes 6148
  209.9 224.3 %all-reduce.4.cloned.1.call-start = ((), (), s32[]{:S(2)}) async-start(), calls=%async_computation.11 | async-start | bytes 4194304 | tf_op jit(solution)/shard_map/psum | solution.py:156
  252.9 185.9 %copy-start.37 = (f32[401]{0:T(512)}, f32[401]{0:T(512)S(1)}, u32[]{:S(2)}) copy-start(f32[401]{0:T(512)S(1)} %slice.199) | copy-start | bytes 4816
  258.7 116.0 %copy-start.45 = (bf16[256,6]{0,1:T(8,128)(2,1)}, bf16[256,6]{0,1:T(8,128)(2,1)S(1)}, u32[]{:S(2)}) copy-start(bf16[256,6]{0,1:T(8,128)(2,1)S(1)} %reshape.314) | copy-start | bytes 9220
  264.2 110.5 %copy-start.44 = (bf16[256,6]{0,1:T(8,128)(2,1)}, bf16[256,6]{0,1:T(8,128)(2,1)S(1)}, u32[]{:S(2)}) copy-start(bf16[256,6]{0,1:T(8,128)(2,1)S(1)} %reshape.312) | copy-start | bytes 9220
  270.7 105.3 %copy-start.42 = (bf16[256,6]{0,1:T(8,128)(2,1)}, bf16[256,6]{0,1:T(8,128)(2,1)S(1)}, u32[]{:S(2)}) copy-start(bf16[256,6]{0,1:T(8,128)(2,1)S(1)} %reshape.316) | copy-start | bytes 9220
  276.1 99.8 %copy-start.40 = (bf16[256,6]{0,1:T(8,128)(2,1)}, bf16[256,6]{0,1:T(8,128)(2,1)S(1)}, u32[]{:S(2)}) copy-start(bf16[256,6]{0,1:T(8,128)(2,1)S(1)} %reshape.318) | copy-start | bytes 9220
  277.4 34.9 %copy-start.46 = (s32[256,1]{0,1:T(1,128)}, s32[256,1]{0,1:T(1,128)S(1)}, u32[]{:S(2)}) copy-start(s32[256,1]{0,1:T(1,128)S(1)} %slice_convert_fusion) | copy-start | bytes 3076
  278.0 156.2 %copy-start.58 = (f32[1024]{0:T(1024)}, f32[1024]{0:T(1024)S(1)}, u32[]{:S(2)}) copy-start(f32[1024]{0:T(1024)S(1)} %get-tuple-element.56) | copy-start | bytes 12292
  373.5 230.6 %reduce-scatter.10.cloned.1.call-start = ((), (), s32[]{:S(2)}) async-start(), calls=%async_computation.10 | async-start | bytes 589824
  437.3 16.4 %copy-start.2 = (bf16[256,1024]{1,0:T(8,128)(2,1)}, bf16[256,1024]{1,0:T(8,128)(2,1)S(1)}, u32[]{:S(2)}) copy-start(bf16[256,1024]{1,0:T(8,128)(2,1)S(1)} %get-tuple-element.79) | copy-start | bytes 1572868
  455.2 12.6 %copy-start.52 = (s32[256,1]{0,1:T(1,128)S(1)}, s32[256,1]{0,1:T(1,128)}, u32[]{:S(2)}) copy-start(s32[256,1]{0,1:T(1,128)} %copy-done.50) | copy-start | bytes 3076
  455.2 12.6 %copy-start.57 = (f32[256]{0:T(256)S(1)}, f32[256]{0:T(256)}, u32[]{:S(2)}) copy-start(f32[256]{0:T(256)} %copy-done.56) | copy-start | bytes 3076
  455.2 12.6 %copy-start.60 = (f32[256]{0:T(256)S(1)}, f32[256]{0:T(256)}, u32[]{:S(2)}) copy-start(f32[256]{0:T(256)} %get-tuple-element.18) | copy-start | bytes 3076
  455.2 12.6 %copy-start.64 = (f32[256,1]{0,1:T(1,128)S(1)}, f32[256,1]{0,1:T(1,128)}, u32[]{:S(2)}) copy-start(f32[256,1]{0,1:T(1,128)} %get-tuple-element.66) | copy-start | bytes 3076
  455.2 13.6 %copy-start.65 = (f32[256]{0:T(256)S(1)}, f32[256]{0:T(256)}, u32[]{:S(2)}) copy-start(f32[256]{0:T(256)} %get-tuple-element.19) | copy-start | bytes 3076
  455.2 13.6 %copy-start.70 = (f32[256,1]{0,1:T(1,128)S(1)}, f32[256,1]{0,1:T(1,128)}, u32[]{:S(2)}) copy-start(f32[256,1]{0,1:T(1,128)} %get-tuple-element.67) | copy-start | bytes 3076
  455.2 13.6 %copy-start.71 = (f32[256]{0:T(256)S(1)}, f32[256]{0:T(256)}, u32[]{:S(2)}) copy-start(f32[256]{0:T(256)} %get-tuple-element.59) | copy-start | bytes 3076
  455.2 13.6 %copy-start.74 = (pred[256]{0:T(512)(128)(4,1)S(1)}, pred[256]{0:T(512)(128)(4,1)}, u32[]{:S(2)}) copy-start(pred[256]{0:T(512)(128)(4,1)} %get-tuple-element.96) | copy-start | bytes 772
  455.3 14.8 %copy-start.11 = (f32[256,320]{0,1:T(8,128)S(1)}, f32[256,320]{0,1:T(8,128)}, u32[]{:S(2)}) copy-start(f32[256,320]{0,1:T(8,128)} %mul.799) | copy-start | bytes 983044
  459.7 12.3 %copy-start.29 = (bf16[256,81]{0,1:T(8,128)(2,1)}, bf16[256,81]{0,1:T(8,128)(2,1)S(1)}, u32[]{:S(2)}) copy-start(bf16[256,81]{0,1:T(8,128)(2,1)S(1)} %multiply_convert_fusion.15) | copy-start | bytes 124420
  472.0 11.2 %copy-start.47 = (s32[256,1]{0,1:T(1,128)S(1)}, s32[256,1]{0,1:T(1,128)}, u32[]{:S(2)}) copy-start(s32[256,1]{0,1:T(1,128)} %copy-done.46) | copy-start | bytes 3076
  472.0 15.6 %copy-start.41 = (bf16[256,6]{0,1:T(8,128)(2,1)S(1)}, bf16[256,6]{0,1:T(8,128)(2,1)}, u32[]{:S(2)}) copy-start(bf16[256,6]{0,1:T(8,128)(2,1)} %copy-done.40) | copy-start | bytes 9220
  474.3 21.9 %copy-start.63 = (f32[256,1]{0,1:T(1,128)S(1)}, f32[256,1]{0,1:T(1,128)}, u32[]{:S(2)}) copy-start(f32[256,1]{0,1:T(1,128)} %get-tuple-element.99) | copy-start | bytes 3076
  474.3 22.8 %copy-start.69 = (f32[256,1]{0,1:T(1,128)S(1)}, f32[256,1]{0,1:T(1,128)}, u32[]{:S(2)}) copy-start(f32[256,1]{0,1:T(1,128)} %get-tuple-element.98) | copy-start | bytes 3076
  474.3 22.8 %copy-start.73 = (pred[256]{0:T(512)(128)(4,1)S(1)}, pred[256]{0:T(512)(128)(4,1)}, u32[]{:S(2)}) copy-start(pred[256]{0:T(512)(128)(4,1)} %get-tuple-element.95) | copy-start | bytes 772
  474.3 25.0 %copy-start.62 = (f32[256,1]{0,1:T(1,128)S(1)}, f32[256,1]{0,1:T(1,128)}, u32[]{:S(2)}) copy-start(f32[256,1]{0,1:T(1,128)} %get-tuple-element.72) | copy-start | bytes 3076
  488.3 12.1 %copy-start.66 = (f32[256]{0:T(256)S(1)}, f32[256]{0:T(256)}, u32[]{:S(2)}) copy-start(f32[256]{0:T(256)} %get-tuple-element.15) | copy-start | bytes 3076
  491.7 11.5 %copy-start.25 = (bf16[256,1024]{1,0:T(8,128)(2,1)S(1)}, bf16[256,1024]{1,0:T(8,128)(2,1)}, u32[]{:S(2)}) copy-start(bf16[256,1024]{1,0:T(8,128)(2,1)} %get-tuple-element.26) | copy-start | bytes 1572868
  491.8 12.8 %copy-start.17 = (f32[256,256]{1,0:T(8,128)S(1)}, f32[256,256]{1,0:T(8,128)}, u32[]{:S(2)}) copy-start(f32[256,256]{1,0:T(8,128)} %copy-done.16) | copy-start | bytes 786436
  500.3 14.1 %copy-start.28 = (bf16[256,81]{0,1:T(8,128)(2,1)}, bf16[256,81]{0,1:T(8,128)(2,1)S(1)}, u32[]{:S(2)}) copy-start(bf16[256,81]{0,1:T(8,128)(2,1)S(1)} %multiply_convert_fusion.12) | copy-start | bytes 124420
  508.2 199.8 %reduce-scatter.8.cloned.1.call-start = ((), (), s32[]{:S(2)}) async-start(), calls=%async_computation.9 | async-start | bytes 2162688 | tf_op jit(solution)/shard_map/reduce_scatter | solution.py:200
  518.7 309.2 %reduce-scatter.6.cloned.1.call-start = ((), (), s32[]{:S(2)}) async-start(), calls=%async_computation.8 | async-start | bytes 7225344 | tf_op jit(solution)/shard_map/reduce_scatter | solution.py:193
  546.4 15.5 %copy-start.76 = (f32[256]{0:T(256)S(1)}, f32[256]{0:T(256)}, u32[]{:S(2)}) copy-start(f32[256]{0:T(256)} %get-tuple-element.42) | copy-start | bytes 3076
  546.4 56.2 %copy-start.39 = (f32[2449]{0:T(1024)S(1)}, f32[2449]{0:T(1024)}, u32[]{:S(2)}) copy-start(f32[2449]{0:T(1024)} %param.37) | copy-start | bytes 29392
  546.4 281.4 %copy-start.1 = (f32[1568,256]{1,0:T(8,128)S(1)}, f32[1568,256]{1,0:T(8,128)}, u32[]{:S(2)}) copy-start(f32[1568,256]{1,0:T(8,128)} %param.28) | copy-start | bytes 4816900
  546.4 281.4 %copy-start.8 = (f32[1568,256]{1,0:T(8,128)S(1)}, f32[1568,256]{1,0:T(8,128)}, u32[]{:S(2)}) copy-start(f32[1568,256]{1,0:T(8,128)} %param.29) | copy-start | bytes 4816900
  (42 other events, 242.3 us)
Sparse Core Ops, SparseCore 0:
  65.3 50.2 all-gather.17
  117.8 100.6 all-gather.11
  220.6 46.1 all-gather.15
  268.7 47.1 all-gather.13
  317.9 47.1 all-gather.9
  373.6 60.5 all-reduce.3
  508.3 61.6 reduce-scatter.9
  572.3 135.7 reduce-scatter.7
  712.1 115.7 reduce-scatter.5
where the time goes:
time: 846 us; the launch traced here: 839 us
  waiting for transfers between devices  265 us (31%)
  matrix products  188 us (22%)
  blocking collectives  175 us (21%)
  local copies, waits for them, and re-layouts  130 us (15%)
  other arithmetic  64 us (8%)
  between operations  18.1 us (2%)
    reduce_scatter x1, waiting for transfers between devices, shards(): lax.psum_scatter(grad_first.astype(jnp.bfloat16), 'wide', scatter_dimensi...  118 us
    reduce_scatter x1, waiting for transfers between devices, shards(): lax.psum_scatter(grad_heads, ('wide', 'tp'), scatter_dimension=0, tiled=T...  101 us
    gather x4, local copies, waits for them, and re-layouts, single_window(): lax.dynamic_slice(maps, (img, lev, row_at, col_at, zero), (1, 1, WIN, WIN...  82.7 us
    dot_general x4, matrix products, window_crops(): jnp.einsum('rau,ruvc->ravc', weights[:, 0], windows, preferred_element_ty...  76.5 us
    all_gather x1, blocking collectives, shards(): lax.all_gather(w_heads.astype(jnp.bfloat16), ('wide', 'tp'), axis=0, tile...  44.2 us
    psum x1, blocking collectives, shards(): lax.psum(jnp.sum(1.0 - crowd.astype(jnp.float32)), ('wide', 'tp'))  42.2 us
    psum x1, blocking collectives, shards(): loss_total, bias_grad = lax.psum((loss_sum, bias_grad), ('wide', 'tp'))  39.3 us
    all_gather x4, waiting for transfers between devices, shards(): lax.all_gather(crops, 'tp', axis=0, tiled=True)  32.5 us
  transfers between devices with their start and end apart: 9, of which 4 were waited for; matrix products, arithmetic and copies ran while one was open for 28% of the time, Pallas kernels for 0%

commit v1 on v0

v1 whole, which is shorter than its diff:
```python
import functools

import jax
import jax.numpy as jnp
import numpy as np
from jax import lax
from jax.experimental import pallas as pl
from jax.experimental.pallas import tpu as pltpu
from jax.sharding import PartitionSpec as P

HID = 1024
CLS = 81
POOL = 7
CELLS = POOL * POOL
WIN = 16
STEP = 10
HEAD = 401
HEADP = 512
CORES = 2
CHUNKS = 4
GROUP = 32
KSTEP = 7
MIB = 2**20

AXES = ("wide", "tp")
rate_first = 0.02
rate_second = 0.06
rate_heads = 0.06
rate_biases = 0.3
decay_one = 0.9
decay_two = 0.999
epsilon = 1e-08
weight_decay = 0.1
GELU_A = 0.7978845608028654
GELU_B = 0.044715

f32 = jnp.float32
bf16 = jnp.bfloat16


def dot(a, b, contract=((1,), (0,))):
    return lax.dot_general(a, b, (contract, ((), ())), preferred_element_type=f32)


def crop_kernel(base_ref, col_ref, maps_ref, wr_ref, wc_ref, rep_ref, tile_ref, out_ref, rows_s, cols_s, left, right):
    step = pl.program_id(0)
    lanes = rows_s.shape[1]
    halves = (left, right)
    rows_s[...] = dot(wr_ref[...], rep_ref[...])
    cols_s[...] = dot(wc_ref[...], tile_ref[...])

    def one(i, carry):
        r = step * GROUP + i
        at = pl.multiple_of(i * 8, 8)
        rows = rows_s[pl.ds(at, 8), :]
        x0 = col_ref[r]
        cols = jnp.concatenate(
            [pltpu.roll(cols_s[pl.ds(at, 8), k : k + 128], x0, 1) for k in range(0, lanes, 128)], axis=1
        )
        both = jnp.concatenate([rows[a : a + 1, :] * cols for a in range(POOL)], axis=0)
        high = both.astype(bf16)
        low = (both - high.astype(f32)).astype(bf16)
        window = maps_ref[pl.ds(base_ref[r], WIN), :, :].reshape(lanes, maps_ref.shape[2])
        got = dot(jnp.concatenate([high, low], axis=0), window)
        got = got[: POOL * 8] + got[POOL * 8 :]
        for h, half in enumerate(halves):
            half[pl.ds(pl.multiple_of(i * POOL * 8, 8), POOL * 8), :] = got[:, h * 128 : (h + 1) * 128]
        return carry

    lax.fori_loop(0, GROUP, one, 0, unroll=4)
    for a in range(POOL):
        for b in range(POOL):
            for h, half in enumerate(halves):
                out_ref[a * POOL + b, :, h * 128 : (h + 1) * 128] = half[
                    pl.ds(a * 8 + b, GROUP, stride=POOL * 8), :
                ].astype(bf16)


def window_crops(maps, base, col, wr, wc):
    count = base.shape[0]
    rows, width, channels = maps.shape
    lanes = WIN * width
    lane = np.arange(lanes)[None]
    unit = np.arange(WIN)[:, None]
    rep = jnp.asarray(lane // width == unit, bf16)
    til = jnp.asarray(lane % width == unit, bf16)
    return pl.pallas_call(
        crop_kernel,
        grid_spec=pltpu.PrefetchScalarGridSpec(
            num_scalar_prefetch=2,
            grid=(count // GROUP,),
            in_specs=[
                pl.BlockSpec(maps.shape, lambda i, *_: (0, 0, 0)),
                pl.BlockSpec((GROUP * 8, WIN), lambda i, *_: (i, 0)),
                pl.BlockSpec((GROUP * 8, WIN), lambda i, *_: (i, 0)),
                pl.BlockSpec(rep.shape, lambda i, *_: (0, 0)),
                pl.BlockSpec(til.shape, lambda i, *_: (0, 0)),
            ],
            out_specs=pl.BlockSpec((CELLS, GROUP, channels), lambda i, *_: (0, i, 0)),
            scratch_shapes=[
                pltpu.VMEM((GROUP * 8, lanes), f32),
                pltpu.VMEM((GROUP * 8, lanes), f32),
                pltpu.VMEM((GROUP * POOL * 8, 128), f32),
                pltpu.VMEM((GROUP * POOL * 8, 128), f32),
            ],
        ),
        out_shape=jax.ShapeDtypeStruct((CELLS, count, channels), bf16),
        compiler_params=pltpu.CompilerParams(vmem_limit_bytes=40 * MIB),
        cost_estimate=pl.CostEstimate(
            flops=2 * count * 112 * lanes * channels * 4, bytes_accessed=12 * MIB, transcendentals=0
        ),
        name="crops",
    )(base, col, maps, wr, wc, rep, til)


def first_kernel(parts, *refs):
    crops, weight, own, send = refs[:parts], refs[parts], refs[parts + 1], refs[parts + 2]
    step = pl.program_id(0)
    blocks, depth, cols = weight.shape
    channels = crops[0].shape[2]

    @pl.when(step == 0)
    def _():
        own[...] = jnp.zeros_like(own)
        send[...] = jnp.zeros_like(send)

    for out, refs_half in ((own, crops[: parts // 2]), (send, crops[parts // 2 :])):
        lhs = jnp.concatenate(
            [jnp.concatenate([ref[j] for ref in refs_half], axis=0) for j in range(depth // channels)], axis=1
        )
        for y in range(blocks):
            out[:, y * cols : (y + 1) * cols] += dot(lhs, weight[y])


def first_layer(crops, weight):
    parts = len(crops)
    blocks, feats, cols = weight.shape
    channels = crops[0].shape[2]
    rows = sum(c.shape[1] for c in crops) // 2
    return pl.pallas_call(
        functools.partial(first_kernel, parts),
        grid=(CELLS // KSTEP,),
        in_specs=[pl.BlockSpec((KSTEP,) + c.shape[1:], lambda i: (i, 0, 0)) for c in crops]
        + [pl.BlockSpec((blocks, KSTEP * channels, cols), lambda i: (0, i, 0))],
        out_specs=[pl.BlockSpec((rows, blocks * cols), lambda i: (0, 0))] * 2,
        out_shape=[jax.ShapeDtypeStruct((rows, blocks * cols), f32)] * 2,
        compiler_params=pltpu.CompilerParams(vmem_limit_bytes=40 * MIB),
        cost_estimate=pl.CostEstimate(
            flops=4 * rows * feats * blocks * cols, bytes_accessed=26 * MIB, transcendentals=0
        ),
        name="first_layer",
    )(*crops, weight)


def first_grad_kernel(parts, cols, *refs):
    crops, own, got, out = refs[:parts], refs[parts], refs[parts + 1], refs[parts + 2]
    channels = crops[0].shape[2]
    grads = jnp.concatenate([own[...], got[...]], axis=0)
    for j in range(crops[0].shape[0]):
        lhs = jnp.concatenate([ref[j] for ref in crops], axis=0)
        res = dot(lhs, grads, ((0,), (0,))).astype(bf16)
        for y in range(out.shape[0]):
            out[y, j * channels : (j + 1) * channels, :] = res[:, y * cols : (y + 1) * cols]


def first_grad(crops, own, got, blocks):
    parts = len(crops)
    rows, units = own.shape
    cols = units // blocks
    channels = crops[0].shape[2]
    return pl.pallas_call(
        functools.partial(first_grad_kernel, parts, cols),
        grid=(CELLS // KSTEP,),
        in_specs=[pl.BlockSpec((KSTEP,) + c.shape[1:], lambda i: (i, 0, 0)) for c in crops]
        + [pl.BlockSpec((rows, units), lambda i: (0, 0))] * 2,
        out_specs=pl.BlockSpec((blocks, KSTEP * channels, cols), lambda i: (0, i, 0)),
        out_shape=jax.ShapeDtypeStruct((blocks, CELLS * channels, cols), bf16),
        compiler_params=pltpu.CompilerParams(vmem_limit_bytes=40 * MIB),
        cost_estimate=pl.CostEstimate(
            flops=4 * rows * CELLS * channels * units, bytes_accessed=26 * MIB, transcendentals=0
        ),
        name="first_grad",
    )(*crops, own, got)


def gelu(x):
    return 0.5 * x * (1.0 + jnp.tanh(GELU_A * (x + GELU_B * x * x * x)))


def gelu_slope(x):
    t = jnp.tanh(GELU_A * (x + GELU_B * x * x * x))
    return 0.5 * (1.0 + t) + 0.5 * x * (1.0 - t * t) * (GELU_A * (1.0 + 3.0 * GELU_B * x * x))


def head_kernel(
    share,
    count_ref,
    pre_own,
    pre_sib,
    w2_own,
    w2_sib,
    wh,
    b1,
    b2,
    bh,
    labels,
    crowd,
    targets,
    g_own,
    g_sib,
    gw2_own,
    gw2_sib,
    gwh,
    gb1,
    gb2,
    gbh,
    loss,
    h1,
    pre2,
    gpre2,
):
    rows, units = pre_own.shape
    sides = ((pre_own, w2_own, g_own, gw2_own, 0), (pre_sib, w2_sib, g_sib, gw2_sib, units))
    pre2[...] = jnp.zeros_like(pre2) + b2[...]
    for pre, w2, _, _, at in sides:
        h1[:, at : at + units] = gelu(pre[...] + b1[:, at : at + units]).astype(bf16)
        for k in range(0, units, share):
            part = dot(h1[:, at + k : at + k + share], w2[k : k + share, :])
            pre2[...] += part.astype(bf16).astype(f32)
    h2 = gelu(pre2[...]).astype(bf16)
    out = dot(h2, wh[...]) + bh[...]
    col = lax.broadcasted_iota(jnp.int32, out.shape, 1)
    label = labels[...]
    valid = 1.0 - crowd[...].astype(f32)
    fore = jnp.where(label > 0, valid, 0.0)
    is_logit = col < CLS
    onehot = jnp.where(col == label, 1.0, 0.0)
    masked = jnp.where(is_logit, out, -jnp.inf)
    top = jnp.max(masked, axis=1, keepdims=True)
    shifted = jnp.exp(masked - top)
    total = jnp.sum(shifted, axis=1, keepdims=True)
    row_loss = valid * (jnp.log(total) + top - jnp.sum(onehot * out, axis=1, keepdims=True))
    scale = 1.0 / count_ref[0, 0]
    grad = (shifted / total - onehot) * (valid * scale)
    base = CLS + 4 * (label - 1)
    for j in range(4):
        mark = (col == base + j) & (col >= CLS)
        err = jnp.sum(jnp.where(mark, out, 0.0), axis=1, keepdims=True) - targets[:, j : j + 1]
        size = jnp.abs(err)
        row_loss += fore * jnp.where(size < 1.0, 0.5 * err * err, size - 0.5)
        grad += jnp.where(mark, jnp.clip(err, -1.0, 1.0) * (fore * scale), 0.0)
    loss[...] = jnp.sum(row_loss, axis=0, keepdims=True)
    g_out = grad.astype(bf16)
    gbh[...] = jnp.sum(g_out.astype(f32), axis=0, keepdims=True)
    gwh[...] = dot(h2, g_out, ((0,), (0,)))
    g_h2 = dot(g_out, wh[...], ((1,), (1,)))
    g2 = (g_h2 * gelu_slope(pre2[...])).astype(bf16)
    gb2[...] = jnp.sum(g2.astype(f32), axis=0, keepdims=True)
    gpre2[...] = g2
    for pre, w2, g1, gw2, at in sides:
        gw2[...] = dot(h1[:, at : at + units], gpre2[...], ((0,), (0,)))
        g_h1 = dot(gpre2[...], w2[...], ((1,), (1,)))
        g = (g_h1 * gelu_slope(pre[...] + b1[:, at : at + units])).astype(bf16)
        gb1[:, at : at + units] = jnp.sum(g.astype(f32), axis=0, keepdims=True)
        g1[...] = g


def heads_step(share, count, pre_own, pre_sib, w2_own, w2_sib, wh, b1, b2, bh, labels, crowd, targets):
    rows, units = pre_own.shape
    vmem = pl.BlockSpec(memory_space=pltpu.VMEM)
    shape = jax.ShapeDtypeStruct
    return pl.pallas_call(
        functools.partial(head_kernel, share),
        in_specs=[pl.BlockSpec(memory_space=pltpu.SMEM)] + [vmem] * 11,
        out_specs=[vmem] * 9,
        out_shape=[
            shape((rows, units), bf16),
            shape((rows, units), bf16),
            shape((units, HID), f32),
            shape((units, HID), f32),
            shape((HID, HEADP), f32),
            shape((1, HID), f32),
            shape((1, HID), f32),
            shape((1, HEADP), f32),
            shape((1, 1), f32),
        ],
        scratch_shapes=[pltpu.VMEM((rows, HID), bf16), pltpu.VMEM((rows, HID), f32), pltpu.VMEM((rows, HID), bf16)],
        compiler_params=pltpu.CompilerParams(vmem_limit_bytes=48 * MIB),
        cost_estimate=pl.CostEstimate(
            flops=6 * rows * HID * (HID + HEADP), bytes_accessed=12 * MIB, transcendentals=8 * rows * HID
        ),
        name="heads",
    )(count, pre_own, pre_sib, w2_own, w2_sib, wh, b1, b2, bh, labels, crowd, targets)


class Grid:
    def __init__(self):
        self.wide = lax.axis_size("wide")
        self.tp = lax.axis_size("tp")
        self.y = self.tp // CORES
        self.x = self.y if self.wide % self.y == 0 else 1
        self.z = self.wide // self.x
        self.size = {"z": self.z, "x": self.x, "y": self.y, "c": CORES}
        wide, tp = lax.axis_index("wide"), lax.axis_index("tp")
        self.at = {"z": wide // self.x, "x": wide % self.x, "y": tp // CORES, "c": tp % CORES}

    def move(self, value, axis, by):
        pairs = []
        for z in range(self.z):
            for x in range(self.x):
                for y in range(self.y):
                    for c in range(CORES):
                        to = {"z": z, "x": x, "y": y, "c": c}
                        to[axis] = (to[axis] + by) % self.size[axis]
                        pairs.append((self.index(z, x, y, c), self.index(to["z"], to["x"], to["y"], to["c"])))
        return lax.ppermute(value, AXES, pairs)

    def index(self, z, x, y, c):
        return ((z * self.x + x) * self.y + y) * CORES + c

    def swap(self, value):
        return self.move(value, "c", 1)


def spread(grid, value, order):
    blocks = {(0, 0, 0): value}
    for axis in order:
        place = "zxy".index(axis)
        for key in list(blocks):
            for by in range(1, grid.size[axis]):
                new = list(key)
                new[place] = by
                blocks[tuple(new)] = grid.move(blocks[key], axis, by)
    return blocks


def spread_stacked(grid, value, order):
    stack = value[None, None, None]
    for axis in order:
        place = "zxy".index(axis)
        stack = jnp.concatenate([stack] + [grid.move(stack, axis, by) for by in range(1, grid.size[axis])], axis=place)
    for place, axis in enumerate("zxy"):
        if grid.size[axis] > 1:
            back = (grid.at[axis] - jnp.arange(grid.size[axis])) % grid.size[axis]
            stack = jnp.take(stack, back, axis=place, mode="clip")
    return stack


def collect_stacked(grid, stack, order):
    left = "zxy"
    total = stack
    for axis in order:
        place = left.index(axis)
        total = total.astype(bf16)

        def block(by):
            at = (grid.at[axis] + by) % grid.size[axis]
            return lax.dynamic_index_in_dim(total, at, place, keepdims=False)

        mine = block(0).astype(f32)
        for by in range(1, grid.size[axis]):
            mine = mine + grid.move(block(by), axis, by).astype(f32)
        total = mine
        left = left.replace(axis, "")
    return total


def collect(grid, get, order):
    keys = [(z, x, y) for z in range(grid.z) for x in range(grid.x) for y in range(grid.y)]
    blocks = {key: get(*key) for key in keys}
    for axis in order:
        place = "zxy".index(axis)
        far_first = sorted((k for k in blocks if k[place]), key=lambda k: (-sum(v > 0 for v in k), k))
        got = {}
        for key in far_first:
            home = list(key)
            home[place] = 0
            got.setdefault(tuple(home), []).append(grid.move(blocks[key], axis, key[place]))
        new = {}
        for home, extra in got.items():
            total = blocks[home].astype(f32)
            for value in extra:
                total = total + value.astype(f32)
            new[home] = total
        blocks = new if got else blocks
        if axis != order[-1]:
            blocks = {k: v.astype(bf16) for k, v in blocks.items()}
    return blocks[(0, 0, 0)].astype(f32)


def all_sum(value):
    count = lax.axis_size("wide") * lax.axis_size("tp")
    if count & (count - 1):
        return lax.psum(value, AXES)
    bit = 1
    while bit < count:
        value = value + lax.ppermute(value, AXES, [(i, i ^ bit) for i in range(count)])
        bit *= 2
    return value


def adam_update(weight, grad, first, second, rate):
    first_new = decay_one * first + (1.0 - decay_one) * grad
    second_new = decay_two * second + (1.0 - decay_two) * grad * grad
    first_hat = first_new / (1.0 - decay_one**STEP)
    second_hat = second_new / (1.0 - decay_two**STEP)
    weight_new = weight - rate * (first_hat / (jnp.sqrt(second_hat) + epsilon) + weight_decay * weight)
    return (weight_new, first_new, second_new)


def shards(
    maps,
    roi_image,
    roi_level,
    roi_corner,
    roi_weights,
    crowd,
    labels,
    box_targets,
    w_first,
    m_first,
    v_first,
    w_second,
    m_second,
    v_second,
    w_heads,
    m_heads,
    v_heads,
    biases,
    bias_m,
    bias_v,
):
    grid = Grid()
    rows = crowd.shape[0]
    feats, cols = w_first.shape
    share, second_cols = w_second.shape
    head_rows = w_heads.shape[0]
    units = HID // CORES
    core = grid.at["c"]
    few = grid.z * grid.x * grid.y <= 16
    orders = ("zxy", "zyx")

    kept = jnp.sum(1 - crowd)
    head_block = jnp.pad(w_heads, ((0, 0), (0, HEADP - HEAD)))
    spot = (lax.broadcasted_iota(jnp.int32, head_block.shape, 0) == 0) * 1
    lane = lax.broadcasted_iota(jnp.int32, head_block.shape, 1)
    head_block = head_block + (
        spot * (jnp.where(lane == HEADP - 1, kept % 128, 0) + jnp.where(lane == HEADP - 2, kept // 128, 0))
    ).astype(f32)
    small = jnp.concatenate(
        [w_second.astype(bf16).reshape(-1, cols), head_block.astype(bf16).reshape(-1, cols)], axis=0
    )
    second_rows = share * second_cols // cols
    small_all = spread_stacked(grid, small, "zxy")

    first_low = w_first.astype(bf16)
    half = feats // 2
    weight = jnp.zeros((grid.y, grid.wide * feats, cols), bf16)
    for p, order in enumerate(orders):
        piece = first_low[p * half : (p + 1) * half]
        if few:
            blocks = spread(grid, piece, order)
            for (bz, bx, by), block in blocks.items():
                z = (grid.at["z"] - bz) % grid.z
                x = (grid.at["x"] - bx) % grid.x
                y = (grid.at["y"] - by) % grid.y
                weight = lax.dynamic_update_slice(weight, block[None], (y, (z * grid.x + x) * feats + p * half, 0))
        else:
            stack = spread_stacked(grid, piece, order).transpose(2, 0, 1, 3, 4)
            weight = weight.reshape(grid.y, grid.z, grid.x, feats, cols)
            weight = weight.at[:, :, :, p * half : (p + 1) * half].set(stack).reshape(grid.y, -1, cols)

    images, levels, height, width, channels = maps.shape
    base = ((roi_image * levels + roi_level) * height + roi_corner[:, 0]).astype(jnp.int32)
    col = roi_corner[:, 1].astype(jnp.int32)
    flat_maps = maps.reshape(images * levels * height, width, channels)
    padded = jnp.pad(roi_weights, ((0, 0), (0, 0), (0, 1), (0, 0)))
    row_w = padded[:, 0].reshape(rows * 8, WIN)
    col_w = padded[:, 1].reshape(rows * 8, WIN)
    step = rows // CHUNKS
    own_crops = []
    for at in range(0, rows, step):
        own_crops.append(
            window_crops(
                flat_maps,
                base[at : at + step],
                col[at : at + step],
                row_w[at * 8 : (at + step) * 8],
                col_w[at * 8 : (at + step) * 8],
            )
        )
    crops = own_crops + [grid.swap(c) for c in own_crops]

    small_all = small_all.reshape(grid.wide, grid.y, *small.shape)
    second_own = (
        small_all[:, :, :second_rows]
        .reshape(grid.wide, grid.y, share, second_cols)
        .transpose(1, 2, 0, 3)
        .reshape(units, HID)
    )
    heads_own = small_all[:, :, second_rows:].reshape(grid.wide, grid.y, head_rows, HEADP)
    second_sib = grid.swap(second_own)
    heads_sib = grid.swap(heads_own)
    head_matrix = jnp.where(
        core == 0, jnp.stack([heads_own, heads_sib], axis=2), jnp.stack([heads_sib, heads_own], axis=2)
    ).reshape(HID, HEADP)
    counts = jnp.sum(head_matrix[:, HEADP - 2 :].astype(f32), axis=0)
    roi_count = counts[0] * 128.0 + counts[1]
    first_bias = biases[:HID].reshape(grid.y, CORES, share)
    bias_rel = jnp.concatenate(
        [
            lax.dynamic_index_in_dim(first_bias, core, 1, keepdims=False).reshape(1, -1),
            lax.dynamic_index_in_dim(first_bias, 1 - core, 1, keepdims=False).reshape(1, -1),
        ],
        axis=1,
    )
    second_bias = biases[HID : 2 * HID].reshape(1, -1)
    head_bias = jnp.pad(biases[2 * HID :], (0, HEADP - HEAD)).reshape(1, -1)

    pre_own, pre_send = first_layer(crops, weight)
    pre_sib = grid.swap(pre_send)
    g_own, g_send, gw2_own, gw2_send, gwh, gb1, gb2, gbh, loss = heads_step(
        share,
        roi_count.reshape(1, 1),
        pre_own,
        pre_sib,
        second_own,
        second_sib,
        head_matrix,
        bias_rel,
        second_bias,
        head_bias,
        labels[:, None],
        crowd[:, None],
        box_targets.astype(f32),
    )
    grad = first_grad(crops, g_own, grid.swap(g_send), grid.y)

    grad = grad.reshape(grid.y, grid.wide, 2, half, cols)
    first_parts = []
    for p, order in enumerate(orders):
        back = order[::-1]
        if few:

            def get(dz, dx, dy):
                z = (grid.at["z"] + dz) % grid.z
                x = (grid.at["x"] + dx) % grid.x
                y = (grid.at["y"] + dy) % grid.y
                return lax.dynamic_slice(grad, (y, z * grid.x + x, p, 0, 0), (1, 1, 1, half, cols))[0, 0, 0]

            first_parts.append(collect(grid, get, back))
        else:
            stack = grad[:, :, p].transpose(1, 0, 2, 3).reshape(grid.z, grid.x, grid.y, half, cols)
            first_parts.append(collect_stacked(grid, stack, back))
    first_total = jnp.concatenate(first_parts, axis=0)

    gw2 = gw2_own + grid.swap(gw2_send)
    gwh = gwh.reshape(grid.wide, grid.y, CORES, head_rows, HEADP)
    gwh = lax.dynamic_index_in_dim(gwh, core, 2, keepdims=False) + grid.swap(
        lax.dynamic_index_in_dim(gwh, 1 - core, 2, keepdims=False)
    )
    gw2 = gw2.astype(bf16).reshape(grid.y, share, grid.wide, second_cols).transpose(2, 0, 1, 3)
    small_grad = jnp.concatenate(
        [
            gw2.reshape(grid.wide, grid.y, second_rows, cols),
            gwh.astype(bf16).reshape(grid.wide, grid.y, -1, cols),
        ],
        axis=2,
    ).reshape(grid.z, grid.x, grid.y, -1, cols)
    small_total = collect_stacked(grid, small_grad, "yxz")
    second_total = small_total[:second_rows].reshape(share, second_cols)
    heads_total = small_total[second_rows:].reshape(head_rows, HEADP)[:, :HEAD]

    gb1 = gb1.reshape(CORES, grid.y, share)
    gb1 = jnp.where(core == 0, gb1, gb1[::-1]).transpose(1, 0, 2).reshape(-1)
    sums = all_sum(jnp.concatenate([gb1, gb2[0], gbh[0, :HEAD], loss[0]]))
    loss_total = sums[-1]
    bias_grad = sums[:-1]

    first_out = adam_update(w_first, first_total, m_first, v_first, rate_first)
    second_out = adam_update(w_second, second_total, m_second, v_second, rate_second)
    heads_out = adam_update(w_heads, heads_total, m_heads, v_heads, rate_heads)
    bias_out = adam_update(biases, bias_grad, bias_m, bias_v, rate_biases)
    return (loss_total, roi_count, *first_out, *second_out, *heads_out, *bias_out)


def solution(mesh):
    rows = P(("wide", "tp"))
    both = P("wide", "tp")
    turned = P("tp", "wide")
    return jax.shard_map(
        shards,
        mesh=mesh,
        in_specs=(rows,) * 8 + (both,) * 3 + (turned,) * 3 + (rows,) * 3 + (P(),) * 3,
        out_specs=(P(), P()) + (both,) * 3 + (turned,) * 3 + (rows,) * 3 + (P(),) * 3,
        check_vma=False,
    )
```

time: 846 us -> 574 us (0.68)
  matrix products: 188 us -> 0 us
  blocking collectives: 175 us -> 0 us
  starting transfers between devices: 0.37 us -> 116 us
  Pallas kernels: 0 us -> 66.4 us
  local copies, waits for them, and re-layouts: 130 us -> 86.6 us
  other arithmetic: 64 us -> 39.3 us
  between operations: 18.1 us -> 6.76 us
    ppermute x0 -> x85, waiting for transfers between devices: none -> 257 us  [the longest x80 244 us: move(): return lax.ppermute(value, AXES, pairs)]
    reduce_scatter x2 -> x0, waiting for transfers between devices: 219 us -> none  [the longest x1 118 us: shards(): lax.psum_scatter(grad_first.astype(jnp.bfloat16), 'wide', scatter_dimensi...]
    dot_general x40 -> x0, matrix products: 188 us -> none  [the longest x4 76.5 us: window_crops(): jnp.einsum('rau,ruvc->ravc', weights[:, 0], windows, preferred_element_ty...]
    ppermute x0 -> x85, starting transfers between devices: none -> 116 us  [the longest x80 112 us: move(): return lax.ppermute(value, AXES, pairs)]
    all_gather x6 -> x0, blocking collectives: 93.3 us -> none  [the longest x1 44.2 us: shards(): lax.all_gather(w_heads.astype(jnp.bfloat16), ('wide', 'tp'), axis=0, tile...]
    psum x2 -> x0, blocking collectives: 81.5 us -> none  [the longest x1 42.2 us: shards(): lax.psum(jnp.sum(1.0 - crowd.astype(jnp.float32)), ('wide', 'tp'))]
    gather x4 -> x5, local copies, waits for them, and re-layouts: 82.7 us -> 13.8 us  [spread_stacked(): stack = jnp.take(stack, back, axis=place, mode='clip')]
    pallas_call x0 -> x7, Pallas kernels: none -> 66.4 us  [the longest x4 31.4 us: window_crops(): pl.pallas_call(crop_kernel, grid_spec=pltpu.PrefetchScalarGridSpec(num_sc...]
  transfers between devices with their start and end apart: 9 -> 85, of which waited for: 4 -> 48; matrix products, arithmetic and copies ran while one was open for 28% -> 19% of each run, Pallas kernels for 0% -> 10%
where the time goes in v1:
time: 574 us; the launch traced here: 572 us
  waiting for transfers between devices  257 us (45%)
  starting transfers between devices  116 us (20%)
  local copies, waits for them, and re-layouts  86.6 us (15%)
  Pallas kernels  66.4 us (12%)
  other arithmetic  39.3 us (7%)
  between operations  6.76 us (1%)
    ppermute x80, waiting for transfers between devices, move(): return lax.ppermute(value, AXES, pairs)  244 us
    ppermute x80, starting transfers between devices, move(): return lax.ppermute(value, AXES, pairs)  112 us
    pallas_call x4, Pallas kernels, window_crops(): pl.pallas_call(crop_kernel, grid_spec=pltpu.PrefetchScalarGridSpec(num_sc...  31.4 us
    dynamic_update_slice x32, local copies, waits for them, and re-layouts, shards(): lax.dynamic_update_slice(weight, block[None], (y, (z * grid.x + x) * feat...  26.5 us
    gather x5, local copies, waits for them, and re-layouts, spread_stacked(): stack = jnp.take(stack, back, axis=place, mode='clip')  13.8 us
    pallas_call x1, Pallas kernels, first_grad(): pl.pallas_call(functools.partial(first_grad_kernel, parts, cols), grid=(C...  13.8 us
    pallas_call x1, Pallas kernels, first_layer(): pl.pallas_call(functools.partial(first_kernel, parts), grid=(CELLS // KST...  13.4 us
    ppermute x5, waiting for transfers between devices, all_sum(): lax.ppermute(value, AXES, [(i, i ^ bit) for i in range(count)])  12.9 us
  transfers between devices with their start and end apart: 85, of which 48 were waited for; matrix products, arithmetic and copies ran while one was open for 19% of the time, Pallas kernels for 10%

profile of v1, /device:TPU:0, one launch (start us, length us, event | category | flops | bytes accessed | tf_op | source)
XLA Modules:
  0.0 572.4 jit_solution(16770595677825261898)
XLA Ops:
  27.9 4.7 copy-done.12
  32.5 7.4 %crops.4.refs_0_ = bf16[49,64,256]{2,1,0:T(8,128)(2,1)S(1)} custom-call(s32[64]{0:T(128)S(1)} %get-tuple-element.103.base_ref, s32[64]{0:T(128)S(1)} %get-tuple-element.98.col_ref, bf16[256,32,256]{2,1,0:T(8,128)(2,1)S(1)} %bitcast.257, bf16[512,16]{1,0:T(8,128)(2,1)S(1)} %bitcast.245, bf16[512,16]{1,0:T(8,128)(2,1)S(1)} %bitcast.247, ...), custom_call_target="tpu_custom_call" | custom-call | flops 7516192768 | bytes 12582912 | tf_op jit(solution)/shard_map/crops/pallas_call | solution.py:87
  40.0 7.4 %crops.5.refs_1_ = bf16[49,64,256]{2,1,0:T(8,128)(2,1)S(1)} custom-call(s32[64]{0:T(128)S(1)} %get-tuple-element.102.base_ref, s32[64]{0:T(128)S(1)} %get-tuple-element.97.col_ref, bf16[256,32,256]{2,1,0:T(8,128)(2,1)S(1)} %bitcast.258, bf16[512,16]{1,0:T(8,128)(2,1)S(1)} %bitcast.250, bf16[512,16]{1,0:T(8,128)(2,1)S(1)} %bitcast.252, ...), custom_call_target="tpu_custom_call" | custom-call | flops 7516192768 | bytes 12582912 | tf_op jit(solution)/shard_map/crops/pallas_call | solution.py:87
  47.5 8.3 %crops.6.refs_2_ = bf16[49,64,256]{2,1,0:T(8,128)(2,1)} custom-call(s32[64]{0:T(128)S(1)} %get-tuple-element.101.base_ref, s32[64]{0:T(128)S(1)} %get-tuple-element.99.col_ref, bf16[256,32,256]{2,1,0:T(8,128)(2,1)S(1)} %bitcast.259, bf16[512,16]{1,0:T(8,128)(2,1)S(1)} %bitcast.249, bf16[512,16]{1,0:T(8,128)(2,1)S(1)} %bitcast.251, ...), custom_call_target="tpu_custom_call" | custom-call | flops 7516192768 | bytes 12582912 | tf_op jit(solution)/shard_map/crops/pallas_call | solution.py:87
  55.8 8.3 %crops.7.refs_3_ = bf16[49,64,256]{2,1,0:T(8,128)(2,1)} custom-call(s32[64]{0:T(128)S(1)} %get-tuple-element.100.base_ref, s32[64]{0:T(128)S(1)} %get-tuple-element.96.col_ref, bf16[256,32,256]{2,1,0:T(8,128)(2,1)S(1)} %bitcast.260, bf16[512,16]{1,0:T(8,128)(2,1)S(1)} %bitcast.246, bf16[512,16]{1,0:T(8,128)(2,1)S(1)} %bitcast.248, ...), custom_call_target="tpu_custom_call" | custom-call | flops 7516192768 | bytes 12582912 | tf_op jit(solution)/shard_map/crops/pallas_call | solution.py:87
  80.0 5.5 collective-permute-done.3
  87.9 6.1 %collective-permute-done.14 = bf16[784,256]{1,0:T(8,128)(2,1)S(1)} collective-permute-done((bf16[784,256]{1,0:T(8,128)(2,1)}, bf16[784,256]{1,0:T(8,128)(2,1)S(1)}, u32[]{:S(2)}, u32[]{:S(2)}) %collective-permute-start.14) | collective-permute-done | bytes 401440 | tf_op jit(solution)/shard_map/ppermute | solution.py:316
  97.0 5.7 collective-permute-done.15
  112.7 8.8 %collective-permute-done.18 = bf16[784,256]{1,0:T(8,128)(2,1)S(1)} collective-permute-done((bf16[784,256]{1,0:T(8,128)(2,1)}, bf16[784,256]{1,0:T(8,128)(2,1)S(1)}, u32[]{:S(2)}, u32[]{:S(2)}) %collective-permute-start.18) | collective-permute-done | bytes 401440 | tf_op jit(solution)/shard_map/ppermute | solution.py:316
  123.9 6.3 %collective-permute-done.19 = bf16[784,256]{1,0:T(8,128)(2,1)S(1)} collective-permute-done((bf16[784,256]{1,0:T(8,128)(2,1)}, bf16[784,256]{1,0:T(8,128)(2,1)S(1)}, u32[]{:S(2)}, u32[]{:S(2)}) %collective-permute-start.19) | collective-permute-done | bytes 401440 | tf_op jit(solution)/shard_map/ppermute | solution.py:316
  132.4 6.3 %collective-permute-done.20 = bf16[784,256]{1,0:T(8,128)(2,1)S(1)} collective-permute-done((bf16[784,256]{1,0:T(8,128)(2,1)S(1)}, bf16[784,256]{1,0:T(8,128)(2,1)S(1)}, u32[]{:S(2)}, u32[]{:S(2)}) %collective-permute-start.20) | collective-permute-done | bytes 401440 | tf_op jit(solution)/shard_map/ppermute | solution.py:316
  141.1 6.3 %collective-permute-done.21 = bf16[784,256]{1,0:T(8,128)(2,1)S(1)} collective-permute-done((bf16[784,256]{1,0:T(8,128)(2,1)S(1)}, bf16[784,256]{1,0:T(8,128)(2,1)S(1)}, u32[]{:S(2)}, u32[]{:S(2)}) %collective-permute-start.21) | collective-permute-done | bytes 401440 | tf_op jit(solution)/shard_map/ppermute | solution.py:316
  149.6 6.3 %collective-permute-done.22 = bf16[784,256]{1,0:T(8,128)(2,1)S(1)} collective-permute-done((bf16[784,256]{1,0:T(8,128)(2,1)S(1)}, bf16[784,256]{1,0:T(8,128)(2,1)S(1)}, u32[]{:S(2)}, u32[]{:S(2)}) %collective-permute-start.22) | collective-permute-done | bytes 401440 | tf_op jit(solution)/shard_map/ppermute | solution.py:316
  158.3 6.3 %collective-permute-done.23 = bf16[784,256]{1,0:T(8,128)(2,1)S(1)} collective-permute-done((bf16[784,256]{1,0:T(8,128)(2,1)S(1)}, bf16[784,256]{1,0:T(8,128)(2,1)S(1)}, u32[]{:S(2)}, u32[]{:S(2)}) %collective-permute-start.23) | collective-permute-done | bytes 401440 | tf_op jit(solution)/shard_map/ppermute | solution.py:316
  184.1 6.3 %collective-permute-done.29 = bf16[784,256]{1,0:T(8,128)(2,1)S(1)} collective-permute-done((bf16[784,256]{1,0:T(8,128)(2,1)S(1)}, bf16[784,256]{1,0:T(8,128)(2,1)S(1)}, u32[]{:S(2)}, u32[]{:S(2)}) %collective-permute-start.29) | collective-permute-done | bytes 401440 | tf_op jit(solution)/shard_map/ppermute | solution.py:316
  192.6 6.3 %collective-permute-done.30 = bf16[784,256]{1,0:T(8,128)(2,1)S(1)} collective-permute-done((bf16[784,256]{1,0:T(8,128)(2,1)S(1)}, bf16[784,256]{1,0:T(8,128)(2,1)S(1)}, u32[]{:S(2)}, u32[]{:S(2)}) %collective-permute-start.30) | collective-permute-done | bytes 401440 | tf_op jit(solution)/shard_map/ppermute | solution.py:316
  201.3 3.3 collective-permute-done.31
  210.3 8.1 %collective-permute-done.36 = bf16[784,256]{1,0:T(8,128)(2,1)S(1)} collective-permute-done((bf16[784,256]{1,0:T(8,128)(2,1)S(1)}, bf16[784,256]{1,0:T(8,128)(2,1)S(1)}, u32[]{:S(2)}, u32[]{:S(2)}) %collective-permute-start.36) | collective-permute-done | bytes 401440 | tf_op jit(solution)/shard_map/ppermute | solution.py:316
  218.5 8.6 %collective-permute-done.37 = bf16[784,256]{1,0:T(8,128)(2,1)S(1)} collective-permute-done((bf16[784,256]{1,0:T(8,128)(2,1)S(1)}, bf16[784,256]{1,0:T(8,128)(2,1)S(1)}, u32[]{:S(2)}, u32[]{:S(2)}) %collective-permute-start.37) | collective-permute-done | bytes 401440 | tf_op jit(solution)/shard_map/ppermute | solution.py:316
  227.1 5.7 collective-permute-done.38
  236.8 4.6 collective-permute-done.39
  246.5 10.3 %collective-permute-done.4 = bf16[4,2,1,192,256]{4,3,2,1,0:T(8,128)(2,1)S(1)} collective-permute-done((bf16[4,2,1,192,256]{4,3,2,1,0:T(8,128)(2,1)S(1)}, bf16[4,2,1,192,256]{4,3,2,1,0:T(8,128)(2,1)S(1)}, u32[]{:S(2)}, u32[]{:S(2)}) %collective-permute-start.4) | collective-permute-done | bytes 786464 | tf_op jit(solution)/shard_map/ppermute | solution.py:316
  282.8 13.4 %first_layer.1 = (f32[256,512]{1,0:T(8,128)S(1)}, f32[256,512]{1,0:T(8,128)}) custom-call(bf16[49,64,256]{2,1,0:T(8,128)(2,1)S(1)} %crops.4.refs_0_, bf16[49,64,256]{2,1,0:T(8,128)(2,1)S(1)} %crops.5.refs_1_, bf16[49,64,256]{2,1,0:T(8,128)(2,1)} %crops.6.refs_2_, bf16[49,64,256]{2,1,0:T(8,128)(2,1)} %crops.7.refs_3_, ...), custom_call_target="tpu_custom_call" | custom-call | flops 6576668672 | bytes 27262976 | tf_op jit(solution)/shard_map/first_layer/pallas_call | solution.py:140
  309.1 7.8 %heads.1 = (bf16[256,512]{1,0:T(8,128)(2,1)S(1)}, bf16[256,512]{1,0:T(8,128)(2,1)}, f32[512,1024]{1,0:T(8,128)}, f32[512,1024]{1,0:T(8,128)}, f32[1024,512]{1,0:...) custom-call(f32[1,1]{1,0:T(1,128)} %bitcast.10.count_ref, ...), custom_call_target="tpu_custom_call" | custom-call | flops 2415919104 | bytes 12582912 | tf_op jit(solution)/shard_map/heads/pallas_call | solution.py:272
  318.9 13.8 %first_grad.1 = bf16[2,12544,256]{2,1,0:T(8,128)(2,1)} custom-call(bf16[49,64,256]{2,1,0:T(8,128)(2,1)S(1)} %crops.4.refs_0_, bf16[49,64,256]{2,1,0:T(8,128)(2,1)S(1)} %crops.5.refs_1_, bf16[49,64,256]{2,1,0:T(8,128)(2,1)} %crops.6.refs_2_, bf16[49,64,256]{2,1,0:T(8,128)(2,1)} %crops.7.refs_3_, bf16[49,64,256]{2,1,0:T(8,128)(2,1)} %collective-permute-done.6.refs_4_, ...), custom_call_target="tpu_custom_call" | custom-call | flops 6576668672 | bytes 27262976 | tf_op jit(solution)/shard_map/first_grad/pallas_call | solution.py:171
  332.7 5.7 dynamic-slice_bitcast_fusion.17
  342.4 8.1 %collective-permute-done.43 = f32[2450]{0:T(1024)S(1)} collective-permute-done((f32[2450]{0:T(1024)S(1)}, f32[2450]{0:T(1024)S(1)}, u32[]{:S(2)}, u32[]{:S(2)}) %collective-permute-start.43) | collective-permute-done | bytes 9832 | tf_op jit(solution)/shard_map/ppermute | solution.py:397
  358.9 8.5 %collective-permute-done.52 = bf16[784,256]{1,0:T(8,128)(2,1)S(1)} collective-permute-done((bf16[784,256]{1,0:T(8,128)(2,1)}, bf16[784,256]{1,0:T(8,128)(2,1)S(1)}, u32[]{:S(2)}, u32[]{:S(2)}) %collective-permute-start.52) | collective-permute-done | bytes 401440 | tf_op jit(solution)/shard_map/ppermute | solution.py:316
  369.0 7.1 %collective-permute-done.56 = bf16[784,256]{1,0:T(8,128)(2,1)S(1)} collective-permute-done((bf16[784,256]{1,0:T(8,128)(2,1)}, bf16[784,256]{1,0:T(8,128)(2,1)S(1)}, u32[]{:S(2)}, u32[]{:S(2)}) %collective-permute-start.56) | collective-permute-done | bytes 401440 | tf_op jit(solution)/shard_map/ppermute | solution.py:316
  377.6 7.1 %collective-permute-done.60 = bf16[784,256]{1,0:T(8,128)(2,1)S(1)} collective-permute-done((bf16[784,256]{1,0:T(8,128)(2,1)}, bf16[784,256]{1,0:T(8,128)(2,1)S(1)}, u32[]{:S(2)}, u32[]{:S(2)}) %collective-permute-start.60) | collective-permute-done | bytes 401440 | tf_op jit(solution)/shard_map/ppermute | solution.py:316
  388.9 4.4 collective-permute-done.51
  394.8 7.1 %collective-permute-done.55 = bf16[784,256]{1,0:T(8,128)(2,1)S(1)} collective-permute-done((bf16[784,256]{1,0:T(8,128)(2,1)}, bf16[784,256]{1,0:T(8,128)(2,1)S(1)}, u32[]{:S(2)}, u32[]{:S(2)}) %collective-permute-start.55) | collective-permute-done | bytes 401440 | tf_op jit(solution)/shard_map/ppermute | solution.py:316
  403.4 4.3 collective-permute-done.59
  413.4 7.1 %collective-permute-done.61 = bf16[784,256]{1,0:T(8,128)(2,1)S(1)} collective-permute-done((bf16[784,256]{1,0:T(8,128)(2,1)S(1)}, bf16[784,256]{1,0:T(8,128)(2,1)S(1)}, u32[]{:S(2)}, u32[]{:S(2)}) %collective-permute-start.61) | collective-permute-done | bytes 401440 | tf_op jit(solution)/shard_map/ppermute | solution.py:316
  423.2 3.3 add_convert_fusion.7
  430.7 7.1 %collective-permute-done.67 = bf16[784,256]{1,0:T(8,128)(2,1)} collective-permute-done((bf16[784,256]{1,0:T(8,128)(2,1)}, bf16[784,256]{1,0:T(8,128)(2,1)}, u32[]{:S(2)}, u32[]{:S(2)}) %collective-permute-start.67) | collective-permute-done | bytes 401440 | tf_op jit(solution)/shard_map/ppermute | solution.py:316
  438.9 7.4 %collective-permute-done.71 = bf16[784,256]{1,0:T(8,128)(2,1)} collective-permute-done((bf16[784,256]{1,0:T(8,128)(2,1)}, bf16[784,256]{1,0:T(8,128)(2,1)}, u32[]{:S(2)}, u32[]{:S(2)}) %collective-permute-start.71) | collective-permute-done | bytes 401440 | tf_op jit(solution)/shard_map/ppermute | solution.py:316
  457.8 5.8 %collective-permute-done.50 = bf16[784,256]{1,0:T(8,128)(2,1)} collective-permute-done((bf16[784,256]{1,0:T(8,128)(2,1)}, bf16[784,256]{1,0:T(8,128)(2,1)}, u32[]{:S(2)}, u32[]{:S(2)}) %collective-permute-start.50) | collective-permute-done | bytes 401440 | tf_op jit(solution)/shard_map/ppermute | solution.py:316
  469.8 4.4 convert_add_fusion.18
  476.3 4.5 collective-permute-done.70
  482.3 4.9 collective-permute-done.74
  488.7 8.7 %collective-permute-done.68 = bf16[784,256]{1,0:T(8,128)(2,1)} collective-permute-done((bf16[784,256]{1,0:T(8,128)(2,1)}, bf16[784,256]{1,0:T(8,128)(2,1)}, u32[]{:S(2)}, u32[]{:S(2)}) %collective-permute-start.68) | collective-permute-done | bytes 401440 | tf_op jit(solution)/shard_map/ppermute | solution.py:316
  499.2 6.8 %collective-permute-done.72 = bf16[784,256]{1,0:T(8,128)(2,1)} collective-permute-done((bf16[784,256]{1,0:T(8,128)(2,1)}, bf16[784,256]{1,0:T(8,128)(2,1)}, u32[]{:S(2)}, u32[]{:S(2)}) %collective-permute-start.72) | collective-permute-done | bytes 401440 | tf_op jit(solution)/shard_map/ppermute | solution.py:316
  506.1 8.6 %collective-permute-done.76 = bf16[784,256]{1,0:T(8,128)(2,1)} collective-permute-done((bf16[784,256]{1,0:T(8,128)(2,1)}, bf16[784,256]{1,0:T(8,128)(2,1)}, u32[]{:S(2)}, u32[]{:S(2)}) %collective-permute-start.76) | collective-permute-done | bytes 401440 | tf_op jit(solution)/shard_map/ppermute | solution.py:316
  517.1 6.4 %collective-permute-start.69 = (bf16[784,256]{1,0:T(8,128)(2,1)S(1)}, bf16[784,256]{1,0:T(8,128)(2,1)S(1)}, u32[]{:S(2)}, u32[]{:S(2)}) collective-permute-start(bf16[784,256]{1,0:T(8,128)(2,1)S(1)} %get-tuple-element.76), channel_id=1, source_target_pairs={{0,8},{1,9},{2,10},{3,11},{4,12},{5,13},{6,14},{7,15},{8,16},{9,17... | collective-permute-start | bytes 1204232 | tf_op jit(solution)/shard_map/ppermute | solution.py:316
  530.8 4.8 collective-permute-done.69
  535.6 13.2 %collective-permute-done.73 = bf16[784,256]{1,0:T(8,128)(2,1)S(1)} collective-permute-done((bf16[784,256]{1,0:T(8,128)(2,1)S(1)}, bf16[784,256]{1,0:T(8,128)(2,1)S(1)}, u32[]{:S(2)}, u32[]{:S(2)}) %collective-permute-start.73) | collective-permute-done | bytes 401440 | tf_op jit(solution)/shard_map/ppermute | solution.py:316
  550.3 9.1 %collective-permute-start.82 = (bf16[192,256]{1,0:T(8,128)(2,1)S(1)}, bf16[192,256]{1,0:T(8,128)(2,1)S(1)}, u32[]{:S(2)}, u32[]{:S(2)}) collective-permute-start(bf16[192,256]{1,0:T(8,128)(2,1)S(1)} %get-tuple-element.81), channel_id=1, source_target_pairs={{0,8},{1,9},{2,10},{3,11},{4,12},{5,13},{6,14},{7,15},{8,16},{9,17... | collective-permute-start | bytes 294920 | tf_op jit(solution)/shard_map/ppermute | solution.py:316
  (331 shorter events, 229.3 us)
Async XLA Ops:
  3.2 66.2 %collective-permute-start.10 = (bf16[784,256]{1,0:T(8,128)(2,1)}, bf16[784,256]{1,0:T(8,128)(2,1)}, u32[]{:S(2)}, u32[]{:S(2)}) collective-permute-start(bf16[784,256]{1,0:T(8,128)(2,1)} %get-tuple-element.80), channel_id=1, source_target_pairs={{0,8},{1,9},{2,10},{3,11},{4,12},{5,13},{6,14},{7,15},{8,16},{9,17... | collective-permute-start | bytes 1204232 | tf_op jit(solution)/shard_map/ppermute | solution.py:316
  6.2 66.2 %collective-permute-start.11 = (bf16[784,256]{1,0:T(8,128)(2,1)}, bf16[784,256]{1,0:T(8,128)(2,1)}, u32[]{:S(2)}, u32[]{:S(2)}) collective-permute-start(bf16[784,256]{1,0:T(8,128)(2,1)} %get-tuple-element.80), channel_id=1, source_target_pairs={{0,16},{1,17},{2,18},{3,19},{4,20},{5,21},{6,22},{7,23},{8,24},{9,... | collective-permute-start | bytes 1204232 | tf_op jit(solution)/shard_map/ppermute | solution.py:316
  15.3 49.1 %collective-permute-start = (bf16[1,1,1,192,256]{4,3,2,1,0:T(8,128)(2,1)}, bf16[1,1,1,192,256]{4,3,2,1,0:T(8,128)(2,1)}, u32[]{:S(2)}, u32[]{:S(2)}) collective-permute-start(bf16[1,1,1,192,256]{4,3,2,1,0:T(8,128)(2,1)} %maximum_bitcast_fusion), channel_id=1, source_target_pairs={{0,8},{1,9},{2,10},{3,11},{4,12},{5,13},{6,14},{7,15},{8,16},{9,17... | collective-permute-start | bytes 294920 | tf_op jit(solution)/shard_map/ppermute | solution.py:316
  15.3 49.7 %collective-permute-start.1 = (bf16[1,1,1,192,256]{4,3,2,1,0:T(8,128)(2,1)}, bf16[1,1,1,192,256]{4,3,2,1,0:T(8,128)(2,1)}, u32[]{:S(2)}, u32[]{:S(2)}) collective-permute-start(bf16[1,1,1,192,256]{4,3,2,1,0:T(8,128)(2,1)} %maximum_bitcast_fusion), channel_id=1, source_target_pairs={{0,16},{1,17},{2,18},{3,19},{4,20},{5,21},{6,22},{7,23},{8,24},{9,... | collective-permute-start | bytes 294920 | tf_op jit(solution)/shard_map/ppermute | solution.py:316
  17.2 49.5 %collective-permute-start.2 = (bf16[1,1,1,192,256]{4,3,2,1,0:T(8,128)(2,1)}, bf16[1,1,1,192,256]{4,3,2,1,0:T(8,128)(2,1)}, u32[]{:S(2)}, u32[]{:S(2)}) collective-permute-start(bf16[1,1,1,192,256]{4,3,2,1,0:T(8,128)(2,1)} %maximum_bitcast_fusion), channel_id=1, source_target_pairs={{0,24},{1,25},{2,26},{3,27},{4,28},{5,29},{6,30},{7,31},{8,0},{9,1... | collective-permute-start | bytes 294920 | tf_op jit(solution)/shard_map/ppermute | solution.py:316
  66.8 44.7 %collective-permute-start.17 = (bf16[784,256]{1,0:T(8,128)(2,1)}, bf16[784,256]{1,0:T(8,128)(2,1)S(1)}, u32[]{:S(2)}, u32[]{:S(2)}) collective-permute-start(bf16[784,256]{1,0:T(8,128)(2,1)} %get-tuple-element.80), channel_id=1, source_target_pairs={{0,2},{1,3},{2,0},{3,1},{4,6},{5,7},{6,4},{7,5},{8,10},{9,11},{10,... | collective-permute-start | bytes 1204232 | tf_op jit(solution)/shard_map/ppermute | solution.py:316
  69.4 97.5 %collective-permute-start.25 = (bf16[784,256]{1,0:T(8,128)(2,1)}, bf16[784,256]{1,0:T(8,128)(2,1)S(1)}, u32[]{:S(2)}, u32[]{:S(2)}) collective-permute-start(bf16[784,256]{1,0:T(8,128)(2,1)} %get-tuple-element.79), channel_id=1, source_target_pairs={{0,8},{1,9},{2,10},{3,11},{4,12},{5,13},{6,14},{7,15},{8,16},{9,17... | collective-permute-start | bytes 1204232 | tf_op jit(solution)/shard_map/ppermute | solution.py:316
  78.4 24.3 %collective-permute-start.15 = (bf16[784,256]{1,0:T(8,128)(2,1)}, bf16[784,256]{1,0:T(8,128)(2,1)S(1)}, u32[]{:S(2)}, u32[]{:S(2)}) collective-permute-start(bf16[784,256]{1,0:T(8,128)(2,1)} %collective-permute-done.11), channel_id=1, source_target_pairs={{0,4},{1,5},{2,6},{3,7},{4,0},{5,1},{6,2},{7,3},{8,12},{9,13},{10,... | collective-permute-start | bytes 1204232 | tf_op jit(solution)/shard_map/ppermute | solution.py:316
  85.5 82.9 %collective-permute-start.26 = (bf16[784,256]{1,0:T(8,128)(2,1)}, bf16[784,256]{1,0:T(8,128)(2,1)S(1)}, u32[]{:S(2)}, u32[]{:S(2)}) collective-permute-start(bf16[784,256]{1,0:T(8,128)(2,1)} %get-tuple-element.79), channel_id=1, source_target_pairs={{0,16},{1,17},{2,18},{3,19},{4,20},{5,21},{6,22},{7,23},{8,24},{9,... | collective-permute-start | bytes 1204232 | tf_op jit(solution)/shard_map/ppermute | solution.py:316
  102.7 66.2 %collective-permute-start.27 = (bf16[784,256]{1,0:T(8,128)(2,1)}, bf16[784,256]{1,0:T(8,128)(2,1)S(1)}, u32[]{:S(2)}, u32[]{:S(2)}) collective-permute-start(bf16[784,256]{1,0:T(8,128)(2,1)} %get-tuple-element.79), channel_id=1, source_target_pairs={{0,24},{1,25},{2,26},{3,27},{4,28},{5,29},{6,30},{7,31},{8,0},{9,1... | collective-permute-start | bytes 1204232 | tf_op jit(solution)/shard_map/ppermute | solution.py:316
  166.9 39.3 %collective-permute-start.32 = (bf16[784,256]{1,0:T(8,128)(2,1)S(1)}, bf16[784,256]{1,0:T(8,128)(2,1)S(1)}, u32[]{:S(2)}, u32[]{:S(2)}) collective-permute-start(bf16[784,256]{1,0:T(8,128)(2,1)S(1)} %copy-done.28), channel_id=1, source_target_pairs={{0,4},{1,5},{2,6},{3,7},{4,0},{5,1},{6,2},{7,3},{8,12},{9,13},{10,... | collective-permute-start | bytes 1204232 | tf_op jit(solution)/shard_map/ppermute | solution.py:316
  168.4 22.0 %collective-permute-start.29 = (bf16[784,256]{1,0:T(8,128)(2,1)S(1)}, bf16[784,256]{1,0:T(8,128)(2,1)S(1)}, u32[]{:S(2)}, u32[]{:S(2)}) collective-permute-start(bf16[784,256]{1,0:T(8,128)(2,1)S(1)} %collective-permute-done.25), channel_id=1, source_target_pairs={{0,2},{1,3},{2,0},{3,1},{4,6},{5,7},{6,4},{7,5},{8,10},{9,11},{10,... | collective-permute-start | bytes 1204232 | tf_op jit(solution)/shard_map/ppermute | solution.py:316
  168.9 30.1 %collective-permute-start.30 = (bf16[784,256]{1,0:T(8,128)(2,1)S(1)}, bf16[784,256]{1,0:T(8,128)(2,1)S(1)}, u32[]{:S(2)}, u32[]{:S(2)}) collective-permute-start(bf16[784,256]{1,0:T(8,128)(2,1)S(1)} %collective-permute-done.26), channel_id=1, source_target_pairs={{0,2},{1,3},{2,0},{3,1},{4,6},{5,7},{6,4},{7,5},{8,10},{9,11},{10,... | collective-permute-start | bytes 1204232 | tf_op jit(solution)/shard_map/ppermute | solution.py:316
  173.2 31.3 %collective-permute-start.31 = (bf16[784,256]{1,0:T(8,128)(2,1)S(1)}, bf16[784,256]{1,0:T(8,128)(2,1)S(1)}, u32[]{:S(2)}, u32[]{:S(2)}) collective-permute-start(bf16[784,256]{1,0:T(8,128)(2,1)S(1)} %collective-permute-done.27), channel_id=1, source_target_pairs={{0,2},{1,3},{2,0},{3,1},{4,6},{5,7},{6,4},{7,5},{8,10},{9,11},{10,... | collective-permute-start | bytes 1204232 | tf_op jit(solution)/shard_map/ppermute | solution.py:316
  181.8 25.5 %collective-permute-start.33 = (bf16[784,256]{1,0:T(8,128)(2,1)S(1)}, bf16[784,256]{1,0:T(8,128)(2,1)S(1)}, u32[]{:S(2)}, u32[]{:S(2)}) collective-permute-start(bf16[784,256]{1,0:T(8,128)(2,1)S(1)} %collective-permute-done.25), channel_id=1, source_target_pairs={{0,4},{1,5},{2,6},{3,7},{4,0},{5,1},{6,2},{7,3},{8,12},{9,13},{10,... | collective-permute-start | bytes 1204232 | tf_op jit(solution)/shard_map/ppermute | solution.py:316
  190.4 19.4 %collective-permute-start.34 = (bf16[784,256]{1,0:T(8,128)(2,1)S(1)}, bf16[784,256]{1,0:T(8,128)(2,1)S(1)}, u32[]{:S(2)}, u32[]{:S(2)}) collective-permute-start(bf16[784,256]{1,0:T(8,128)(2,1)S(1)} %collective-permute-done.26), channel_id=1, source_target_pairs={{0,4},{1,5},{2,6},{3,7},{4,0},{5,1},{6,2},{7,3},{8,12},{9,13},{10,... | collective-permute-start | bytes 1204232 | tf_op jit(solution)/shard_map/ppermute | solution.py:316
  206.2 20.9 %collective-permute-start.37 = (bf16[784,256]{1,0:T(8,128)(2,1)S(1)}, bf16[784,256]{1,0:T(8,128)(2,1)S(1)}, u32[]{:S(2)}, u32[]{:S(2)}) collective-permute-start(bf16[784,256]{1,0:T(8,128)(2,1)S(1)} %collective-permute-done.29), channel_id=1, source_target_pairs={{0,4},{1,5},{2,6},{3,7},{4,0},{5,1},{6,2},{7,3},{8,12},{9,13},{10,... | collective-permute-start | bytes 1204232 | tf_op jit(solution)/shard_map/ppermute | solution.py:316
  207.3 25.4 %collective-permute-start.38 = (bf16[784,256]{1,0:T(8,128)(2,1)S(1)}, bf16[784,256]{1,0:T(8,128)(2,1)S(1)}, u32[]{:S(2)}, u32[]{:S(2)}) collective-permute-start(bf16[784,256]{1,0:T(8,128)(2,1)S(1)} %collective-permute-done.30), channel_id=1, source_target_pairs={{0,4},{1,5},{2,6},{3,7},{4,0},{5,1},{6,2},{7,3},{8,12},{9,13},{10,... | collective-permute-start | bytes 1204232 | tf_op jit(solution)/shard_map/ppermute | solution.py:316
  209.8 72.4 %collective-permute-start.6 = (bf16[49,64,256]{2,1,0:T(8,128)(2,1)S(1)}, bf16[49,64,256]{2,1,0:T(8,128)(2,1)}, u32[]{:S(2)}, u32[]{:S(2)}) collective-permute-start(bf16[49,64,256]{2,1,0:T(8,128)(2,1)S(1)} %crops.4.refs_0_), channel_id=1, source_target_pairs={{0,1},{1,0},{2,3},{3,2},{4,5},{5,4},{6,7},{7,6},{8,9},{9,8},{10,11... | collective-permute-start | bytes 4816904 | tf_op jit(solution)/shard_map/ppermute | solution.py:316
  209.9 72.9 %collective-permute-start.7 = (bf16[49,64,256]{2,1,0:T(8,128)(2,1)S(1)}, bf16[49,64,256]{2,1,0:T(8,128)(2,1)}, u32[]{:S(2)}, u32[]{:S(2)}) collective-permute-start(bf16[49,64,256]{2,1,0:T(8,128)(2,1)S(1)} %crops.5.refs_1_), channel_id=1, source_target_pairs={{0,1},{1,0},{2,3},{3,2},{4,5},{5,4},{6,7},{7,6},{8,9},{9,8},{10,11... | collective-permute-start | bytes 4816904 | tf_op jit(solution)/shard_map/ppermute | solution.py:316
  218.5 64.3 %collective-permute-start.8 = (bf16[49,64,256]{2,1,0:T(8,128)(2,1)}, bf16[49,64,256]{2,1,0:T(8,128)(2,1)}, u32[]{:S(2)}, u32[]{:S(2)}) collective-permute-start(bf16[49,64,256]{2,1,0:T(8,128)(2,1)} %crops.6.refs_2_), channel_id=1, source_target_pairs={{0,1},{1,0},{2,3},{3,2},{4,5},{5,4},{6,7},{7,6},{8,9},{9,8},{10,11... | collective-permute-start | bytes 4816904 | tf_op jit(solution)/shard_map/ppermute | solution.py:316
  227.1 55.7 %collective-permute-start.9 = (bf16[49,64,256]{2,1,0:T(8,128)(2,1)}, bf16[49,64,256]{2,1,0:T(8,128)(2,1)}, u32[]{:S(2)}, u32[]{:S(2)}) collective-permute-start(bf16[49,64,256]{2,1,0:T(8,128)(2,1)} %crops.7.refs_3_), channel_id=1, source_target_pairs={{0,1},{1,0},{2,3},{3,2},{4,5},{5,4},{6,7},{7,6},{8,9},{9,8},{10,11... | collective-permute-start | bytes 4816904 | tf_op jit(solution)/shard_map/ppermute | solution.py:316
  280.2 25.2 %collective-permute-start.41 = (bf16[512,1024]{1,0:T(8,128)(2,1)}, bf16[512,1024]{1,0:T(8,128)(2,1)}, u32[]{:S(2)}, u32[]{:S(2)}) collective-permute-start(bf16[512,1024]{1,0:T(8,128)(2,1)} %bitcast.240.w2_own), channel_id=1, source_target_pairs={{0,1},{1,0},{2,3},{3,2},{4,5},{5,4},{6,7},{7,6},{8,9},{9,8},{10,11... | collective-permute-start | bytes 3145736 | tf_op jit(solution)/shard_map/ppermute | solution.py:316
  317.4 130.5 %collective-permute-start.78 = (f32[512,1024]{1,0:T(8,128)}, f32[512,1024]{1,0:T(8,128)}, u32[]{:S(2)}, u32[]{:S(2)}) collective-permute-start(f32[512,1024]{1,0:T(8,128)} %get-tuple-element.34), channel_id=1, source_target_pairs={{0,1},{1,0},{2,3},{3,2},{4,5},{5,4},{6,7},{7,6},{8,9},{9,8},{10,11... | collective-permute-start | bytes 6291464 | tf_op jit(solution)/shard_map/ppermute | solution.py:316
  338.4 20.5 %collective-permute-start.49 = (bf16[784,256]{1,0:T(8,128)(2,1)}, bf16[784,256]{1,0:T(8,128)(2,1)}, u32[]{:S(2)}, u32[]{:S(2)}) collective-permute-start(bf16[784,256]{1,0:T(8,128)(2,1)} %get-tuple-element.68), channel_id=1, source_target_pairs={{0,2},{1,3},{2,0},{3,1},{4,6},{5,7},{6,4},{7,5},{8,10},{9,11},{10,... | collective-permute-start | bytes 1204232 | tf_op jit(solution)/shard_map/ppermute | solution.py:316
  356.5 19.5 %collective-permute-start.56 = (bf16[784,256]{1,0:T(8,128)(2,1)}, bf16[784,256]{1,0:T(8,128)(2,1)S(1)}, u32[]{:S(2)}, u32[]{:S(2)}) collective-permute-start(bf16[784,256]{1,0:T(8,128)(2,1)} %get-tuple-element.64), channel_id=1, source_target_pairs={{0,2},{1,3},{2,0},{3,1},{4,6},{5,7},{6,4},{7,5},{8,10},{9,11},{10,... | collective-permute-start | bytes 1204232 | tf_op jit(solution)/shard_map/ppermute | solution.py:316
  357.9 26.8 %collective-permute-start.60 = (bf16[784,256]{1,0:T(8,128)(2,1)}, bf16[784,256]{1,0:T(8,128)(2,1)S(1)}, u32[]{:S(2)}, u32[]{:S(2)}) collective-permute-start(bf16[784,256]{1,0:T(8,128)(2,1)} %get-tuple-element.62), channel_id=1, source_target_pairs={{0,2},{1,3},{2,0},{3,1},{4,6},{5,7},{6,4},{7,5},{8,10},{9,11},{10,... | collective-permute-start | bytes 1204232 | tf_op jit(solution)/shard_map/ppermute | solution.py:316
  358.9 50.3 %collective-permute-start.79 = (f32[8,2,32,512]{3,2,1,0:T(8,128)S(1)}, f32[8,2,32,512]{3,2,1,0:T(8,128)S(1)}, u32[]{:S(2)}, u32[]{:S(2)}) collective-permute-start(f32[8,2,32,512]{3,2,1,0:T(8,128)S(1)} %dynamic-slice_bitcast_fusion), channel_id=1, source_target_pairs={{0,1},{1,0},{2,3},{3,2},{4,5},{5,4},{6,7},{7,6},{8,9},{9,8},{10,11... | collective-permute-start | bytes 3145736 | tf_op jit(solution)/shard_map/ppermute | solution.py:316
  367.4 25.8 %collective-permute-start.51 = (bf16[784,256]{1,0:T(8,128)(2,1)}, bf16[784,256]{1,0:T(8,128)(2,1)S(1)}, u32[]{:S(2)}, u32[]{:S(2)}) collective-permute-start(bf16[784,256]{1,0:T(8,128)(2,1)} %get-tuple-element.67), channel_id=1, source_target_pairs={{0,2},{1,3},{2,0},{3,1},{4,6},{5,7},{6,4},{7,5},{8,10},{9,11},{10,... | collective-permute-start | bytes 1204232 | tf_op jit(solution)/shard_map/ppermute | solution.py:316
  376.1 25.8 %collective-permute-start.55 = (bf16[784,256]{1,0:T(8,128)(2,1)}, bf16[784,256]{1,0:T(8,128)(2,1)S(1)}, u32[]{:S(2)}, u32[]{:S(2)}) collective-permute-start(bf16[784,256]{1,0:T(8,128)(2,1)} %get-tuple-element.65), channel_id=1, source_target_pairs={{0,2},{1,3},{2,0},{3,1},{4,6},{5,7},{6,4},{7,5},{8,10},{9,11},{10,... | collective-permute-start | bytes 1204232 | tf_op jit(solution)/shard_map/ppermute | solution.py:316
  384.7 23.0 %collective-permute-start.59 = (bf16[784,256]{1,0:T(8,128)(2,1)}, bf16[784,256]{1,0:T(8,128)(2,1)S(1)}, u32[]{:S(2)}, u32[]{:S(2)}) collective-permute-start(bf16[784,256]{1,0:T(8,128)(2,1)} %get-tuple-element.63), channel_id=1, source_target_pairs={{0,2},{1,3},{2,0},{3,1},{4,6},{5,7},{6,4},{7,5},{8,10},{9,11},{10,... | collective-permute-start | bytes 1204232 | tf_op jit(solution)/shard_map/ppermute | solution.py:316
  411.9 25.9 %collective-permute-start.67 = (bf16[784,256]{1,0:T(8,128)(2,1)}, bf16[784,256]{1,0:T(8,128)(2,1)}, u32[]{:S(2)}, u32[]{:S(2)}) collective-permute-start(bf16[784,256]{1,0:T(8,128)(2,1)} %get-tuple-element.58), channel_id=1, source_target_pairs={{0,4},{1,5},{2,6},{3,7},{4,0},{5,1},{6,2},{7,3},{8,12},{9,13},{10,... | collective-permute-start | bytes 1204232 | tf_op jit(solution)/shard_map/ppermute | solution.py:316
  420.5 25.9 %collective-permute-start.71 = (bf16[784,256]{1,0:T(8,128)(2,1)}, bf16[784,256]{1,0:T(8,128)(2,1)}, u32[]{:S(2)}, u32[]{:S(2)}) collective-permute-start(bf16[784,256]{1,0:T(8,128)(2,1)} %get-tuple-element.56), channel_id=1, source_target_pairs={{0,4},{1,5},{2,6},{3,7},{4,0},{5,1},{6,2},{7,3},{8,12},{9,13},{10,... | collective-permute-start | bytes 1204232 | tf_op jit(solution)/shard_map/ppermute | solution.py:316
  426.5 30.3 %collective-permute-start.75 = (bf16[784,256]{1,0:T(8,128)(2,1)}, bf16[784,256]{1,0:T(8,128)(2,1)}, u32[]{:S(2)}, u32[]{:S(2)}) collective-permute-start(bf16[784,256]{1,0:T(8,128)(2,1)} %get-tuple-element.54), channel_id=1, source_target_pairs={{0,4},{1,5},{2,6},{3,7},{4,0},{5,1},{6,2},{7,3},{8,12},{9,13},{10,... | collective-permute-start | bytes 1204232 | tf_op jit(solution)/shard_map/ppermute | solution.py:316
  429.2 34.4 %collective-permute-start.50 = (bf16[784,256]{1,0:T(8,128)(2,1)}, bf16[784,256]{1,0:T(8,128)(2,1)}, u32[]{:S(2)}, u32[]{:S(2)}) collective-permute-start(bf16[784,256]{1,0:T(8,128)(2,1)} %get-tuple-element.69), channel_id=1, source_target_pairs={{0,4},{1,5},{2,6},{3,7},{4,0},{5,1},{6,2},{7,3},{8,12},{9,13},{10,... | collective-permute-start | bytes 1204232 | tf_op jit(solution)/shard_map/ppermute | solution.py:316
  437.8 28.2 %collective-permute-start.54 = (bf16[784,256]{1,0:T(8,128)(2,1)}, bf16[784,256]{1,0:T(8,128)(2,1)}, u32[]{:S(2)}, u32[]{:S(2)}) collective-permute-start(bf16[784,256]{1,0:T(8,128)(2,1)} %get-tuple-element.73), channel_id=1, source_target_pairs={{0,8},{1,9},{2,10},{3,11},{4,12},{5,13},{6,14},{7,15},{8,16},{9,17... | collective-permute-start | bytes 1204232 | tf_op jit(solution)/shard_map/ppermute | solution.py:316
  446.4 21.4 %collective-permute-start.58 = (bf16[784,256]{1,0:T(8,128)(2,1)}, bf16[784,256]{1,0:T(8,128)(2,1)}, u32[]{:S(2)}, u32[]{:S(2)}) collective-permute-start(bf16[784,256]{1,0:T(8,128)(2,1)} %get-tuple-element.75), channel_id=1, source_target_pairs={{0,16},{1,17},{2,18},{3,19},{4,20},{5,21},{6,22},{7,23},{8,24},{9,... | collective-permute-start | bytes 1204232 | tf_op jit(solution)/shard_map/ppermute | solution.py:316
  447.9 20.2 %collective-permute-start.62 = (bf16[784,256]{1,0:T(8,128)(2,1)}, bf16[784,256]{1,0:T(8,128)(2,1)}, u32[]{:S(2)}, u32[]{:S(2)}) collective-permute-start(bf16[784,256]{1,0:T(8,128)(2,1)} %get-tuple-element.74), channel_id=1, source_target_pairs={{0,24},{1,25},{2,26},{3,27},{4,28},{5,29},{6,30},{7,31},{8,0},{9,1... | collective-permute-start | bytes 1204232 | tf_op jit(solution)/shard_map/ppermute | solution.py:316
  467.7 19.5 %collective-permute-start.74 = (bf16[784,256]{1,0:T(8,128)(2,1)}, bf16[784,256]{1,0:T(8,128)(2,1)}, u32[]{:S(2)}, u32[]{:S(2)}) collective-permute-start(bf16[784,256]{1,0:T(8,128)(2,1)} %get-tuple-element.55), channel_id=1, source_target_pairs={{0,4},{1,5},{2,6},{3,7},{4,0},{5,1},{6,2},{7,3},{8,12},{9,13},{10,... | collective-permute-start | bytes 1204232 | tf_op jit(solution)/shard_map/ppermute | solution.py:316
  468.1 57.8 %collective-permute-start.80 = (bf16[4,2,192,256]{3,2,1,0:T(8,128)(2,1)}, bf16[4,2,192,256]{3,2,1,0:T(8,128)(2,1)}, u32[]{:S(2)}, u32[]{:S(2)}) collective-permute-start(bf16[4,2,192,256]{3,2,1,0:T(8,128)(2,1)} %dynamic-slice_bitcast_fusion.1), channel_id=1, source_target_pairs={{0,2},{1,3},{2,0},{3,1},{4,6},{5,7},{6,4},{7,5},{8,10},{9,11},{10,... | collective-permute-start | bytes 2359304 | tf_op jit(solution)/shard_map/ppermute | solution.py:316
  474.2 23.3 %collective-permute-start.68 = (bf16[784,256]{1,0:T(8,128)(2,1)}, bf16[784,256]{1,0:T(8,128)(2,1)}, u32[]{:S(2)}, u32[]{:S(2)}) collective-permute-start(bf16[784,256]{1,0:T(8,128)(2,1)} %get-tuple-element.51), channel_id=1, source_target_pairs={{0,2},{1,3},{2,0},{3,1},{4,6},{5,7},{6,4},{7,5},{8,10},{9,11},{10,... | collective-permute-start | bytes 1204232 | tf_op jit(solution)/shard_map/ppermute | solution.py:316
  475.5 30.5 %collective-permute-start.72 = (bf16[784,256]{1,0:T(8,128)(2,1)}, bf16[784,256]{1,0:T(8,128)(2,1)}, u32[]{:S(2)}, u32[]{:S(2)}) collective-permute-start(bf16[784,256]{1,0:T(8,128)(2,1)} %get-tuple-element.50), channel_id=1, source_target_pairs={{0,2},{1,3},{2,0},{3,1},{4,6},{5,7},{6,4},{7,5},{8,10},{9,11},{10,... | collective-permute-start | bytes 1204232 | tf_op jit(solution)/shard_map/ppermute | solution.py:316
  480.8 33.9 %collective-permute-start.76 = (bf16[784,256]{1,0:T(8,128)(2,1)}, bf16[784,256]{1,0:T(8,128)(2,1)}, u32[]{:S(2)}, u32[]{:S(2)}) collective-permute-start(bf16[784,256]{1,0:T(8,128)(2,1)} %get-tuple-element.49), channel_id=1, source_target_pairs={{0,2},{1,3},{2,0},{3,1},{4,6},{5,7},{6,4},{7,5},{8,10},{9,11},{10,... | collective-permute-start | bytes 1204232 | tf_op jit(solution)/shard_map/ppermute | solution.py:316
  487.2 40.0 %collective-permute-start.63 = (bf16[784,256]{1,0:T(8,128)(2,1)}, bf16[784,256]{1,0:T(8,128)(2,1)S(1)}, u32[]{:S(2)}, u32[]{:S(2)}) collective-permute-start(bf16[784,256]{1,0:T(8,128)(2,1)} %get-tuple-element.61), channel_id=1, source_target_pairs={{0,4},{1,5},{2,6},{3,7},{4,0},{5,1},{6,2},{7,3},{8,12},{9,13},{10,... | collective-permute-start | bytes 1204232 | tf_op jit(solution)/shard_map/ppermute | solution.py:316
  497.5 33.4 %collective-permute-start.65 = (bf16[784,256]{1,0:T(8,128)(2,1)}, bf16[784,256]{1,0:T(8,128)(2,1)S(1)}, u32[]{:S(2)}, u32[]{:S(2)}) collective-permute-start(bf16[784,256]{1,0:T(8,128)(2,1)} %get-tuple-element.52), channel_id=1, source_target_pairs={{0,2},{1,3},{2,0},{3,1},{4,6},{5,7},{6,4},{7,5},{8,10},{9,11},{10,... | collective-permute-start | bytes 1204232 | tf_op jit(solution)/shard_map/ppermute | solution.py:316
  523.5 25.3 %collective-permute-start.73 = (bf16[784,256]{1,0:T(8,128)(2,1)S(1)}, bf16[784,256]{1,0:T(8,128)(2,1)S(1)}, u32[]{:S(2)}, u32[]{:S(2)}) collective-permute-start(bf16[784,256]{1,0:T(8,128)(2,1)S(1)} %get-tuple-element.78), channel_id=1, source_target_pairs={{0,16},{1,17},{2,18},{3,19},{4,20},{5,21},{6,22},{7,23},{8,24},{9,... | collective-permute-start | bytes 1204232 | tf_op jit(solution)/shard_map/ppermute | solution.py:316
  525.9 22.9 %collective-permute-start.77 = (bf16[784,256]{1,0:T(8,128)(2,1)S(1)}, bf16[784,256]{1,0:T(8,128)(2,1)S(1)}, u32[]{:S(2)}, u32[]{:S(2)}) collective-permute-start(bf16[784,256]{1,0:T(8,128)(2,1)S(1)} %get-tuple-element.77), channel_id=1, source_target_pairs={{0,24},{1,25},{2,26},{3,27},{4,28},{5,29},{6,30},{7,31},{8,0},{9,1... | collective-permute-start | bytes 1204232 | tf_op jit(solution)/shard_map/ppermute | solution.py:316
  527.3 22.9 %collective-permute-start.81 = (bf16[4,192,256]{2,1,0:T(8,128)(2,1)S(1)}, bf16[4,192,256]{2,1,0:T(8,128)(2,1)S(1)}, u32[]{:S(2)}, u32[]{:S(2)}) collective-permute-start(bf16[4,192,256]{2,1,0:T(8,128)(2,1)S(1)} %dynamic-slice_bitcast_fusion.18), channel_id=1, source_target_pairs={{0,4},{1,5},{2,6},{3,7},{4,0},{5,1},{6,2},{7,3},{8,12},{9,13},{10,... | collective-permute-start | bytes 1179656 | tf_op jit(solution)/shard_map/ppermute | solution.py:316
  (73 other events, 1707.1 us)

commit v2 on v1

v2 whole, which is shorter than its diff:
```python
import functools

import jax
import jax.numpy as jnp
import numpy as np
from jax import lax
from jax.experimental import pallas as pl
from jax.experimental.pallas import tpu as pltpu
from jax.sharding import PartitionSpec as P

HID = 1024
CLS = 81
POOL = 7
CELLS = POOL * POOL
WIN = 16
STEP = 10
HEAD = 401
HEADP = 512
CORES = 2
CHUNKS = 4
GROUP = 32
KSTEP = 7
LATE_OUT = 192
LATE_BACK = 160
TERMS = 3
EXTRA = 16
MIB = 2**20
LIGHT = pl.CostEstimate(flops=0, bytes_accessed=1024, transcendentals=0)

AXES = ("wide", "tp")
rate_first = 0.02
rate_second = 0.06
rate_heads = 0.06
rate_biases = 0.3
decay_one = 0.9
decay_two = 0.999
epsilon = 1e-08
weight_decay = 0.1
GELU_A = 0.7978845608028654
GELU_B = 0.044715

f32 = jnp.float32
bf16 = jnp.bfloat16


def dot(a, b, contract=((1,), (0,))):
    return lax.dot_general(a, b, (contract, ((), ())), preferred_element_type=f32)


def crop_kernel(first, base_ref, col_ref, maps_ref, wr_ref, wc_ref, rep_ref, tile_ref, *refs):
    out_ref, rows_s, cols_s, left, right = refs
    step = pl.program_id(0)
    lanes = rows_s.shape[1]
    halves = (left, right)
    rows_s[...] = dot(wr_ref[...], rep_ref[...])
    cols_s[...] = dot(wc_ref[...], tile_ref[...])

    def one(i, carry):
        r = first + step * GROUP + i
        at = pl.multiple_of(i * 8, 8)
        rows = rows_s[pl.ds(at, 8), :]
        x0 = col_ref[r]
        cols = jnp.concatenate(
            [pltpu.roll(cols_s[pl.ds(at, 8), k : k + 128], x0, 1) for k in range(0, lanes, 128)], axis=1
        )
        both = jnp.concatenate([rows[a : a + 1, :] * cols for a in range(POOL)], axis=0)
        high = both.astype(bf16)
        low = (both - high.astype(f32)).astype(bf16)
        window = maps_ref[pl.ds(base_ref[r], WIN), :, :].reshape(lanes, maps_ref.shape[2])
        got = dot(jnp.concatenate([high, low], axis=0), window)
        got = got[: POOL * 8] + got[POOL * 8 :]
        for h, half in enumerate(halves):
            half[pl.ds(pl.multiple_of(i * POOL * 8, 8), POOL * 8), :] = got[:, h * 128 : (h + 1) * 128]
        return carry

    lax.fori_loop(0, GROUP, one, 0, unroll=4)
    for a in range(POOL):
        for b in range(POOL):
            for h, half in enumerate(halves):
                out_ref[a * POOL + b, :, h * 128 : (h + 1) * 128] = half[
                    pl.ds(a * 8 + b, GROUP, stride=POOL * 8), :
                ].astype(bf16)


def window_crops(maps, base, col, wr, wc, first, count):
    rows, width, channels = maps.shape
    lanes = WIN * width
    lane = np.arange(lanes)[None]
    unit = np.arange(WIN)[:, None]
    rep = jnp.asarray(lane // width == unit, bf16)
    til = jnp.asarray(lane % width == unit, bf16)
    return pl.pallas_call(
        functools.partial(crop_kernel, first),
        grid_spec=pltpu.PrefetchScalarGridSpec(
            num_scalar_prefetch=2,
            grid=(count // GROUP,),
            in_specs=[
                pl.BlockSpec(maps.shape, lambda i, *_: (0, 0, 0)),
                pl.BlockSpec((GROUP * 8, WIN), lambda i, *_: (first // GROUP + i, 0)),
                pl.BlockSpec((GROUP * 8, WIN), lambda i, *_: (first // GROUP + i, 0)),
                pl.BlockSpec(rep.shape, lambda i, *_: (0, 0)),
                pl.BlockSpec(til.shape, lambda i, *_: (0, 0)),
            ],
            out_specs=pl.BlockSpec((CELLS, GROUP, channels), lambda i, *_: (0, i, 0)),
            scratch_shapes=[
                pltpu.VMEM((GROUP * 8, lanes), f32),
                pltpu.VMEM((GROUP * 8, lanes), f32),
                pltpu.VMEM((GROUP * POOL * 8, 128), f32),
                pltpu.VMEM((GROUP * POOL * 8, 128), f32),
            ],
        ),
        out_shape=jax.ShapeDtypeStruct((CELLS, count, channels), bf16),
        compiler_params=pltpu.CompilerParams(vmem_limit_bytes=18 * MIB),
        cost_estimate=LIGHT,
        name="crops",
    )(base, col, maps, wr, wc, rep, til)


def first_kernel(parts, *refs):
    crops, weight, own, send = refs[:parts], refs[parts], refs[parts + 1], refs[parts + 2]
    step = pl.program_id(0)
    blocks, depth, cols = weight.shape
    channels = crops[0].shape[2]

    @pl.when(step == 0)
    def _():
        own[...] = jnp.zeros_like(own)
        send[...] = jnp.zeros_like(send)

    for out, refs_half in ((own, crops[: parts // 2]), (send, crops[parts // 2 :])):
        lhs = jnp.concatenate(
            [jnp.concatenate([ref[j] for ref in refs_half], axis=0) for j in range(depth // channels)], axis=1
        )
        for y in range(blocks):
            out[:, y * cols : (y + 1) * cols] += dot(lhs, weight[y])


def first_layer(crops, weight):
    parts = len(crops)
    blocks, feats, cols = weight.shape
    channels = crops[0].shape[2]
    rows = sum(c.shape[1] for c in crops) // 2
    return pl.pallas_call(
        functools.partial(first_kernel, parts),
        grid=(CELLS // KSTEP,),
        in_specs=[pl.BlockSpec((KSTEP,) + c.shape[1:], lambda i: (i, 0, 0)) for c in crops]
        + [pl.BlockSpec((blocks, KSTEP * channels, cols), lambda i: (0, i, 0))],
        out_specs=[pl.BlockSpec((rows, blocks * cols), lambda i: (0, 0))] * 2,
        out_shape=[jax.ShapeDtypeStruct((rows, blocks * cols), f32)] * 2,
        compiler_params=pltpu.CompilerParams(vmem_limit_bytes=60 * MIB),
        cost_estimate=LIGHT,
        name="first_layer",
    )(*crops, weight)


def first_grad_kernel(parts, cols, *refs):
    crops, own, got, out = refs[:parts], refs[parts], refs[parts + 1], refs[parts + 2]
    channels = crops[0].shape[2]
    grads = jnp.concatenate([own[...], got[...]], axis=0)
    for j in range(crops[0].shape[0]):
        lhs = jnp.concatenate([ref[j] for ref in crops], axis=0)
        res = dot(lhs, grads, ((0,), (0,))).astype(bf16)
        for y in range(out.shape[0]):
            out[y, j * channels : (j + 1) * channels, :] = res[:, y * cols : (y + 1) * cols]


def first_grad(crops, own, got, blocks):
    parts = len(crops)
    rows, units = own.shape
    cols = units // blocks
    channels = crops[0].shape[2]
    return pl.pallas_call(
        functools.partial(first_grad_kernel, parts, cols),
        grid=(CELLS // KSTEP,),
        in_specs=[pl.BlockSpec((KSTEP,) + c.shape[1:], lambda i: (i, 0, 0)) for c in crops]
        + [pl.BlockSpec((rows, units), lambda i: (0, 0))] * 2,
        out_specs=pl.BlockSpec((blocks, KSTEP * channels, cols), lambda i: (0, i, 0)),
        out_shape=jax.ShapeDtypeStruct((blocks, CELLS * channels, cols), bf16),
        compiler_params=pltpu.CompilerParams(vmem_limit_bytes=60 * MIB),
        cost_estimate=LIGHT,
        name="first_grad",
    )(*crops, own, got)


def block_span(feats, wide, channels):
    span = max(-(-((w * feats) % channels + feats) // channels) for w in range(wide))
    return span if all(w * feats // channels + span <= CELLS for w in range(wide)) else 0


def cell_copies(crops, start, span, cells, sems):
    found = []
    at = 0
    for n, ref in enumerate(crops):
        rows = ref.shape[1]
        found.append(pltpu.make_async_copy(ref.at[pl.ds(start, span)], cells.at[:, pl.ds(at, rows)], sems.at[n]))
        at += rows
    return found


def block_kernel(span, items, feats, most, parts, fresh, place, *refs):
    count = len(items)
    crops, rest = refs[:parts], refs[parts:]
    own, send, pad, cells, sems = rest[-5:]
    before, inputs = (None, rest[:-5]) if fresh else (rest[:2], rest[2:-5])
    step = pl.program_id(0)
    rows = own.shape[0]
    channels = cells.shape[3]
    cols = inputs[0].shape[1]
    firsts = [sum(len(ys) + 1 for _, ys in items[:i]) for i in range(count)]

    def copies(i):
        slot = i % 2
        start = place[i] * feats
        at = pl.multiple_of(start % channels, 16)
        side, ys = items[i]
        found = cell_copies(crops, start // channels, span, cells.at[slot], sems.at[slot])
        group = inputs[firsts[i] : firsts[i] + len(ys) + 1]
        for k, y in enumerate(ys):
            lanes = pl.ds(y * cols, cols)
            found.append(
                pltpu.make_async_copy(
                    group[k].at[pl.ds(0, most)], pad.at[slot, pl.ds(at, most), lanes], sems.at[slot, parts + 2 * k]
                )
            )
            found.append(
                pltpu.make_async_copy(
                    group[-1].at[y, side, pl.ds(0, feats - most)],
                    pad.at[slot, pl.ds(pl.multiple_of(at + most, 16), feats - most), lanes],
                    sems.at[slot, parts + 1 + 2 * k],
                )
            )
        return found

    def edges(i):
        pad[i % 2, :channels, :] = jnp.zeros((channels, pad.shape[2]), bf16)
        pad[i % 2, pad.shape[1] - channels :, :] = jnp.zeros((channels, pad.shape[2]), bf16)

    @pl.when(step == 0)
    def _():
        edges(0)
        for copy in copies(0):
            copy.start()
        if fresh:
            own[...] = jnp.zeros_like(own)
            send[...] = jnp.zeros_like(send)
        else:
            own[...] = before[0][...]
            send[...] = before[1][...]

    def multiply(lanes):
        slot = lax.rem(step, 2)
        weight = pad[slot, :, lanes]
        for at, out in ((0, own), (rows, send)):
            lhs = jnp.concatenate([cells[slot, j, at : at + rows, :] for j in range(span)], axis=1)
            out[:, lanes] += dot(lhs, weight)

    for i in range(count):

        @pl.when(step == i)
        def _(i=i):
            if i + 1 < count:
                edges(i + 1)
                for copy in copies(i + 1):
                    copy.start()
            for copy in copies(i):
                copy.wait()

    every = tuple(range(pad.shape[2] // cols))
    for ys in sorted({ys for _, ys in items}):
        here = [i for i, item in enumerate(items) if item[1] == ys]
        lanes = slice(0, pad.shape[2]) if ys == every else slice(ys[0] * cols, (ys[0] + 1) * cols)

        @pl.when(functools.reduce(jnp.logical_or, [step == i for i in here]))
        def _(lanes=lanes):
            multiply(lanes)


def whole(shape):
    return pl.BlockSpec(shape, lambda i, place: (0,) * len(shape))


def first_blocks(place, crops, inputs, items, feats, most, span, blocks, before):
    rows = sum(c.shape[1] for c in crops) // 2
    channels = crops[0].shape[2]
    units = blocks * inputs[0].shape[1]
    lead = [] if before is None else list(before)
    away = pl.BlockSpec(memory_space=pl.ANY)
    parts = len(crops)
    return pl.pallas_call(
        functools.partial(block_kernel, span, items, feats, most, parts, before is None),
        grid_spec=pltpu.PrefetchScalarGridSpec(
            num_scalar_prefetch=1,
            grid=(len(items),),
            in_specs=[away] * parts + [whole((rows, units))] * len(lead) + [away] * len(inputs),
            out_specs=[whole((rows, units))] * 2,
            scratch_shapes=[
                pltpu.VMEM((2, span * channels, units), bf16),
                pltpu.VMEM((2, span, 2 * rows, channels), bf16),
                pltpu.SemaphoreType.DMA((2, parts + 2 * blocks)),
            ],
        ),
        out_shape=[jax.ShapeDtypeStruct((rows, units), f32)] * 2,
        input_output_aliases={} if before is None else {1 + parts: 0, 2 + parts: 1},
        compiler_params=pltpu.CompilerParams(vmem_limit_bytes=60 * MIB),
        cost_estimate=LIGHT,
        name="first_blocks",
    )(place, *crops, *lead, *inputs)


def block_grad_kernel(span, feats, blocks, parts, place, *refs):
    crops, (own, got), rest = refs[:parts], refs[parts : parts + 2], refs[parts + 2 :]
    outs, (full, cells, in_sems, out_sems) = rest[:-4], rest[-4:]
    step = pl.program_id(0)
    count = len(outs) // (2 * blocks)
    channels = cells.shape[3]
    cols = full.shape[2] // blocks

    def loads(i):
        return cell_copies(crops, (place[i] * feats) // channels, span, cells.at[i % 2], in_sems.at[i % 2])

    def stores(i):
        at = pl.multiple_of((place[i] * feats) % channels, 16)
        found = []
        for y in range(blocks):
            main, late = outs[(i * blocks + y) * 2], outs[(i * blocks + y) * 2 + 1]
            most = main.shape[0]
            lanes = pl.ds(y * cols, cols)
            found.append(pltpu.make_async_copy(full.at[i % 2, pl.ds(at, most), lanes], main, out_sems.at[i % 2, 2 * y]))
            found.append(
                pltpu.make_async_copy(
                    full.at[i % 2, pl.ds(pl.multiple_of(at + most, 16), feats - most), lanes],
                    late,
                    out_sems.at[i % 2, 2 * y + 1],
                )
            )
        return found

    @pl.when(step == 0)
    def _():
        for copy in loads(0):
            copy.start()

    for i in range(count):

        @pl.when(step == i)
        def _(i=i):
            if i + 1 < count:
                for copy in loads(i + 1):
                    copy.start()
            for copy in loads(i):
                copy.wait()
            if i >= 2:
                for copy in stores(i - 2):
                    copy.wait()

    slot = lax.rem(step, 2)
    grads = jnp.concatenate([own[...], got[...]], axis=0)
    for j in range(span):
        full[slot, j * channels : (j + 1) * channels, :] = dot(cells[slot, j], grads, ((0,), (0,))).astype(bf16)

    for i in range(count):

        @pl.when(step == i)
        def _(i=i):
            for copy in stores(i):
                copy.start()
            if i == count - 1:
                for k in range(max(0, count - 2), count):
                    for copy in stores(k):
                        copy.wait()


def first_grad_blocks(place, crops, own, got, feats, late, blocks, span):
    rows, units = own.shape
    channels = crops[0].shape[2]
    cols = units // blocks
    count = place.shape[0]
    parts = len(crops)
    outs = [(feats - late, cols), (late, cols)] * (count * blocks)
    away = pl.BlockSpec(memory_space=pl.ANY)
    return pl.pallas_call(
        functools.partial(block_grad_kernel, span, feats, blocks, parts),
        grid_spec=pltpu.PrefetchScalarGridSpec(
            num_scalar_prefetch=1,
            grid=(count,),
            in_specs=[away] * parts + [whole((rows, units))] * 2,
            out_specs=[away] * len(outs),
            scratch_shapes=[
                pltpu.VMEM((2, span * channels, units), bf16),
                pltpu.VMEM((2, span, 2 * rows, channels), bf16),
                pltpu.SemaphoreType.DMA((2, parts)),
                pltpu.SemaphoreType.DMA((2, 2 * blocks)),
            ],
        ),
        out_shape=[jax.ShapeDtypeStruct(v, bf16) for v in outs],
        compiler_params=pltpu.CompilerParams(vmem_limit_bytes=60 * MIB),
        cost_estimate=LIGHT,
        name="first_grad",
    )(place, *crops, own, got)


def small_place(half, begin, end):
    lane = 0 if end <= half else 128
    back = half if lane else 0
    return slice(begin - back, end - back), slice(lane, lane + 128)


def prepare_kernel(first, second, heads, crowd, mine, low, wide_heads):
    feats = first.shape[0]
    share = second.shape[0]
    rows = heads.shape[0]
    half = mine.shape[0] - feats
    value = first[...].astype(bf16)
    mine[:feats, :] = value
    low[...] = value[: low.shape[0], :]
    kept = jnp.sum(1 - crowd[...], axis=1, keepdims=True)
    wide_heads[...] = jnp.zeros_like(wide_heads)
    wide_heads[:, :HEAD] = heads[...]
    lane = lax.broadcasted_iota(jnp.int32, (rows, 128), 1)
    row = lax.broadcasted_iota(jnp.int32, (rows, 128), 0)
    marks = jnp.where(lane == 127, kept % 128, jnp.where(lane == 126, kept // 128, 0))
    wide_heads[:, HEADP - 128 :] += jnp.where(row == 0, marks, 0).astype(f32)
    for begin, end in ((0, min(share, half)), (half, share)):
        if begin < end:
            at, lanes = small_place(half, begin, end)
            mine[feats + at.start : feats + at.stop, lanes] = second[begin:end, :].astype(bf16)
    for k in range(HEADP // 128):
        at, lanes = small_place(half, share + k * rows, share + (k + 1) * rows)
        mine[feats + at.start : feats + at.stop, lanes] = wide_heads[:, k * 128 : (k + 1) * 128].astype(bf16)


def prepare(first, second, heads, crowd, most):
    feats, cols = first.shape
    half = (second.shape[0] + heads.shape[0] * HEADP // 128) // 2
    vmem = pl.BlockSpec(memory_space=pltpu.VMEM)
    return pl.pallas_call(
        prepare_kernel,
        in_specs=[vmem] * 4,
        out_specs=[vmem] * 2,
        out_shape=[jax.ShapeDtypeStruct((feats + half, cols), bf16), jax.ShapeDtypeStruct((most, cols), bf16)],
        scratch_shapes=[pltpu.VMEM((heads.shape[0], HEADP), f32)],
        cost_estimate=LIGHT,
        compiler_params=pltpu.CompilerParams(vmem_limit_bytes=16 * MIB),
        name="prepare",
    )(first, second, heads, crowd[None, :])


def unpack_kernel(depth, core_ref, wide_ref, *refs):
    stacks_own, stacks_sib = refs[:depth], refs[depth : 2 * depth]
    w2_own, w2_sib, wh = refs[2 * depth :]
    blocks, xs, half, _ = stacks_sib[0].shape
    share = w2_own.shape[0] // blocks
    count = depth * xs
    rows = wh.shape[0] // (count * blocks * CORES)
    for n in range(count):
        at = wide_ref[n]
        for y in range(blocks):
            turned = lax.rem(wide_ref[count] + blocks - y, blocks)
            for stacks, w2, side in ((stacks_own, w2_own, core_ref[0]), (stacks_sib, w2_sib, 1 - core_ref[0])):
                stack = stacks[n // xs]
                skip = stack.shape[2] - half

                def small(begin, end):
                    rows_at, lanes_at = small_place(half, begin, end)
                    return stack[y, n % xs, skip + rows_at.start : skip + rows_at.stop, lanes_at]

                lanes = pl.ds(pl.multiple_of(at * 128, 128), 128)
                for begin, end in ((0, min(share, half)), (half, share)):
                    if begin < end:
                        w2[y * share + begin : y * share + end, lanes] = small(begin, end)
                to = pl.multiple_of(((at * blocks + turned) * CORES + side) * rows, rows)
                for k in range(HEADP // 128):
                    wh[pl.ds(to, rows), k * 128 : (k + 1) * 128] = small(share + k * rows, share + (k + 1) * rows)


def unpack(core, wide, own, sib, units):
    smem = pl.BlockSpec(memory_space=pltpu.SMEM)
    vmem = pl.BlockSpec(memory_space=pltpu.VMEM)
    return pl.pallas_call(
        functools.partial(unpack_kernel, len(own)),
        in_specs=[smem, smem] + [vmem] * (2 * len(own)),
        out_specs=[vmem] * 3,
        out_shape=[jax.ShapeDtypeStruct((units, HID), bf16)] * 2 + [jax.ShapeDtypeStruct((HID, HEADP), bf16)],
        cost_estimate=LIGHT,
        compiler_params=pltpu.CompilerParams(vmem_limit_bytes=16 * MIB),
        name="unpack",
    )(core, wide, *own, *sib)


def pack_kernel(core_ref, wide_ref, gw2, gw2_got, gwh, gwh_got, sums, out):
    depth, blocks, xs, half, _ = out.shape
    half -= EXTRA
    share = gw2.shape[0] // blocks
    count = depth * xs
    rows = gwh.shape[0] // (count * blocks * CORES)
    for n in range(count):
        at = wide_ref[n]
        lanes = pl.ds(pl.multiple_of(at * 128, 128), 128)
        for y in range(blocks):

            def small(begin, end, value):
                rows_at, lanes_at = small_place(half, begin, end)
                out[n // xs, y, n % xs, rows_at, lanes_at] = value.astype(bf16)

            ahead = lax.rem(wide_ref[count] + y, blocks)
            turned = (blocks - y) % blocks
            for begin, end in ((0, min(share, half)), (half, share)):
                if begin < end:
                    part = slice(turned * share + begin, turned * share + end)
                    small(begin, end, gw2[part, lanes] + gw2_got[part, lanes].astype(f32))
            here = pl.ds(pl.multiple_of(((at * blocks + ahead) * CORES + core_ref[0]) * rows, rows), rows)
            for k in range(HEADP // 128):
                group = slice(k * 128, (k + 1) * 128)
                small(share + k * rows, share + (k + 1) * rows, gwh[here, group] + gwh_got[here, group].astype(f32))
    rest = sums[...]
    rows_left = []
    for _ in range(TERMS):
        term = rest.astype(bf16).astype(f32)
        rest = rest - term
        rows_left += [term[:, k : k + 256] for k in range(0, term.shape[1], 256)]
    rows_left += [jnp.zeros_like(rows_left[0])] * (-len(rows_left) % 8)
    each = len(rows_left) // (blocks * xs)
    for y in range(blocks):
        for x in range(xs):
            n = y * xs + x
            some = rows_left[n * each : (n + 1) * each] + [jnp.zeros_like(rows_left[0])] * (EXTRA - each)
            some = jnp.concatenate(some, axis=0).astype(bf16)
            for dz in range(depth):
                out[dz, y, x, half:, :] = some if dz >= 2 else jnp.zeros_like(some)


def pack(core, wide, gw2, gw2_got, gwh, gwh_got, sums, shape):
    smem = pl.BlockSpec(memory_space=pltpu.SMEM)
    vmem = pl.BlockSpec(memory_space=pltpu.VMEM)
    return pl.pallas_call(
        pack_kernel,
        in_specs=[smem, smem] + [vmem] * 5,
        out_specs=vmem,
        out_shape=jax.ShapeDtypeStruct(shape, bf16),
        cost_estimate=LIGHT,
        compiler_params=pltpu.CompilerParams(vmem_limit_bytes=18 * MIB),
        name="pack",
    )(core, wide, gw2, gw2_got, gwh, gwh_got, sums)


def gelu(x):
    return 0.5 * x * (1.0 + jnp.tanh(GELU_A * (x + GELU_B * x * x * x)))


def gelu_slope(x):
    t = jnp.tanh(GELU_A * (x + GELU_B * x * x * x))
    return 0.5 * (1.0 + t) + 0.5 * x * (1.0 - t * t) * (GELU_A * (1.0 + 3.0 * GELU_B * x * x))


def head_kernel(
    share,
    at_ref,
    pre_own,
    pre_sib,
    w2_own,
    w2_sib,
    wh,
    b1,
    b2,
    bh,
    tags,
    g_own,
    g_sib,
    gw2_own,
    gw2_sib,
    gwh,
    gwh_low,
    sums,
    count,
    h1,
    pre2,
    gpre2,
):
    rows, units = pre_own.shape
    sides = ((pre_own, w2_own, g_own, gw2_own, 0), (pre_sib, w2_sib, g_sib, gw2_sib, units))
    pre2[...] = jnp.zeros_like(pre2) + b2[...]
    for pre, w2, _, _, at in sides:
        h1[:, at : at + units] = gelu(pre[...] + b1[:, at : at + units]).astype(bf16)
        for k in range(0, units, share):
            part = dot(h1[:, at + k : at + k + share], w2[k : k + share, :])
            pre2[...] += part.astype(bf16).astype(f32)
    h2 = gelu(pre2[...]).astype(bf16)
    out = dot(h2, wh[...]) + bh[...]
    col = lax.broadcasted_iota(jnp.int32, out.shape, 1)
    label = tags[:, 4:5].astype(jnp.int32)
    valid = 1.0 - tags[:, 5:6]
    fore = jnp.where(label > 0, valid, 0.0)
    is_logit = col < CLS
    onehot = jnp.where(col == label, 1.0, 0.0)
    masked = jnp.where(is_logit, out, -jnp.inf)
    top = jnp.max(masked, axis=1, keepdims=True)
    shifted = jnp.exp(masked - top)
    total = jnp.sum(shifted, axis=1, keepdims=True)
    row_loss = valid * (jnp.log(total) + top - jnp.sum(onehot * out, axis=1, keepdims=True))
    ends = jnp.sum(wh[:, HEADP - 128 :].astype(f32), axis=0, keepdims=True)
    kept = 128.0 * ends[:, 126:127] + ends[:, 127:128]
    count[...] = kept
    scale = 1.0 / kept
    grad = (shifted / total - onehot) * (valid * scale)
    base = CLS + 4 * (label - 1)
    for j in range(4):
        mark = (col == base + j) & (col >= CLS)
        err = jnp.sum(jnp.where(mark, out, 0.0), axis=1, keepdims=True) - tags[:, j : j + 1]
        size = jnp.abs(err)
        row_loss += fore * jnp.where(size < 1.0, 0.5 * err * err, size - 0.5)
        grad += jnp.where(mark, jnp.clip(err, -1.0, 1.0) * (fore * scale), 0.0)
    g_out = grad.astype(bf16)
    head_sums = jnp.sum(g_out.astype(f32), axis=0, keepdims=True)
    lane = lax.broadcasted_iota(jnp.int32, head_sums.shape, 1)
    loss = jnp.sum(row_loss, axis=0, keepdims=True)
    sums[:, 2 * HID : 2 * HID + HEADP] = jnp.where(lane == HEAD, loss, head_sums)
    gwh[...] = dot(h2, g_out, ((0,), (0,)))
    gwh_low[...] = gwh[...].astype(bf16)
    g_h2 = dot(g_out, wh[...], ((1,), (1,)))
    g2 = (g_h2 * gelu_slope(pre2[...])).astype(bf16)
    sums[:, HID : 2 * HID] = jnp.sum(g2.astype(f32), axis=0, keepdims=True)
    gpre2[...] = g2
    for n, (pre, w2, g1, gw2, at) in enumerate(sides):
        g_h1 = dot(gpre2[...], w2[...], ((1,), (1,)))
        g = (g_h1 * gelu_slope(pre[...] + b1[:, at : at + units])).astype(bf16)
        g1[...] = g
        columns = jnp.sum(g.astype(f32), axis=0, keepdims=True)
        for k in range(units // share):
            to = pl.multiple_of(at_ref[n * (units // share) + k] * share, share)
            sums[:, pl.ds(to, share)] = columns[:, k * share : (k + 1) * share]
        gw2[...] = dot(h1[:, at : at + units], gpre2[...], ((0,), (0,))).astype(gw2.dtype)


def heads_step(share, at, pre_own, pre_sib, w2_own, w2_sib, wh, b1, b2, bh, tags):
    rows, units = pre_own.shape
    vmem = pl.BlockSpec(memory_space=pltpu.VMEM)
    shape = jax.ShapeDtypeStruct
    return pl.pallas_call(
        functools.partial(head_kernel, share),
        in_specs=[pl.BlockSpec(memory_space=pltpu.SMEM)] + [vmem] * 9,
        out_specs=[vmem] * 8,
        out_shape=[
            shape((rows, units), bf16),
            shape((rows, units), bf16),
            shape((units, HID), f32),
            shape((units, HID), bf16),
            shape((HID, HEADP), f32),
            shape((HID, HEADP), bf16),
            shape((1, 2 * HID + HEADP), f32),
            shape((1, 1), f32),
        ],
        scratch_shapes=[pltpu.VMEM((rows, HID), bf16), pltpu.VMEM((rows, HID), f32), pltpu.VMEM((rows, HID), bf16)],
        compiler_params=pltpu.CompilerParams(vmem_limit_bytes=26 * MIB),
        cost_estimate=LIGHT,
        name="heads",
    )(at, pre_own, pre_sib, w2_own, w2_sib, wh, b1, b2, bh, tags)


class Grid:
    def __init__(self):
        self.wide = lax.axis_size("wide")
        self.tp = lax.axis_size("tp")
        self.y = self.tp // CORES
        self.x = self.y if self.wide % self.y == 0 else 1
        self.z = self.wide // self.x
        self.size = {"z": self.z, "x": self.x, "y": self.y, "c": CORES}
        wide, tp = lax.axis_index("wide"), lax.axis_index("tp")
        self.at = {"z": wide // self.x, "x": wide % self.x, "y": tp // CORES, "c": tp % CORES}

    def move(self, value, axis, by):
        pairs = []
        for z in range(self.z):
            for x in range(self.x):
                for y in range(self.y):
                    for c in range(CORES):
                        to = {"z": z, "x": x, "y": y, "c": c}
                        for a in axis:
                            to[a] = (to[a] + by) % self.size[a]
                        pairs.append((self.index(z, x, y, c), self.index(to["z"], to["x"], to["y"], to["c"])))
        return lax.ppermute(value, AXES, pairs)

    def flip(self, value, axis, bit):
        unit = {"c": 1, "y": CORES, "x": CORES * self.y, "z": CORES * self.y * self.x}
        step = bit * sum(unit[a] for a in axis)
        return lax.ppermute(value, AXES, [(i, i ^ step) for i in range(self.wide * self.tp)])

    def index(self, z, x, y, c):
        return ((z * self.x + x) * self.y + y) * CORES + c

    def swap(self, value):
        return self.move(value, "c", 1)


def spread_stacked(grid, value, order):
    stack = value[None, None, None]
    for axis in order:
        place = "zxy".index(axis)
        stack = jnp.concatenate([stack] + [grid.move(stack, axis, by) for by in range(1, grid.size[axis])], axis=place)
    for place, axis in enumerate("zxy"):
        if grid.size[axis] > 1:
            back = (grid.at[axis] - jnp.arange(grid.size[axis])) % grid.size[axis]
            stack = jnp.take(stack, back, axis=place, mode="clip")
    return stack


def collect_stacked(grid, stack, order):
    left = "zxy"
    total = stack
    for axis in order:
        place = left.index(axis)
        total = total.astype(bf16)

        def block(by):
            at = (grid.at[axis] + by) % grid.size[axis]
            return lax.dynamic_index_in_dim(total, at, place, keepdims=False)

        mine = block(0).astype(f32)
        for by in range(1, grid.size[axis]):
            mine = mine + grid.move(block(by), axis, by).astype(f32)
        total = mine
        left = left.replace(axis, "")
    return total


def all_sum(value):
    count = lax.axis_size("wide") * lax.axis_size("tp")
    if count & (count - 1):
        return lax.psum(value, AXES)
    bit = 1
    while bit < count:
        value = value + lax.ppermute(value, AXES, [(i, i ^ bit) for i in range(count)])
        bit *= 2
    return value


def after(value, *others):
    return lax.optimization_barrier((value, *others))[0]


class Links:
    def __init__(self, grid):
        self.grid = grid
        self.last = {}
        self.slots = [{}, {}, {}]

    def next(self):
        self.slots.append({})

    def send(self, value, axis, by=1):
        step = self.slots[-2 if axis == "z" else -3]
        before = [step[a] for a in "zxy" if a in step and a != axis]
        if axis in self.last:
            before.append(self.last[axis])
        sent = self.grid.move(after(value, *before) if before else value, axis, by)
        self.last[axis] = self.slots[-1][axis] = sent
        return sent


def adam_update(weight, grad, first, second, rate):
    first_new = decay_one * first + (1.0 - decay_one) * grad
    second_new = decay_two * second + (1.0 - decay_two) * grad * grad
    first_hat = first_new / (1.0 - decay_one**STEP)
    second_hat = second_new / (1.0 - decay_two**STEP)
    weight_new = weight - rate * (first_hat / (jnp.sqrt(second_hat) + epsilon) + weight_decay * weight)
    return (weight_new, first_new, second_new)


def by_blocks(grid, feats, cols, share, second_cols, head_rows, channels, rows):
    return (
        (grid.z, grid.x, grid.y) == (4, 2, 2)
        and feats % 16 == 0
        and feats > max(LATE_OUT, LATE_BACK)
        and cols == channels == 256
        and second_cols == 128
        and (share, head_rows) == (256, 32)
        and rows % (CHUNKS * GROUP) == 0
        and block_span(feats, grid.wide, channels) > 0
    )


def wide_places(grid, sign):
    places = [
        ((grid.at["z"] + sign * dz) % grid.z) * grid.x + (grid.at["x"] + sign * dx) % grid.x
        for dz in range(grid.z)
        for dx in range(grid.x)
    ]
    return jnp.stack(places + [grid.at["y"]]).astype(jnp.int32)


def low_sum(first, *others):
    total = first.astype(f32)
    for value in others:
        total = total + value.astype(f32)
    return total.astype(bf16)


def terms(value):
    found = []
    for _ in range(TERMS):
        found.append(lax.optimization_barrier(value.astype(bf16)))
        value = value - found[-1].astype(f32)
    return jnp.concatenate(found, axis=0)


def from_terms(rows):
    count = rows.shape[0] // TERMS
    total = rows[:count].astype(f32)
    for k in range(1, TERMS):
        total = total + rows[k * count : (k + 1) * count].astype(f32)
    return total


def blocks_step(grid, make_crops, w_first, w_second, w_heads, biases, crowd, tags):
    feats, cols = w_first.shape
    share, _ = w_second.shape
    head_rows = w_heads.shape[0]
    core = grid.at["c"]
    core_ref = core.reshape(1).astype(jnp.int32)

    links = Links(grid)
    most = feats - LATE_OUT
    mine, first_low = prepare(w_first, w_second, w_heads, crowd, most)
    half = mine.shape[0] - feats
    m = {(0, 0, 0): mine}
    stacks = {}

    m[0, 1, 0] = grid.move(mine, "x", 1)
    m[0, 0, 1] = grid.move(mine, "y", 1)
    m[0, 1, 1] = grid.move(mine, "xy", 1)
    m[1, 0, 0] = grid.move(first_low, "z", 1)
    m[3, 0, 0] = grid.move(first_low, "z", 3)
    own_crops = [make_crops(i) for i in range(CHUNKS)]
    made = own_crops + [m[key] for key in ((0, 1, 0), (0, 0, 1), (0, 1, 1), (1, 0, 0), (3, 0, 0))]
    stacks[0] = jnp.stack([jnp.stack([m[0, x, y][most:] for x in range(grid.x)]) for y in range(grid.y)])
    m[2, 0, 0] = links.send(after(m[1, 0, 0], *made), "z", 1)
    m[1, 1, 0] = links.send(after(m[1, 0, 0], *made), "x")
    m[1, 0, 1] = links.send(after(m[1, 0, 0], *made), "y")
    links.next()
    stacks[1] = links.send(stacks[0], "z", 1)
    m[3, 1, 0] = links.send(m[3, 0, 0], "x")
    m[3, 0, 1] = links.send(m[3, 0, 0], "y")
    links.next()
    stacks[3] = links.send(stacks[0], "z", 3)
    m[2, 1, 0] = links.send(m[2, 0, 0], "x")
    m[2, 0, 1] = links.send(m[2, 0, 0], "y")
    links.next()
    stacks[2] = links.send(stacks[1], "z", 1)
    m[1, 1, 1] = links.send(m[1, 0, 1], "x")
    m[2, 1, 1] = links.send(m[2, 1, 0], "y")
    links.next()
    m[3, 1, 1] = links.send(m[3, 0, 1], "x")
    sib_crops = []
    for chunk in own_crops:
        sib_crops.append(grid.swap(after(chunk, *made)))
    crops = own_crops + sib_crops

    def place(dz, dx, sign):
        z = (grid.at["z"] + sign * dz) % grid.z
        x = (grid.at["x"] + sign * dx) % grid.x
        return z * grid.x + x

    def places(keys, sign):
        return jnp.stack([place(*key, sign) for key in keys]).astype(jnp.int32)

    span = block_span(feats, grid.wide, cols)
    pre = None
    both = (0, 1)
    for work in (
        ((0, 0, both), (0, 1, both), (1, 0, both)),
        ((3, 0, both), (1, 1, both), (2, 0, both), (2, 1, both), (3, 1, (0,))),
        ((3, 1, (1,)),),
    ):
        inputs = [v for dz, dx, ys in work for v in [m[dz, dx, y] for y in ys] + [stacks[dz]]]
        keys = [(dz, dx) for dz, dx, _ in work]
        items = tuple((dx, ys) for _, dx, ys in work)
        pre = first_blocks(places(keys, -1), crops, inputs, items, feats, most, span, grid.y, pre)

    second_own, second_sib, head_matrix = unpack(
        core_ref,
        wide_places(grid, -1),
        [stacks[z] for z in range(4)],
        [grid.swap(stacks[z][:, :, LATE_OUT:]) for z in range(4)],
        HID // CORES,
    )
    bias = biases[:HID].reshape(grid.y, CORES, share)
    bias = jnp.where(grid.at["y"] == 0, bias, bias[::-1])
    bias = jnp.where(core == 0, bias, bias[:, ::-1]).transpose(1, 0, 2).reshape(1, -1)
    unit_at = [2 * ((grid.at["y"] + y) % grid.y) + c for c in (core, 1 - core) for y in range(grid.y)]
    g_own, g_send, gw2, gw2_send, gwh, gwh_low, sums, roi_count = heads_step(
        share,
        jnp.stack(unit_at).astype(jnp.int32),
        pre[0],
        grid.swap(pre[1]),
        second_own,
        second_sib,
        head_matrix,
        bias,
        biases[HID : 2 * HID].reshape(1, -1),
        jnp.pad(biases[2 * HID :], (0, HEADP - HEAD)).reshape(1, -1),
        tags,
    )

    g_got = grid.swap(g_send)
    m = {}
    parts = {}

    def gradients(keys, wait=()):
        where = places(keys, 1)
        outs = first_grad_blocks(after(where, *wait), crops, g_own, g_got, feats, LATE_BACK, grid.y, span)
        for i, (dz, dx) in enumerate(keys):
            for y in range(grid.y):
                m[dz, dx, y], parts[dz, dx, y] = outs[(i * grid.y + y) * 2 : (i * grid.y + y) * 2 + 2]

    gradients([(2, 1), (3, 1)])
    gradients([(2, 0)])
    shape = (grid.z, grid.y, grid.x, half + EXTRA, cols)
    packed = pack(core_ref, wide_places(grid, 1), gw2, grid.swap(gw2_send), gwh, grid.swap(gwh_low), sums, shape)

    def stack_of(dz):
        first = jnp.stack([jnp.stack([parts[dz, dx, y] for dx in range(grid.x)]) for y in range(grid.y)])
        return jnp.concatenate([first, packed[dz]], axis=2)

    links = Links(grid)
    far = stack_of(2)
    gradients([(3, 0), (1, 1)], [far])
    gradients([(1, 0), (0, 1)], [far])
    gradients([(0, 0)], [far])
    x0 = links.send(m[3, 1, 1], "x")
    y0 = links.send(m[2, 1, 1], "y")
    z0 = links.send(far, "z", 1)
    links.next()
    z1 = links.send(stack_of(3), "z", 3)
    x1 = links.send(m[3, 1, 0], "x")
    y1 = links.send(m[2, 0, 1], "y")
    links.next()
    z2 = links.send(low_sum(stack_of(1), z0), "z", 1)
    x2 = links.send(low_sum(m[2, 1, 0], y0), "x")
    y2 = links.send(low_sum(m[3, 0, 1], x0), "y")
    links.next()
    z3 = links.send(low_sum(m[2, 0, 0], x2, y1), "z", 1)
    x3 = links.send(m[1, 1, 1], "x")
    y3 = links.send(m[0, 1, 1], "y")
    links.next()
    z4 = links.send(low_sum(m[3, 0, 0], x1, y2), "z", 3)
    x4 = links.send(m[1, 1, 0], "x")
    y4 = links.send(low_sum(m[1, 0, 1], x3), "y")

    def extra_rows(stack):
        rows = stack[:, :, -EXTRA : 8 - EXTRA].reshape(-1, cols)
        return from_terms(rows[: TERMS * (sums.shape[1] // cols)])

    odd = grid.at["z"] % 2 == 1
    below, above, opposite = extra_rows(z0), extra_rows(z1), extra_rows(z2)
    total = sums.reshape(-1, cols)
    total = (total + jnp.where(odd, below, above)) + (opposite + jnp.where(odd, above, below))
    count = TERMS * total.shape[0]
    late = low_sum(stack_of(0), z1, z2)
    links.next()
    y5 = links.send(jnp.concatenate([late[1].reshape(-1, cols), terms(total)], axis=0), "y")
    x5 = links.send(low_sum(m[0, 1, 0], y3), "x")
    z5 = links.send(low_sum(m[1, 0, 0], x4, y4, z3), "z", 1)
    links.next()
    y6 = links.send(m[0, 0, 1], "y")
    total = total + from_terms(y5[-count:])
    late = low_sum(late[0], y5[:-count].reshape(late[0].shape))
    x6 = links.send(jnp.concatenate([late[1], terms(total)], axis=0), "x")
    total = total + from_terms(x6[-count:])
    total = total + grid.swap(total)
    sums = total.reshape(1, -1)
    main = m[0, 0, 0].astype(f32)
    for value in (x5, y6, z4, z5):
        main = main + value.astype(f32)
    late = late[0].astype(f32) + x6[:-count].astype(f32)

    first_total = jnp.concatenate([main, late[:LATE_BACK]], axis=0)
    late = late[LATE_BACK : LATE_BACK + half]
    total = jnp.concatenate([late[:, :128], late[:, 128:]], axis=0)
    heads_total = jnp.concatenate(
        [total[share + k * head_rows : share + (k + 1) * head_rows] for k in range(HEADP // 128)], axis=1
    )[:, :HEAD]
    return roi_count.reshape(()), sums, first_total, total[:share], heads_total


def stacked_step(grid, make_crops, w_first, w_second, w_heads, biases, crowd, tags):
    feats, cols = w_first.shape
    share, second_cols = w_second.shape
    head_rows = w_heads.shape[0]
    units = HID // CORES
    core = grid.at["c"]
    kept = jnp.sum(1 - crowd)
    head_block = jnp.pad(w_heads, ((0, 0), (0, HEADP - HEAD)))
    spot = (lax.broadcasted_iota(jnp.int32, head_block.shape, 0) == 0) * 1
    lane = lax.broadcasted_iota(jnp.int32, head_block.shape, 1)
    head_block = head_block + (
        spot * (jnp.where(lane == HEADP - 1, kept % 128, 0) + jnp.where(lane == HEADP - 2, kept // 128, 0))
    ).astype(f32)
    small = jnp.concatenate(
        [w_second.astype(bf16).reshape(-1, cols), head_block.astype(bf16).reshape(-1, cols)], axis=0
    )
    second_rows = share * second_cols // cols
    small_all = spread_stacked(grid, small, "zxy").reshape(grid.wide, grid.y, *small.shape)
    weight = spread_stacked(grid, w_first.astype(bf16), "zxy")
    weight = weight.transpose(2, 0, 1, 3, 4).reshape(grid.y, grid.wide * feats, cols)
    crops = [make_crops(i) for i in range(CHUNKS)]
    crops = crops + [grid.swap(c) for c in crops]
    second_own = (
        small_all[:, :, :second_rows]
        .reshape(grid.wide, grid.y, share, second_cols)
        .transpose(1, 2, 0, 3)
        .reshape(units, HID)
    )
    heads_own = small_all[:, :, second_rows:].reshape(grid.wide, grid.y, head_rows, HEADP)
    heads_sib = grid.swap(heads_own)
    head_matrix = jnp.where(
        core == 0, jnp.stack([heads_own, heads_sib], axis=2), jnp.stack([heads_sib, heads_own], axis=2)
    ).reshape(HID, HEADP)
    bias = biases[:HID].reshape(grid.y, CORES, share)
    bias = jnp.where(core == 0, bias, bias[:, ::-1]).transpose(1, 0, 2).reshape(1, -1)
    pre_own, pre_send = first_layer(crops, weight)
    unit_at = [2 * y + c for c in (core, 1 - core) for y in range(grid.y)]
    g_own, g_send, gw2_own, gw2_send, gwh, _, sums, roi_count = heads_step(
        share,
        jnp.stack([jnp.asarray(v) for v in unit_at]).astype(jnp.int32),
        pre_own,
        grid.swap(pre_send),
        second_own,
        grid.swap(second_own),
        head_matrix,
        bias,
        biases[HID : 2 * HID].reshape(1, -1),
        jnp.pad(biases[2 * HID :], (0, HEADP - HEAD)).reshape(1, -1),
        tags,
    )
    grad = first_grad(crops, g_own, grid.swap(g_send), grid.y)
    grad = grad.reshape(grid.y, grid.wide, feats, cols).transpose(1, 0, 2, 3)
    first_total = collect_stacked(grid, grad.reshape(grid.z, grid.x, grid.y, feats, cols), "yxz")
    gw2 = gw2_own + grid.swap(gw2_send).astype(f32)
    gwh = gwh.reshape(grid.wide, grid.y, CORES, head_rows, HEADP)
    gwh = lax.dynamic_index_in_dim(gwh, core, 2, keepdims=False) + grid.swap(
        lax.dynamic_index_in_dim(gwh, 1 - core, 2, keepdims=False)
    )
    gw2 = gw2.astype(bf16).reshape(grid.y, share, grid.wide, second_cols).transpose(2, 0, 1, 3)
    small_grad = jnp.concatenate(
        [
            gw2.reshape(grid.wide, grid.y, second_rows, cols),
            gwh.astype(bf16).reshape(grid.wide, grid.y, -1, cols),
        ],
        axis=2,
    ).reshape(grid.z, grid.x, grid.y, -1, cols)
    small_total = collect_stacked(grid, small_grad, "yxz")
    second_total = small_total[:second_rows].reshape(share, second_cols)
    heads_total = small_total[second_rows:].reshape(head_rows, HEADP)[:, :HEAD]
    sums = all_sum(sums)
    return roi_count.reshape(()), sums, first_total, second_total, heads_total


def shards(
    maps,
    roi_image,
    roi_level,
    roi_corner,
    roi_weights,
    crowd,
    labels,
    box_targets,
    w_first,
    m_first,
    v_first,
    w_second,
    m_second,
    v_second,
    w_heads,
    m_heads,
    v_heads,
    biases,
    bias_m,
    bias_v,
):
    grid = Grid()
    rows = crowd.shape[0]

    images, levels, height, width, channels = maps.shape
    base = ((roi_image * levels + roi_level) * height + roi_corner[:, 0]).astype(jnp.int32)
    col = roi_corner[:, 1].astype(jnp.int32)
    flat_maps = maps.reshape(images * levels * height, width, channels)
    padded = jnp.pad(roi_weights, ((0, 0), (0, 0), (0, 1), (0, 0)))
    row_w = padded[:, 0].reshape(rows * 8, WIN)
    col_w = padded[:, 1].reshape(rows * 8, WIN)
    step = rows // CHUNKS
    tags = jnp.concatenate(
        [box_targets.astype(f32), labels[:, None].astype(f32), crowd[:, None].astype(f32)], axis=1
    )

    def make_crops(i):
        return window_crops(flat_maps, base, col, row_w, col_w, i * step, step)

    shapes = (*w_first.shape, *w_second.shape, w_heads.shape[0], channels, rows)
    run = blocks_step if by_blocks(grid, *shapes) else stacked_step
    roi_count, sums, first_total, second_total, heads_total = run(
        grid, make_crops, w_first, w_second, w_heads, biases, crowd, tags
    )
    loss_total = sums[0, 2 * HID + HEAD]
    bias_grad = sums[0, : 2 * HID + HEAD]

    first_out = adam_update(w_first, first_total, m_first, v_first, rate_first)
    second_out = adam_update(w_second, second_total, m_second, v_second, rate_second)
    heads_out = adam_update(w_heads, heads_total, m_heads, v_heads, rate_heads)
    bias_out = adam_update(biases, bias_grad, bias_m, bias_v, rate_biases)
    return (loss_total, roi_count, *first_out, *second_out, *heads_out, *bias_out)


def solution(mesh):
    rows = P(("wide", "tp"))
    both = P("wide", "tp")
    turned = P("tp", "wide")
    return jax.shard_map(
        shards,
        mesh=mesh,
        in_specs=(rows,) * 8 + (both,) * 3 + (turned,) * 3 + (rows,) * 3 + (P(),) * 3,
        out_specs=(P(), P()) + (both,) * 3 + (turned,) * 3 + (rows,) * 3 + (P(),) * 3,
        check_vma=False,
    )
```

time: 574 us -> 336 us (0.59)
  waiting for transfers between devices: 257 us -> 139 us
  starting transfers between devices: 116 us -> 43.5 us
  local copies, waits for them, and re-layouts: 86.6 us -> 29.5 us
  Pallas kernels: 66.4 us -> 99.6 us
  other arithmetic: 39.3 us -> 21.2 us
    ppermute x80 -> x51, waiting for transfers between devices: 244 us -> 139 us  [move(): return lax.ppermute(value, AXES, pairs)]
    ppermute x80 -> x51, starting transfers between devices: 112 us -> 43.5 us  [move(): return lax.ppermute(value, AXES, pairs)]
    pallas_call x6 -> x15, Pallas kernels: 58.6 us -> 93.5 us  [the longest x5 31.7 us: first_grad_blocks(): pl.pallas_call(functools.partial(block_grad_kernel, span, feats, blocks,...]
    dynamic_update_slice x32 -> x0, local copies, waits for them, and re-layouts: 26.5 us -> none  [shards(): lax.dynamic_update_slice(weight, block[None], (y, (z * grid.x + x) * feat...]
    gather x5 -> x0, local copies, waits for them, and re-layouts: 13.8 us -> none  [spread_stacked(): stack = jnp.take(stack, back, axis=place, mode='clip')]
    ppermute x5 -> x0, waiting for transfers between devices: 12.9 us -> none  [all_sum(): lax.ppermute(value, AXES, [(i, i ^ bit) for i in range(count)])]
    unnamed x74 -> x171, local copies, waits for them, and re-layouts: 12.3 us -> 19.7 us
    another operation x0 -> x16, other arithmetic: none -> 7.34 us  [the longest x7 3.96 us: stack_of(): jnp.stack([jnp.stack([parts[dz, dx, y] for dx in range(grid.x)]) for y in...]
  transfers between devices with their start and end apart: 85 -> 51, of which waited for: 48 -> 22; matrix products, arithmetic and copies ran while one was open for 19% -> 8% of each run, Pallas kernels for 10% -> 24%
where the time goes in v2:
time: 336 us; the launch traced here: 334 us
  waiting for transfers between devices  139 us (41%)
  Pallas kernels  99.6 us (30%)
  starting transfers between devices  43.5 us (13%)
  local copies, waits for them, and re-layouts  29.5 us (9%)
  other arithmetic  21.2 us (6%)
    ppermute x51, waiting for transfers between devices, move(): return lax.ppermute(value, AXES, pairs)  139 us
    ppermute x51, starting transfers between devices, move(): return lax.ppermute(value, AXES, pairs)  43.5 us
    pallas_call x5, Pallas kernels, first_grad_blocks(): pl.pallas_call(functools.partial(block_grad_kernel, span, feats, blocks,...  31.7 us
    pallas_call x4, Pallas kernels, window_crops(): pl.pallas_call(functools.partial(crop_kernel, first), grid_spec=pltpu.Pre...  31.2 us
    pallas_call x3, Pallas kernels, first_blocks(): pl.pallas_call(functools.partial(block_kernel, span, items, feats, most,...  25.1 us
    unnamed x171, local copies, waits for them, and re-layouts  19.7 us
    convert_element_type x10, other arithmetic, low_sum(): return total.astype(bf16)  7.94 us
  transfers between devices with their start and end apart: 51, of which 22 were waited for; matrix products, arithmetic and copies ran while one was open for 8% of the time, Pallas kernels for 24%

profile of v2, /device:TPU:0, one launch (start us, length us, event | category | flops | bytes accessed | tf_op | source)
XLA Modules:
  0.0 334.4 jit_solution(395934291150953319)
XLA Ops:
  5.8 2.9 collective-permute-start
  10.3 2.1 collective-permute-start.3
  12.3 2.0 collective-permute-start.4
  15.5 2.2 copy-done.2
  17.7 7.4 %crops.4.refs_0_ = bf16[49,64,256]{2,1,0:T(8,128)(2,1)S(1)} custom-call(s32[256]{0:T(256)S(1)} %multiply_add_fusion.4.base_ref, s32[256]{0:T(256)S(1)} %bitcast.121, bf16[256,32,256]{2,1,0:T(8,128)(2,1)S(1)} %bitcast.109, bf16[2048,16]{1,0:T(8,128)(2,1)S(1)} %bitcast.113, bf16[2048,16]{1,0:T(8,128)(2,1)S(1)} %bitcast.117, bf16[16,512]{1,0:T(8,128)(2,1)S(1)} %copy-done.21, ...), custom_call_target="tpu_custom_call" | custom-call | bytes 1024 | tf_op jit(solution)/shard_map/crops/pallas_call | solution.py:92
  27.9 7.4 %crops.5.refs_1_ = bf16[49,64,256]{2,1,0:T(8,128)(2,1)S(1)} custom-call(s32[256]{0:T(256)S(1)} %multiply_add_fusion.4.base_ref, s32[256]{0:T(256)S(1)} %bitcast.122, bf16[256,32,256]{2,1,0:T(8,128)(2,1)S(1)} %bitcast.110, bf16[2048,16]{1,0:T(8,128)(2,1)S(1)} %bitcast.114, bf16[2048,16]{1,0:T(8,128)(2,1)S(1)} %bitcast.118, bf16[16,512]{1,0:T(8,128)(2,1)S(1)} %copy-done.21, ...), custom_call_target="tpu_custom_call" | custom-call | bytes 1024 | tf_op jit(solution)/shard_map/crops/pallas_call | solution.py:92
  35.3 8.2 %crops.6.refs_2_ = bf16[49,64,256]{2,1,0:T(8,128)(2,1)} custom-call(s32[256]{0:T(256)S(1)} %multiply_add_fusion.4.base_ref, s32[256]{0:T(256)S(1)} %bitcast.123, bf16[256,32,256]{2,1,0:T(8,128)(2,1)S(1)} %bitcast.111, bf16[2048,16]{1,0:T(8,128)(2,1)S(1)} %bitcast.115, bf16[2048,16]{1,0:T(8,128)(2,1)S(1)} %bitcast.119, bf16[16,512]{1,0:T(8,128)(2,1)S(1)} %copy-done.21, ...), custom_call_target="tpu_custom_call" | custom-call | bytes 1024 | tf_op jit(solution)/shard_map/crops/pallas_call | solution.py:92
  43.5 8.2 %crops.7.refs_3_ = bf16[49,64,256]{2,1,0:T(8,128)(2,1)} custom-call(s32[256]{0:T(256)S(1)} %multiply_add_fusion.4.base_ref, s32[256]{0:T(256)S(1)} %bitcast.124, bf16[256,32,256]{2,1,0:T(8,128)(2,1)S(1)} %bitcast.112, bf16[2048,16]{1,0:T(8,128)(2,1)S(1)} %bitcast.116, bf16[2048,16]{1,0:T(8,128)(2,1)S(1)} %bitcast.120, bf16[16,512]{1,0:T(8,128)(2,1)S(1)} %copy-done.21, ...), custom_call_target="tpu_custom_call" | custom-call | bytes 1024 | tf_op jit(solution)/shard_map/crops/pallas_call | solution.py:92
  52.8 1.8 collective-permute-start.9
  59.2 10.2 %collective-permute-done.9.refs_15_ = bf16[1376,256]{1,0:T(8,128)(2,1)S(1)} collective-permute-done((bf16[1376,256]{1,0:T(8,128)(2,1)}, bf16[1376,256]{1,0:T(8,128)(2,1)S(1)}, u32[]{:S(2)}, u32[]{:S(2)}) %collective-permute-start.9) | collective-permute-done | bytes 704544 | tf_op jit(solution)/shard_map/ppermute | solution.py:680
  69.4 1.5 collective-permute-start.13
  73.8 14.1 %collective-permute-done.14.refs_22_ = bf16[1376,256]{1,0:T(8,128)(2,1)S(1)} collective-permute-done((bf16[1376,256]{1,0:T(8,128)(2,1)}, bf16[1376,256]{1,0:T(8,128)(2,1)S(1)}, u32[]{:S(2)}, u32[]{:S(2)}) %collective-permute-start.14) | collective-permute-done | bytes 704544 | tf_op jit(solution)/shard_map/ppermute | solution.py:680
  89.9 2.2 collective-permute-done.12.refs_16_.refs_15_.refs_1_
  92.1 10.1 %collective-permute-done.16.refs_19_ = bf16[1376,256]{1,0:T(8,128)(2,1)} collective-permute-done((bf16[1376,256]{1,0:T(8,128)(2,1)S(1)}, bf16[1376,256]{1,0:T(8,128)(2,1)}, u32[]{:S(2)}, u32[]{:S(2)}) %collective-permute-start.16) | collective-permute-done | bytes 704544 | tf_op jit(solution)/shard_map/ppermute | solution.py:680
  102.7 7.1 %collective-permute-done.15.refs_12_.refs_23_.refs_11_.refs_3_ = bf16[2,2,384,256]{3,2,1,0:T(8,128)(2,1)S(1)} collective-permute-done((bf16[2,2,384,256]{3,2,1,0:T(8,128)(2,1)S(1)}, bf16[2,2,384,256]{3,2,1,0:T(8,128)(2,1)S(1)}, u32[]{:S(2)}, u32[]{:S(2)}) %collective-permute-start.15) | collective-permute-done | bytes 786464 | tf_op jit(solution)/shard_map/ppermute | solution.py:680
  110.4 15.6 %collective-permute-done.17.refs_14_ = bf16[1376,256]{1,0:T(8,128)(2,1)S(1)} collective-permute-done((bf16[1376,256]{1,0:T(8,128)(2,1)S(1)}, bf16[1376,256]{1,0:T(8,128)(2,1)S(1)}, u32[]{:S(2)}, u32[]{:S(2)}) %collective-permute-start.17) | collective-permute-done | bytes 704544 | tf_op jit(solution)/shard_map/ppermute | solution.py:680
  126.0 2.0 collective-permute-start.20
  130.7 8.3 %first_blocks.3 = (f32[256,512]{1,0:T(8,128)}, f32[256,512]{1,0:T(8,128)}) custom-call(s32[3]{0:T(128)} %pad_add_fusion.1.place, bf16[49,64,256]{2,1,0:T(8,128)(2,1)} %copy-done, bf16[49,64,256]{2,1,0:T(8,128)(2,1)} %copy-done.1, bf16[49,64,256]{2,1,0:T(8,128)(2,1)} %crops.6.refs_2_, bf16[49,64,256]{2,1,0:T(8,128)(2,1)} %crops.7.refs_3_, ...), custom_call_target="tpu_custom_call" | custom-call | bytes 1024 | tf_op jit(solution)/shard_map/first_blocks/pallas_call | solution.py:289
  138.9 3.4 %collective-permute-done.20.refs_20_ = bf16[1376,256]{1,0:T(8,128)(2,1)} collective-permute-done((bf16[1376,256]{1,0:T(8,128)(2,1)}, bf16[1376,256]{1,0:T(8,128)(2,1)}, u32[]{:S(2)}, u32[]{:S(2)}) %collective-permute-start.20) | collective-permute-done | bytes 704544 | tf_op jit(solution)/shard_map/ppermute | solution.py:680
  143.2 11.9 %first_blocks.4 = (f32[256,512]{1,0:T(8,128)}, f32[256,512]{1,0:T(8,128)}) custom-call(s32[5]{0:T(128)} %stack.248.place, bf16[49,64,256]{2,1,0:T(8,128)(2,1)} %copy-done, bf16[49,64,256]{2,1,0:T(8,128)(2,1)} %copy-done.1, bf16[49,64,256]{2,1,0:T(8,128)(2,1)} %crops.6.refs_2_, ...), custom_call_target="tpu_custom_call", output_to_operand_aliasing={{0}: (9, {}), {1}: (10, {})} | custom-call | bytes 1024 | tf_op jit(solution)/shard_map/first_blocks/pallas_call | solution.py:289
  155.9 5.0 %first_blocks.5 = (f32[256,512]{1,0:T(8,128)}, f32[256,512]{1,0:T(8,128)}) custom-call(s32[1]{0:T(128)} %bitcast.4.place, bf16[49,64,256]{2,1,0:T(8,128)(2,1)} %copy-done, bf16[49,64,256]{2,1,0:T(8,128)(2,1)} %copy-done.1, bf16[49,64,256]{2,1,0:T(8,128)(2,1)} %crops.6.refs_2_, ...), custom_call_target="tpu_custom_call", output_to_operand_aliasing={{0}: (9, {}), {1}: (10, {})} | custom-call | bytes 1024 | tf_op jit(solution)/shard_map/first_blocks/pallas_call | solution.py:289
  162.3 1.8 slice.248
  168.3 2.3 unpack.1
  170.6 6.1 %heads.3 = (bf16[256,512]{1,0:T(8,128)(2,1)S(1)}, bf16[256,512]{1,0:T(8,128)(2,1)S(1)}, f32[512,1024]{1,0:T(8,128)S(1)}, bf16[512,1024]{1,0:T(8,128)(2,1)S(1)}, ...) custom-call(s32[4]{0:T(128)S(1)} %pad_add_fusion.at_ref, ...), custom_call_target="tpu_custom_call" | custom-call | bytes 1024 | tf_op jit(solution)/shard_map/heads/pallas_call | solution.py:638
  183.0 7.0 %first_grad.6 = (bf16[1408,256]{1,0:T(8,128)(2,1)}, bf16[160,256]{1,0:T(8,128)(2,1)}, bf16[1408,256]{1,0:T(8,128)(2,1)}, bf16[160,256]{1,0:T(8,128)(2,1)}, bf16[...) custom-call(s32[2]{0:T(128)} %pad_add_fusion.2.place, ...), custom_call_target="tpu_custom_call" | custom-call | bytes 1024 | tf_op jit(solution)/shard_map/first_grad/pallas_call | solution.py:381
  190.5 1.7 collective-permute-start.32
  194.1 5.2 %first_grad.5 = (bf16[1408,256]{1,0:T(8,128)(2,1)}, bf16[160,256]{1,0:T(8,128)(2,1)}, bf16[1408,256]{1,0:T(8,128)(2,1)}, bf16[160,256]{1,0:T(8,128)(2,1)}) custom-call(s32[1]{0:T(128)} %bitcast.31.place, bf16[49,64,256]{2,1,0:T(8,128)(2,1)} %copy-done, bf16[49,64,256]{2,1,0:T(8,128)(2,1)} %copy-done.1, bf16[49,64,256]{2,1,0:T(8,128)(2,1)} %crops.6.refs_2_, ...), custom_call_target="tpu_custom_call" | custom-call | bytes 1024 | tf_op jit(solution)/shard_map/first_grad/pallas_call | solution.py:381
  200.5 8.1 %collective-permute-done.31 = bf16[1408,256]{1,0:T(8,128)(2,1)} collective-permute-done((bf16[1408,256]{1,0:T(8,128)(2,1)}, bf16[1408,256]{1,0:T(8,128)(2,1)}, u32[]{:S(2)}, u32[]{:S(2)}) %collective-permute-start.31) | collective-permute-done | bytes 720928 | tf_op jit(solution)/shard_map/ppermute | solution.py:680
  209.0 1.7 collective-permute-start.35
  210.8 2.4 add_convert_fusion.8
  213.2 1.9 pack.1
  216.3 7.0 %first_grad.7 = (bf16[1408,256]{1,0:T(8,128)(2,1)}, bf16[160,256]{1,0:T(8,128)(2,1)}, bf16[1408,256]{1,0:T(8,128)(2,1)}, bf16[160,256]{1,0:T(8,128)(2,1)}, bf16[...) custom-call(s32[2]{0:T(128)} %pad_add_fusion.3.place, ...), custom_call_target="tpu_custom_call" | custom-call | bytes 1024 | tf_op jit(solution)/shard_map/first_grad/pallas_call | solution.py:381
  223.4 7.2 %first_grad.8 = (bf16[1408,256]{1,0:T(8,128)(2,1)}, bf16[160,256]{1,0:T(8,128)(2,1)}, bf16[1408,256]{1,0:T(8,128)(2,1)}, bf16[160,256]{1,0:T(8,128)(2,1)}, bf16[...) custom-call(s32[2]{0:T(128)} %pad_add_fusion.4.place, ...), custom_call_target="tpu_custom_call" | custom-call | bytes 1024 | tf_op jit(solution)/shard_map/first_grad/pallas_call | solution.py:381
  231.6 5.3 %first_grad.9 = (bf16[1408,256]{1,0:T(8,128)(2,1)}, bf16[160,256]{1,0:T(8,128)(2,1)}, bf16[1408,256]{1,0:T(8,128)(2,1)}, bf16[160,256]{1,0:T(8,128)(2,1)}) custom-call(s32[1]{0:T(128)} %bitcast.15.place, bf16[49,64,256]{2,1,0:T(8,128)(2,1)} %copy-done, bf16[49,64,256]{2,1,0:T(8,128)(2,1)} %copy-done.1, bf16[49,64,256]{2,1,0:T(8,128)(2,1)} %crops.6.refs_2_, ...), custom_call_target="tpu_custom_call" | custom-call | bytes 1024 | tf_op jit(solution)/shard_map/first_grad/pallas_call | solution.py:381
  239.0 4.1 %collective-permute-start.33 = (bf16[2,2,368,256]{3,2,1,0:T(8,128)(2,1)S(1)}, bf16[2,2,368,256]{3,2,1,0:T(8,128)(2,1)S(1)}, u32[]{:S(2)}, u32[]{:S(2)}) collective-permute-start(bf16[2,2,368,256]{3,2,1,0:T(8,128)(2,1)S(1)} %pad_maximum_fusion.3), channel_id=1, source_target_pairs={{0,24},{1,25},{2,26},{3,27},{4,28},{5,29},{6,30},{7,31},{8,0},{9,1... | collective-permute-start | bytes 2261000 | tf_op jit(solution)/shard_map/ppermute | solution.py:680
  246.6 13.1 %collective-permute-done.37 = bf16[1408,256]{1,0:T(8,128)(2,1)S(1)} collective-permute-done((bf16[1408,256]{1,0:T(8,128)(2,1)S(1)}, bf16[1408,256]{1,0:T(8,128)(2,1)S(1)}, u32[]{:S(2)}, u32[]{:S(2)}) %collective-permute-start.37) | collective-permute-done | bytes 720928 | tf_op jit(solution)/shard_map/ppermute | solution.py:680
  259.7 1.6 collective-permute-start.40
  264.6 10.7 %collective-permute-done.40 = bf16[1408,256]{1,0:T(8,128)(2,1)S(1)} collective-permute-done((bf16[1408,256]{1,0:T(8,128)(2,1)S(1)}, bf16[1408,256]{1,0:T(8,128)(2,1)S(1)}, u32[]{:S(2)}, u32[]{:S(2)}) %collective-permute-start.40) | collective-permute-done | bytes 720928 | tf_op jit(solution)/shard_map/ppermute | solution.py:680
  275.5 5.0 %collective-permute-done.36 = bf16[2,2,368,256]{3,2,1,0:T(8,128)(2,1)S(1)} collective-permute-done((bf16[2,2,368,256]{3,2,1,0:T(8,128)(2,1)S(1)}, bf16[2,2,368,256]{3,2,1,0:T(8,128)(2,1)S(1)}, u32[]{:S(2)}, u32[]{:S(2)}) %collective-permute-start.36) | collective-permute-done | bytes 753696 | tf_op jit(solution)/shard_map/ppermute | solution.py:680
  282.0 15.6 %collective-permute-done.39 = bf16[1408,256]{1,0:T(8,128)(2,1)S(1)} collective-permute-done((bf16[1408,256]{1,0:T(8,128)(2,1)S(1)}, bf16[1408,256]{1,0:T(8,128)(2,1)S(1)}, u32[]{:S(2)}, u32[]{:S(2)}) %collective-permute-start.39) | collective-permute-done | bytes 720928 | tf_op jit(solution)/shard_map/ppermute | solution.py:680
  297.8 3.5 %collective-permute-start.44 = (bf16[1408,256]{1,0:T(8,128)(2,1)S(1)}, bf16[1408,256]{1,0:T(8,128)(2,1)S(1)}, u32[]{:S(2)}, u32[]{:S(2)}) collective-permute-start(bf16[1408,256]{1,0:T(8,128)(2,1)S(1)} %add_convert_fusion.4), channel_id=1, source_target_pairs={{0,24},{1,25},{2,26},{3,27},{4,28},{5,29},{6,30},{7,31},{8,0},{9,1... | collective-permute-start | bytes 2162696 | tf_op jit(solution)/shard_map/ppermute | solution.py:680
  301.8 3.5 %collective-permute-done.43 = bf16[766,256]{1,0:T(8,128)(2,1)S(1)} collective-permute-done((bf16[766,256]{1,0:T(8,128)(2,1)S(1)}, bf16[766,256]{1,0:T(8,128)(2,1)S(1)}, u32[]{:S(2)}, u32[]{:S(2)}) %collective-permute-start.43) | collective-permute-done | bytes 392224 | tf_op jit(solution)/shard_map/ppermute | solution.py:680
  305.6 6.7 %collective-permute-done.44 = bf16[1408,256]{1,0:T(8,128)(2,1)S(1)} collective-permute-done((bf16[1408,256]{1,0:T(8,128)(2,1)S(1)}, bf16[1408,256]{1,0:T(8,128)(2,1)S(1)}, u32[]{:S(2)}, u32[]{:S(2)}) %collective-permute-start.44) | collective-permute-done | bytes 720928 | tf_op jit(solution)/shard_map/ppermute | solution.py:680
  312.3 2.4 collective-permute-done.46
  316.3 2.0 collective-permute-start.49
  318.3 2.2 collective-permute-done.47
  323.5 5.5 %collective-permute-done.50 = bf16[1408,256]{1,0:T(8,128)(2,1)S(1)} collective-permute-done((bf16[1408,256]{1,0:T(8,128)(2,1)S(1)}, bf16[1408,256]{1,0:T(8,128)(2,1)S(1)}, u32[]{:S(2)}, u32[]{:S(2)}) %collective-permute-start.50) | collective-permute-done | bytes 720928 | tf_op jit(solution)/shard_map/ppermute | solution.py:680
  331.4 3.0 multiply_subtract_fusion
  (331 shorter events, 62.1 us)
Async XLA Ops:
  5.8 46.9 %collective-permute-start = (bf16[1760,256]{1,0:T(8,128)(2,1)}, bf16[1760,256]{1,0:T(8,128)(2,1)}, u32[]{:S(2)}, u32[]{:S(2)}) collective-permute-start(bf16[1760,256]{1,0:T(8,128)(2,1)} %get-tuple-element.100.refs_8_), channel_id=1, source_target_pairs={{0,4},{1,5},{2,6},{3,7},{4,0},{5,1},{6,2},{7,3},{8,12},{9,13},{10,... | collective-permute-start | bytes 2703368 | tf_op jit(solution)/shard_map/ppermute | solution.py:680
  8.7 44.0 %collective-permute-start.1 = (bf16[1760,256]{1,0:T(8,128)(2,1)}, bf16[1760,256]{1,0:T(8,128)(2,1)}, u32[]{:S(2)}, u32[]{:S(2)}) collective-permute-start(bf16[1760,256]{1,0:T(8,128)(2,1)} %get-tuple-element.100.refs_8_), channel_id=1, source_target_pairs={{0,2},{1,3},{2,0},{3,1},{4,6},{5,7},{6,4},{7,5},{8,10},{9,11},{10,... | collective-permute-start | bytes 2703368 | tf_op jit(solution)/shard_map/ppermute | solution.py:680
  10.3 42.5 %collective-permute-start.2 = (bf16[1760,256]{1,0:T(8,128)(2,1)}, bf16[1760,256]{1,0:T(8,128)(2,1)}, u32[]{:S(2)}, u32[]{:S(2)}) collective-permute-start(bf16[1760,256]{1,0:T(8,128)(2,1)} %get-tuple-element.100.refs_8_), channel_id=1, source_target_pairs={{0,6},{1,7},{2,4},{3,5},{4,2},{5,3},{6,0},{7,1},{8,14},{9,15},{10,... | collective-permute-start | bytes 2703368 | tf_op jit(solution)/shard_map/ppermute | solution.py:680
  10.3 42.5 %collective-permute-start.3 = (bf16[1376,256]{1,0:T(8,128)(2,1)}, bf16[1376,256]{1,0:T(8,128)(2,1)}, u32[]{:S(2)}, u32[]{:S(2)}) collective-permute-start(bf16[1376,256]{1,0:T(8,128)(2,1)} %get-tuple-element.101), channel_id=1, source_target_pairs={{0,8},{1,9},{2,10},{3,11},{4,12},{5,13},{6,14},{7,15},{8,16},{9,17... | collective-permute-start | bytes 2113544 | tf_op jit(solution)/shard_map/ppermute | solution.py:680
  12.3 40.4 %collective-permute-start.4 = (bf16[1376,256]{1,0:T(8,128)(2,1)}, bf16[1376,256]{1,0:T(8,128)(2,1)}, u32[]{:S(2)}, u32[]{:S(2)}) collective-permute-start(bf16[1376,256]{1,0:T(8,128)(2,1)} %get-tuple-element.101), channel_id=1, source_target_pairs={{0,24},{1,25},{2,26},{3,27},{4,28},{5,29},{6,30},{7,31},{8,0},{9,1... | collective-permute-start | bytes 2113544 | tf_op jit(solution)/shard_map/ppermute | solution.py:680
  52.8 16.7 %collective-permute-start.9 = (bf16[1376,256]{1,0:T(8,128)(2,1)}, bf16[1376,256]{1,0:T(8,128)(2,1)S(1)}, u32[]{:S(2)}, u32[]{:S(2)}) collective-permute-start(bf16[1376,256]{1,0:T(8,128)(2,1)} %collective-permute-done.3.refs_14_), channel_id=1, source_target_pairs={{0,2},{1,3},{2,0},{3,1},{4,6},{5,7},{6,4},{7,5},{8,10},{9,11},{10,... | collective-permute-start | bytes 2113544 | tf_op jit(solution)/shard_map/ppermute | solution.py:680
  54.6 16.4 %collective-permute-start.10 = (bf16[1376,256]{1,0:T(8,128)(2,1)}, bf16[1376,256]{1,0:T(8,128)(2,1)S(1)}, u32[]{:S(2)}, u32[]{:S(2)}) collective-permute-start(bf16[1376,256]{1,0:T(8,128)(2,1)} %collective-permute-done.3.refs_14_), channel_id=1, source_target_pairs={{0,4},{1,5},{2,6},{3,7},{4,0},{5,1},{6,2},{7,3},{8,12},{9,13},{10,... | collective-permute-start | bytes 2113544 | tf_op jit(solution)/shard_map/ppermute | solution.py:680
  56.1 17.6 %collective-permute-start.11 = (bf16[1376,256]{1,0:T(8,128)(2,1)}, bf16[1376,256]{1,0:T(8,128)(2,1)S(1)}, u32[]{:S(2)}, u32[]{:S(2)}) collective-permute-start(bf16[1376,256]{1,0:T(8,128)(2,1)} %collective-permute-done.3.refs_14_), channel_id=1, source_target_pairs={{0,8},{1,9},{2,10},{3,11},{4,12},{5,13},{6,14},{7,15},{8,16},{9,17... | collective-permute-start | bytes 2113544 | tf_op jit(solution)/shard_map/ppermute | solution.py:680
  69.4 19.9 %collective-permute-start.13 = (bf16[1376,256]{1,0:T(8,128)(2,1)}, bf16[1376,256]{1,0:T(8,128)(2,1)}, u32[]{:S(2)}, u32[]{:S(2)}) collective-permute-start(bf16[1376,256]{1,0:T(8,128)(2,1)} %collective-permute-done.4.refs_10_), channel_id=1, source_target_pairs={{0,2},{1,3},{2,0},{3,1},{4,6},{5,7},{6,4},{7,5},{8,10},{9,11},{10,... | collective-permute-start | bytes 2113544 | tf_op jit(solution)/shard_map/ppermute | solution.py:680
  71.8 16.1 %collective-permute-start.14 = (bf16[1376,256]{1,0:T(8,128)(2,1)}, bf16[1376,256]{1,0:T(8,128)(2,1)S(1)}, u32[]{:S(2)}, u32[]{:S(2)}) collective-permute-start(bf16[1376,256]{1,0:T(8,128)(2,1)} %collective-permute-done.4.refs_10_), channel_id=1, source_target_pairs={{0,4},{1,5},{2,6},{3,7},{4,0},{5,1},{6,2},{7,3},{8,12},{9,13},{10,... | collective-permute-start | bytes 2113544 | tf_op jit(solution)/shard_map/ppermute | solution.py:680
  73.7 18.4 %collective-permute-start.12 = (bf16[2,2,384,256]{3,2,1,0:T(8,128)(2,1)S(1)}, bf16[2,2,384,256]{3,2,1,0:T(8,128)(2,1)}, u32[]{:S(2)}, u32[]{:S(2)}) collective-permute-start(bf16[2,2,384,256]{3,2,1,0:T(8,128)(2,1)S(1)} %pad_maximum_fusion.1.refs_10_.refs_13_.refs_0_), channel_id=1, source_target_pairs={{0,8},{1,9},{2,10},{3,11},{4,12},{5,13},{6,14},{7,15},{8,16},{9,17... | collective-permute-start | bytes 2359304 | tf_op jit(solution)/shard_map/ppermute | solution.py:680
  73.7 36.7 %collective-permute-start.5 = (bf16[49,64,256]{2,1,0:T(8,128)(2,1)S(1)}, bf16[49,64,256]{2,1,0:T(8,128)(2,1)S(1)}, u32[]{:S(2)}, u32[]{:S(2)}) collective-permute-start(bf16[49,64,256]{2,1,0:T(8,128)(2,1)S(1)} %crops.4.refs_0_), channel_id=1, source_target_pairs={{0,1},{1,0},{2,3},{3,2},{4,5},{5,4},{6,7},{7,6},{8,9},{9,8},{10,11... | collective-permute-start | bytes 4816904 | tf_op jit(solution)/shard_map/ppermute | solution.py:680
  87.9 14.3 %collective-permute-start.16 = (bf16[1376,256]{1,0:T(8,128)(2,1)S(1)}, bf16[1376,256]{1,0:T(8,128)(2,1)}, u32[]{:S(2)}, u32[]{:S(2)}) collective-permute-start(bf16[1376,256]{1,0:T(8,128)(2,1)S(1)} %collective-permute-done.11.refs_16_), channel_id=1, source_target_pairs={{0,4},{1,5},{2,6},{3,7},{4,0},{5,1},{6,2},{7,3},{8,12},{9,13},{10,... | collective-permute-start | bytes 2113544 | tf_op jit(solution)/shard_map/ppermute | solution.py:680
  89.4 13.0 %collective-permute-start.18 = (bf16[1376,256]{1,0:T(8,128)(2,1)S(1)}, bf16[1376,256]{1,0:T(8,128)(2,1)S(1)}, u32[]{:S(2)}, u32[]{:S(2)}) collective-permute-start(bf16[1376,256]{1,0:T(8,128)(2,1)S(1)} %collective-permute-done.11.refs_16_), channel_id=1, source_target_pairs={{0,2},{1,3},{2,0},{3,1},{4,6},{5,7},{6,4},{7,5},{8,10},{9,11},{10,... | collective-permute-start | bytes 2113544 | tf_op jit(solution)/shard_map/ppermute | solution.py:680
  89.9 38.1 %collective-permute-start.6 = (bf16[49,64,256]{2,1,0:T(8,128)(2,1)S(1)}, bf16[49,64,256]{2,1,0:T(8,128)(2,1)S(1)}, u32[]{:S(2)}, u32[]{:S(2)}) collective-permute-start(bf16[49,64,256]{2,1,0:T(8,128)(2,1)S(1)} %crops.5.refs_1_), channel_id=1, source_target_pairs={{0,1},{1,0},{2,3},{3,2},{4,5},{5,4},{6,7},{7,6},{8,9},{9,8},{10,11... | collective-permute-start | bytes 4816904 | tf_op jit(solution)/shard_map/ppermute | solution.py:680
  92.1 17.8 %collective-permute-start.15 = (bf16[2,2,384,256]{3,2,1,0:T(8,128)(2,1)S(1)}, bf16[2,2,384,256]{3,2,1,0:T(8,128)(2,1)S(1)}, u32[]{:S(2)}, u32[]{:S(2)}) collective-permute-start(bf16[2,2,384,256]{3,2,1,0:T(8,128)(2,1)S(1)} %pad_maximum_fusion.1.refs_10_.refs_13_.refs_0_), channel_id=1, source_target_pairs={{0,24},{1,25},{2,26},{3,27},{4,28},{5,29},{6,30},{7,31},{8,0},{9,1... | collective-permute-start | bytes 2359304 | tf_op jit(solution)/shard_map/ppermute | solution.py:680
  102.2 28.4 %collective-permute-start.7 = (bf16[49,64,256]{2,1,0:T(8,128)(2,1)}, bf16[49,64,256]{2,1,0:T(8,128)(2,1)}, u32[]{:S(2)}, u32[]{:S(2)}) collective-permute-start(bf16[49,64,256]{2,1,0:T(8,128)(2,1)} %crops.6.refs_2_), channel_id=1, source_target_pairs={{0,1},{1,0},{2,3},{3,2},{4,5},{5,4},{6,7},{7,6},{8,9},{9,8},{10,11... | collective-permute-start | bytes 4816904 | tf_op jit(solution)/shard_map/ppermute | solution.py:680
  102.4 28.2 %collective-permute-start.8 = (bf16[49,64,256]{2,1,0:T(8,128)(2,1)}, bf16[49,64,256]{2,1,0:T(8,128)(2,1)}, u32[]{:S(2)}, u32[]{:S(2)}) collective-permute-start(bf16[49,64,256]{2,1,0:T(8,128)(2,1)} %crops.7.refs_3_), channel_id=1, source_target_pairs={{0,1},{1,0},{2,3},{3,2},{4,5},{5,4},{6,7},{7,6},{8,9},{9,8},{10,11... | collective-permute-start | bytes 4816904 | tf_op jit(solution)/shard_map/ppermute | solution.py:680
  109.9 16.2 %collective-permute-start.17 = (bf16[1376,256]{1,0:T(8,128)(2,1)S(1)}, bf16[1376,256]{1,0:T(8,128)(2,1)S(1)}, u32[]{:S(2)}, u32[]{:S(2)}) collective-permute-start(bf16[1376,256]{1,0:T(8,128)(2,1)S(1)} %collective-permute-done.9.refs_15_), channel_id=1, source_target_pairs={{0,4},{1,5},{2,6},{3,7},{4,0},{5,1},{6,2},{7,3},{8,12},{9,13},{10,... | collective-permute-start | bytes 2113544 | tf_op jit(solution)/shard_map/ppermute | solution.py:680
  110.4 31.9 %collective-permute-start.19 = (bf16[2,2,384,256]{3,2,1,0:T(8,128)(2,1)}, bf16[2,2,384,256]{3,2,1,0:T(8,128)(2,1)S(1)}, u32[]{:S(2)}, u32[]{:S(2)}) collective-permute-start(bf16[2,2,384,256]{3,2,1,0:T(8,128)(2,1)} %collective-permute-done.12.refs_16_.refs_15_.refs_1_), channel_id=1, source_target_pairs={{0,8},{1,9},{2,10},{3,11},{4,12},{5,13},{6,14},{7,15},{8,16},{9,17... | collective-permute-start | bytes 2359304 | tf_op jit(solution)/shard_map/ppermute | solution.py:680
  126.0 16.3 %collective-permute-start.20 = (bf16[1376,256]{1,0:T(8,128)(2,1)}, bf16[1376,256]{1,0:T(8,128)(2,1)}, u32[]{:S(2)}, u32[]{:S(2)}) collective-permute-start(bf16[1376,256]{1,0:T(8,128)(2,1)} %collective-permute-done.16.refs_19_), channel_id=1, source_target_pairs={{0,2},{1,3},{2,0},{3,1},{4,6},{5,7},{6,4},{7,5},{8,10},{9,11},{10,... | collective-permute-start | bytes 2113544 | tf_op jit(solution)/shard_map/ppermute | solution.py:680
  128.0 27.1 %collective-permute-start.21 = (bf16[1376,256]{1,0:T(8,128)(2,1)}, bf16[1376,256]{1,0:T(8,128)(2,1)S(1)}, u32[]{:S(2)}, u32[]{:S(2)}) collective-permute-start(bf16[1376,256]{1,0:T(8,128)(2,1)} %collective-permute-done.13.refs_11_), channel_id=1, source_target_pairs={{0,4},{1,5},{2,6},{3,7},{4,0},{5,1},{6,2},{7,3},{8,12},{9,13},{10,... | collective-permute-start | bytes 2113544 | tf_op jit(solution)/shard_map/ppermute | solution.py:680
  161.0 9.7 %collective-permute-start.22 = (f32[256,512]{1,0:T(8,128)}, f32[256,512]{1,0:T(8,128)S(1)}, u32[]{:S(2)}, u32[]{:S(2)}) collective-permute-start(f32[256,512]{1,0:T(8,128)} %get-tuple-element.122), channel_id=1, source_target_pairs={{0,1},{1,0},{2,3},{3,2},{4,5},{5,4},{6,7},{7,6},{8,9},{9,8},{10,11... | collective-permute-start | bytes 1572872 | tf_op jit(solution)/shard_map/ppermute | solution.py:680
  161.9 4.8 %collective-permute-start.23 = (bf16[2,2,192,256]{3,2,1,0:T(8,128)(2,1)}, bf16[2,2,192,256]{3,2,1,0:T(8,128)(2,1)S(1)}, u32[]{:S(2)}, u32[]{:S(2)}) collective-permute-start(bf16[2,2,192,256]{3,2,1,0:T(8,128)(2,1)} %fusion.2), channel_id=1, source_target_pairs={{0,1},{1,0},{2,3},{3,2},{4,5},{5,4},{6,7},{7,6},{8,9},{9,8},{10,11... | collective-permute-start | bytes 1179656 | tf_op jit(solution)/shard_map/ppermute | solution.py:680
  164.1 2.5 collective-permute-start.24
  165.0 2.1 collective-permute-start.26
  190.0 18.6 %collective-permute-start.31 = (bf16[1408,256]{1,0:T(8,128)(2,1)}, bf16[1408,256]{1,0:T(8,128)(2,1)}, u32[]{:S(2)}, u32[]{:S(2)}) collective-permute-start(bf16[1408,256]{1,0:T(8,128)(2,1)} %get-tuple-element.142), channel_id=1, source_target_pairs={{0,4},{1,5},{2,6},{3,7},{4,0},{5,1},{6,2},{7,3},{8,12},{9,13},{10,... | collective-permute-start | bytes 2162696 | tf_op jit(solution)/shard_map/ppermute | solution.py:680
  190.5 18.5 %collective-permute-start.32 = (bf16[1408,256]{1,0:T(8,128)(2,1)}, bf16[1408,256]{1,0:T(8,128)(2,1)}, u32[]{:S(2)}, u32[]{:S(2)}) collective-permute-start(bf16[1408,256]{1,0:T(8,128)(2,1)} %get-tuple-element.143), channel_id=1, source_target_pairs={{0,2},{1,3},{2,0},{3,1},{4,6},{5,7},{6,4},{7,5},{8,10},{9,11},{10,... | collective-permute-start | bytes 2162696 | tf_op jit(solution)/shard_map/ppermute | solution.py:680
  192.3 20.9 %collective-permute-start.28 = (bf16[512,1024]{1,0:T(8,128)(2,1)}, bf16[512,1024]{1,0:T(8,128)(2,1)S(1)}, u32[]{:S(2)}, u32[]{:S(2)}) collective-permute-start(bf16[512,1024]{1,0:T(8,128)(2,1)} %copy-done.28), channel_id=1, source_target_pairs={{0,1},{1,0},{2,3},{3,2},{4,5},{5,4},{6,7},{7,6},{8,9},{9,8},{10,11... | collective-permute-start | bytes 3145736 | tf_op jit(solution)/shard_map/ppermute | solution.py:680
  192.3 20.9 %collective-permute-start.29 = (bf16[1024,512]{1,0:T(8,128)(2,1)}, bf16[1024,512]{1,0:T(8,128)(2,1)}, u32[]{:S(2)}, u32[]{:S(2)}) collective-permute-start(bf16[1024,512]{1,0:T(8,128)(2,1)} %copy-done.27), channel_id=1, source_target_pairs={{0,1},{1,0},{2,3},{3,2},{4,5},{5,4},{6,7},{7,6},{8,9},{9,8},{10,11... | collective-permute-start | bytes 3145736 | tf_op jit(solution)/shard_map/ppermute | solution.py:680
  208.5 34.6 %collective-permute-start.34 = (bf16[1408,256]{1,0:T(8,128)(2,1)}, bf16[1408,256]{1,0:T(8,128)(2,1)}, u32[]{:S(2)}, u32[]{:S(2)}) collective-permute-start(bf16[1408,256]{1,0:T(8,128)(2,1)} %get-tuple-element.151), channel_id=1, source_target_pairs={{0,4},{1,5},{2,6},{3,7},{4,0},{5,1},{6,2},{7,3},{8,12},{9,13},{10,... | collective-permute-start | bytes 2162696 | tf_op jit(solution)/shard_map/ppermute | solution.py:680
  209.0 37.0 %collective-permute-start.35 = (bf16[1408,256]{1,0:T(8,128)(2,1)}, bf16[1408,256]{1,0:T(8,128)(2,1)}, u32[]{:S(2)}, u32[]{:S(2)}) collective-permute-start(bf16[1408,256]{1,0:T(8,128)(2,1)} %get-tuple-element.153), channel_id=1, source_target_pairs={{0,2},{1,3},{2,0},{3,1},{4,6},{5,7},{6,4},{7,5},{8,10},{9,11},{10,... | collective-permute-start | bytes 2162696 | tf_op jit(solution)/shard_map/ppermute | solution.py:680
  215.3 23.8 %collective-permute-start.30 = (bf16[2,2,368,256]{3,2,1,0:T(8,128)(2,1)S(1)}, bf16[2,2,368,256]{3,2,1,0:T(8,128)(2,1)S(1)}, u32[]{:S(2)}, u32[]{:S(2)}) collective-permute-start(bf16[2,2,368,256]{3,2,1,0:T(8,128)(2,1)S(1)} %pad_maximum_fusion.2), channel_id=1, source_target_pairs={{0,8},{1,9},{2,10},{3,11},{4,12},{5,13},{6,14},{7,15},{8,16},{9,17... | collective-permute-start | bytes 2261000 | tf_op jit(solution)/shard_map/ppermute | solution.py:680
  239.0 20.6 %collective-permute-start.33 = (bf16[2,2,368,256]{3,2,1,0:T(8,128)(2,1)S(1)}, bf16[2,2,368,256]{3,2,1,0:T(8,128)(2,1)S(1)}, u32[]{:S(2)}, u32[]{:S(2)}) collective-permute-start(bf16[2,2,368,256]{3,2,1,0:T(8,128)(2,1)S(1)} %pad_maximum_fusion.3), channel_id=1, source_target_pairs={{0,24},{1,25},{2,26},{3,27},{4,28},{5,29},{6,30},{7,31},{8,0},{9,1... | collective-permute-start | bytes 2261000 | tf_op jit(solution)/shard_map/ppermute | solution.py:680
  243.2 16.5 %collective-permute-start.37 = (bf16[1408,256]{1,0:T(8,128)(2,1)S(1)}, bf16[1408,256]{1,0:T(8,128)(2,1)S(1)}, u32[]{:S(2)}, u32[]{:S(2)}) collective-permute-start(bf16[1408,256]{1,0:T(8,128)(2,1)S(1)} %copy-done.44), channel_id=1, source_target_pairs={{0,4},{1,5},{2,6},{3,7},{4,0},{5,1},{6,2},{7,3},{8,12},{9,13},{10,... | collective-permute-start | bytes 2162696 | tf_op jit(solution)/shard_map/ppermute | solution.py:680
  246.0 16.8 %collective-permute-start.38 = (bf16[1408,256]{1,0:T(8,128)(2,1)S(1)}, bf16[1408,256]{1,0:T(8,128)(2,1)S(1)}, u32[]{:S(2)}, u32[]{:S(2)}) collective-permute-start(bf16[1408,256]{1,0:T(8,128)(2,1)S(1)} %add_convert_fusion.6), channel_id=1, source_target_pairs={{0,2},{1,3},{2,0},{3,1},{4,6},{5,7},{6,4},{7,5},{8,10},{9,11},{10,... | collective-permute-start | bytes 2162696 | tf_op jit(solution)/shard_map/ppermute | solution.py:680
  259.7 15.7 %collective-permute-start.40 = (bf16[1408,256]{1,0:T(8,128)(2,1)S(1)}, bf16[1408,256]{1,0:T(8,128)(2,1)S(1)}, u32[]{:S(2)}, u32[]{:S(2)}) collective-permute-start(bf16[1408,256]{1,0:T(8,128)(2,1)S(1)} %copy-done.84), channel_id=1, source_target_pairs={{0,4},{1,5},{2,6},{3,7},{4,0},{5,1},{6,2},{7,3},{8,12},{9,13},{10,... | collective-permute-start | bytes 2162696 | tf_op jit(solution)/shard_map/ppermute | solution.py:680
  262.7 17.9 %collective-permute-start.36 = (bf16[2,2,368,256]{3,2,1,0:T(8,128)(2,1)S(1)}, bf16[2,2,368,256]{3,2,1,0:T(8,128)(2,1)S(1)}, u32[]{:S(2)}, u32[]{:S(2)}) collective-permute-start(bf16[2,2,368,256]{3,2,1,0:T(8,128)(2,1)S(1)} %add_convert_fusion.1), channel_id=1, source_target_pairs={{0,8},{1,9},{2,10},{3,11},{4,12},{5,13},{6,14},{7,15},{8,16},{9,17... | collective-permute-start | bytes 2261000 | tf_op jit(solution)/shard_map/ppermute | solution.py:680
  264.3 16.4 %collective-permute-start.41 = (bf16[1408,256]{1,0:T(8,128)(2,1)S(1)}, bf16[1408,256]{1,0:T(8,128)(2,1)S(1)}, u32[]{:S(2)}, u32[]{:S(2)}) collective-permute-start(bf16[1408,256]{1,0:T(8,128)(2,1)S(1)} %copy-done.83), channel_id=1, source_target_pairs={{0,2},{1,3},{2,0},{3,1},{4,6},{5,7},{6,4},{7,5},{8,10},{9,11},{10,... | collective-permute-start | bytes 2162696 | tf_op jit(solution)/shard_map/ppermute | solution.py:680
  280.6 17.0 %collective-permute-start.39 = (bf16[1408,256]{1,0:T(8,128)(2,1)S(1)}, bf16[1408,256]{1,0:T(8,128)(2,1)S(1)}, u32[]{:S(2)}, u32[]{:S(2)}) collective-permute-start(bf16[1408,256]{1,0:T(8,128)(2,1)S(1)} %add_convert_fusion.7), channel_id=1, source_target_pairs={{0,8},{1,9},{2,10},{3,11},{4,12},{5,13},{6,14},{7,15},{8,16},{9,17... | collective-permute-start | bytes 2162696 | tf_op jit(solution)/shard_map/ppermute | solution.py:680
  280.7 16.9 %collective-permute-start.42 = (bf16[1408,256]{1,0:T(8,128)(2,1)S(1)}, bf16[1408,256]{1,0:T(8,128)(2,1)S(1)}, u32[]{:S(2)}, u32[]{:S(2)}) collective-permute-start(bf16[1408,256]{1,0:T(8,128)(2,1)S(1)} %add_convert_fusion.5), channel_id=1, source_target_pairs={{0,2},{1,3},{2,0},{3,1},{4,6},{5,7},{6,4},{7,5},{8,10},{9,11},{10,... | collective-permute-start | bytes 2162696 | tf_op jit(solution)/shard_map/ppermute | solution.py:680
  281.0 20.3 %collective-permute-start.45 = (bf16[1408,256]{1,0:T(8,128)(2,1)S(1)}, bf16[1408,256]{1,0:T(8,128)(2,1)S(1)}, u32[]{:S(2)}, u32[]{:S(2)}) collective-permute-start(bf16[1408,256]{1,0:T(8,128)(2,1)S(1)} %copy-done.82), channel_id=1, source_target_pairs={{0,4},{1,5},{2,6},{3,7},{4,0},{5,1},{6,2},{7,3},{8,12},{9,13},{10,... | collective-permute-start | bytes 2162696 | tf_op jit(solution)/shard_map/ppermute | solution.py:680
  297.6 7.8 %collective-permute-start.43 = (bf16[766,256]{1,0:T(8,128)(2,1)S(1)}, bf16[766,256]{1,0:T(8,128)(2,1)S(1)}, u32[]{:S(2)}, u32[]{:S(2)}) collective-permute-start(bf16[766,256]{1,0:T(8,128)(2,1)S(1)} %pad_maximum_fusion.4), channel_id=1, source_target_pairs={{0,2},{1,3},{2,0},{3,1},{4,6},{5,7},{6,4},{7,5},{8,10},{9,11},{10,... | collective-permute-start | bytes 1176584 | tf_op jit(solution)/shard_map/ppermute | solution.py:680
  297.8 14.5 %collective-permute-start.44 = (bf16[1408,256]{1,0:T(8,128)(2,1)S(1)}, bf16[1408,256]{1,0:T(8,128)(2,1)S(1)}, u32[]{:S(2)}, u32[]{:S(2)}) collective-permute-start(bf16[1408,256]{1,0:T(8,128)(2,1)S(1)} %add_convert_fusion.4), channel_id=1, source_target_pairs={{0,24},{1,25},{2,26},{3,27},{4,28},{5,29},{6,30},{7,31},{8,0},{9,1... | collective-permute-start | bytes 2162696 | tf_op jit(solution)/shard_map/ppermute | solution.py:680
  301.3 13.4 %collective-permute-start.46 = (bf16[1408,256]{1,0:T(8,128)(2,1)S(1)}, bf16[1408,256]{1,0:T(8,128)(2,1)S(1)}, u32[]{:S(2)}, u32[]{:S(2)}) collective-permute-start(bf16[1408,256]{1,0:T(8,128)(2,1)S(1)} %add_convert_fusion.3), channel_id=1, source_target_pairs={{0,4},{1,5},{2,6},{3,7},{4,0},{5,1},{6,2},{7,3},{8,12},{9,13},{10,... | collective-permute-start | bytes 2162696 | tf_op jit(solution)/shard_map/ppermute | solution.py:680
  314.7 5.8 %collective-permute-start.47 = (bf16[398,256]{1,0:T(8,128)(2,1)S(1)}, bf16[398,256]{1,0:T(8,128)(2,1)S(1)}, u32[]{:S(2)}, u32[]{:S(2)}) collective-permute-start(bf16[398,256]{1,0:T(8,128)(2,1)S(1)} %pad_maximum_fusion.5), channel_id=1, source_target_pairs={{0,4},{1,5},{2,6},{3,7},{4,0},{5,1},{6,2},{7,3},{8,12},{9,13},{10,... | collective-permute-start | bytes 611336 | tf_op jit(solution)/shard_map/ppermute | solution.py:680
  315.6 13.4 %collective-permute-start.50 = (bf16[1408,256]{1,0:T(8,128)(2,1)S(1)}, bf16[1408,256]{1,0:T(8,128)(2,1)S(1)}, u32[]{:S(2)}, u32[]{:S(2)}) collective-permute-start(bf16[1408,256]{1,0:T(8,128)(2,1)S(1)} %add_convert_fusion.2), channel_id=1, source_target_pairs={{0,8},{1,9},{2,10},{3,11},{4,12},{5,13},{6,14},{7,15},{8,16},{9,17... | collective-permute-start | bytes 2162696 | tf_op jit(solution)/shard_map/ppermute | solution.py:680
  316.3 12.8 %collective-permute-start.49 = (bf16[1408,256]{1,0:T(8,128)(2,1)S(1)}, bf16[1408,256]{1,0:T(8,128)(2,1)S(1)}, u32[]{:S(2)}, u32[]{:S(2)}) collective-permute-start(bf16[1408,256]{1,0:T(8,128)(2,1)S(1)} %copy-done.81), channel_id=1, source_target_pairs={{0,2},{1,3},{2,0},{3,1},{4,6},{5,7},{6,4},{7,5},{8,10},{9,11},{10,... | collective-permute-start | bytes 2162696 | tf_op jit(solution)/shard_map/ppermute | solution.py:680
  (91 other events, 1121.2 us)

commit v3 on v2

--- a/solution.py
+++ b/solution.py
@@ -21,9 +21,10 @@
 GROUP = 32
 KSTEP = 7
 LATE_OUT = 192
-LATE_BACK = 160
+LATE_BACK = 208
 TERMS = 3
 EXTRA = 16
+WIDE = 60
 MIB = 2**20
 LIGHT = pl.CostEstimate(flops=0, bytes_accessed=1024, transcendentals=0)
 
@@ -249,10 +250,9 @@
 
     def multiply(lanes):
         slot = lax.rem(step, 2)
-        weight = pad[slot, :, lanes]
-        for at, out in ((0, own), (rows, send)):
-            lhs = jnp.concatenate([cells[slot, j, at : at + rows, :] for j in range(span)], axis=1)
-            out[:, lanes] += dot(lhs, weight)
+        got = dot(jnp.concatenate([cells[slot, j] for j in range(span)], axis=1), pad[slot, :, lanes])
+        own[:, lanes] += got[:rows]
+        send[:, lanes] += got[rows:]
 
     for i in range(count):
 
@@ -301,7 +301,7 @@
         ),
         out_shape=[jax.ShapeDtypeStruct((rows, units), f32)] * 2,
         input_output_aliases={} if before is None else {1 + parts: 0, 2 + parts: 1},
-        compiler_params=pltpu.CompilerParams(vmem_limit_bytes=60 * MIB),
+        compiler_params=pltpu.CompilerParams(vmem_limit_bytes=WIDE * MIB),
         cost_estimate=LIGHT,
         name="first_blocks",
     )(place, *crops, *lead, *inputs)
@@ -393,7 +393,7 @@
             ],
         ),
         out_shape=[jax.ShapeDtypeStruct(v, bf16) for v in outs],
-        compiler_params=pltpu.CompilerParams(vmem_limit_bytes=60 * MIB),
+        compiler_params=pltpu.CompilerParams(vmem_limit_bytes=WIDE * MIB),
         cost_estimate=LIGHT,
         name="first_grad",
     )(place, *crops, own, got)
@@ -446,53 +446,62 @@
 
 
 def unpack_kernel(depth, core_ref, wide_ref, *refs):
-    stacks_own, stacks_sib = refs[:depth], refs[depth : 2 * depth]
-    w2_own, w2_sib, wh = refs[2 * depth :]
-    blocks, xs, half, _ = stacks_sib[0].shape
+    stacks = refs[: 2 * depth]
+    w2_own, w2_sib, wh, small, sems = refs[2 * depth :]
+    _, blocks, xs, half, _ = small.shape
     share = w2_own.shape[0] // blocks
     count = depth * xs
     rows = wh.shape[0] // (count * blocks * CORES)
+    copies = [
+        pltpu.make_async_copy(ref.at[:, :, pl.ds(ref.shape[2] - half, half)], small.at[n], sems.at[n])
+        for n, ref in enumerate(stacks)
+    ]
+    for copy in copies:
+        copy.start()
+    for copy in copies:
+        copy.wait()
     for n in range(count):
         at = wide_ref[n]
+        lanes = pl.ds(pl.multiple_of(at * 128, 128), 128)
         for y in range(blocks):
             turned = lax.rem(wide_ref[count] + blocks - y, blocks)
-            for stacks, w2, side in ((stacks_own, w2_own, core_ref[0]), (stacks_sib, w2_sib, 1 - core_ref[0])):
-                stack = stacks[n // xs]
-                skip = stack.shape[2] - half
-
-                def small(begin, end):
+            for first, w2, side in ((0, w2_own, core_ref[0]), (depth, w2_sib, 1 - core_ref[0])):
+
+                def piece(begin, end):
                     rows_at, lanes_at = small_place(half, begin, end)
-                    return stack[y, n % xs, skip + rows_at.start : skip + rows_at.stop, lanes_at]
-
-                lanes = pl.ds(pl.multiple_of(at * 128, 128), 128)
+                    return small[first + n // xs, y, n % xs, rows_at, lanes_at]
+
                 for begin, end in ((0, min(share, half)), (half, share)):
                     if begin < end:
-                        w2[y * share + begin : y * share + end, lanes] = small(begin, end)
+                        w2[y * share + begin : y * share + end, lanes] = piece(begin, end)
                 to = pl.multiple_of(((at * blocks + turned) * CORES + side) * rows, rows)
                 for k in range(HEADP // 128):
-                    wh[pl.ds(to, rows), k * 128 : (k + 1) * 128] = small(share + k * rows, share + (k + 1) * rows)
-
-
-def unpack(core, wide, own, sib, units):
+                    wh[pl.ds(to, rows), k * 128 : (k + 1) * 128] = piece(share + k * rows, share + (k + 1) * rows)
+
+
+def unpack(core, wide, own, sib, half, units):
     smem = pl.BlockSpec(memory_space=pltpu.SMEM)
     vmem = pl.BlockSpec(memory_space=pltpu.VMEM)
+    count = 2 * len(own)
+    blocks, xs, _, cols = own[0].shape
     return pl.pallas_call(
         functools.partial(unpack_kernel, len(own)),
-        in_specs=[smem, smem] + [vmem] * (2 * len(own)),
+        in_specs=[smem, smem] + [pl.BlockSpec(memory_space=pl.ANY)] * count,
         out_specs=[vmem] * 3,
         out_shape=[jax.ShapeDtypeStruct((units, HID), bf16)] * 2 + [jax.ShapeDtypeStruct((HID, HEADP), bf16)],
+        scratch_shapes=[pltpu.VMEM((count, blocks, xs, half, cols), bf16), pltpu.SemaphoreType.DMA((count,))],
         cost_estimate=LIGHT,
-        compiler_params=pltpu.CompilerParams(vmem_limit_bytes=16 * MIB),
+        compiler_params=pltpu.CompilerParams(vmem_limit_bytes=WIDE * MIB),
         name="unpack",
     )(core, wide, *own, *sib)
 
 
-def pack_kernel(core_ref, wide_ref, gw2, gw2_got, gwh, gwh_got, sums, out):
+def pack_kernel(wide_ref, gw2, gw2_got, gwh, gwh_got, sums, out):
     depth, blocks, xs, half, _ = out.shape
     half -= EXTRA
     share = gw2.shape[0] // blocks
     count = depth * xs
-    rows = gwh.shape[0] // (count * blocks * CORES)
+    rows = gwh.shape[0] // (count * blocks)
     for n in range(count):
         at = wide_ref[n]
         lanes = pl.ds(pl.multiple_of(at * 128, 128), 128)
@@ -507,11 +516,12 @@
             for begin, end in ((0, min(share, half)), (half, share)):
                 if begin < end:
                     part = slice(turned * share + begin, turned * share + end)
-                    small(begin, end, gw2[part, lanes] + gw2_got[part, lanes].astype(f32))
-            here = pl.ds(pl.multiple_of(((at * blocks + ahead) * CORES + core_ref[0]) * rows, rows), rows)
+                    small(begin, end, gw2[part, lanes].astype(f32) + gw2_got[part, lanes].astype(f32))
+            here = pl.ds(pl.multiple_of((at * blocks + ahead) * rows, rows), rows)
             for k in range(HEADP // 128):
                 group = slice(k * 128, (k + 1) * 128)
-                small(share + k * rows, share + (k + 1) * rows, gwh[here, group] + gwh_got[here, group].astype(f32))
+                both = gwh[here, group].astype(f32) + gwh_got[here, group].astype(f32)
+                small(share + k * rows, share + (k + 1) * rows, both)
     rest = sums[...]
     rows_left = []
     for _ in range(TERMS):
@@ -529,18 +539,18 @@
                 out[dz, y, x, half:, :] = some if dz >= 2 else jnp.zeros_like(some)
 
 
-def pack(core, wide, gw2, gw2_got, gwh, gwh_got, sums, shape):
+def pack(wide, gw2, gw2_got, gwh, gwh_got, sums, shape):
     smem = pl.BlockSpec(memory_space=pltpu.SMEM)
     vmem = pl.BlockSpec(memory_space=pltpu.VMEM)
     return pl.pallas_call(
         pack_kernel,
-        in_specs=[smem, smem] + [vmem] * 5,
+        in_specs=[smem] + [vmem] * 5,
         out_specs=vmem,
         out_shape=jax.ShapeDtypeStruct(shape, bf16),
         cost_estimate=LIGHT,
-        compiler_params=pltpu.CompilerParams(vmem_limit_bytes=18 * MIB),
+        compiler_params=pltpu.CompilerParams(vmem_limit_bytes=WIDE * MIB),
         name="pack",
-    )(core, wide, gw2, gw2_got, gwh, gwh_got, sums)
+    )(wide, gw2, gw2_got, gwh, gwh_got, sums)
 
 
 def gelu(x):
@@ -554,6 +564,7 @@
 
 def head_kernel(
     share,
+    wide,
     at_ref,
     pre_own,
     pre_sib,
@@ -568,13 +579,14 @@
     g_sib,
     gw2_own,
     gw2_sib,
-    gwh,
-    gwh_low,
+    gwh_own,
+    gwh_sib,
     sums,
     count,
     h1,
     pre2,
     gpre2,
+    gwh,
 ):
     rows, units = pre_own.shape
     sides = ((pre_own, w2_own, g_own, gw2_own, 0), (pre_sib, w2_sib, g_sib, gw2_sib, units))
@@ -615,7 +627,16 @@
     loss = jnp.sum(row_loss, axis=0, keepdims=True)
     sums[:, 2 * HID : 2 * HID + HEADP] = jnp.where(lane == HEAD, loss, head_sums)
     gwh[...] = dot(h2, g_out, ((0,), (0,)))
-    gwh_low[...] = gwh[...].astype(bf16)
+    each = HID // (HID // share * wide)
+    for side in range(CORES):
+
+        @pl.when(at_ref[HID // share] == side)
+        def _(side=side):
+            for n in range(HID // each // CORES):
+                for c, part in ((side, gwh_own), (1 - side, gwh_sib)):
+                    row = (n * CORES + c) * each
+                    part[n * each : (n + 1) * each, :] = gwh[row : row + each, :].astype(bf16)
+
     g_h2 = dot(g_out, wh[...], ((1,), (1,)))
     g2 = (g_h2 * gelu_slope(pre2[...])).astype(bf16)
     sums[:, HID : 2 * HID] = jnp.sum(g2.astype(f32), axis=0, keepdims=True)
@@ -631,26 +652,31 @@
         gw2[...] = dot(h1[:, at : at + units], gpre2[...], ((0,), (0,))).astype(gw2.dtype)
 
 
-def heads_step(share, at, pre_own, pre_sib, w2_own, w2_sib, wh, b1, b2, bh, tags):
+def heads_step(share, wide, at, pre_own, pre_sib, w2_own, w2_sib, wh, b1, b2, bh, tags):
     rows, units = pre_own.shape
     vmem = pl.BlockSpec(memory_space=pltpu.VMEM)
     shape = jax.ShapeDtypeStruct
     return pl.pallas_call(
-        functools.partial(head_kernel, share),
+        functools.partial(head_kernel, share, wide),
         in_specs=[pl.BlockSpec(memory_space=pltpu.SMEM)] + [vmem] * 9,
         out_specs=[vmem] * 8,
         out_shape=[
             shape((rows, units), bf16),
             shape((rows, units), bf16),
-            shape((units, HID), f32),
             shape((units, HID), bf16),
-            shape((HID, HEADP), f32),
-            shape((HID, HEADP), bf16),
+            shape((units, HID), bf16),
+            shape((HID // CORES, HEADP), bf16),
+            shape((HID // CORES, HEADP), bf16),
             shape((1, 2 * HID + HEADP), f32),
             shape((1, 1), f32),
         ],
-        scratch_shapes=[pltpu.VMEM((rows, HID), bf16), pltpu.VMEM((rows, HID), f32), pltpu.VMEM((rows, HID), bf16)],
-        compiler_params=pltpu.CompilerParams(vmem_limit_bytes=26 * MIB),
+        scratch_shapes=[
+            pltpu.VMEM((rows, HID), bf16),
+            pltpu.VMEM((rows, HID), f32),
+            pltpu.VMEM((rows, HID), bf16),
+            pltpu.VMEM((HID, HEADP), f32),
+        ],
+        compiler_params=pltpu.CompilerParams(vmem_limit_bytes=WIDE * MIB),
         cost_estimate=LIGHT,
         name="heads",
     )(at, pre_own, pre_sib, w2_own, w2_sib, wh, b1, b2, bh, tags)
@@ -738,17 +764,17 @@
 
 
 class Links:
-    def __init__(self, grid):
+    def __init__(self, grid, in_step):
         self.grid = grid
+        self.in_step = in_step
         self.last = {}
-        self.slots = [{}, {}, {}]
+        self.slots = [{}, {}]
 
     def next(self):
         self.slots.append({})
 
     def send(self, value, axis, by=1):
-        step = self.slots[-2 if axis == "z" else -3]
-        before = [step[a] for a in "zxy" if a in step and a != axis]
+        before = [self.slots[-2]["x"]] if self.in_step and axis == "z" and "x" in self.slots[-2] else []
         if axis in self.last:
             before.append(self.last[axis])
         sent = self.grid.move(after(value, *before) if before else value, axis, by)
@@ -817,7 +843,7 @@
     core = grid.at["c"]
     core_ref = core.reshape(1).astype(jnp.int32)
 
-    links = Links(grid)
+    links = Links(grid, True)
     most = feats - LATE_OUT
     mine, first_low = prepare(w_first, w_second, w_heads, crowd, most)
     half = mine.shape[0] - feats
@@ -829,10 +855,11 @@
     m[0, 1, 1] = grid.move(mine, "xy", 1)
     m[1, 0, 0] = grid.move(first_low, "z", 1)
     m[3, 0, 0] = grid.move(first_low, "z", 3)
-    own_crops = [make_crops(i) for i in range(CHUNKS)]
+    own_crops = [make_crops(i) for i in range(CHUNKS - 1)]
+    own_crops.append(make_crops(CHUNKS - 1, m[1, 0, 0]))
     made = own_crops + [m[key] for key in ((0, 1, 0), (0, 0, 1), (0, 1, 1), (1, 0, 0), (3, 0, 0))]
     stacks[0] = jnp.stack([jnp.stack([m[0, x, y][most:] for x in range(grid.x)]) for y in range(grid.y)])
-    m[2, 0, 0] = links.send(after(m[1, 0, 0], *made), "z", 1)
+    m[2, 0, 0] = links.send(m[1, 0, 0], "z", 1)
     m[1, 1, 0] = links.send(after(m[1, 0, 0], *made), "x")
     m[1, 0, 1] = links.send(after(m[1, 0, 0], *made), "y")
     links.next()
@@ -848,7 +875,6 @@
     m[1, 1, 1] = links.send(m[1, 0, 1], "x")
     m[2, 1, 1] = links.send(m[2, 1, 0], "y")
     links.next()
-    m[3, 1, 1] = links.send(m[3, 0, 1], "x")
     sib_crops = []
     for chunk in own_crops:
         sib_crops.append(grid.swap(after(chunk, *made)))
@@ -863,32 +889,38 @@
         return jnp.stack([place(*key, sign) for key in keys]).astype(jnp.int32)
 
     span = block_span(feats, grid.wide, cols)
-    pre = None
     both = (0, 1)
-    for work in (
-        ((0, 0, both), (0, 1, both), (1, 0, both)),
-        ((3, 0, both), (1, 1, both), (2, 0, both), (2, 1, both), (3, 1, (0,))),
-        ((3, 1, (1,)),),
-    ):
+
+    def products(work, before, *wait):
         inputs = [v for dz, dx, ys in work for v in [m[dz, dx, y] for y in ys] + [stacks[dz]]]
-        keys = [(dz, dx) for dz, dx, _ in work]
+        where = after(places([(dz, dx) for dz, dx, _ in work], -1), *wait)
         items = tuple((dx, ys) for _, dx, ys in work)
-        pre = first_blocks(places(keys, -1), crops, inputs, items, feats, most, span, grid.y, pre)
-
+        return first_blocks(where, crops, inputs, items, feats, most, span, grid.y, before)
+
+    m[3, 1, 1] = links.send(m[3, 0, 1], "x")
+    pre = products([(0, 0, both), (0, 1, both), (1, 0, both), (3, 0, both), (1, 1, both), (3, 1, (0,))], None)
+    first_pre = pre[0]
+    pre = products([(2, 0, both), (2, 1, both), (3, 1, (1,))], pre)
+    sib_stacks = {2: grid.swap(after(stacks[2], first_pre))}
+    sib_stacks[0] = grid.swap(stacks[0])
+    sib_stacks[1] = grid.swap(after(stacks[1], sib_stacks[0]))
+    sib_stacks[3] = grid.swap(after(stacks[3], sib_stacks[1], first_pre))
     second_own, second_sib, head_matrix = unpack(
         core_ref,
         wide_places(grid, -1),
         [stacks[z] for z in range(4)],
-        [grid.swap(stacks[z][:, :, LATE_OUT:]) for z in range(4)],
+        [sib_stacks[z] for z in range(4)],
+        half,
         HID // CORES,
     )
     bias = biases[:HID].reshape(grid.y, CORES, share)
     bias = jnp.where(grid.at["y"] == 0, bias, bias[::-1])
     bias = jnp.where(core == 0, bias, bias[:, ::-1]).transpose(1, 0, 2).reshape(1, -1)
     unit_at = [2 * ((grid.at["y"] + y) % grid.y) + c for c in (core, 1 - core) for y in range(grid.y)]
-    g_own, g_send, gw2, gw2_send, gwh, gwh_low, sums, roi_count = heads_step(
+    g_own, g_send, gw2, gw2_send, gwh, gwh_send, sums, roi_count = heads_step(
         share,
-        jnp.stack(unit_at).astype(jnp.int32),
+        grid.wide,
+        jnp.stack(unit_at + [core]).astype(jnp.int32),
         pre[0],
         grid.swap(pre[1]),
         second_own,
@@ -911,36 +943,30 @@
             for y in range(grid.y):
                 m[dz, dx, y], parts[dz, dx, y] = outs[(i * grid.y + y) * 2 : (i * grid.y + y) * 2 + 2]
 
-    gradients([(2, 1), (3, 1)])
-    gradients([(2, 0)])
+    gradients([(2, 1), (2, 0), (3, 1), (3, 0)])
     shape = (grid.z, grid.y, grid.x, half + EXTRA, cols)
-    packed = pack(core_ref, wide_places(grid, 1), gw2, grid.swap(gw2_send), gwh, grid.swap(gwh_low), sums, shape)
+    packed = pack(wide_places(grid, 1), gw2, grid.swap(gw2_send), gwh, grid.swap(gwh_send), sums, shape)
 
     def stack_of(dz):
         first = jnp.stack([jnp.stack([parts[dz, dx, y] for dx in range(grid.x)]) for y in range(grid.y)])
         return jnp.concatenate([first, packed[dz]], axis=2)
 
-    links = Links(grid)
+    links = Links(grid, False)
     far = stack_of(2)
-    gradients([(3, 0), (1, 1)], [far])
-    gradients([(1, 0), (0, 1)], [far])
-    gradients([(0, 0)], [far])
-    x0 = links.send(m[3, 1, 1], "x")
-    y0 = links.send(m[2, 1, 1], "y")
-    z0 = links.send(far, "z", 1)
-    links.next()
+    gradients([(1, 1), (1, 0), (0, 1), (0, 0)], [far])
+    begun = (far, m[3, 1, 1])
+    z0 = links.send(after(far, *begun[1:]), "z", 1)
+    y0 = links.send(after(m[2, 1, 1], *begun), "y")
+    x0 = links.send(after(m[3, 1, 1], *begun[:1]), "x")
     z1 = links.send(stack_of(3), "z", 3)
+    y1 = links.send(m[2, 0, 1], "y")
     x1 = links.send(m[3, 1, 0], "x")
-    y1 = links.send(m[2, 0, 1], "y")
-    links.next()
     z2 = links.send(low_sum(stack_of(1), z0), "z", 1)
     x2 = links.send(low_sum(m[2, 1, 0], y0), "x")
     y2 = links.send(low_sum(m[3, 0, 1], x0), "y")
-    links.next()
     z3 = links.send(low_sum(m[2, 0, 0], x2, y1), "z", 1)
     x3 = links.send(m[1, 1, 1], "x")
     y3 = links.send(m[0, 1, 1], "y")
-    links.next()
     z4 = links.send(low_sum(m[3, 0, 0], x1, y2), "z", 3)
     x4 = links.send(m[1, 1, 0], "x")
     y4 = links.send(low_sum(m[1, 0, 1], x3), "y")
@@ -955,22 +981,20 @@
     total = (total + jnp.where(odd, below, above)) + (opposite + jnp.where(odd, above, below))
     count = TERMS * total.shape[0]
     late = low_sum(stack_of(0), z1, z2)
-    links.next()
-    y5 = links.send(jnp.concatenate([late[1].reshape(-1, cols), terms(total)], axis=0), "y")
-    x5 = links.send(low_sum(m[0, 1, 0], y3), "x")
+    x5 = links.send(jnp.concatenate([late[:, 1].reshape(-1, cols), terms(total)], axis=0), "x")
+    x6 = links.send(low_sum(m[0, 1, 0], y3), "x")
     z5 = links.send(low_sum(m[1, 0, 0], x4, y4, z3), "z", 1)
-    links.next()
-    y6 = links.send(m[0, 0, 1], "y")
-    total = total + from_terms(y5[-count:])
-    late = low_sum(late[0], y5[:-count].reshape(late[0].shape))
-    x6 = links.send(jnp.concatenate([late[1], terms(total)], axis=0), "x")
-    total = total + from_terms(x6[-count:])
+    y5 = links.send(m[0, 0, 1], "y")
+    total = total + from_terms(x5[-count:])
+    late = low_sum(late[:, 0], x5[:-count].reshape(late[:, 0].shape))
+    y6 = links.send(jnp.concatenate([late[1], terms(total)], axis=0), "y")
+    total = total + from_terms(y6[-count:])
     total = total + grid.swap(total)
     sums = total.reshape(1, -1)
     main = m[0, 0, 0].astype(f32)
-    for value in (x5, y6, z4, z5):
+    for value in (x6, y5, z4, z5):
         main = main + value.astype(f32)
-    late = late[0].astype(f32) + x6[:-count].astype(f32)
+    late = late[0].astype(f32) + y6[:-count].astype(f32)
 
     first_total = jnp.concatenate([main, late[:LATE_BACK]], axis=0)
     late = late[LATE_BACK : LATE_BACK + half]
@@ -1018,9 +1042,10 @@
     bias = jnp.where(core == 0, bias, bias[:, ::-1]).transpose(1, 0, 2).reshape(1, -1)
     pre_own, pre_send = first_layer(crops, weight)
     unit_at = [2 * y + c for c in (core, 1 - core) for y in range(grid.y)]
-    g_own, g_send, gw2_own, gw2_send, gwh, _, sums, roi_count = heads_step(
+    g_own, g_send, gw2_own, gw2_send, gwh, gwh_send, sums, roi_count = heads_step(
         share,
-        jnp.stack([jnp.asarray(v) for v in unit_at]).astype(jnp.int32),
+        grid.wide,
+        jnp.stack([jnp.asarray(v) for v in unit_at + [core]]).astype(jnp.int32),
         pre_own,
         grid.swap(pre_send),
         second_own,
@@ -1034,11 +1059,8 @@
     grad = first_grad(crops, g_own, grid.swap(g_send), grid.y)
     grad = grad.reshape(grid.y, grid.wide, feats, cols).transpose(1, 0, 2, 3)
     first_total = collect_stacked(grid, grad.reshape(grid.z, grid.x, grid.y, feats, cols), "yxz")
-    gw2 = gw2_own + grid.swap(gw2_send).astype(f32)
-    gwh = gwh.reshape(grid.wide, grid.y, CORES, head_rows, HEADP)
-    gwh = lax.dynamic_index_in_dim(gwh, core, 2, keepdims=False) + grid.swap(
-        lax.dynamic_index_in_dim(gwh, 1 - core, 2, keepdims=False)
-    )
+    gw2 = gw2_own.astype(f32) + grid.swap(gw2_send).astype(f32)
+    gwh = gwh.astype(f32) + grid.swap(gwh_send).astype(f32)
     gw2 = gw2.astype(bf16).reshape(grid.y, share, grid.wide, second_cols).transpose(2, 0, 1, 3)
     small_grad = jnp.concatenate(
         [
@@ -1091,8 +1113,8 @@
         [box_targets.astype(f32), labels[:, None].astype(f32), crowd[:, None].astype(f32)], axis=1
     )
 
-    def make_crops(i):
-        return window_crops(flat_maps, base, col, row_w, col_w, i * step, step)
+    def make_crops(i, *wait):
+        return window_crops(flat_maps, after(base, *wait) if wait else base, col, row_w, col_w, i * step, step)
 
     shapes = (*w_first.shape, *w_second.shape, w_heads.shape[0], channels, rows)
     run = blocks_step if by_blocks(grid, *shapes) else stacked_step

time: 336 us -> 313 us (0.932)
  waiting for transfers between devices: 139 us -> 129 us
  Pallas kernels: 99.6 us -> 91.5 us
  other arithmetic: 21.2 us -> 14.2 us
  starting transfers between devices: 43.5 us -> 47.2 us
    pallas_call x5 -> x2, Pallas kernels: 31.7 us -> 20.8 us  [first_grad_blocks(): pl.pallas_call(functools.partial(block_grad_kernel, span, feats, blocks,...]
    ppermute x51, waiting for transfers between devices: 139 us -> 129 us  [move(): return lax.ppermute(value, AXES, pairs)]
    pallas_call x2, Pallas kernels: 8.02 us -> 13.9 us  [the longest x1 10.2 us: heads_step(): pl.pallas_call(functools.partial(head_kernel, share, wide), in_specs=[pl....]
    pallas_call x3 -> x2, Pallas kernels: 25.1 us -> 21 us  [first_blocks(): pl.pallas_call(functools.partial(block_kernel, span, items, feats, most,...]
    unnamed x171 -> x163, local copies, waits for them, and re-layouts: 19.7 us -> 16 us
    ppermute x51, starting transfers between devices: 43.5 us -> 47.2 us  [move(): return lax.ppermute(value, AXES, pairs)]
  transfers between devices with their start and end apart: 51 -> 51, of which waited for: 22 -> 21; matrix products, arithmetic and copies ran while one was open for 8% -> 7% of each run, Pallas kernels for 24% -> 24%
where the time goes in v3:
time: 313 us; the launch traced here: 312 us
  waiting for transfers between devices  129 us (41%)
  Pallas kernels  91.5 us (29%)
  starting transfers between devices  47.2 us (15%)
  local copies, waits for them, and re-layouts  27.9 us (9%)
  other arithmetic  14.2 us (5%)
    ppermute x51, waiting for transfers between devices, move(): return lax.ppermute(value, AXES, pairs)  129 us
    ppermute x51, starting transfers between devices, move(): return lax.ppermute(value, AXES, pairs)  47.2 us
    pallas_call x4, Pallas kernels, window_crops(): pl.pallas_call(functools.partial(crop_kernel, first), grid_spec=pltpu.Pre...  29.6 us
    pallas_call x2, Pallas kernels, first_blocks(): pl.pallas_call(functools.partial(block_kernel, span, items, feats, most,...  21 us
    pallas_call x2, Pallas kernels, first_grad_blocks(): pl.pallas_call(functools.partial(block_grad_kernel, span, feats, blocks,...  20.8 us
    unnamed x163, local copies, waits for them, and re-layouts  16 us
    pallas_call x1, Pallas kernels, heads_step(): pl.pallas_call(functools.partial(head_kernel, share, wide), in_specs=[pl....  10.2 us
  transfers between devices with their start and end apart: 51, of which 21 were waited for; matrix products, arithmetic and copies ran while one was open for 7% of the time, Pallas kernels for 24%

profile of v3, /device:TPU:0, one launch (start us, length us, event | category | flops | bytes accessed | tf_op | source)
XLA Modules:
  0.0 311.7 jit_solution(13989266760204650804)
XLA Ops:
  5.8 2.9 collective-permute-start.1
  8.7 1.5 collective-permute-start.2
  10.3 2.1 collective-permute-start
  12.3 2.0 collective-permute-start.4
  15.5 2.2 copy-done
  17.7 7.4 %crops.4.refs_0_ = bf16[49,64,256]{2,1,0:T(8,128)(2,1)S(1)} custom-call(s32[256]{0:T(256)S(1)} %multiply_add_fusion.4.base_ref, s32[256]{0:T(256)S(1)} %bitcast.121, bf16[256,32,256]{2,1,0:T(8,128)(2,1)S(1)} %bitcast.109, bf16[2048,16]{1,0:T(8,128)(2,1)S(1)} %bitcast.113, bf16[2048,16]{1,0:T(8,128)(2,1)S(1)} %bitcast.117, bf16[16,512]{1,0:T(8,128)(2,1)S(1)} %copy-done.13, ...), custom_call_target="tpu_custom_call" | custom-call | bytes 1024 | tf_op jit(solution)/shard_map/crops/pallas_call | solution.py:93
  27.9 7.4 %crops.5.refs_1_ = bf16[49,64,256]{2,1,0:T(8,128)(2,1)S(1)} custom-call(s32[256]{0:T(256)S(1)} %multiply_add_fusion.4.base_ref, s32[256]{0:T(256)S(1)} %bitcast.122, bf16[256,32,256]{2,1,0:T(8,128)(2,1)S(1)} %bitcast.110, bf16[2048,16]{1,0:T(8,128)(2,1)S(1)} %bitcast.114, bf16[2048,16]{1,0:T(8,128)(2,1)S(1)} %bitcast.118, bf16[16,512]{1,0:T(8,128)(2,1)S(1)} %copy-done.13, ...), custom_call_target="tpu_custom_call" | custom-call | bytes 1024 | tf_op jit(solution)/shard_map/crops/pallas_call | solution.py:93
  35.3 7.4 %crops.6.refs_2_ = bf16[49,64,256]{2,1,0:T(8,128)(2,1)S(1)} custom-call(s32[256]{0:T(256)S(1)} %multiply_add_fusion.4.base_ref, s32[256]{0:T(256)S(1)} %bitcast.123, bf16[256,32,256]{2,1,0:T(8,128)(2,1)S(1)} %bitcast.111, bf16[2048,16]{1,0:T(8,128)(2,1)S(1)} %bitcast.115, bf16[2048,16]{1,0:T(8,128)(2,1)S(1)} %bitcast.119, bf16[16,512]{1,0:T(8,128)(2,1)S(1)} %copy-done.13, ...), custom_call_target="tpu_custom_call" | custom-call | bytes 1024 | tf_op jit(solution)/shard_map/crops/pallas_call | solution.py:93
  43.9 7.4 %crops.7.refs_3_ = bf16[49,64,256]{2,1,0:T(8,128)(2,1)S(1)} custom-call(s32[256]{0:T(256)S(1)} %multiply_add_fusion.4.base_ref, s32[256]{0:T(256)S(1)} %bitcast.124, bf16[256,32,256]{2,1,0:T(8,128)(2,1)S(1)} %bitcast.112, bf16[2048,16]{1,0:T(8,128)(2,1)S(1)} %bitcast.116, bf16[2048,16]{1,0:T(8,128)(2,1)S(1)} %bitcast.120, bf16[16,512]{1,0:T(8,128)(2,1)S(1)} %copy-done.13, ...), custom_call_target="tpu_custom_call" | custom-call | bytes 1024 | tf_op jit(solution)/shard_map/crops/pallas_call | solution.py:93
  51.4 1.7 collective-permute-start.10
  53.2 1.5 collective-permute-start.9
  57.7 10.4 %collective-permute-done.10.refs_20_ = bf16[1376,256]{1,0:T(8,128)(2,1)S(1)} collective-permute-done((bf16[1376,256]{1,0:T(8,128)(2,1)}, bf16[1376,256]{1,0:T(8,128)(2,1)S(1)}, u32[]{:S(2)}, u32[]{:S(2)}) %collective-permute-start.10) | collective-permute-done | bytes 704544 | tf_op jit(solution)/shard_map/ppermute | solution.py:706
  68.1 1.5 collective-permute-start.14
  69.6 1.5 collective-permute-start.13
  72.8 11.4 %collective-permute-done.14.refs_23_ = bf16[1376,256]{1,0:T(8,128)(2,1)S(1)} collective-permute-done((bf16[1376,256]{1,0:T(8,128)(2,1)}, bf16[1376,256]{1,0:T(8,128)(2,1)S(1)}, u32[]{:S(2)}, u32[]{:S(2)}) %collective-permute-start.14) | collective-permute-done | bytes 704544 | tf_op jit(solution)/shard_map/ppermute | solution.py:706
  85.7 1.5 collective-permute-start.18
  87.3 5.9 %collective-permute-done.12.refs_16_.refs_22_.refs_1_ = bf16[2,2,384,256]{3,2,1,0:T(8,128)(2,1)} collective-permute-done((bf16[2,2,384,256]{3,2,1,0:T(8,128)(2,1)S(1)}, bf16[2,2,384,256]{3,2,1,0:T(8,128)(2,1)}, u32[]{:S(2)}, u32[]{:S(2)}) %collective-permute-start.12) | collective-permute-done | bytes 786464 | tf_op jit(solution)/shard_map/ppermute | solution.py:706
  93.7 5.3 %collective-permute-done.16.refs_13_ = bf16[1376,256]{1,0:T(8,128)(2,1)} collective-permute-done((bf16[1376,256]{1,0:T(8,128)(2,1)S(1)}, bf16[1376,256]{1,0:T(8,128)(2,1)}, u32[]{:S(2)}, u32[]{:S(2)}) %collective-permute-start.16) | collective-permute-done | bytes 704544 | tf_op jit(solution)/shard_map/ppermute | solution.py:706
  99.0 4.1 %collective-permute-start.15 = (bf16[2,2,384,256]{3,2,1,0:T(8,128)(2,1)S(1)}, bf16[2,2,384,256]{3,2,1,0:T(8,128)(2,1)S(1)}, u32[]{:S(2)}, u32[]{:S(2)}) collective-permute-start(bf16[2,2,384,256]{3,2,1,0:T(8,128)(2,1)S(1)} %pad_maximum_fusion.3.refs_10_.refs_13_.refs_0_), channel_id=1, source_target_pairs={{0,24},{1,25},{2,26},{3,27},{4,28},{5,29},{6,30},{7,31},{8,0},{9,1... | collective-permute-start | bytes 2359304 | tf_op jit(solution)/shard_map/ppermute | solution.py:706
  103.1 1.6 collective-permute-start.17
  104.7 10.3 %collective-permute-done.15.refs_19_.refs_24_.refs_17_.refs_3_ = bf16[2,2,384,256]{3,2,1,0:T(8,128)(2,1)S(1)} collective-permute-done((bf16[2,2,384,256]{3,2,1,0:T(8,128)(2,1)S(1)}, bf16[2,2,384,256]{3,2,1,0:T(8,128)(2,1)S(1)}, u32[]{:S(2)}, u32[]{:S(2)}) %collective-permute-start.15) | collective-permute-done | bytes 786464 | tf_op jit(solution)/shard_map/ppermute | solution.py:706
  116.7 1.5 collective-permute-start.21
  120.3 12.2 %first_blocks.2 = (f32[256,512]{1,0:T(8,128)}, f32[256,512]{1,0:T(8,128)}) custom-call(s32[6]{0:T(128)} %stack.253.place, bf16[49,64,256]{2,1,0:T(8,128)(2,1)} %copy-done.1, bf16[49,64,256]{2,1,0:T(8,128)(2,1)} %copy-done.2, bf16[49,64,256]{2,1,0:T(8,128)(2,1)} %copy-done.3, bf16[49,64,256]{2,1,0:T(8,128)(2,1)} %copy-done.4, ...), custom_call_target="tpu_custom_call" | custom-call | bytes 1024 | tf_op jit(solution)/shard_map/first_blocks/pallas_call | solution.py:289
  132.6 5.2 %collective-permute-done.19.refs_12_.refs_15_.refs_2_ = bf16[2,2,384,256]{3,2,1,0:T(8,128)(2,1)} collective-permute-done((bf16[2,2,384,256]{3,2,1,0:T(8,128)(2,1)}, bf16[2,2,384,256]{3,2,1,0:T(8,128)(2,1)}, u32[]{:S(2)}, u32[]{:S(2)}) %collective-permute-start.19) | collective-permute-done | bytes 786464 | tf_op jit(solution)/shard_map/ppermute | solution.py:706
  138.5 8.8 %first_blocks.3 = (f32[256,512]{1,0:T(8,128)}, f32[256,512]{1,0:T(8,128)}) custom-call(s32[3]{0:T(128)} %pad_add_fusion.place, bf16[49,64,256]{2,1,0:T(8,128)(2,1)} %copy-done.1, bf16[49,64,256]{2,1,0:T(8,128)(2,1)} %copy-done.2, bf16[49,64,256]{2,1,0:T(8,128)(2,1)} %copy-done.3, ...), custom_call_target="tpu_custom_call", output_to_operand_aliasing={{0}: (9, {}), {1}: (10, {})} | custom-call | bytes 1024 | tf_op jit(solution)/shard_map/first_blocks/pallas_call | solution.py:289
  152.4 5.0 %unpack.1 = (bf16[512,1024]{1,0:T(8,128)(2,1)}, bf16[512,1024]{1,0:T(8,128)(2,1)}, bf16[1024,512]{1,0:T(8,128)(2,1)}) custom-call(s32[1]{0:T(128)} %bitcast.4.core_ref, s32[9]{0:T(128)} %stack.264.wide_ref, bf16[2,2,384,256]{3,2,1,0:T(8,128)(2,1)} %copy-done.24, bf16[2,2,384,256]{3,2,1,0:T(8,128)(2,1)} %collective-permute-done.12.refs_16_.refs_22_.refs_1_, ...), custom_call_target="tpu_custom_call" | custom-call | bytes 1024 | tf_op jit(solution)/shard_map/unpack/pallas_call | solution.py:487
  158.2 10.2 %heads.3 = (bf16[256,512]{1,0:T(8,128)(2,1)}, bf16[256,512]{1,0:T(8,128)(2,1)}, bf16[512,1024]{1,0:T(8,128)(2,1)}, bf16[512,1024]{1,0:T(8,128)(2,1)}, bf16[512,5...) custom-call(s32[5]{0:T(128)} %stack.243.at_ref, ...), custom_call_target="tpu_custom_call" | custom-call | bytes 1024 | tf_op jit(solution)/shard_map/heads/pallas_call | solution.py:659
  170.3 2.1 collective-permute-done.27.refs_9_
  173.1 10.4 %first_grad.2 = (bf16[1360,256]{1,0:T(8,128)(2,1)}, bf16[208,256]{1,0:T(8,128)(2,1)}, bf16[1360,256]{1,0:T(8,128)(2,1)}, bf16[208,256]{1,0:T(8,128)(2,1)}, bf16[...) custom-call(s32[4]{0:T(128)} %pad_add_fusion.1.place, ...), custom_call_target="tpu_custom_call" | custom-call | bytes 1024 | tf_op jit(solution)/shard_map/first_grad/pallas_call | solution.py:381
  185.7 3.7 %pack.1 = bf16[4,2,2,208,256]{4,3,2,1,0:T(8,128)(2,1)} custom-call(s32[9]{0:T(128)} %stack.282.wide_ref, bf16[512,1024]{1,0:T(8,128)(2,1)} %get-tuple-element.138.gw2, bf16[512,1024]{1,0:T(8,128)(2,1)} %copy-done.27, bf16[512,512]{1,0:T(8,128)(2,1)} %get-tuple-element.140.gwh, bf16[512,512]{1,0:T(8,128)(2,1)} %copy-done.47, f32[1,2560]{1,0:T(1,128)} %get-tuple-element.131.sums), custom_call_target="tpu_custom_call" | custom-call | bytes 1024 | tf_op jit(solution)/shard_map/pack/pallas_call | solution.py:545
  189.5 1.5 slice_bitcast_fusion.1
  194.4 10.4 %first_grad.3 = (bf16[1360,256]{1,0:T(8,128)(2,1)}, bf16[208,256]{1,0:T(8,128)(2,1)}, bf16[1360,256]{1,0:T(8,128)(2,1)}, bf16[208,256]{1,0:T(8,128)(2,1)}, bf16[...) custom-call(s32[4]{0:T(128)} %pad_add_fusion.2.place, ...), custom_call_target="tpu_custom_call" | custom-call | bytes 1024 | tf_op jit(solution)/shard_map/first_grad/pallas_call | solution.py:381
  205.0 4.1 %collective-permute-done.33 = bf16[1360,256]{1,0:T(8,128)(2,1)} collective-permute-done((bf16[1360,256]{1,0:T(8,128)(2,1)}, bf16[1360,256]{1,0:T(8,128)(2,1)}, u32[]{:S(2)}, u32[]{:S(2)}) %collective-permute-start.33) | collective-permute-done | bytes 696352 | tf_op jit(solution)/shard_map/ppermute | solution.py:706
  213.1 3.3 %collective-permute-done.30 = bf16[2,2,416,256]{3,2,1,0:T(8,128)(2,1)S(1)} collective-permute-done((bf16[2,2,416,256]{3,2,1,0:T(8,128)(2,1)S(1)}, bf16[2,2,416,256]{3,2,1,0:T(8,128)(2,1)S(1)}, u32[]{:S(2)}, u32[]{:S(2)}) %collective-permute-start.30) | collective-permute-done | bytes 852000 | tf_op jit(solution)/shard_map/ppermute | solution.py:706
  216.4 1.7 add_convert_fusion.8
  218.1 8.1 %collective-permute-done.40 = bf16[1360,256]{1,0:T(8,128)(2,1)S(1)} collective-permute-done((bf16[1360,256]{1,0:T(8,128)(2,1)}, bf16[1360,256]{1,0:T(8,128)(2,1)S(1)}, u32[]{:S(2)}, u32[]{:S(2)}) %collective-permute-start.40) | collective-permute-done | bytes 696352 | tf_op jit(solution)/shard_map/ppermute | solution.py:706
  229.2 6.3 %collective-permute-done.31 = bf16[2,2,416,256]{3,2,1,0:T(8,128)(2,1)S(1)} collective-permute-done((bf16[2,2,416,256]{3,2,1,0:T(8,128)(2,1)S(1)}, bf16[2,2,416,256]{3,2,1,0:T(8,128)(2,1)S(1)}, u32[]{:S(2)}, u32[]{:S(2)}) %collective-permute-start.31) | collective-permute-done | bytes 852000 | tf_op jit(solution)/shard_map/ppermute | solution.py:706
  235.5 6.6 %collective-permute-done.41 = bf16[1360,256]{1,0:T(8,128)(2,1)S(1)} collective-permute-done((bf16[1360,256]{1,0:T(8,128)(2,1)S(1)}, bf16[1360,256]{1,0:T(8,128)(2,1)S(1)}, u32[]{:S(2)}, u32[]{:S(2)}) %collective-permute-start.41) | collective-permute-done | bytes 696352 | tf_op jit(solution)/shard_map/ppermute | solution.py:706
  245.3 10.1 %collective-permute-done.32 = bf16[2,2,416,256]{3,2,1,0:T(8,128)(2,1)S(1)} collective-permute-done((bf16[2,2,416,256]{3,2,1,0:T(8,128)(2,1)S(1)}, bf16[2,2,416,256]{3,2,1,0:T(8,128)(2,1)S(1)}, u32[]{:S(2)}, u32[]{:S(2)}) %collective-permute-start.32) | collective-permute-done | bytes 852000 | tf_op jit(solution)/shard_map/ppermute | solution.py:706
  255.9 3.1 collective-permute-done.37
  261.4 13.4 %collective-permute-done.38 = bf16[1360,256]{1,0:T(8,128)(2,1)S(1)} collective-permute-done((bf16[1360,256]{1,0:T(8,128)(2,1)S(1)}, bf16[1360,256]{1,0:T(8,128)(2,1)S(1)}, u32[]{:S(2)}, u32[]{:S(2)}) %collective-permute-start.38) | collective-permute-done | bytes 696352 | tf_op jit(solution)/shard_map/ppermute | solution.py:706
  276.4 1.8 collective-permute-start.49
  278.2 4.8 %collective-permute-done.39 = bf16[862,256]{1,0:T(8,128)(2,1)S(1)} collective-permute-done((bf16[862,256]{1,0:T(8,128)(2,1)S(1)}, bf16[862,256]{1,0:T(8,128)(2,1)S(1)}, u32[]{:S(2)}, u32[]{:S(2)}) %collective-permute-start.39) | collective-permute-done | bytes 441376 | tf_op jit(solution)/shard_map/ppermute | solution.py:706
  283.3 8.4 %collective-permute-done.44 = bf16[1360,256]{1,0:T(8,128)(2,1)S(1)} collective-permute-done((bf16[1360,256]{1,0:T(8,128)(2,1)S(1)}, bf16[1360,256]{1,0:T(8,128)(2,1)S(1)}, u32[]{:S(2)}, u32[]{:S(2)}) %collective-permute-start.44) | collective-permute-done | bytes 696352 | tf_op jit(solution)/shard_map/ppermute | solution.py:706
  294.0 3.7 %collective-permute-done.45 = bf16[446,256]{1,0:T(8,128)(2,1)S(1)} collective-permute-done((bf16[446,256]{1,0:T(8,128)(2,1)S(1)}, bf16[446,256]{1,0:T(8,128)(2,1)S(1)}, u32[]{:S(2)}, u32[]{:S(2)}) %collective-permute-start.45) | collective-permute-done | bytes 228384 | tf_op jit(solution)/shard_map/ppermute | solution.py:706
  300.8 3.0 collective-permute-done.47
  303.7 2.6 collective-permute-done.50
  308.7 3.0 multiply_subtract_fusion
  (312 shorter events, 57.5 us)
Async XLA Ops:
  5.8 45.6 %collective-permute-start.1 = (bf16[1760,256]{1,0:T(8,128)(2,1)}, bf16[1760,256]{1,0:T(8,128)(2,1)}, u32[]{:S(2)}, u32[]{:S(2)}) collective-permute-start(bf16[1760,256]{1,0:T(8,128)(2,1)} %get-tuple-element.105.refs_8_), channel_id=1, source_target_pairs={{0,4},{1,5},{2,6},{3,7},{4,0},{5,1},{6,2},{7,3},{8,12},{9,13},{10,... | collective-permute-start | bytes 2703368 | tf_op jit(solution)/shard_map/ppermute | solution.py:706
  8.7 42.7 %collective-permute-start.2 = (bf16[1760,256]{1,0:T(8,128)(2,1)}, bf16[1760,256]{1,0:T(8,128)(2,1)}, u32[]{:S(2)}, u32[]{:S(2)}) collective-permute-start(bf16[1760,256]{1,0:T(8,128)(2,1)} %get-tuple-element.105.refs_8_), channel_id=1, source_target_pairs={{0,2},{1,3},{2,0},{3,1},{4,6},{5,7},{6,4},{7,5},{8,10},{9,11},{10,... | collective-permute-start | bytes 2703368 | tf_op jit(solution)/shard_map/ppermute | solution.py:706
  10.3 41.2 %collective-permute-start.3 = (bf16[1760,256]{1,0:T(8,128)(2,1)}, bf16[1760,256]{1,0:T(8,128)(2,1)}, u32[]{:S(2)}, u32[]{:S(2)}) collective-permute-start(bf16[1760,256]{1,0:T(8,128)(2,1)} %get-tuple-element.105.refs_8_), channel_id=1, source_target_pairs={{0,6},{1,7},{2,4},{3,5},{4,2},{5,3},{6,0},{7,1},{8,14},{9,15},{10,... | collective-permute-start | bytes 2703368 | tf_op jit(solution)/shard_map/ppermute | solution.py:706
  10.3 33.7 %collective-permute-start = (bf16[1376,256]{1,0:T(8,128)(2,1)}, bf16[1376,256]{1,0:T(8,128)(2,1)}, u32[]{:S(2)}, u32[]{:S(2)}) collective-permute-start(bf16[1376,256]{1,0:T(8,128)(2,1)} %get-tuple-element.103), channel_id=1, source_target_pairs={{0,8},{1,9},{2,10},{3,11},{4,12},{5,13},{6,14},{7,15},{8,16},{9,17... | collective-permute-start | bytes 2113544 | tf_op jit(solution)/shard_map/ppermute | solution.py:706
  12.3 39.1 %collective-permute-start.4 = (bf16[1376,256]{1,0:T(8,128)(2,1)}, bf16[1376,256]{1,0:T(8,128)(2,1)}, u32[]{:S(2)}, u32[]{:S(2)}) collective-permute-start(bf16[1376,256]{1,0:T(8,128)(2,1)} %get-tuple-element.103), channel_id=1, source_target_pairs={{0,24},{1,25},{2,26},{3,27},{4,28},{5,29},{6,30},{7,31},{8,0},{9,1... | collective-permute-start | bytes 2113544 | tf_op jit(solution)/shard_map/ppermute | solution.py:706
  51.3 20.0 %collective-permute-start.11 = (bf16[1376,256]{1,0:T(8,128)(2,1)}, bf16[1376,256]{1,0:T(8,128)(2,1)S(1)}, u32[]{:S(2)}, u32[]{:S(2)}) collective-permute-start(bf16[1376,256]{1,0:T(8,128)(2,1)} %collective-permute-done.refs_14_), channel_id=1, source_target_pairs={{0,8},{1,9},{2,10},{3,11},{4,12},{5,13},{6,14},{7,15},{8,16},{9,17... | collective-permute-start | bytes 2113544 | tf_op jit(solution)/shard_map/ppermute | solution.py:706
  51.4 16.7 %collective-permute-start.10 = (bf16[1376,256]{1,0:T(8,128)(2,1)}, bf16[1376,256]{1,0:T(8,128)(2,1)S(1)}, u32[]{:S(2)}, u32[]{:S(2)}) collective-permute-start(bf16[1376,256]{1,0:T(8,128)(2,1)} %collective-permute-done.refs_14_), channel_id=1, source_target_pairs={{0,4},{1,5},{2,6},{3,7},{4,0},{5,1},{6,2},{7,3},{8,12},{9,13},{10,... | collective-permute-start | bytes 2113544 | tf_op jit(solution)/shard_map/ppermute | solution.py:706
  53.2 16.4 %collective-permute-start.9 = (bf16[1376,256]{1,0:T(8,128)(2,1)}, bf16[1376,256]{1,0:T(8,128)(2,1)S(1)}, u32[]{:S(2)}, u32[]{:S(2)}) collective-permute-start(bf16[1376,256]{1,0:T(8,128)(2,1)} %collective-permute-done.refs_14_), channel_id=1, source_target_pairs={{0,2},{1,3},{2,0},{3,1},{4,6},{5,7},{6,4},{7,5},{8,10},{9,11},{10,... | collective-permute-start | bytes 2113544 | tf_op jit(solution)/shard_map/ppermute | solution.py:706
  54.7 38.4 %collective-permute-start.8 = (bf16[49,64,256]{2,1,0:T(8,128)(2,1)S(1)}, bf16[49,64,256]{2,1,0:T(8,128)(2,1)S(1)}, u32[]{:S(2)}, u32[]{:S(2)}) collective-permute-start(bf16[49,64,256]{2,1,0:T(8,128)(2,1)S(1)} %crops.7.refs_3_), channel_id=1, source_target_pairs={{0,1},{1,0},{2,3},{3,2},{4,5},{5,4},{6,7},{7,6},{8,9},{9,8},{10,11... | collective-permute-start | bytes 4816904 | tf_op jit(solution)/shard_map/ppermute | solution.py:706
  68.1 16.1 %collective-permute-start.14 = (bf16[1376,256]{1,0:T(8,128)(2,1)}, bf16[1376,256]{1,0:T(8,128)(2,1)S(1)}, u32[]{:S(2)}, u32[]{:S(2)}) collective-permute-start(bf16[1376,256]{1,0:T(8,128)(2,1)} %collective-permute-done.4.refs_17_), channel_id=1, source_target_pairs={{0,4},{1,5},{2,6},{3,7},{4,0},{5,1},{6,2},{7,3},{8,12},{9,13},{10,... | collective-permute-start | bytes 2113544 | tf_op jit(solution)/shard_map/ppermute | solution.py:706
  69.6 16.1 %collective-permute-start.13 = (bf16[1376,256]{1,0:T(8,128)(2,1)}, bf16[1376,256]{1,0:T(8,128)(2,1)}, u32[]{:S(2)}, u32[]{:S(2)}) collective-permute-start(bf16[1376,256]{1,0:T(8,128)(2,1)} %collective-permute-done.4.refs_17_), channel_id=1, source_target_pairs={{0,2},{1,3},{2,0},{3,1},{4,6},{5,7},{6,4},{7,5},{8,10},{9,11},{10,... | collective-permute-start | bytes 2113544 | tf_op jit(solution)/shard_map/ppermute | solution.py:706
  71.2 16.0 %collective-permute-start.23 = (bf16[2,2,384,256]{3,2,1,0:T(8,128)(2,1)S(1)}, bf16[2,2,384,256]{3,2,1,0:T(8,128)(2,1)S(1)}, u32[]{:S(2)}, u32[]{:S(2)}) collective-permute-start(bf16[2,2,384,256]{3,2,1,0:T(8,128)(2,1)S(1)} %pad_maximum_fusion.3.refs_10_.refs_13_.refs_0_), channel_id=1, source_target_pairs={{0,1},{1,0},{2,3},{3,2},{4,5},{5,4},{6,7},{7,6},{8,9},{9,8},{10,11... | collective-permute-start | bytes 2359304 | tf_op jit(solution)/shard_map/ppermute | solution.py:706
  71.3 21.8 %collective-permute-start.12 = (bf16[2,2,384,256]{3,2,1,0:T(8,128)(2,1)S(1)}, bf16[2,2,384,256]{3,2,1,0:T(8,128)(2,1)}, u32[]{:S(2)}, u32[]{:S(2)}) collective-permute-start(bf16[2,2,384,256]{3,2,1,0:T(8,128)(2,1)S(1)} %pad_maximum_fusion.3.refs_10_.refs_13_.refs_0_), channel_id=1, source_target_pairs={{0,8},{1,9},{2,10},{3,11},{4,12},{5,13},{6,14},{7,15},{8,16},{9,17... | collective-permute-start | bytes 2359304 | tf_op jit(solution)/shard_map/ppermute | solution.py:706
  84.2 14.8 %collective-permute-start.16 = (bf16[1376,256]{1,0:T(8,128)(2,1)S(1)}, bf16[1376,256]{1,0:T(8,128)(2,1)}, u32[]{:S(2)}, u32[]{:S(2)}) collective-permute-start(bf16[1376,256]{1,0:T(8,128)(2,1)S(1)} %collective-permute-done.11.refs_10_), channel_id=1, source_target_pairs={{0,4},{1,5},{2,6},{3,7},{4,0},{5,1},{6,2},{7,3},{8,12},{9,13},{10,... | collective-permute-start | bytes 2113544 | tf_op jit(solution)/shard_map/ppermute | solution.py:706
  85.7 17.5 %collective-permute-start.18 = (bf16[1376,256]{1,0:T(8,128)(2,1)S(1)}, bf16[1376,256]{1,0:T(8,128)(2,1)S(1)}, u32[]{:S(2)}, u32[]{:S(2)}) collective-permute-start(bf16[1376,256]{1,0:T(8,128)(2,1)S(1)} %collective-permute-done.11.refs_10_), channel_id=1, source_target_pairs={{0,2},{1,3},{2,0},{3,1},{4,6},{5,7},{6,4},{7,5},{8,10},{9,11},{10,... | collective-permute-start | bytes 2113544 | tf_op jit(solution)/shard_map/ppermute | solution.py:706
  87.2 28.3 %collective-permute-start.7 = (bf16[49,64,256]{2,1,0:T(8,128)(2,1)S(1)}, bf16[49,64,256]{2,1,0:T(8,128)(2,1)S(1)}, u32[]{:S(2)}, u32[]{:S(2)}) collective-permute-start(bf16[49,64,256]{2,1,0:T(8,128)(2,1)S(1)} %crops.6.refs_2_), channel_id=1, source_target_pairs={{0,1},{1,0},{2,3},{3,2},{4,5},{5,4},{6,7},{7,6},{8,9},{9,8},{10,11... | collective-permute-start | bytes 4816904 | tf_op jit(solution)/shard_map/ppermute | solution.py:706
  93.2 23.5 %collective-permute-start.6 = (bf16[49,64,256]{2,1,0:T(8,128)(2,1)S(1)}, bf16[49,64,256]{2,1,0:T(8,128)(2,1)S(1)}, u32[]{:S(2)}, u32[]{:S(2)}) collective-permute-start(bf16[49,64,256]{2,1,0:T(8,128)(2,1)S(1)} %crops.5.refs_1_), channel_id=1, source_target_pairs={{0,1},{1,0},{2,3},{3,2},{4,5},{5,4},{6,7},{7,6},{8,9},{9,8},{10,11... | collective-permute-start | bytes 4816904 | tf_op jit(solution)/shard_map/ppermute | solution.py:706
  93.2 27.1 %collective-permute-start.5 = (bf16[49,64,256]{2,1,0:T(8,128)(2,1)S(1)}, bf16[49,64,256]{2,1,0:T(8,128)(2,1)}, u32[]{:S(2)}, u32[]{:S(2)}) collective-permute-start(bf16[49,64,256]{2,1,0:T(8,128)(2,1)S(1)} %crops.4.refs_0_), channel_id=1, source_target_pairs={{0,1},{1,0},{2,3},{3,2},{4,5},{5,4},{6,7},{7,6},{8,9},{9,8},{10,11... | collective-permute-start | bytes 4816904 | tf_op jit(solution)/shard_map/ppermute | solution.py:706
  99.0 16.0 %collective-permute-start.15 = (bf16[2,2,384,256]{3,2,1,0:T(8,128)(2,1)S(1)}, bf16[2,2,384,256]{3,2,1,0:T(8,128)(2,1)S(1)}, u32[]{:S(2)}, u32[]{:S(2)}) collective-permute-start(bf16[2,2,384,256]{3,2,1,0:T(8,128)(2,1)S(1)} %pad_maximum_fusion.3.refs_10_.refs_13_.refs_0_), channel_id=1, source_target_pairs={{0,24},{1,25},{2,26},{3,27},{4,28},{5,29},{6,30},{7,31},{8,0},{9,1... | collective-permute-start | bytes 2359304 | tf_op jit(solution)/shard_map/ppermute | solution.py:706
  103.1 12.4 %collective-permute-start.17 = (bf16[1376,256]{1,0:T(8,128)(2,1)S(1)}, bf16[1376,256]{1,0:T(8,128)(2,1)S(1)}, u32[]{:S(2)}, u32[]{:S(2)}) collective-permute-start(bf16[1376,256]{1,0:T(8,128)(2,1)S(1)} %collective-permute-done.9.refs_15_), channel_id=1, source_target_pairs={{0,4},{1,5},{2,6},{3,7},{4,0},{5,1},{6,2},{7,3},{8,12},{9,13},{10,... | collective-permute-start | bytes 2113544 | tf_op jit(solution)/shard_map/ppermute | solution.py:706
  115.0 17.5 %collective-permute-start.24 = (bf16[2,2,384,256]{3,2,1,0:T(8,128)(2,1)}, bf16[2,2,384,256]{3,2,1,0:T(8,128)(2,1)}, u32[]{:S(2)}, u32[]{:S(2)}) collective-permute-start(bf16[2,2,384,256]{3,2,1,0:T(8,128)(2,1)} %collective-permute-done.12.refs_16_.refs_22_.refs_1_), channel_id=1, source_target_pairs={{0,1},{1,0},{2,3},{3,2},{4,5},{5,4},{6,7},{7,6},{8,9},{9,8},{10,11... | collective-permute-start | bytes 2359304 | tf_op jit(solution)/shard_map/ppermute | solution.py:706
  115.5 22.4 %collective-permute-start.19 = (bf16[2,2,384,256]{3,2,1,0:T(8,128)(2,1)}, bf16[2,2,384,256]{3,2,1,0:T(8,128)(2,1)}, u32[]{:S(2)}, u32[]{:S(2)}) collective-permute-start(bf16[2,2,384,256]{3,2,1,0:T(8,128)(2,1)} %collective-permute-done.12.refs_16_.refs_22_.refs_1_), channel_id=1, source_target_pairs={{0,8},{1,9},{2,10},{3,11},{4,12},{5,13},{6,14},{7,15},{8,16},{9,17... | collective-permute-start | bytes 2359304 | tf_op jit(solution)/shard_map/ppermute | solution.py:706
  115.5 23.0 %collective-permute-start.20 = (bf16[1376,256]{1,0:T(8,128)(2,1)}, bf16[1376,256]{1,0:T(8,128)(2,1)}, u32[]{:S(2)}, u32[]{:S(2)}) collective-permute-start(bf16[1376,256]{1,0:T(8,128)(2,1)} %collective-permute-done.16.refs_13_), channel_id=1, source_target_pairs={{0,2},{1,3},{2,0},{3,1},{4,6},{5,7},{6,4},{7,5},{8,10},{9,11},{10,... | collective-permute-start | bytes 2113544 | tf_op jit(solution)/shard_map/ppermute | solution.py:706
  116.7 21.8 %collective-permute-start.21 = (bf16[1376,256]{1,0:T(8,128)(2,1)}, bf16[1376,256]{1,0:T(8,128)(2,1)}, u32[]{:S(2)}, u32[]{:S(2)}) collective-permute-start(bf16[1376,256]{1,0:T(8,128)(2,1)} %collective-permute-done.13.refs_18_), channel_id=1, source_target_pairs={{0,4},{1,5},{2,6},{3,7},{4,0},{5,1},{6,2},{7,3},{8,12},{9,13},{10,... | collective-permute-start | bytes 2113544 | tf_op jit(solution)/shard_map/ppermute | solution.py:706
  132.5 18.0 %collective-permute-start.26 = (bf16[2,2,384,256]{3,2,1,0:T(8,128)(2,1)S(1)}, bf16[2,2,384,256]{3,2,1,0:T(8,128)(2,1)S(1)}, u32[]{:S(2)}, u32[]{:S(2)}) collective-permute-start(bf16[2,2,384,256]{3,2,1,0:T(8,128)(2,1)S(1)} %copy-done.23), channel_id=1, source_target_pairs={{0,1},{1,0},{2,3},{3,2},{4,5},{5,4},{6,7},{7,6},{8,9},{9,8},{10,11... | collective-permute-start | bytes 2359304 | tf_op jit(solution)/shard_map/ppermute | solution.py:706
  137.9 12.7 %collective-permute-start.25 = (bf16[2,2,384,256]{3,2,1,0:T(8,128)(2,1)}, bf16[2,2,384,256]{3,2,1,0:T(8,128)(2,1)S(1)}, u32[]{:S(2)}, u32[]{:S(2)}) collective-permute-start(bf16[2,2,384,256]{3,2,1,0:T(8,128)(2,1)} %collective-permute-done.19.refs_12_.refs_15_.refs_2_), channel_id=1, source_target_pairs={{0,1},{1,0},{2,3},{3,2},{4,5},{5,4},{6,7},{7,6},{8,9},{9,8},{10,11... | collective-permute-start | bytes 2359304 | tf_op jit(solution)/shard_map/ppermute | solution.py:706
  147.3 10.1 %collective-permute-start.22 = (f32[256,512]{1,0:T(8,128)}, f32[256,512]{1,0:T(8,128)S(1)}, u32[]{:S(2)}, u32[]{:S(2)}) collective-permute-start(f32[256,512]{1,0:T(8,128)} %get-tuple-element.124), channel_id=1, source_target_pairs={{0,1},{1,0},{2,3},{3,2},{4,5},{5,4},{6,7},{7,6},{8,9},{9,8},{10,11... | collective-permute-start | bytes 1572872 | tf_op jit(solution)/shard_map/ppermute | solution.py:706
  168.4 16.2 %collective-permute-start.28 = (bf16[512,1024]{1,0:T(8,128)(2,1)}, bf16[512,1024]{1,0:T(8,128)(2,1)S(1)}, u32[]{:S(2)}, u32[]{:S(2)}) collective-permute-start(bf16[512,1024]{1,0:T(8,128)(2,1)} %get-tuple-element.139), channel_id=1, source_target_pairs={{0,1},{1,0},{2,3},{3,2},{4,5},{5,4},{6,7},{7,6},{8,9},{9,8},{10,11... | collective-permute-start | bytes 3145736 | tf_op jit(solution)/shard_map/ppermute | solution.py:706
  168.5 16.1 %collective-permute-start.29 = (bf16[512,512]{1,0:T(8,128)(2,1)}, bf16[512,512]{1,0:T(8,128)(2,1)S(1)}, u32[]{:S(2)}, u32[]{:S(2)}) collective-permute-start(bf16[512,512]{1,0:T(8,128)(2,1)} %get-tuple-element.141), channel_id=1, source_target_pairs={{0,1},{1,0},{2,3},{3,2},{4,5},{5,4},{6,7},{7,6},{8,9},{9,8},{10,11... | collective-permute-start | bytes 1572872 | tf_op jit(solution)/shard_map/ppermute | solution.py:706
  191.1 18.0 %collective-permute-start.33 = (bf16[1360,256]{1,0:T(8,128)(2,1)}, bf16[1360,256]{1,0:T(8,128)(2,1)}, u32[]{:S(2)}, u32[]{:S(2)}) collective-permute-start(bf16[1360,256]{1,0:T(8,128)(2,1)} %get-tuple-element.163), channel_id=1, source_target_pairs={{0,2},{1,3},{2,0},{3,1},{4,6},{5,7},{6,4},{7,5},{8,10},{9,11},{10,... | collective-permute-start | bytes 2088968 | tf_op jit(solution)/shard_map/ppermute | solution.py:706
  192.3 18.0 %collective-permute-start.34 = (bf16[1360,256]{1,0:T(8,128)(2,1)}, bf16[1360,256]{1,0:T(8,128)(2,1)}, u32[]{:S(2)}, u32[]{:S(2)}) collective-permute-start(bf16[1360,256]{1,0:T(8,128)(2,1)} %get-tuple-element.165), channel_id=1, source_target_pairs={{0,4},{1,5},{2,6},{3,7},{4,0},{5,1},{6,2},{7,3},{8,12},{9,13},{10,... | collective-permute-start | bytes 2088968 | tf_op jit(solution)/shard_map/ppermute | solution.py:706
  193.7 22.7 %collective-permute-start.30 = (bf16[2,2,416,256]{3,2,1,0:T(8,128)(2,1)S(1)}, bf16[2,2,416,256]{3,2,1,0:T(8,128)(2,1)S(1)}, u32[]{:S(2)}, u32[]{:S(2)}) collective-permute-start(bf16[2,2,416,256]{3,2,1,0:T(8,128)(2,1)S(1)} %pad_maximum_fusion.1), channel_id=1, source_target_pairs={{0,8},{1,9},{2,10},{3,11},{4,12},{5,13},{6,14},{7,15},{8,16},{9,17... | collective-permute-start | bytes 2555912 | tf_op jit(solution)/shard_map/ppermute | solution.py:706
  209.1 17.0 %collective-permute-start.40 = (bf16[1360,256]{1,0:T(8,128)(2,1)}, bf16[1360,256]{1,0:T(8,128)(2,1)S(1)}, u32[]{:S(2)}, u32[]{:S(2)}) collective-permute-start(bf16[1360,256]{1,0:T(8,128)(2,1)} %get-tuple-element.176), channel_id=1, source_target_pairs={{0,2},{1,3},{2,0},{3,1},{4,6},{5,7},{6,4},{7,5},{8,10},{9,11},{10,... | collective-permute-start | bytes 2088968 | tf_op jit(solution)/shard_map/ppermute | solution.py:706
  210.3 17.0 %collective-permute-start.35 = (bf16[1360,256]{1,0:T(8,128)(2,1)S(1)}, bf16[1360,256]{1,0:T(8,128)(2,1)S(1)}, u32[]{:S(2)}, u32[]{:S(2)}) collective-permute-start(bf16[1360,256]{1,0:T(8,128)(2,1)S(1)} %copy-done.78), channel_id=1, source_target_pairs={{0,4},{1,5},{2,6},{3,7},{4,0},{5,1},{6,2},{7,3},{8,12},{9,13},{10,... | collective-permute-start | bytes 2088968 | tf_op jit(solution)/shard_map/ppermute | solution.py:706
  216.4 19.1 %collective-permute-start.31 = (bf16[2,2,416,256]{3,2,1,0:T(8,128)(2,1)S(1)}, bf16[2,2,416,256]{3,2,1,0:T(8,128)(2,1)S(1)}, u32[]{:S(2)}, u32[]{:S(2)}) collective-permute-start(bf16[2,2,416,256]{3,2,1,0:T(8,128)(2,1)S(1)} %pad_maximum_fusion.2), channel_id=1, source_target_pairs={{0,24},{1,25},{2,26},{3,27},{4,28},{5,29},{6,30},{7,31},{8,0},{9,1... | collective-permute-start | bytes 2555912 | tf_op jit(solution)/shard_map/ppermute | solution.py:706
  226.2 15.9 %collective-permute-start.41 = (bf16[1360,256]{1,0:T(8,128)(2,1)S(1)}, bf16[1360,256]{1,0:T(8,128)(2,1)S(1)}, u32[]{:S(2)}, u32[]{:S(2)}) collective-permute-start(bf16[1360,256]{1,0:T(8,128)(2,1)S(1)} %add_convert_fusion.6), channel_id=1, source_target_pairs={{0,2},{1,3},{2,0},{3,1},{4,6},{5,7},{6,4},{7,5},{8,10},{9,11},{10,... | collective-permute-start | bytes 2088968 | tf_op jit(solution)/shard_map/ppermute | solution.py:706
  227.3 15.9 %collective-permute-start.36 = (bf16[1360,256]{1,0:T(8,128)(2,1)S(1)}, bf16[1360,256]{1,0:T(8,128)(2,1)S(1)}, u32[]{:S(2)}, u32[]{:S(2)}) collective-permute-start(bf16[1360,256]{1,0:T(8,128)(2,1)S(1)} %add_convert_fusion.8), channel_id=1, source_target_pairs={{0,4},{1,5},{2,6},{3,7},{4,0},{5,1},{6,2},{7,3},{8,12},{9,13},{10,... | collective-permute-start | bytes 2088968 | tf_op jit(solution)/shard_map/ppermute | solution.py:706
  235.5 19.9 %collective-permute-start.32 = (bf16[2,2,416,256]{3,2,1,0:T(8,128)(2,1)S(1)}, bf16[2,2,416,256]{3,2,1,0:T(8,128)(2,1)S(1)}, u32[]{:S(2)}, u32[]{:S(2)}) collective-permute-start(bf16[2,2,416,256]{3,2,1,0:T(8,128)(2,1)S(1)} %add_convert_fusion.1), channel_id=1, source_target_pairs={{0,8},{1,9},{2,10},{3,11},{4,12},{5,13},{6,14},{7,15},{8,16},{9,17... | collective-permute-start | bytes 2555912 | tf_op jit(solution)/shard_map/ppermute | solution.py:706
  242.1 18.6 %collective-permute-start.42 = (bf16[1360,256]{1,0:T(8,128)(2,1)S(1)}, bf16[1360,256]{1,0:T(8,128)(2,1)S(1)}, u32[]{:S(2)}, u32[]{:S(2)}) collective-permute-start(bf16[1360,256]{1,0:T(8,128)(2,1)S(1)} %copy-done.79), channel_id=1, source_target_pairs={{0,2},{1,3},{2,0},{3,1},{4,6},{5,7},{6,4},{7,5},{8,10},{9,11},{10,... | collective-permute-start | bytes 2088968 | tf_op jit(solution)/shard_map/ppermute | solution.py:706
  243.2 15.8 %collective-permute-start.37 = (bf16[1360,256]{1,0:T(8,128)(2,1)S(1)}, bf16[1360,256]{1,0:T(8,128)(2,1)S(1)}, u32[]{:S(2)}, u32[]{:S(2)}) collective-permute-start(bf16[1360,256]{1,0:T(8,128)(2,1)S(1)} %copy-done.80), channel_id=1, source_target_pairs={{0,4},{1,5},{2,6},{3,7},{4,0},{5,1},{6,2},{7,3},{8,12},{9,13},{10,... | collective-permute-start | bytes 2088968 | tf_op jit(solution)/shard_map/ppermute | solution.py:706
  255.4 20.9 %collective-permute-start.48 = (bf16[1360,256]{1,0:T(8,128)(2,1)S(1)}, bf16[1360,256]{1,0:T(8,128)(2,1)S(1)}, u32[]{:S(2)}, u32[]{:S(2)}) collective-permute-start(bf16[1360,256]{1,0:T(8,128)(2,1)S(1)} %add_convert_fusion.3), channel_id=1, source_target_pairs={{0,8},{1,9},{2,10},{3,11},{4,12},{5,13},{6,14},{7,15},{8,16},{9,17... | collective-permute-start | bytes 2088968 | tf_op jit(solution)/shard_map/ppermute | solution.py:706
  259.0 15.8 %collective-permute-start.38 = (bf16[1360,256]{1,0:T(8,128)(2,1)S(1)}, bf16[1360,256]{1,0:T(8,128)(2,1)S(1)}, u32[]{:S(2)}, u32[]{:S(2)}) collective-permute-start(bf16[1360,256]{1,0:T(8,128)(2,1)S(1)} %copy-done.77), channel_id=1, source_target_pairs={{0,4},{1,5},{2,6},{3,7},{4,0},{5,1},{6,2},{7,3},{8,12},{9,13},{10,... | collective-permute-start | bytes 2088968 | tf_op jit(solution)/shard_map/ppermute | solution.py:706
  260.7 17.5 %collective-permute-start.43 = (bf16[1360,256]{1,0:T(8,128)(2,1)S(1)}, bf16[1360,256]{1,0:T(8,128)(2,1)S(1)}, u32[]{:S(2)}, u32[]{:S(2)}) collective-permute-start(bf16[1360,256]{1,0:T(8,128)(2,1)S(1)} %add_convert_fusion.7), channel_id=1, source_target_pairs={{0,2},{1,3},{2,0},{3,1},{4,6},{5,7},{6,4},{7,5},{8,10},{9,11},{10,... | collective-permute-start | bytes 2088968 | tf_op jit(solution)/shard_map/ppermute | solution.py:706
  274.8 8.3 %collective-permute-start.39 = (bf16[862,256]{1,0:T(8,128)(2,1)S(1)}, bf16[862,256]{1,0:T(8,128)(2,1)S(1)}, u32[]{:S(2)}, u32[]{:S(2)}) collective-permute-start(bf16[862,256]{1,0:T(8,128)(2,1)S(1)} %pad_maximum_fusion.4), channel_id=1, source_target_pairs={{0,4},{1,5},{2,6},{3,7},{4,0},{5,1},{6,2},{7,3},{8,12},{9,13},{10,... | collective-permute-start | bytes 1324040 | tf_op jit(solution)/shard_map/ppermute | solution.py:706
  276.4 17.1 %collective-permute-start.49 = (bf16[1360,256]{1,0:T(8,128)(2,1)S(1)}, bf16[1360,256]{1,0:T(8,128)(2,1)S(1)}, u32[]{:S(2)}, u32[]{:S(2)}) collective-permute-start(bf16[1360,256]{1,0:T(8,128)(2,1)S(1)} %add_convert_fusion.4), channel_id=1, source_target_pairs={{0,24},{1,25},{2,26},{3,27},{4,28},{5,29},{6,30},{7,31},{8,0},{9,1... | collective-permute-start | bytes 2088968 | tf_op jit(solution)/shard_map/ppermute | solution.py:706
  278.2 13.5 %collective-permute-start.44 = (bf16[1360,256]{1,0:T(8,128)(2,1)S(1)}, bf16[1360,256]{1,0:T(8,128)(2,1)S(1)}, u32[]{:S(2)}, u32[]{:S(2)}) collective-permute-start(bf16[1360,256]{1,0:T(8,128)(2,1)S(1)} %copy-done.76), channel_id=1, source_target_pairs={{0,2},{1,3},{2,0},{3,1},{4,6},{5,7},{6,4},{7,5},{8,10},{9,11},{10,... | collective-permute-start | bytes 2088968 | tf_op jit(solution)/shard_map/ppermute | solution.py:706
  292.7 11.1 %collective-permute-start.47 = (bf16[1360,256]{1,0:T(8,128)(2,1)S(1)}, bf16[1360,256]{1,0:T(8,128)(2,1)S(1)}, u32[]{:S(2)}, u32[]{:S(2)}) collective-permute-start(bf16[1360,256]{1,0:T(8,128)(2,1)S(1)} %add_convert_fusion.5), channel_id=1, source_target_pairs={{0,4},{1,5},{2,6},{3,7},{4,0},{5,1},{6,2},{7,3},{8,12},{9,13},{10,... | collective-permute-start | bytes 2088968 | tf_op jit(solution)/shard_map/ppermute | solution.py:706
  293.5 12.8 %collective-permute-start.50 = (bf16[1360,256]{1,0:T(8,128)(2,1)S(1)}, bf16[1360,256]{1,0:T(8,128)(2,1)S(1)}, u32[]{:S(2)}, u32[]{:S(2)}) collective-permute-start(bf16[1360,256]{1,0:T(8,128)(2,1)S(1)} %add_convert_fusion.2), channel_id=1, source_target_pairs={{0,8},{1,9},{2,10},{3,11},{4,12},{5,13},{6,14},{7,15},{8,16},{9,17... | collective-permute-start | bytes 2088968 | tf_op jit(solution)/shard_map/ppermute | solution.py:706
  (86 other events, 1038.1 us)

commit v4 on v3

--- a/solution.py
+++ b/solution.py
@@ -18,6 +18,7 @@
 HEADP = 512
 CORES = 2
 CHUNKS = 4
+EARLY = 2
 GROUP = 32
 KSTEP = 7
 LATE_OUT = 192
@@ -198,7 +199,16 @@
     return found
 
 
-def block_kernel(span, items, feats, most, parts, fresh, place, *refs):
+def rows_of(kind, feats, most):
+    return {"all": (0, feats), "most": (0, most), "last": (most, feats)}[kind]
+
+
+def kind_span(kind, feats, most, wide, channels):
+    begin, end = rows_of(kind, feats, most)
+    return max(-(-((w * feats + begin) % channels + end - begin) // channels) for w in range(wide))
+
+
+def block_kernel(items, feats, most, wide, parts, fresh, table, *refs):
     count = len(items)
     crops, rest = refs[:parts], refs[parts:]
     own, send, pad, cells, sems = rest[-5:]
@@ -206,35 +216,40 @@
     step = pl.program_id(0)
     rows = own.shape[0]
     channels = cells.shape[3]
-    cols = inputs[0].shape[1]
-    firsts = [sum(len(ys) + 1 for _, ys in items[:i]) for i in range(count)]
+    cols = channels
+    needs = [len(item[2]) * (item[3] != "last") + (item[3] != "most") for item in items]
+    spans = [kind_span(item[3], feats, most, wide, channels) for item in items]
 
     def copies(i):
         slot = i % 2
-        start = place[i] * feats
-        at = pl.multiple_of(start % channels, 16)
-        side, ys = items[i]
-        found = cell_copies(crops, start // channels, span, cells.at[slot], sems.at[slot])
-        group = inputs[firsts[i] : firsts[i] + len(ys) + 1]
+        number, side, ys, kind = items[i]
+        begin, end = rows_of(kind, feats, most)
+        start = table[number] * feats + begin
+        cell = jnp.minimum(start // channels, CELLS - spans[i])
+        at = pl.multiple_of(start - cell * channels, 16)
+        found = cell_copies(crops, cell, spans[i], cells.at[slot, pl.ds(0, spans[i])], sems.at[slot])
+        group = inputs[sum(needs[:i]) : sum(needs[: i + 1])]
         for k, y in enumerate(ys):
             lanes = pl.ds(y * cols, cols)
-            found.append(
-                pltpu.make_async_copy(
-                    group[k].at[pl.ds(0, most)], pad.at[slot, pl.ds(at, most), lanes], sems.at[slot, parts + 2 * k]
+            if kind != "last":
+                source = group[k].at[pl.ds(0, most)]
+                found.append(
+                    pltpu.make_async_copy(source, pad.at[slot, pl.ds(at, most), lanes], sems.at[slot, parts + 2 * k])
                 )
-            )
-            found.append(
-                pltpu.make_async_copy(
-                    group[-1].at[y, side, pl.ds(0, feats - most)],
-                    pad.at[slot, pl.ds(pl.multiple_of(at + most, 16), feats - most), lanes],
-                    sems.at[slot, parts + 1 + 2 * k],
-                )
-            )
+            if kind != "most":
+                source = group[-1].at[y, side, pl.ds(0, feats - most)]
+                to = pl.ds(pl.multiple_of(at + most - begin, 16), feats - most)
+                found.append(pltpu.make_async_copy(source, pad.at[slot, to, lanes], sems.at[slot, parts + 1 + 2 * k]))
         return found
 
     def edges(i):
-        pad[i % 2, :channels, :] = jnp.zeros((channels, pad.shape[2]), bf16)
-        pad[i % 2, pad.shape[1] - channels :, :] = jnp.zeros((channels, pad.shape[2]), bf16)
+        begin, end = rows_of(items[i][3], feats, most)
+        deep = spans[i] * channels
+        low = (end - begin) // channels * channels
+        lanes = pad.shape[2]
+        if low:
+            pad[i % 2, :channels, :] = jnp.zeros((channels, lanes), bf16)
+        pad[i % 2, low:deep, :] = jnp.zeros((deep - low, lanes), bf16)
 
     @pl.when(step == 0)
     def _():
@@ -248,12 +263,6 @@
             own[...] = before[0][...]
             send[...] = before[1][...]
 
-    def multiply(lanes):
-        slot = lax.rem(step, 2)
-        got = dot(jnp.concatenate([cells[slot, j] for j in range(span)], axis=1), pad[slot, :, lanes])
-        own[:, lanes] += got[:rows]
-        send[:, lanes] += got[rows:]
-
     for i in range(count):
 
         @pl.when(step == i)
@@ -265,29 +274,34 @@
             for copy in copies(i):
                 copy.wait()
 
-    every = tuple(range(pad.shape[2] // cols))
-    for ys in sorted({ys for _, ys in items}):
-        here = [i for i, item in enumerate(items) if item[1] == ys]
-        lanes = slice(0, pad.shape[2]) if ys == every else slice(ys[0] * cols, (ys[0] + 1) * cols)
-
-        @pl.when(functools.reduce(jnp.logical_or, [step == i for i in here]))
-        def _(lanes=lanes):
-            multiply(lanes)
+    slot = lax.rem(step, 2)
+    forms = [(span, item[2]) for span, item in zip(spans, items)]
+    for form in sorted(set(forms)):
+        span, ys = form
+        lanes = slice(ys[0] * cols, (ys[-1] + 1) * cols)
+
+        @pl.when(functools.reduce(jnp.logical_or, [step == i for i in range(count) if forms[i] == form]))
+        def _(span=span, lanes=lanes):
+            lhs = jnp.concatenate([cells[slot, j] for j in range(span)], axis=1)
+            got = dot(lhs, pad[slot, : span * channels, lanes])
+            own[:, lanes] += got[:rows]
+            send[:, lanes] += got[rows:]
 
 
 def whole(shape):
     return pl.BlockSpec(shape, lambda i, place: (0,) * len(shape))
 
 
-def first_blocks(place, crops, inputs, items, feats, most, span, blocks, before):
+def first_blocks(table, crops, inputs, items, feats, most, wide, blocks, before):
     rows = sum(c.shape[1] for c in crops) // 2
     channels = crops[0].shape[2]
-    units = blocks * inputs[0].shape[1]
+    units = blocks * channels
     lead = [] if before is None else list(before)
     away = pl.BlockSpec(memory_space=pl.ANY)
     parts = len(crops)
+    span = kind_span("all", feats, most, wide, channels)
     return pl.pallas_call(
-        functools.partial(block_kernel, span, items, feats, most, parts, before is None),
+        functools.partial(block_kernel, items, feats, most, wide, parts, before is None),
         grid_spec=pltpu.PrefetchScalarGridSpec(
             num_scalar_prefetch=1,
             grid=(len(items),),
@@ -304,10 +318,10 @@
         compiler_params=pltpu.CompilerParams(vmem_limit_bytes=WIDE * MIB),
         cost_estimate=LIGHT,
         name="first_blocks",
-    )(place, *crops, *lead, *inputs)
-
-
-def block_grad_kernel(span, feats, blocks, parts, place, *refs):
+    )(table, *crops, *lead, *inputs)
+
+
+def block_grad_kernel(span, numbers, feats, blocks, parts, table, *refs):
     crops, (own, got), rest = refs[:parts], refs[parts : parts + 2], refs[parts + 2 :]
     outs, (full, cells, in_sems, out_sems) = rest[:-4], rest[-4:]
     step = pl.program_id(0)
@@ -316,10 +330,10 @@
     cols = full.shape[2] // blocks
 
     def loads(i):
-        return cell_copies(crops, (place[i] * feats) // channels, span, cells.at[i % 2], in_sems.at[i % 2])
+        return cell_copies(crops, (table[numbers[i]] * feats) // channels, span, cells.at[i % 2], in_sems.at[i % 2])
 
     def stores(i):
-        at = pl.multiple_of((place[i] * feats) % channels, 16)
+        at = pl.multiple_of((table[numbers[i]] * feats) % channels, 16)
         found = []
         for y in range(blocks):
             main, late = outs[(i * blocks + y) * 2], outs[(i * blocks + y) * 2 + 1]
@@ -370,16 +384,16 @@
                         copy.wait()
 
 
-def first_grad_blocks(place, crops, own, got, feats, late, blocks, span):
+def first_grad_blocks(table, numbers, crops, own, got, feats, late, blocks, span):
     rows, units = own.shape
     channels = crops[0].shape[2]
     cols = units // blocks
-    count = place.shape[0]
+    count = len(numbers)
     parts = len(crops)
     outs = [(feats - late, cols), (late, cols)] * (count * blocks)
     away = pl.BlockSpec(memory_space=pl.ANY)
     return pl.pallas_call(
-        functools.partial(block_grad_kernel, span, feats, blocks, parts),
+        functools.partial(block_grad_kernel, span, numbers, feats, blocks, parts),
         grid_spec=pltpu.PrefetchScalarGridSpec(
             num_scalar_prefetch=1,
             grid=(count,),
@@ -396,7 +410,7 @@
         compiler_params=pltpu.CompilerParams(vmem_limit_bytes=WIDE * MIB),
         cost_estimate=LIGHT,
         name="first_grad",
-    )(place, *crops, own, got)
+    )(table, *crops, own, got)
 
 
 def small_place(half, begin, end):
@@ -445,112 +459,103 @@
     )(first, second, heads, crowd[None, :])
 
 
-def unpack_kernel(depth, core_ref, wide_ref, *refs):
-    stacks = refs[: 2 * depth]
-    w2_own, w2_sib, wh, small, sems = refs[2 * depth :]
-    _, blocks, xs, half, _ = small.shape
-    share = w2_own.shape[0] // blocks
-    count = depth * xs
-    rows = wh.shape[0] // (count * blocks * CORES)
-    copies = [
-        pltpu.make_async_copy(ref.at[:, :, pl.ds(ref.shape[2] - half, half)], small.at[n], sems.at[n])
-        for n, ref in enumerate(stacks)
+def pack_kernel(table, *refs):
+    lates, sides, sums = refs[:8], refs[8:12], refs[12]
+    stack_two, stack_three, near_out, near, far, gw2s, gwhs, late_sems, in_sems, small_sems = refs[13:]
+    gw2, gw2_got, gwh, gwh_got = gw2s.at[0], gw2s.at[1], gwhs.at[0], gwhs.at[1]
+    arrive = [
+        pltpu.make_async_copy(ref, to, in_sems.at[n]) for n, (ref, to) in enumerate(zip(sides, (gw2, gw2_got, gwh, gwh_got)))
     ]
-    for copy in copies:
+    for copy in arrive:
         copy.start()
-    for copy in copies:
-        copy.wait()
-    for n in range(count):
-        at = wide_ref[n]
-        lanes = pl.ds(pl.multiple_of(at * 128, 128), 128)
-        for y in range(blocks):
-            turned = lax.rem(wide_ref[count] + blocks - y, blocks)
-            for first, w2, side in ((0, w2_own, core_ref[0]), (depth, w2_sib, 1 - core_ref[0])):
-
-                def piece(begin, end):
-                    rows_at, lanes_at = small_place(half, begin, end)
-                    return small[first + n // xs, y, n % xs, rows_at, lanes_at]
-
-                for begin, end in ((0, min(share, half)), (half, share)):
-                    if begin < end:
-                        w2[y * share + begin : y * share + end, lanes] = piece(begin, end)
-                to = pl.multiple_of(((at * blocks + turned) * CORES + side) * rows, rows)
-                for k in range(HEADP // 128):
-                    wh[pl.ds(to, rows), k * 128 : (k + 1) * 128] = piece(share + k * rows, share + (k + 1) * rows)
-
-
-def unpack(core, wide, own, sib, half, units):
-    smem = pl.BlockSpec(memory_space=pltpu.SMEM)
-    vmem = pl.BlockSpec(memory_space=pltpu.VMEM)
-    count = 2 * len(own)
-    blocks, xs, _, cols = own[0].shape
-    return pl.pallas_call(
-        functools.partial(unpack_kernel, len(own)),
-        in_specs=[smem, smem] + [pl.BlockSpec(memory_space=pl.ANY)] * count,
-        out_specs=[vmem] * 3,
-        out_shape=[jax.ShapeDtypeStruct((units, HID), bf16)] * 2 + [jax.ShapeDtypeStruct((HID, HEADP), bf16)],
-        scratch_shapes=[pltpu.VMEM((count, blocks, xs, half, cols), bf16), pltpu.SemaphoreType.DMA((count,))],
-        cost_estimate=LIGHT,
-        compiler_params=pltpu.CompilerParams(vmem_limit_bytes=WIDE * MIB),
-        name="unpack",
-    )(core, wide, *own, *sib)
-
-
-def pack_kernel(wide_ref, gw2, gw2_got, gwh, gwh_got, sums, out):
-    depth, blocks, xs, half, _ = out.shape
-    half -= EXTRA
+    depth = near.shape[0] + far.shape[0]
+    _, blocks, xs, tall, _ = near.shape
+    half = tall - EXTRA
     share = gw2.shape[0] // blocks
     count = depth * xs
     rows = gwh.shape[0] // (count * blocks)
-    for n in range(count):
-        at = wide_ref[n]
-        lanes = pl.ds(pl.multiple_of(at * 128, 128), 128)
+    long = lates[0].shape[0]
+    stacks = (stack_two, stack_three)
+    copies = []
+    for d in range(2):
         for y in range(blocks):
-
-            def small(begin, end, value):
-                rows_at, lanes_at = small_place(half, begin, end)
-                out[n // xs, y, n % xs, rows_at, lanes_at] = value.astype(bf16)
-
-            ahead = lax.rem(wide_ref[count] + y, blocks)
-            turned = (blocks - y) % blocks
-            for begin, end in ((0, min(share, half)), (half, share)):
-                if begin < end:
-                    part = slice(turned * share + begin, turned * share + end)
-                    small(begin, end, gw2[part, lanes].astype(f32) + gw2_got[part, lanes].astype(f32))
-            here = pl.ds(pl.multiple_of((at * blocks + ahead) * rows, rows), rows)
-            for k in range(HEADP // 128):
-                group = slice(k * 128, (k + 1) * 128)
-                both = gwh[here, group].astype(f32) + gwh_got[here, group].astype(f32)
-                small(share + k * rows, share + (k + 1) * rows, both)
+            for x in range(xs):
+                n = (d * blocks + y) * xs + x
+                copies.append(pltpu.make_async_copy(lates[n], far.at[d, y, x, pl.ds(0, long)], late_sems.at[n]))
+    for copy in copies:
+        copy.start()
     rest = sums[...]
     rows_left = []
     for _ in range(TERMS):
         term = rest.astype(bf16).astype(f32)
         rest = rest - term
         rows_left += [term[:, k : k + 256] for k in range(0, term.shape[1], 256)]
-    rows_left += [jnp.zeros_like(rows_left[0])] * (-len(rows_left) % 8)
+    rows_left += [jnp.zeros_like(rows_left[0])] * (-len(rows_left) % (blocks * xs))
     each = len(rows_left) // (blocks * xs)
-    for y in range(blocks):
-        for x in range(xs):
-            n = y * xs + x
-            some = rows_left[n * each : (n + 1) * each] + [jnp.zeros_like(rows_left[0])] * (EXTRA - each)
-            some = jnp.concatenate(some, axis=0).astype(bf16)
-            for dz in range(depth):
-                out[dz, y, x, half:, :] = some if dz >= 2 else jnp.zeros_like(some)
-
-
-def pack(wide, gw2, gw2_got, gwh, gwh_got, sums, shape):
+    for copy in arrive:
+        copy.wait()
+    for dz in (2, 3, 1, 0):
+        out, at, skip = (far, dz - 2, long) if dz >= 2 else (near, dz, 0)
+        for y in range(blocks):
+            for x in range(xs):
+                here = table[count + dz * xs + x]
+                lanes = pl.ds(pl.multiple_of(here * 128, 128), 128)
+
+                def small(begin, end, value):
+                    rows_at, lanes_at = small_place(half, begin, end)
+                    out[at, y, x, skip + rows_at.start : skip + rows_at.stop, lanes_at] = value.astype(bf16)
+
+                turned = (blocks - y) % blocks
+                for begin, end in ((0, min(share, half)), (half, share)):
+                    if begin < end:
+                        part = slice(turned * share + begin, turned * share + end)
+                        small(begin, end, gw2[part, lanes].astype(f32) + gw2_got[part, lanes].astype(f32))
+                ahead = lax.rem(table[2 * count] + y, blocks)
+                block = pl.ds(pl.multiple_of((here * blocks + ahead) * rows, rows), rows)
+                for k in range(HEADP // 128):
+                    group = slice(k * 128, (k + 1) * 128)
+                    value = gwh[block, group].astype(f32) + gwh_got[block, group].astype(f32)
+                    small(share + k * rows, share + (k + 1) * rows, value)
+                n = y * xs + x
+                some = rows_left[n * each : (n + 1) * each] + [jnp.zeros_like(rows_left[0])] * (EXTRA - each)
+                some = jnp.concatenate(some, axis=0).astype(bf16)
+                out[at, y, x, skip + half :, :] = some if dz >= 2 else jnp.zeros_like(some)
+        if dz >= 2:
+            for copy in copies[at * blocks * xs : (at + 1) * blocks * xs]:
+                copy.wait()
+            pltpu.make_async_copy(far.at[at], stacks[at], small_sems.at[at]).start()
+    last = pltpu.make_async_copy(near, near_out, small_sems.at[2])
+    last.start()
+    for at in range(2):
+        pltpu.make_async_copy(far.at[at], stacks[at], small_sems.at[at]).wait()
+    last.wait()
+
+
+def pack(table, lates, gw2, gwh, sums, half, places):
     smem = pl.BlockSpec(memory_space=pltpu.SMEM)
     vmem = pl.BlockSpec(memory_space=pltpu.VMEM)
+    away = pl.BlockSpec(memory_space=pl.ANY)
+    long, cols = lates[0].shape
+    tall = half + EXTRA
+    stack = jax.ShapeDtypeStruct((*places, long + tall, cols), bf16)
     return pl.pallas_call(
         pack_kernel,
-        in_specs=[smem] + [vmem] * 5,
-        out_specs=vmem,
-        out_shape=jax.ShapeDtypeStruct(shape, bf16),
+        in_specs=[smem] + [away] * (len(lates) + 4) + [vmem],
+        out_specs=[away] * 3,
+        out_shape=[stack, stack, jax.ShapeDtypeStruct((2, *places, tall, cols), bf16)],
+        scratch_shapes=[
+            pltpu.VMEM((2, *places, tall, cols), bf16),
+            pltpu.VMEM((2, *places, long + tall, cols), bf16),
+            pltpu.VMEM((2, *gw2[0].shape), bf16),
+            pltpu.VMEM((2, *gwh[0].shape), bf16),
+            pltpu.SemaphoreType.DMA((len(lates),)),
+            pltpu.SemaphoreType.DMA((4,)),
+            pltpu.SemaphoreType.DMA((3,)),
+        ],
         cost_estimate=LIGHT,
         compiler_params=pltpu.CompilerParams(vmem_limit_bytes=WIDE * MIB),
         name="pack",
-    )(wide, gw2, gw2_got, gwh, gwh_got, sums)
+    )(table, *lates, *gw2, *gwh, sums)
 
 
 def gelu(x):
@@ -560,6 +565,170 @@
 def gelu_slope(x):
     t = jnp.tanh(GELU_A * (x + GELU_B * x * x * x))
     return 0.5 * (1.0 + t) + 0.5 * x * (1.0 - t * t) * (GELU_A * (1.0 + 3.0 * GELU_B * x * x))
+
+
+def kept_count(wh):
+    ends = jnp.sum(wh[:, HEADP - 128 :].astype(f32), axis=0, keepdims=True)
+    return 128.0 * ends[:, 126:127] + ends[:, 127:128]
+
+
+def losses(out, label, valid, targets, kept):
+    col = lax.broadcasted_iota(jnp.int32, out.shape, 1)
+    fore = jnp.where(label > 0, valid, 0.0)
+    is_logit = col < CLS
+    onehot = jnp.where(col == label, 1.0, 0.0)
+    masked = jnp.where(is_logit, out, -jnp.inf)
+    top = jnp.max(masked, axis=1, keepdims=True)
+    shifted = jnp.exp(masked - top)
+    total = jnp.sum(shifted, axis=1, keepdims=True)
+    row_loss = valid * (jnp.log(total) + top - jnp.sum(onehot * out, axis=1, keepdims=True))
+    scale = 1.0 / kept
+    grad = (shifted / total - onehot) * (valid * scale)
+    base = CLS + 4 * (label - 1)
+    for j in range(4):
+        mark = (col == base + j) & (col >= CLS)
+        err = jnp.sum(jnp.where(mark, out, 0.0), axis=1, keepdims=True) - targets[:, j : j + 1]
+        size = jnp.abs(err)
+        row_loss += fore * jnp.where(size < 1.0, 0.5 * err * err, size - 0.5)
+        grad += jnp.where(mark, jnp.clip(err, -1.0, 1.0) * (fore * scale), 0.0)
+    return row_loss, grad
+
+
+def head_blocks_kernel(share, depth, table, *refs):
+    stacks, (pre_own, pre_sib, biases, labels, crowd, targets) = refs[: 2 * depth], refs[2 * depth : 2 * depth + 6]
+    g_outs, gw2_outs, gwh_outs = refs[2 * depth + 6 : 2 * depth + 8], refs[2 * depth + 8 : 2 * depth + 10], refs[
+        2 * depth + 10 : 2 * depth + 12
+    ]
+    sums, kept_out, small, w2, wh, pre1, h1, pre2, gpre2, gwh, g, gw2, gwhs, bias, in_sems, out_sems = refs[2 * depth + 12 :]
+    rows, units = pre_own.shape
+    blocks, xs, half, _ = small.shape[1:]
+    count = depth * xs
+    each = HID // (count * blocks * CORES)
+    copies = [
+        pltpu.make_async_copy(ref.at[:, :, pl.ds(ref.shape[2] - half, half)], small.at[n], in_sems.at[n])
+        for n, ref in enumerate(stacks)
+    ]
+    for copy in copies:
+        copy.start()
+    core = table[2 * count + 1]
+    for side, pre in enumerate((pre_own, pre_sib)):
+        for k in range(blocks):
+            unit = table[2 * count + 2 + side * blocks + k]
+            lanes = slice(side * units + k * share, side * units + (k + 1) * share)
+            first_bias = biases[:, pl.ds(pl.multiple_of(unit * share, share), share)]
+            pre1[:, lanes] = pre[:, k * share : (k + 1) * share] + first_bias
+        lanes = slice(side * units, (side + 1) * units)
+        h1[:, lanes] = gelu(pre1[:, lanes]).astype(bf16)
+    for copy in copies:
+        copy.wait()
+    for n in range(count):
+        at = table[n]
+        lanes = pl.ds(pl.multiple_of(at * 128, 128), 128)
+        for y in range(blocks):
+            turned = lax.rem(table[2 * count] + blocks - y, blocks)
+            for side in range(CORES):
+
+                def piece(begin, end):
+                    rows_at, lanes_at = small_place(half, begin, end)
+                    return small[side * depth + n // xs, y, n % xs, rows_at, lanes_at]
+
+                for begin, end in ((0, min(share, half)), (half, share)):
+                    if begin < end:
+                        w2[side, y * share + begin : y * share + end, lanes] = piece(begin, end)
+                owner = core if side == 0 else 1 - core
+                to = pl.multiple_of(((at * blocks + turned) * CORES + owner) * each, each)
+                for k in range(HEADP // 128):
+                    wh[pl.ds(to, each), k * 128 : (k + 1) * 128] = piece(share + k * each, share + (k + 1) * each)
+    bias[...] = jnp.zeros_like(bias)
+    bias[:, :HEAD] = biases[:, 2 * HID :]
+    pre2[...] = jnp.zeros_like(pre2) + biases[:, HID : 2 * HID]
+    for side in range(CORES):
+        for k in range(0, units, share):
+            part = dot(h1[:, side * units + k : side * units + k + share], w2[side, k : k + share, :])
+            pre2[...] += part.astype(bf16).astype(f32)
+    h2 = gelu(pre2[...]).astype(bf16)
+    out = dot(h2, wh[...]) + bias[...]
+    flags = jnp.concatenate([labels[...], crowd[...]], axis=0).astype(f32)
+    flags = jnp.concatenate([flags, targets[...].astype(f32), jnp.zeros((2, rows), f32)], axis=0)
+    flags = jnp.transpose(flags)
+    kept = kept_count(wh)
+    kept_out[...] = kept
+    row_loss, grad = losses(out, flags[:, 0:1].astype(jnp.int32), 1.0 - flags[:, 1:2], flags[:, 2:6], kept)
+    g_out = grad.astype(bf16)
+    g_h2 = dot(g_out, wh[...], ((1,), (1,)))
+    g2 = (g_h2 * gelu_slope(pre2[...])).astype(bf16)
+    gpre2[...] = g2
+    sums[:, HID : 2 * HID] = jnp.sum(g2.astype(f32), axis=0, keepdims=True)
+    sent = []
+    for side in (1, 0):
+        lanes = slice(side * units, (side + 1) * units)
+        g_h1 = dot(gpre2[...], w2[side], ((1,), (1,)))
+        g[side] = (g_h1 * gelu_slope(pre1[:, lanes])).astype(bf16)
+        sent.append(pltpu.make_async_copy(g.at[side], g_outs[side], out_sems.at[side]))
+        sent[-1].start()
+    for side in (1, 0):
+        lanes = slice(side * units, (side + 1) * units)
+        gw2[side] = dot(h1[:, lanes], gpre2[...], ((0,), (0,))).astype(bf16)
+        sent.append(pltpu.make_async_copy(gw2.at[side], gw2_outs[side], out_sems.at[CORES + side]))
+        sent[-1].start()
+    gwh[...] = dot(h2, g_out, ((0,), (0,)))
+    for n in range(count * blocks):
+        for side in (1, 0):
+            owner = core if side == 0 else 1 - core
+            row = pl.multiple_of((n * CORES + owner) * each, each)
+            gwhs[side, n * each : (n + 1) * each, :] = gwh[pl.ds(row, each), :].astype(bf16)
+    for side in (1, 0):
+        sent.append(pltpu.make_async_copy(gwhs.at[side], gwh_outs[side], out_sems.at[2 * CORES + side]))
+        sent[-1].start()
+    for side in range(CORES):
+        columns = jnp.sum(g[side].astype(f32), axis=0, keepdims=True)
+        for k in range(blocks):
+            unit = table[2 * count + 2 + side * blocks + k]
+            sums[:, pl.ds(pl.multiple_of(unit * share, share), share)] = columns[:, k * share : (k + 1) * share]
+    head_sums = jnp.sum(g_out.astype(f32), axis=0, keepdims=True)
+    lane = lax.broadcasted_iota(jnp.int32, head_sums.shape, 1)
+    loss = jnp.sum(row_loss, axis=0, keepdims=True)
+    sums[:, 2 * HID : 2 * HID + HEADP] = jnp.where(lane == HEAD, loss, head_sums)
+    for copy in sent:
+        copy.wait()
+
+
+def heads_blocks(share, half, table, own, sib, pre_own, pre_sib, biases, labels, crowd, targets):
+    rows, units = pre_own.shape
+    depth = len(own)
+    blocks, xs, _, cols = own[0].shape
+    smem = pl.BlockSpec(memory_space=pltpu.SMEM)
+    vmem = pl.BlockSpec(memory_space=pltpu.VMEM)
+    away = pl.BlockSpec(memory_space=pl.ANY)
+    shape = jax.ShapeDtypeStruct
+    return pl.pallas_call(
+        functools.partial(head_blocks_kernel, share, depth),
+        in_specs=[smem] + [away] * (2 * depth) + [vmem] * 6,
+        out_specs=[away] * 6 + [vmem] * 2,
+        out_shape=[shape((rows, units), bf16)] * 2
+        + [shape((units, HID), bf16)] * 2
+        + [shape((HID // CORES, HEADP), bf16)] * 2
+        + [shape((1, 2 * HID + HEADP), f32), shape((1, 1), f32)],
+        scratch_shapes=[
+            pltpu.VMEM((2 * depth, blocks, xs, half, cols), bf16),
+            pltpu.VMEM((CORES, units, HID), bf16),
+            pltpu.VMEM((HID, HEADP), bf16),
+            pltpu.VMEM((rows, HID), f32),
+            pltpu.VMEM((rows, HID), bf16),
+            pltpu.VMEM((rows, HID), f32),
+            pltpu.VMEM((rows, HID), bf16),
+            pltpu.VMEM((HID, HEADP), f32),
+            pltpu.VMEM((CORES, rows, units), bf16),
+            pltpu.VMEM((CORES, units, HID), bf16),
+            pltpu.VMEM((CORES, HID // CORES, HEADP), bf16),
+            pltpu.VMEM((1, HEADP), f32),
+            pltpu.SemaphoreType.DMA((2 * depth,)),
+            pltpu.SemaphoreType.DMA((3 * CORES,)),
+        ],
+        compiler_params=pltpu.CompilerParams(vmem_limit_bytes=WIDE * MIB),
+        cost_estimate=LIGHT,
+        name="heads",
+    )(table, *own, *sib, pre_own, pre_sib, biases, labels, crowd, targets)
 
 
 def head_kernel(
@@ -598,29 +767,10 @@
             pre2[...] += part.astype(bf16).astype(f32)
     h2 = gelu(pre2[...]).astype(bf16)
     out = dot(h2, wh[...]) + bh[...]
-    col = lax.broadcasted_iota(jnp.int32, out.shape, 1)
     label = tags[:, 4:5].astype(jnp.int32)
-    valid = 1.0 - tags[:, 5:6]
-    fore = jnp.where(label > 0, valid, 0.0)
-    is_logit = col < CLS
-    onehot = jnp.where(col == label, 1.0, 0.0)
-    masked = jnp.where(is_logit, out, -jnp.inf)
-    top = jnp.max(masked, axis=1, keepdims=True)
-    shifted = jnp.exp(masked - top)
-    total = jnp.sum(shifted, axis=1, keepdims=True)
-    row_loss = valid * (jnp.log(total) + top - jnp.sum(onehot * out, axis=1, keepdims=True))
-    ends = jnp.sum(wh[:, HEADP - 128 :].astype(f32), axis=0, keepdims=True)
-    kept = 128.0 * ends[:, 126:127] + ends[:, 127:128]
+    kept = kept_count(wh)
     count[...] = kept
-    scale = 1.0 / kept
-    grad = (shifted / total - onehot) * (valid * scale)
-    base = CLS + 4 * (label - 1)
-    for j in range(4):
-        mark = (col == base + j) & (col >= CLS)
-        err = jnp.sum(jnp.where(mark, out, 0.0), axis=1, keepdims=True) - tags[:, j : j + 1]
-        size = jnp.abs(err)
-        row_loss += fore * jnp.where(size < 1.0, 0.5 * err * err, size - 0.5)
-        grad += jnp.where(mark, jnp.clip(err, -1.0, 1.0) * (fore * scale), 0.0)
+    row_loss, grad = losses(out, label, 1.0 - tags[:, 5:6], tags[:, :4], kept)
     g_out = grad.astype(bf16)
     head_sums = jnp.sum(g_out.astype(f32), axis=0, keepdims=True)
     lane = lax.broadcasted_iota(jnp.int32, head_sums.shape, 1)
@@ -804,13 +954,17 @@
     )
 
 
-def wide_places(grid, sign):
-    places = [
-        ((grid.at["z"] + sign * dz) % grid.z) * grid.x + (grid.at["x"] + sign * dx) % grid.x
-        for dz in range(grid.z)
-        for dx in range(grid.x)
-    ]
-    return jnp.stack(places + [grid.at["y"]]).astype(jnp.int32)
+def place_table(grid):
+    found = []
+    for sign in (-1, 1):
+        for dz in range(grid.z):
+            for dx in range(grid.x):
+                z, x = (grid.at["z"] + sign * dz) % grid.z, (grid.at["x"] + sign * dx) % grid.x
+                found.append(z * grid.x + x)
+    y, core = grid.at["y"], grid.at["c"]
+    found += [y, core]
+    found += [CORES * ((y + k) % grid.y) + c for c in (core, 1 - core) for k in range(grid.y)]
+    return jnp.stack(found).astype(jnp.int32)
 
 
 def low_sum(first, *others):
@@ -836,12 +990,12 @@
     return total
 
 
-def blocks_step(grid, make_crops, w_first, w_second, w_heads, biases, crowd, tags):
+def blocks_step(grid, make_crops, w_first, w_second, w_heads, biases, labels, crowd, targets):
     feats, cols = w_first.shape
     share, _ = w_second.shape
     head_rows = w_heads.shape[0]
-    core = grid.at["c"]
-    core_ref = core.reshape(1).astype(jnp.int32)
+    table = place_table(grid)
+    count = grid.z * grid.x
 
     links = Links(grid, True)
     most = feats - LATE_OUT
@@ -852,84 +1006,64 @@
 
     m[0, 1, 0] = grid.move(mine, "x", 1)
     m[0, 0, 1] = grid.move(mine, "y", 1)
-    m[0, 1, 1] = grid.move(mine, "xy", 1)
     m[1, 0, 0] = grid.move(first_low, "z", 1)
-    m[3, 0, 0] = grid.move(first_low, "z", 3)
-    own_crops = [make_crops(i) for i in range(CHUNKS - 1)]
-    own_crops.append(make_crops(CHUNKS - 1, m[1, 0, 0]))
-    made = own_crops + [m[key] for key in ((0, 1, 0), (0, 0, 1), (0, 1, 1), (1, 0, 0), (3, 0, 0))]
+    own_crops = [make_crops(i) for i in range(CHUNKS)]
+    made = own_crops[:EARLY] + [m[key] for key in ((0, 1, 0), (0, 0, 1), (1, 0, 0))]
+    m[3, 0, 0] = links.send(after(first_low, *made), "z", 3)
+    m[1, 1, 0] = links.send(after(m[1, 0, 0], *made), "x")
+    m[0, 1, 1] = links.send(after(m[0, 1, 0], *made), "y")
     stacks[0] = jnp.stack([jnp.stack([m[0, x, y][most:] for x in range(grid.x)]) for y in range(grid.y)])
+    links.next()
     m[2, 0, 0] = links.send(m[1, 0, 0], "z", 1)
-    m[1, 1, 0] = links.send(after(m[1, 0, 0], *made), "x")
-    m[1, 0, 1] = links.send(after(m[1, 0, 0], *made), "y")
+    m[3, 1, 0] = links.send(m[3, 0, 0], "x")
+    m[1, 0, 1] = links.send(m[1, 0, 0], "y")
     links.next()
     stacks[1] = links.send(stacks[0], "z", 1)
-    m[3, 1, 0] = links.send(m[3, 0, 0], "x")
+    m[2, 1, 0] = links.send(m[2, 0, 0], "x")
     m[3, 0, 1] = links.send(m[3, 0, 0], "y")
     links.next()
     stacks[3] = links.send(stacks[0], "z", 3)
-    m[2, 1, 0] = links.send(m[2, 0, 0], "x")
+    m[1, 1, 1] = links.send(m[1, 0, 1], "x")
     m[2, 0, 1] = links.send(m[2, 0, 0], "y")
     links.next()
     stacks[2] = links.send(stacks[1], "z", 1)
-    m[1, 1, 1] = links.send(m[1, 0, 1], "x")
+    m[3, 1, 1] = links.send(m[3, 0, 1], "x")
     m[2, 1, 1] = links.send(m[2, 1, 0], "y")
-    links.next()
     sib_crops = []
     for chunk in own_crops:
         sib_crops.append(grid.swap(after(chunk, *made)))
     crops = own_crops + sib_crops
 
-    def place(dz, dx, sign):
-        z = (grid.at["z"] + sign * dz) % grid.z
-        x = (grid.at["x"] + sign * dx) % grid.x
-        return z * grid.x + x
-
-    def places(keys, sign):
-        return jnp.stack([place(*key, sign) for key in keys]).astype(jnp.int32)
-
     span = block_span(feats, grid.wide, cols)
     both = (0, 1)
 
-    def products(work, before, *wait):
-        inputs = [v for dz, dx, ys in work for v in [m[dz, dx, y] for y in ys] + [stacks[dz]]]
-        where = after(places([(dz, dx) for dz, dx, _ in work], -1), *wait)
-        items = tuple((dx, ys) for _, dx, ys in work)
-        return first_blocks(where, crops, inputs, items, feats, most, span, grid.y, before)
-
-    m[3, 1, 1] = links.send(m[3, 0, 1], "x")
-    pre = products([(0, 0, both), (0, 1, both), (1, 0, both), (3, 0, both), (1, 1, both), (3, 1, (0,))], None)
-    first_pre = pre[0]
-    pre = products([(2, 0, both), (2, 1, both), (3, 1, (1,))], pre)
-    sib_stacks = {2: grid.swap(after(stacks[2], first_pre))}
+    def products(work, before):
+        inputs = []
+        for dz, dx, ys, kind in work:
+            inputs += [m[dz, dx, y] for y in ys if kind != "last"] + [stacks[dz]] * (kind != "most")
+        items = tuple((dz * grid.x + dx, dx, ys, kind) for dz, dx, ys, kind in work)
+        return first_blocks(table, crops, inputs, items, feats, most, grid.wide, grid.y, before)
+
+    work = [(dz, dx, both, "all") for dz, dx in ((0, 0), (0, 1), (1, 0), (3, 0), (1, 1))]
+    first_pre = products(work + [(3, 1, (0,), "all"), (2, 0, both, "most"), (2, 1, (0,), "most")], None)
+    work = [(2, 0, both, "last"), (2, 1, both, "last"), (2, 1, (1,), "most"), (3, 1, (1,), "all")]
+    pre = products(work, first_pre)
+    sib_stacks = {2: grid.swap(after(stacks[2], first_pre[0]))}
     sib_stacks[0] = grid.swap(stacks[0])
     sib_stacks[1] = grid.swap(after(stacks[1], sib_stacks[0]))
-    sib_stacks[3] = grid.swap(after(stacks[3], sib_stacks[1], first_pre))
-    second_own, second_sib, head_matrix = unpack(
-        core_ref,
-        wide_places(grid, -1),
+    sib_stacks[3] = grid.swap(after(stacks[3], sib_stacks[1], first_pre[0]))
+    g_own, g_send, gw2, gw2_send, gwh, gwh_send, sums, roi_count = heads_blocks(
+        share,
+        half,
+        table,
         [stacks[z] for z in range(4)],
         [sib_stacks[z] for z in range(4)],
-        half,
-        HID // CORES,
-    )
-    bias = biases[:HID].reshape(grid.y, CORES, share)
-    bias = jnp.where(grid.at["y"] == 0, bias, bias[::-1])
-    bias = jnp.where(core == 0, bias, bias[:, ::-1]).transpose(1, 0, 2).reshape(1, -1)
-    unit_at = [2 * ((grid.at["y"] + y) % grid.y) + c for c in (core, 1 - core) for y in range(grid.y)]
-    g_own, g_send, gw2, gw2_send, gwh, gwh_send, sums, roi_count = heads_step(
-        share,
-        grid.wide,
-        jnp.stack(unit_at + [core]).astype(jnp.int32),
         pre[0],
         grid.swap(pre[1]),
-        second_own,
-        second_sib,
-        head_matrix,
-        bias,
-        biases[HID : 2 * HID].reshape(1, -1),
-        jnp.pad(biases[2 * HID :], (0, HEADP - HEAD)).reshape(1, -1),
-        tags,
+        biases[None, :],
+        labels[None, :],
+        crowd[None, :],
+        targets.T,
     )
 
     g_got = grid.swap(g_send)
@@ -937,19 +1071,29 @@
     parts = {}
 
     def gradients(keys, wait=()):
-        where = places(keys, 1)
-        outs = first_grad_blocks(after(where, *wait), crops, g_own, g_got, feats, LATE_BACK, grid.y, span)
+        numbers = tuple(count + dz * grid.x + dx for dz, dx in keys)
+        outs = first_grad_blocks(after(table, *wait), numbers, crops, g_own, g_got, feats, LATE_BACK, grid.y, span)
         for i, (dz, dx) in enumerate(keys):
             for y in range(grid.y):
                 m[dz, dx, y], parts[dz, dx, y] = outs[(i * grid.y + y) * 2 : (i * grid.y + y) * 2 + 2]
 
     gradients([(2, 1), (2, 0), (3, 1), (3, 0)])
-    shape = (grid.z, grid.y, grid.x, half + EXTRA, cols)
-    packed = pack(wide_places(grid, 1), gw2, grid.swap(gw2_send), gwh, grid.swap(gwh_send), sums, shape)
+    lates = [parts[dz, dx, y] for dz in (2, 3) for y in range(grid.y) for dx in range(grid.x)]
+    packed = pack(
+        table,
+        lates,
+        (gw2, grid.swap(after(gw2_send, g_got))),
+        (gwh, grid.swap(after(gwh_send, g_got))),
+        sums,
+        half,
+        (grid.y, grid.x),
+    )
 
     def stack_of(dz):
+        if dz >= 2:
+            return packed[dz - 2]
         first = jnp.stack([jnp.stack([parts[dz, dx, y] for dx in range(grid.x)]) for y in range(grid.y)])
-        return jnp.concatenate([first, packed[dz]], axis=2)
+        return jnp.concatenate([first, packed[2][dz]], axis=2)
 
     links = Links(grid, False)
     far = stack_of(2)
@@ -979,22 +1123,22 @@
     below, above, opposite = extra_rows(z0), extra_rows(z1), extra_rows(z2)
     total = sums.reshape(-1, cols)
     total = (total + jnp.where(odd, below, above)) + (opposite + jnp.where(odd, above, below))
-    count = TERMS * total.shape[0]
+    extra = TERMS * total.shape[0]
     late = low_sum(stack_of(0), z1, z2)
     x5 = links.send(jnp.concatenate([late[:, 1].reshape(-1, cols), terms(total)], axis=0), "x")
     x6 = links.send(low_sum(m[0, 1, 0], y3), "x")
     z5 = links.send(low_sum(m[1, 0, 0], x4, y4, z3), "z", 1)
     y5 = links.send(m[0, 0, 1], "y")
-    total = total + from_terms(x5[-count:])
-    late = low_sum(late[:, 0], x5[:-count].reshape(late[:, 0].shape))
+    total = total + from_terms(x5[-extra:])
+    late = low_sum(late[:, 0], x5[:-extra].reshape(late[:, 0].shape))
     y6 = links.send(jnp.concatenate([late[1], terms(total)], axis=0), "y")
-    total = total + from_terms(y6[-count:])
+    total = total + from_terms(y6[-extra:])
     total = total + grid.swap(total)
     sums = total.reshape(1, -1)
     main = m[0, 0, 0].astype(f32)
     for value in (x6, y5, z4, z5):
         main = main + value.astype(f32)
-    late = late[0].astype(f32) + y6[:-count].astype(f32)
+    late = late[0].astype(f32) + y6[:-extra].astype(f32)
 
     first_total = jnp.concatenate([main, late[:LATE_BACK]], axis=0)
     late = late[LATE_BACK : LATE_BACK + half]
@@ -1005,7 +1149,10 @@
     return roi_count.reshape(()), sums, first_total, total[:share], heads_total
 
 
-def stacked_step(grid, make_crops, w_first, w_second, w_heads, biases, crowd, tags):
+def stacked_step(grid, make_crops, w_first, w_second, w_heads, biases, labels, crowd, targets):
+    tags = jnp.concatenate(
+        [targets.astype(f32), labels[:, None].astype(f32), crowd[:, None].astype(f32)], axis=1
+    )
     feats, cols = w_first.shape
     share, second_cols = w_second.shape
     head_rows = w_heads.shape[0]
@@ -1109,17 +1256,13 @@
     row_w = padded[:, 0].reshape(rows * 8, WIN)
     col_w = padded[:, 1].reshape(rows * 8, WIN)
     step = rows // CHUNKS
-    tags = jnp.concatenate(
-        [box_targets.astype(f32), labels[:, None].astype(f32), crowd[:, None].astype(f32)], axis=1
-    )
-
     def make_crops(i, *wait):
         return window_crops(flat_maps, after(base, *wait) if wait else base, col, row_w, col_w, i * step, step)
 
     shapes = (*w_first.shape, *w_second.shape, w_heads.shape[0], channels, rows)
     run = blocks_step if by_blocks(grid, *shapes) else stacked_step
     roi_count, sums, first_total, second_total, heads_total = run(
-        grid, make_crops, w_first, w_second, w_heads, biases, crowd, tags
+        grid, make_crops, w_first, w_second, w_heads, biases, labels, crowd, box_targets
     )
     loss_total = sums[0, 2 * HID + HEAD]
     bias_grad = sums[0, : 2 * HID + HEAD]

time: 313 us -> 301 us (0.962)
  waiting for transfers between devices: 129 us -> 140 us
  starting transfers between devices: 47.2 us -> 36.5 us
  local copies, waits for them, and re-layouts: 27.9 us -> 21.6 us
  other arithmetic: 14.2 us -> 8.57 us
    ppermute x51, waiting for transfers between devices: 129 us -> 140 us  [move(): return lax.ppermute(value, AXES, pairs)]
    ppermute x51, starting transfers between devices: 47.2 us -> 36.5 us  [move(): return lax.ppermute(value, AXES, pairs)]
    pallas_call x7 -> x6, Pallas kernels: 60.7 us -> 60.9 us  [the longest x2 23.6 us: first_blocks(): pl.pallas_call(functools.partial(block_kernel, items, feats, most, wide,...]
    unnamed x163 -> x153, local copies, waits for them, and re-layouts: 16 us -> 15.8 us
  transfers between devices with their start and end apart: 51 -> 51, of which waited for: 21 -> 24; matrix products, arithmetic and copies ran while one was open for 7% -> 4% of each run, Pallas kernels for 24% -> 25%
where the time goes in v4:
time: 301 us; the launch traced here: 300 us
  waiting for transfers between devices  140 us (47%)
  Pallas kernels  91.8 us (30%)
  starting transfers between devices  36.5 us (12%)
  local copies, waits for them, and re-layouts  21.6 us (7%)
  other arithmetic  8.57 us (3%)
    ppermute x51, waiting for transfers between devices, move(): return lax.ppermute(value, AXES, pairs)  140 us
    ppermute x51, starting transfers between devices, move(): return lax.ppermute(value, AXES, pairs)  36.5 us
    pallas_call x4, Pallas kernels, window_crops(): pl.pallas_call(functools.partial(crop_kernel, first), grid_spec=pltpu.Pre...  29.6 us
    pallas_call x2, Pallas kernels, first_blocks(): pl.pallas_call(functools.partial(block_kernel, items, feats, most, wide,...  23.6 us
    pallas_call x2, Pallas kernels, first_grad_blocks(): pl.pallas_call(functools.partial(block_grad_kernel, span, numbers, feats,...  21.2 us
    unnamed x153, local copies, waits for them, and re-layouts  15.8 us
    pallas_call x1, Pallas kernels, heads_blocks(): pl.pallas_call(functools.partial(head_blocks_kernel, share, depth), in_sp...  11.3 us
  transfers between devices with their start and end apart: 51, of which 24 were waited for; matrix products, arithmetic and copies ran while one was open for 4% of the time, Pallas kernels for 25%

profile of v4, /device:TPU:0, one launch (start us, length us, event | category | flops | bytes accessed | tf_op | source)
XLA Modules:
  0.0 300.0 jit_solution(10961789607255219206)
XLA Ops:
  0.7 1.4 copy-done.9
  5.8 2.9 collective-permute-start
  8.7 1.5 collective-permute-start.1
  10.3 1.6 collective-permute-start.2
  13.0 2.2 copy-done
  15.2 7.4 %crops.5.refs_1_ = bf16[49,64,256]{2,1,0:T(8,128)(2,1)S(1)} custom-call(s32[256]{0:T(256)S(1)} %multiply_add_fusion.4.base_ref, s32[256]{0:T(256)S(1)} %bitcast.97, bf16[256,32,256]{2,1,0:T(8,128)(2,1)S(1)} %bitcast.85, bf16[2048,16]{1,0:T(8,128)(2,1)S(1)} %bitcast.89, bf16[2048,16]{1,0:T(8,128)(2,1)S(1)} %bitcast.93, bf16[16,512]{1,0:T(8,128)(2,1)S(1)} %copy-done.13, ...), custom_call_target="tpu_custom_call" | custom-call | bytes 1024 | tf_op jit(solution)/shard_map/crops/pallas_call | solution.py:94
  25.4 7.4 %crops.4.refs_0_ = bf16[49,64,256]{2,1,0:T(8,128)(2,1)S(1)} custom-call(s32[256]{0:T(256)S(1)} %multiply_add_fusion.4.base_ref, s32[256]{0:T(256)S(1)} %bitcast.98, bf16[256,32,256]{2,1,0:T(8,128)(2,1)S(1)} %bitcast.86, bf16[2048,16]{1,0:T(8,128)(2,1)S(1)} %bitcast.90, bf16[2048,16]{1,0:T(8,128)(2,1)S(1)} %bitcast.94, bf16[16,512]{1,0:T(8,128)(2,1)S(1)} %copy-done.13, ...), custom_call_target="tpu_custom_call" | custom-call | bytes 1024 | tf_op jit(solution)/shard_map/crops/pallas_call | solution.py:94
  32.9 2.3 collective-permute-start.4
  36.2 7.4 %crops.7.refs_3_ = bf16[49,64,256]{2,1,0:T(8,128)(2,1)S(1)} custom-call(s32[256]{0:T(256)S(1)} %multiply_add_fusion.4.base_ref, s32[256]{0:T(256)S(1)} %bitcast.99, bf16[256,32,256]{2,1,0:T(8,128)(2,1)S(1)} %bitcast.87, bf16[2048,16]{1,0:T(8,128)(2,1)S(1)} %bitcast.91, bf16[2048,16]{1,0:T(8,128)(2,1)S(1)} %bitcast.95, bf16[16,512]{1,0:T(8,128)(2,1)S(1)} %copy-done.13, ...), custom_call_target="tpu_custom_call" | custom-call | bytes 1024 | tf_op jit(solution)/shard_map/crops/pallas_call | solution.py:94
  45.8 4.0 %collective-permute-done.4.refs_17_ = bf16[1376,256]{1,0:T(8,128)(2,1)S(1)} collective-permute-done((bf16[1376,256]{1,0:T(8,128)(2,1)}, bf16[1376,256]{1,0:T(8,128)(2,1)S(1)}, u32[]{:S(2)}, u32[]{:S(2)}) %collective-permute-start.4) | collective-permute-done | bytes 704544 | tf_op jit(solution)/shard_map/ppermute | solution.py:856
  49.8 2.0 collective-permute-done.5.refs_20_
  53.4 2.9 collective-permute-done.3.refs_12_
  57.4 12.0 %collective-permute-done.7.refs_25_ = bf16[1376,256]{1,0:T(8,128)(2,1)S(1)} collective-permute-done((bf16[1376,256]{1,0:T(8,128)(2,1)}, bf16[1376,256]{1,0:T(8,128)(2,1)S(1)}, u32[]{:S(2)}, u32[]{:S(2)}) %collective-permute-start.7) | collective-permute-done | bytes 704544 | tf_op jit(solution)/shard_map/ppermute | solution.py:856
  72.4 13.9 %collective-permute-done.10.refs_27_ = bf16[1376,256]{1,0:T(8,128)(2,1)} collective-permute-done((bf16[1376,256]{1,0:T(8,128)(2,1)S(1)}, bf16[1376,256]{1,0:T(8,128)(2,1)}, u32[]{:S(2)}, u32[]{:S(2)}) %collective-permute-start.10) | collective-permute-done | bytes 704544 | tf_op jit(solution)/shard_map/ppermute | solution.py:856
  86.8 7.4 %crops.6.refs_2_ = bf16[49,64,256]{2,1,0:T(8,128)(2,1)S(1)} custom-call(s32[256]{0:T(256)S(1)} %multiply_add_fusion.4.base_ref, s32[256]{0:T(256)S(1)} %bitcast.100, bf16[256,32,256]{2,1,0:T(8,128)(2,1)S(1)} %bitcast.88, bf16[2048,16]{1,0:T(8,128)(2,1)S(1)} %bitcast.92, bf16[2048,16]{1,0:T(8,128)(2,1)S(1)} %bitcast.96, bf16[16,512]{1,0:T(8,128)(2,1)S(1)} %copy-done.13, ...), custom_call_target="tpu_custom_call" | custom-call | bytes 1024 | tf_op jit(solution)/shard_map/crops/pallas_call | solution.py:94
  95.0 1.5 collective-permute-start.12
  96.5 3.5 %collective-permute-done.11.refs_21_ = bf16[1376,256]{1,0:T(8,128)(2,1)S(1)} collective-permute-done((bf16[1376,256]{1,0:T(8,128)(2,1)S(1)}, bf16[1376,256]{1,0:T(8,128)(2,1)S(1)}, u32[]{:S(2)}, u32[]{:S(2)}) %collective-permute-start.11) | collective-permute-done | bytes 704544 | tf_op jit(solution)/shard_map/ppermute | solution.py:856
  100.5 14.4 %collective-permute-done.12.refs_19_.refs_24_.refs_14_.refs_3_ = bf16[2,2,384,256]{3,2,1,0:T(8,128)(2,1)S(1)} collective-permute-done((bf16[2,2,384,256]{3,2,1,0:T(8,128)(2,1)S(1)}, bf16[2,2,384,256]{3,2,1,0:T(8,128)(2,1)S(1)}, u32[]{:S(2)}, u32[]{:S(2)}) %collective-permute-start.12) | collective-permute-done | bytes 786464 | tf_op jit(solution)/shard_map/ppermute | solution.py:856
  115.0 1.5 collective-permute-start.25
  118.4 15.5 %first_blocks.2 = (f32[256,512]{1,0:T(8,128)}, f32[256,512]{1,0:T(8,128)}) custom-call(s32[22]{0:T(128)} %stack.169.table, bf16[49,64,256]{2,1,0:T(8,128)(2,1)} %copy-done.2, bf16[49,64,256]{2,1,0:T(8,128)(2,1)} %copy-done.1, bf16[49,64,256]{2,1,0:T(8,128)(2,1)} %copy-done.4, bf16[49,64,256]{2,1,0:T(8,128)(2,1)} %copy-done.3, ...), custom_call_target="tpu_custom_call" | custom-call | bytes 1024 | tf_op jit(solution)/shard_map/first_blocks/pallas_call | solution.py:303
  134.2 2.8 collective-permute-done.13.refs_10_.refs_11_.refs_2_
  137.0 8.1 %first_blocks.3 = (f32[256,512]{1,0:T(8,128)}, f32[256,512]{1,0:T(8,128)}) custom-call(s32[22]{0:T(128)} %stack.169.table, bf16[49,64,256]{2,1,0:T(8,128)(2,1)} %copy-done.2, bf16[49,64,256]{2,1,0:T(8,128)(2,1)} %copy-done.1, bf16[49,64,256]{2,1,0:T(8,128)(2,1)} %copy-done.4, ...), custom_call_target="tpu_custom_call", output_to_operand_aliasing={{0}: (9, {}), {1}: (10, {})} | custom-call | bytes 1024 | tf_op jit(solution)/shard_map/first_blocks/pallas_call | solution.py:303
  148.5 11.3 %heads.3 = (bf16[256,512]{1,0:T(8,128)(2,1)}, bf16[256,512]{1,0:T(8,128)(2,1)}, bf16[512,1024]{1,0:T(8,128)(2,1)}, bf16[512,1024]{1,0:T(8,128)(2,1)}, bf16[512,5...) custom-call(s32[22]{0:T(128)} %stack.169.table, ...), custom_call_target="tpu_custom_call" | custom-call | bytes 1024 | tf_op jit(solution)/shard_map/heads/pallas_call | solution.py:704
  162.4 10.4 %first_grad.2 = (bf16[1360,256]{1,0:T(8,128)(2,1)}, bf16[208,256]{1,0:T(8,128)(2,1)}, bf16[1360,256]{1,0:T(8,128)(2,1)}, bf16[208,256]{1,0:T(8,128)(2,1)}, bf16[...) custom-call(s32[22]{0:T(128)} %stack.169.table, ...), custom_call_target="tpu_custom_call" | custom-call | bytes 1024 | tf_op jit(solution)/shard_map/first_grad/pallas_call | solution.py:395
  173.9 4.8 %pack.1 = (bf16[2,2,416,256]{3,2,1,0:T(8,128)(2,1)}, bf16[2,2,416,256]{3,2,1,0:T(8,128)(2,1)}, bf16[2,2,2,208,256]{4,3,2,1,0:T(8,128)(2,1)}) custom-call(s32[22]{0:T(128)} %stack.169.table, bf16[208,256]{1,0:T(8,128)(2,1)} %get-tuple-element.139.refs_0_, bf16[208,256]{1,0:T(8,128)(2,1)} %get-tuple-element.140.refs_1_, ...), custom_call_target="tpu_custom_call" | custom-call | bytes 1024 | tf_op jit(solution)/shard_map/pack/pallas_call | solution.py:541
  179.3 1.4 collective-permute-start.34
  180.8 10.8 %first_grad.3 = (bf16[1360,256]{1,0:T(8,128)(2,1)}, bf16[208,256]{1,0:T(8,128)(2,1)}, bf16[1360,256]{1,0:T(8,128)(2,1)}, bf16[208,256]{1,0:T(8,128)(2,1)}, bf16[...) custom-call(s32[22]{0:T(128)} %stack.169.table, ...), custom_call_target="tpu_custom_call" | custom-call | bytes 1024 | tf_op jit(solution)/shard_map/first_grad/pallas_call | solution.py:395
  191.6 5.3 %collective-permute-done.33 = bf16[1360,256]{1,0:T(8,128)(2,1)S(1)} collective-permute-done((bf16[1360,256]{1,0:T(8,128)(2,1)}, bf16[1360,256]{1,0:T(8,128)(2,1)S(1)}, u32[]{:S(2)}, u32[]{:S(2)}) %collective-permute-start.33) | collective-permute-done | bytes 696352 | tf_op jit(solution)/shard_map/ppermute | solution.py:856
  197.4 1.4 collective-permute-start.35
  199.1 4.6 %collective-permute-done.30 = bf16[2,2,416,256]{3,2,1,0:T(8,128)(2,1)S(1)} collective-permute-done((bf16[2,2,416,256]{3,2,1,0:T(8,128)(2,1)}, bf16[2,2,416,256]{3,2,1,0:T(8,128)(2,1)S(1)}, u32[]{:S(2)}, u32[]{:S(2)}) %collective-permute-start.30) | collective-permute-done | bytes 852000 | tf_op jit(solution)/shard_map/ppermute | solution.py:856
  203.9 10.2 %collective-permute-done.40 = bf16[1360,256]{1,0:T(8,128)(2,1)S(1)} collective-permute-done((bf16[1360,256]{1,0:T(8,128)(2,1)}, bf16[1360,256]{1,0:T(8,128)(2,1)S(1)}, u32[]{:S(2)}, u32[]{:S(2)}) %collective-permute-start.40) | collective-permute-done | bytes 696352 | tf_op jit(solution)/shard_map/ppermute | solution.py:856
  214.7 1.4 collective-permute-start.36
  216.6 6.6 %collective-permute-done.31 = bf16[2,2,416,256]{3,2,1,0:T(8,128)(2,1)S(1)} collective-permute-done((bf16[2,2,416,256]{3,2,1,0:T(8,128)(2,1)S(1)}, bf16[2,2,416,256]{3,2,1,0:T(8,128)(2,1)S(1)}, u32[]{:S(2)}, u32[]{:S(2)}) %collective-permute-start.31) | collective-permute-done | bytes 852000 | tf_op jit(solution)/shard_map/ppermute | solution.py:856
  223.2 7.1 %collective-permute-done.41 = bf16[1360,256]{1,0:T(8,128)(2,1)S(1)} collective-permute-done((bf16[1360,256]{1,0:T(8,128)(2,1)S(1)}, bf16[1360,256]{1,0:T(8,128)(2,1)S(1)}, u32[]{:S(2)}, u32[]{:S(2)}) %collective-permute-start.41) | collective-permute-done | bytes 696352 | tf_op jit(solution)/shard_map/ppermute | solution.py:856
  230.8 1.4 collective-permute-start.37
  232.9 10.6 %collective-permute-done.32 = bf16[2,2,416,256]{3,2,1,0:T(8,128)(2,1)S(1)} collective-permute-done((bf16[2,2,416,256]{3,2,1,0:T(8,128)(2,1)S(1)}, bf16[2,2,416,256]{3,2,1,0:T(8,128)(2,1)S(1)}, u32[]{:S(2)}, u32[]{:S(2)}) %collective-permute-start.32) | collective-permute-done | bytes 852000 | tf_op jit(solution)/shard_map/ppermute | solution.py:856
  244.0 2.6 collective-permute-done.37
  248.3 1.6 collective-permute-start.43
  250.0 12.4 %collective-permute-done.38 = bf16[1360,256]{1,0:T(8,128)(2,1)S(1)} collective-permute-done((bf16[1360,256]{1,0:T(8,128)(2,1)S(1)}, bf16[1360,256]{1,0:T(8,128)(2,1)S(1)}, u32[]{:S(2)}, u32[]{:S(2)}) %collective-permute-start.38) | collective-permute-done | bytes 696352 | tf_op jit(solution)/shard_map/ppermute | solution.py:856
  264.0 1.4 collective-permute-start.49
  265.5 1.4 collective-permute-start.44
  266.9 3.8 %collective-permute-done.39 = bf16[862,256]{1,0:T(8,128)(2,1)S(1)} collective-permute-done((bf16[862,256]{1,0:T(8,128)(2,1)S(1)}, bf16[862,256]{1,0:T(8,128)(2,1)S(1)}, u32[]{:S(2)}, u32[]{:S(2)}) %collective-permute-start.39) | collective-permute-done | bytes 441376 | tf_op jit(solution)/shard_map/ppermute | solution.py:856
  270.9 8.3 %collective-permute-done.44 = bf16[1360,256]{1,0:T(8,128)(2,1)S(1)} collective-permute-done((bf16[1360,256]{1,0:T(8,128)(2,1)S(1)}, bf16[1360,256]{1,0:T(8,128)(2,1)S(1)}, u32[]{:S(2)}, u32[]{:S(2)}) %collective-permute-start.44) | collective-permute-done | bytes 696352 | tf_op jit(solution)/shard_map/ppermute | solution.py:856
  279.2 1.4 collective-permute-start.45
  282.2 3.0 %collective-permute-done.45 = bf16[446,256]{1,0:T(8,128)(2,1)S(1)} collective-permute-done((bf16[446,256]{1,0:T(8,128)(2,1)S(1)}, bf16[446,256]{1,0:T(8,128)(2,1)S(1)}, u32[]{:S(2)}, u32[]{:S(2)}) %collective-permute-start.45) | collective-permute-done | bytes 228384 | tf_op jit(solution)/shard_map/ppermute | solution.py:856
  288.3 3.9 %collective-permute-done.47 = bf16[1360,256]{1,0:T(8,128)(2,1)S(1)} collective-permute-done((bf16[1360,256]{1,0:T(8,128)(2,1)S(1)}, bf16[1360,256]{1,0:T(8,128)(2,1)S(1)}, u32[]{:S(2)}, u32[]{:S(2)}) %collective-permute-start.47) | collective-permute-done | bytes 696352 | tf_op jit(solution)/shard_map/ppermute | solution.py:856
  292.2 2.4 collective-permute-done.50
  297.0 3.0 multiply_subtract_fusion
  (275 shorter events, 41.8 us)
Async XLA Ops:
  5.8 27.0 %collective-permute-start = (bf16[1760,256]{1,0:T(8,128)(2,1)}, bf16[1760,256]{1,0:T(8,128)(2,1)}, u32[]{:S(2)}, u32[]{:S(2)}) collective-permute-start(bf16[1760,256]{1,0:T(8,128)(2,1)} %get-tuple-element.108.refs_8_), channel_id=1, source_target_pairs={{0,4},{1,5},{2,6},{3,7},{4,0},{5,1},{6,2},{7,3},{8,12},{9,13},{10,... | collective-permute-start | bytes 2703368 | tf_op jit(solution)/shard_map/ppermute | solution.py:856
  8.7 24.1 %collective-permute-start.1 = (bf16[1760,256]{1,0:T(8,128)(2,1)}, bf16[1760,256]{1,0:T(8,128)(2,1)}, u32[]{:S(2)}, u32[]{:S(2)}) collective-permute-start(bf16[1760,256]{1,0:T(8,128)(2,1)} %get-tuple-element.108.refs_8_), channel_id=1, source_target_pairs={{0,2},{1,3},{2,0},{3,1},{4,6},{5,7},{6,4},{7,5},{8,10},{9,11},{10,... | collective-permute-start | bytes 2703368 | tf_op jit(solution)/shard_map/ppermute | solution.py:856
  10.3 22.6 %collective-permute-start.2 = (bf16[1376,256]{1,0:T(8,128)(2,1)}, bf16[1376,256]{1,0:T(8,128)(2,1)}, u32[]{:S(2)}, u32[]{:S(2)}) collective-permute-start(bf16[1376,256]{1,0:T(8,128)(2,1)} %get-tuple-element.111), channel_id=1, source_target_pairs={{0,8},{1,9},{2,10},{3,11},{4,12},{5,13},{6,14},{7,15},{8,16},{9,17... | collective-permute-start | bytes 2113544 | tf_op jit(solution)/shard_map/ppermute | solution.py:856
  32.9 17.0 %collective-permute-start.4 = (bf16[1376,256]{1,0:T(8,128)(2,1)}, bf16[1376,256]{1,0:T(8,128)(2,1)S(1)}, u32[]{:S(2)}, u32[]{:S(2)}) collective-permute-start(bf16[1376,256]{1,0:T(8,128)(2,1)} %get-tuple-element.111), channel_id=1, source_target_pairs={{0,24},{1,25},{2,26},{3,27},{4,28},{5,29},{6,30},{7,31},{8,0},{9,1... | collective-permute-start | bytes 2113544 | tf_op jit(solution)/shard_map/ppermute | solution.py:856
  35.2 16.7 %collective-permute-start.5 = (bf16[1376,256]{1,0:T(8,128)(2,1)}, bf16[1376,256]{1,0:T(8,128)(2,1)S(1)}, u32[]{:S(2)}, u32[]{:S(2)}) collective-permute-start(bf16[1376,256]{1,0:T(8,128)(2,1)} %collective-permute-done.2.refs_14_), channel_id=1, source_target_pairs={{0,4},{1,5},{2,6},{3,7},{4,0},{5,1},{6,2},{7,3},{8,12},{9,13},{10,... | collective-permute-start | bytes 2113544 | tf_op jit(solution)/shard_map/ppermute | solution.py:856
  35.7 20.6 %collective-permute-start.3 = (bf16[1760,256]{1,0:T(8,128)(2,1)}, bf16[1760,256]{1,0:T(8,128)(2,1)S(1)}, u32[]{:S(2)}, u32[]{:S(2)}) collective-permute-start(bf16[1760,256]{1,0:T(8,128)(2,1)} %collective-permute-done.refs_11_), channel_id=1, source_target_pairs={{0,2},{1,3},{2,0},{3,1},{4,6},{5,7},{6,4},{7,5},{8,10},{9,11},{10,... | collective-permute-start | bytes 2703368 | tf_op jit(solution)/shard_map/ppermute | solution.py:856
  44.8 49.5 %collective-permute-start.19 = (bf16[49,64,256]{2,1,0:T(8,128)(2,1)S(1)}, bf16[49,64,256]{2,1,0:T(8,128)(2,1)S(1)}, u32[]{:S(2)}, u32[]{:S(2)}) collective-permute-start(bf16[49,64,256]{2,1,0:T(8,128)(2,1)S(1)} %crops.7.refs_3_), channel_id=1, source_target_pairs={{0,1},{1,0},{2,3},{3,2},{4,5},{5,4},{6,7},{7,6},{8,9},{9,8},{10,11... | collective-permute-start | bytes 4816904 | tf_op jit(solution)/shard_map/ppermute | solution.py:856
  51.9 17.5 %collective-permute-start.7 = (bf16[1376,256]{1,0:T(8,128)(2,1)}, bf16[1376,256]{1,0:T(8,128)(2,1)S(1)}, u32[]{:S(2)}, u32[]{:S(2)}) collective-permute-start(bf16[1376,256]{1,0:T(8,128)(2,1)} %collective-permute-done.2.refs_14_), channel_id=1, source_target_pairs={{0,8},{1,9},{2,10},{3,11},{4,12},{5,13},{6,14},{7,15},{8,16},{9,17... | collective-permute-start | bytes 2113544 | tf_op jit(solution)/shard_map/ppermute | solution.py:856
  51.9 17.5 %collective-permute-start.6 = (bf16[1376,256]{1,0:T(8,128)(2,1)S(1)}, bf16[1376,256]{1,0:T(8,128)(2,1)S(1)}, u32[]{:S(2)}, u32[]{:S(2)}) collective-permute-start(bf16[1376,256]{1,0:T(8,128)(2,1)S(1)} %collective-permute-done.4.refs_17_), channel_id=1, source_target_pairs={{0,4},{1,5},{2,6},{3,7},{4,0},{5,1},{6,2},{7,3},{8,12},{9,13},{10,... | collective-permute-start | bytes 2113544 | tf_op jit(solution)/shard_map/ppermute | solution.py:856
  56.3 15.5 %collective-permute-start.9 = (bf16[1376,256]{1,0:T(8,128)(2,1)}, bf16[1376,256]{1,0:T(8,128)(2,1)S(1)}, u32[]{:S(2)}, u32[]{:S(2)}) collective-permute-start(bf16[1376,256]{1,0:T(8,128)(2,1)} %collective-permute-done.2.refs_14_), channel_id=1, source_target_pairs={{0,2},{1,3},{2,0},{3,1},{4,6},{5,7},{6,4},{7,5},{8,10},{9,11},{10,... | collective-permute-start | bytes 2113544 | tf_op jit(solution)/shard_map/ppermute | solution.py:856
  70.3 15.9 %collective-permute-start.10 = (bf16[1376,256]{1,0:T(8,128)(2,1)S(1)}, bf16[1376,256]{1,0:T(8,128)(2,1)}, u32[]{:S(2)}, u32[]{:S(2)}) collective-permute-start(bf16[1376,256]{1,0:T(8,128)(2,1)S(1)} %collective-permute-done.7.refs_25_), channel_id=1, source_target_pairs={{0,4},{1,5},{2,6},{3,7},{4,0},{5,1},{6,2},{7,3},{8,12},{9,13},{10,... | collective-permute-start | bytes 2113544 | tf_op jit(solution)/shard_map/ppermute | solution.py:856
  71.0 23.4 %collective-permute-start.14 = (bf16[2,2,384,256]{3,2,1,0:T(8,128)(2,1)S(1)}, bf16[2,2,384,256]{3,2,1,0:T(8,128)(2,1)S(1)}, u32[]{:S(2)}, u32[]{:S(2)}) collective-permute-start(bf16[2,2,384,256]{3,2,1,0:T(8,128)(2,1)S(1)} %pad_maximum_fusion.1.refs_10_.refs_13_.refs_0_), channel_id=1, source_target_pairs={{0,1},{1,0},{2,3},{3,2},{4,5},{5,4},{6,7},{7,6},{8,9},{9,8},{10,11... | collective-permute-start | bytes 2359304 | tf_op jit(solution)/shard_map/ppermute | solution.py:856
  71.1 23.9 %collective-permute-start.8 = (bf16[2,2,384,256]{3,2,1,0:T(8,128)(2,1)S(1)}, bf16[2,2,384,256]{3,2,1,0:T(8,128)(2,1)}, u32[]{:S(2)}, u32[]{:S(2)}) collective-permute-start(bf16[2,2,384,256]{3,2,1,0:T(8,128)(2,1)S(1)} %pad_maximum_fusion.1.refs_10_.refs_13_.refs_0_), channel_id=1, source_target_pairs={{0,8},{1,9},{2,10},{3,11},{4,12},{5,13},{6,14},{7,15},{8,16},{9,17... | collective-permute-start | bytes 2359304 | tf_op jit(solution)/shard_map/ppermute | solution.py:856
  71.8 23.2 %collective-permute-start.20 = (bf16[1376,256]{1,0:T(8,128)(2,1)S(1)}, bf16[1376,256]{1,0:T(8,128)(2,1)}, u32[]{:S(2)}, u32[]{:S(2)}) collective-permute-start(bf16[1376,256]{1,0:T(8,128)(2,1)S(1)} %collective-permute-done.4.refs_17_), channel_id=1, source_target_pairs={{0,2},{1,3},{2,0},{3,1},{4,6},{5,7},{6,4},{7,5},{8,10},{9,11},{10,... | collective-permute-start | bytes 2113544 | tf_op jit(solution)/shard_map/ppermute | solution.py:856
  86.3 13.8 %collective-permute-start.11 = (bf16[1376,256]{1,0:T(8,128)(2,1)S(1)}, bf16[1376,256]{1,0:T(8,128)(2,1)S(1)}, u32[]{:S(2)}, u32[]{:S(2)}) collective-permute-start(bf16[1376,256]{1,0:T(8,128)(2,1)S(1)} %collective-permute-done.9.refs_15_), channel_id=1, source_target_pairs={{0,4},{1,5},{2,6},{3,7},{4,0},{5,1},{6,2},{7,3},{8,12},{9,13},{10,... | collective-permute-start | bytes 2113544 | tf_op jit(solution)/shard_map/ppermute | solution.py:856
  94.3 20.7 %collective-permute-start.18 = (bf16[49,64,256]{2,1,0:T(8,128)(2,1)S(1)}, bf16[49,64,256]{2,1,0:T(8,128)(2,1)S(1)}, u32[]{:S(2)}, u32[]{:S(2)}) collective-permute-start(bf16[49,64,256]{2,1,0:T(8,128)(2,1)S(1)} %crops.6.refs_2_), channel_id=1, source_target_pairs={{0,1},{1,0},{2,3},{3,2},{4,5},{5,4},{6,7},{7,6},{8,9},{9,8},{10,11... | collective-permute-start | bytes 4816904 | tf_op jit(solution)/shard_map/ppermute | solution.py:856
  94.4 22.1 %collective-permute-start.17 = (bf16[49,64,256]{2,1,0:T(8,128)(2,1)S(1)}, bf16[49,64,256]{2,1,0:T(8,128)(2,1)S(1)}, u32[]{:S(2)}, u32[]{:S(2)}) collective-permute-start(bf16[49,64,256]{2,1,0:T(8,128)(2,1)S(1)} %crops.5.refs_1_), channel_id=1, source_target_pairs={{0,1},{1,0},{2,3},{3,2},{4,5},{5,4},{6,7},{7,6},{8,9},{9,8},{10,11... | collective-permute-start | bytes 4816904 | tf_op jit(solution)/shard_map/ppermute | solution.py:856
  94.9 23.5 %collective-permute-start.16 = (bf16[49,64,256]{2,1,0:T(8,128)(2,1)S(1)}, bf16[49,64,256]{2,1,0:T(8,128)(2,1)}, u32[]{:S(2)}, u32[]{:S(2)}) collective-permute-start(bf16[49,64,256]{2,1,0:T(8,128)(2,1)S(1)} %crops.4.refs_0_), channel_id=1, source_target_pairs={{0,1},{1,0},{2,3},{3,2},{4,5},{5,4},{6,7},{7,6},{8,9},{9,8},{10,11... | collective-permute-start | bytes 4816904 | tf_op jit(solution)/shard_map/ppermute | solution.py:856
  95.0 19.9 %collective-permute-start.12 = (bf16[2,2,384,256]{3,2,1,0:T(8,128)(2,1)S(1)}, bf16[2,2,384,256]{3,2,1,0:T(8,128)(2,1)S(1)}, u32[]{:S(2)}, u32[]{:S(2)}) collective-permute-start(bf16[2,2,384,256]{3,2,1,0:T(8,128)(2,1)S(1)} %pad_maximum_fusion.1.refs_10_.refs_13_.refs_0_), channel_id=1, source_target_pairs={{0,24},{1,25},{2,26},{3,27},{4,28},{5,29},{6,30},{7,31},{8,0},{9,1... | collective-permute-start | bytes 2359304 | tf_op jit(solution)/shard_map/ppermute | solution.py:856
  100.0 14.9 %collective-permute-start.21 = (bf16[1376,256]{1,0:T(8,128)(2,1)S(1)}, bf16[1376,256]{1,0:T(8,128)(2,1)S(1)}, u32[]{:S(2)}, u32[]{:S(2)}) collective-permute-start(bf16[1376,256]{1,0:T(8,128)(2,1)S(1)} %collective-permute-done.7.refs_25_), channel_id=1, source_target_pairs={{0,2},{1,3},{2,0},{3,1},{4,6},{5,7},{6,4},{7,5},{8,10},{9,11},{10,... | collective-permute-start | bytes 2113544 | tf_op jit(solution)/shard_map/ppermute | solution.py:856
  114.9 19.0 %collective-permute-start.15 = (bf16[2,2,384,256]{3,2,1,0:T(8,128)(2,1)}, bf16[2,2,384,256]{3,2,1,0:T(8,128)(2,1)}, u32[]{:S(2)}, u32[]{:S(2)}) collective-permute-start(bf16[2,2,384,256]{3,2,1,0:T(8,128)(2,1)} %collective-permute-done.8.refs_16_.refs_22_.refs_1_), channel_id=1, source_target_pairs={{0,1},{1,0},{2,3},{3,2},{4,5},{5,4},{6,7},{7,6},{8,9},{9,8},{10,11... | collective-permute-start | bytes 2359304 | tf_op jit(solution)/shard_map/ppermute | solution.py:856
  114.9 22.1 %collective-permute-start.13 = (bf16[2,2,384,256]{3,2,1,0:T(8,128)(2,1)}, bf16[2,2,384,256]{3,2,1,0:T(8,128)(2,1)}, u32[]{:S(2)}, u32[]{:S(2)}) collective-permute-start(bf16[2,2,384,256]{3,2,1,0:T(8,128)(2,1)} %collective-permute-done.8.refs_16_.refs_22_.refs_1_), channel_id=1, source_target_pairs={{0,8},{1,9},{2,10},{3,11},{4,12},{5,13},{6,14},{7,15},{8,16},{9,17... | collective-permute-start | bytes 2359304 | tf_op jit(solution)/shard_map/ppermute | solution.py:856
  115.0 22.0 %collective-permute-start.25 = (bf16[1376,256]{1,0:T(8,128)(2,1)}, bf16[1376,256]{1,0:T(8,128)(2,1)}, u32[]{:S(2)}, u32[]{:S(2)}) collective-permute-start(bf16[1376,256]{1,0:T(8,128)(2,1)} %collective-permute-done.20.refs_18_), channel_id=1, source_target_pairs={{0,4},{1,5},{2,6},{3,7},{4,0},{5,1},{6,2},{7,3},{8,12},{9,13},{10,... | collective-permute-start | bytes 2113544 | tf_op jit(solution)/shard_map/ppermute | solution.py:856
  116.5 20.5 %collective-permute-start.24 = (bf16[1376,256]{1,0:T(8,128)(2,1)}, bf16[1376,256]{1,0:T(8,128)(2,1)}, u32[]{:S(2)}, u32[]{:S(2)}) collective-permute-start(bf16[1376,256]{1,0:T(8,128)(2,1)} %collective-permute-done.10.refs_27_), channel_id=1, source_target_pairs={{0,2},{1,3},{2,0},{3,1},{4,6},{5,7},{6,4},{7,5},{8,10},{9,11},{10,... | collective-permute-start | bytes 2113544 | tf_op jit(solution)/shard_map/ppermute | solution.py:856
  134.0 12.3 %collective-permute-start.23 = (bf16[2,2,384,256]{3,2,1,0:T(8,128)(2,1)S(1)}, bf16[2,2,384,256]{3,2,1,0:T(8,128)(2,1)S(1)}, u32[]{:S(2)}, u32[]{:S(2)}) collective-permute-start(bf16[2,2,384,256]{3,2,1,0:T(8,128)(2,1)S(1)} %copy-done.22), channel_id=1, source_target_pairs={{0,1},{1,0},{2,3},{3,2},{4,5},{5,4},{6,7},{7,6},{8,9},{9,8},{10,11... | collective-permute-start | bytes 2359304 | tf_op jit(solution)/shard_map/ppermute | solution.py:856
  137.0 10.4 %collective-permute-start.22 = (bf16[2,2,384,256]{3,2,1,0:T(8,128)(2,1)}, bf16[2,2,384,256]{3,2,1,0:T(8,128)(2,1)S(1)}, u32[]{:S(2)}, u32[]{:S(2)}) collective-permute-start(bf16[2,2,384,256]{3,2,1,0:T(8,128)(2,1)} %collective-permute-done.13.refs_10_.refs_11_.refs_2_), channel_id=1, source_target_pairs={{0,1},{1,0},{2,3},{3,2},{4,5},{5,4},{6,7},{7,6},{8,9},{9,8},{10,11... | collective-permute-start | bytes 2359304 | tf_op jit(solution)/shard_map/ppermute | solution.py:856
  161.7 11.2 %collective-permute-start.28 = (bf16[512,1024]{1,0:T(8,128)(2,1)}, bf16[512,1024]{1,0:T(8,128)(2,1)S(1)}, u32[]{:S(2)}, u32[]{:S(2)}) collective-permute-start(bf16[512,1024]{1,0:T(8,128)(2,1)} %get-tuple-element.149), channel_id=1, source_target_pairs={{0,1},{1,0},{2,3},{3,2},{4,5},{5,4},{6,7},{7,6},{8,9},{9,8},{10,11... | collective-permute-start | bytes 3145736 | tf_op jit(solution)/shard_map/ppermute | solution.py:856
  162.0 10.8 %collective-permute-start.29 = (bf16[512,512]{1,0:T(8,128)(2,1)}, bf16[512,512]{1,0:T(8,128)(2,1)S(1)}, u32[]{:S(2)}, u32[]{:S(2)}) collective-permute-start(bf16[512,512]{1,0:T(8,128)(2,1)} %get-tuple-element.152), channel_id=1, source_target_pairs={{0,1},{1,0},{2,3},{3,2},{4,5},{5,4},{6,7},{7,6},{8,9},{9,8},{10,11... | collective-permute-start | bytes 1572872 | tf_op jit(solution)/shard_map/ppermute | solution.py:856
  178.7 18.2 %collective-permute-start.33 = (bf16[1360,256]{1,0:T(8,128)(2,1)}, bf16[1360,256]{1,0:T(8,128)(2,1)S(1)}, u32[]{:S(2)}, u32[]{:S(2)}) collective-permute-start(bf16[1360,256]{1,0:T(8,128)(2,1)} %get-tuple-element.173), channel_id=1, source_target_pairs={{0,2},{1,3},{2,0},{3,1},{4,6},{5,7},{6,4},{7,5},{8,10},{9,11},{10,... | collective-permute-start | bytes 2088968 | tf_op jit(solution)/shard_map/ppermute | solution.py:856
  179.3 18.1 %collective-permute-start.34 = (bf16[1360,256]{1,0:T(8,128)(2,1)}, bf16[1360,256]{1,0:T(8,128)(2,1)S(1)}, u32[]{:S(2)}, u32[]{:S(2)}) collective-permute-start(bf16[1360,256]{1,0:T(8,128)(2,1)} %get-tuple-element.175), channel_id=1, source_target_pairs={{0,4},{1,5},{2,6},{3,7},{4,0},{5,1},{6,2},{7,3},{8,12},{9,13},{10,... | collective-permute-start | bytes 2088968 | tf_op jit(solution)/shard_map/ppermute | solution.py:856
  180.7 22.9 %collective-permute-start.30 = (bf16[2,2,416,256]{3,2,1,0:T(8,128)(2,1)}, bf16[2,2,416,256]{3,2,1,0:T(8,128)(2,1)S(1)}, u32[]{:S(2)}, u32[]{:S(2)}) collective-permute-start(bf16[2,2,416,256]{3,2,1,0:T(8,128)(2,1)} %get-tuple-element.155), channel_id=1, source_target_pairs={{0,8},{1,9},{2,10},{3,11},{4,12},{5,13},{6,14},{7,15},{8,16},{9,17... | collective-permute-start | bytes 2555912 | tf_op jit(solution)/shard_map/ppermute | solution.py:856
  196.9 17.3 %collective-permute-start.40 = (bf16[1360,256]{1,0:T(8,128)(2,1)}, bf16[1360,256]{1,0:T(8,128)(2,1)S(1)}, u32[]{:S(2)}, u32[]{:S(2)}) collective-permute-start(bf16[1360,256]{1,0:T(8,128)(2,1)} %get-tuple-element.186), channel_id=1, source_target_pairs={{0,2},{1,3},{2,0},{3,1},{4,6},{5,7},{6,4},{7,5},{8,10},{9,11},{10,... | collective-permute-start | bytes 2088968 | tf_op jit(solution)/shard_map/ppermute | solution.py:856
  197.4 17.3 %collective-permute-start.35 = (bf16[1360,256]{1,0:T(8,128)(2,1)}, bf16[1360,256]{1,0:T(8,128)(2,1)S(1)}, u32[]{:S(2)}, u32[]{:S(2)}) collective-permute-start(bf16[1360,256]{1,0:T(8,128)(2,1)} %get-tuple-element.176), channel_id=1, source_target_pairs={{0,4},{1,5},{2,6},{3,7},{4,0},{5,1},{6,2},{7,3},{8,12},{9,13},{10,... | collective-permute-start | bytes 2088968 | tf_op jit(solution)/shard_map/ppermute | solution.py:856
  203.7 19.5 %collective-permute-start.31 = (bf16[2,2,416,256]{3,2,1,0:T(8,128)(2,1)S(1)}, bf16[2,2,416,256]{3,2,1,0:T(8,128)(2,1)S(1)}, u32[]{:S(2)}, u32[]{:S(2)}) collective-permute-start(bf16[2,2,416,256]{3,2,1,0:T(8,128)(2,1)S(1)} %copy-done.71), channel_id=1, source_target_pairs={{0,24},{1,25},{2,26},{3,27},{4,28},{5,29},{6,30},{7,31},{8,0},{9,1... | collective-permute-start | bytes 2555912 | tf_op jit(solution)/shard_map/ppermute | solution.py:856
  214.1 16.2 %collective-permute-start.41 = (bf16[1360,256]{1,0:T(8,128)(2,1)S(1)}, bf16[1360,256]{1,0:T(8,128)(2,1)S(1)}, u32[]{:S(2)}, u32[]{:S(2)}) collective-permute-start(bf16[1360,256]{1,0:T(8,128)(2,1)S(1)} %add_convert_fusion.6), channel_id=1, source_target_pairs={{0,2},{1,3},{2,0},{3,1},{4,6},{5,7},{6,4},{7,5},{8,10},{9,11},{10,... | collective-permute-start | bytes 2088968 | tf_op jit(solution)/shard_map/ppermute | solution.py:856
  214.7 16.2 %collective-permute-start.36 = (bf16[1360,256]{1,0:T(8,128)(2,1)S(1)}, bf16[1360,256]{1,0:T(8,128)(2,1)S(1)}, u32[]{:S(2)}, u32[]{:S(2)}) collective-permute-start(bf16[1360,256]{1,0:T(8,128)(2,1)S(1)} %add_convert_fusion.8), channel_id=1, source_target_pairs={{0,4},{1,5},{2,6},{3,7},{4,0},{5,1},{6,2},{7,3},{8,12},{9,13},{10,... | collective-permute-start | bytes 2088968 | tf_op jit(solution)/shard_map/ppermute | solution.py:856
  223.1 20.4 %collective-permute-start.32 = (bf16[2,2,416,256]{3,2,1,0:T(8,128)(2,1)S(1)}, bf16[2,2,416,256]{3,2,1,0:T(8,128)(2,1)S(1)}, u32[]{:S(2)}, u32[]{:S(2)}) collective-permute-start(bf16[2,2,416,256]{3,2,1,0:T(8,128)(2,1)S(1)} %add_convert_fusion.1), channel_id=1, source_target_pairs={{0,8},{1,9},{2,10},{3,11},{4,12},{5,13},{6,14},{7,15},{8,16},{9,17... | collective-permute-start | bytes 2555912 | tf_op jit(solution)/shard_map/ppermute | solution.py:856
  230.3 18.0 %collective-permute-start.42 = (bf16[1360,256]{1,0:T(8,128)(2,1)S(1)}, bf16[1360,256]{1,0:T(8,128)(2,1)S(1)}, u32[]{:S(2)}, u32[]{:S(2)}) collective-permute-start(bf16[1360,256]{1,0:T(8,128)(2,1)S(1)} %copy-done.74), channel_id=1, source_target_pairs={{0,2},{1,3},{2,0},{3,1},{4,6},{5,7},{6,4},{7,5},{8,10},{9,11},{10,... | collective-permute-start | bytes 2088968 | tf_op jit(solution)/shard_map/ppermute | solution.py:856
  230.8 15.8 %collective-permute-start.37 = (bf16[1360,256]{1,0:T(8,128)(2,1)S(1)}, bf16[1360,256]{1,0:T(8,128)(2,1)S(1)}, u32[]{:S(2)}, u32[]{:S(2)}) collective-permute-start(bf16[1360,256]{1,0:T(8,128)(2,1)S(1)} %copy-done.75), channel_id=1, source_target_pairs={{0,4},{1,5},{2,6},{3,7},{4,0},{5,1},{6,2},{7,3},{8,12},{9,13},{10,... | collective-permute-start | bytes 2088968 | tf_op jit(solution)/shard_map/ppermute | solution.py:856
  243.6 20.4 %collective-permute-start.48 = (bf16[1360,256]{1,0:T(8,128)(2,1)S(1)}, bf16[1360,256]{1,0:T(8,128)(2,1)S(1)}, u32[]{:S(2)}, u32[]{:S(2)}) collective-permute-start(bf16[1360,256]{1,0:T(8,128)(2,1)S(1)} %add_convert_fusion.3), channel_id=1, source_target_pairs={{0,8},{1,9},{2,10},{3,11},{4,12},{5,13},{6,14},{7,15},{8,16},{9,17... | collective-permute-start | bytes 2088968 | tf_op jit(solution)/shard_map/ppermute | solution.py:856
  246.6 15.8 %collective-permute-start.38 = (bf16[1360,256]{1,0:T(8,128)(2,1)S(1)}, bf16[1360,256]{1,0:T(8,128)(2,1)S(1)}, u32[]{:S(2)}, u32[]{:S(2)}) collective-permute-start(bf16[1360,256]{1,0:T(8,128)(2,1)S(1)} %copy-done.73), channel_id=1, source_target_pairs={{0,4},{1,5},{2,6},{3,7},{4,0},{5,1},{6,2},{7,3},{8,12},{9,13},{10,... | collective-permute-start | bytes 2088968 | tf_op jit(solution)/shard_map/ppermute | solution.py:856
  248.3 17.2 %collective-permute-start.43 = (bf16[1360,256]{1,0:T(8,128)(2,1)S(1)}, bf16[1360,256]{1,0:T(8,128)(2,1)S(1)}, u32[]{:S(2)}, u32[]{:S(2)}) collective-permute-start(bf16[1360,256]{1,0:T(8,128)(2,1)S(1)} %add_convert_fusion.7), channel_id=1, source_target_pairs={{0,2},{1,3},{2,0},{3,1},{4,6},{5,7},{6,4},{7,5},{8,10},{9,11},{10,... | collective-permute-start | bytes 2088968 | tf_op jit(solution)/shard_map/ppermute | solution.py:856
  262.4 8.3 %collective-permute-start.39 = (bf16[862,256]{1,0:T(8,128)(2,1)S(1)}, bf16[862,256]{1,0:T(8,128)(2,1)S(1)}, u32[]{:S(2)}, u32[]{:S(2)}) collective-permute-start(bf16[862,256]{1,0:T(8,128)(2,1)S(1)} %pad_maximum_fusion.2), channel_id=1, source_target_pairs={{0,4},{1,5},{2,6},{3,7},{4,0},{5,1},{6,2},{7,3},{8,12},{9,13},{10,... | collective-permute-start | bytes 1324040 | tf_op jit(solution)/shard_map/ppermute | solution.py:856
  264.0 17.8 %collective-permute-start.49 = (bf16[1360,256]{1,0:T(8,128)(2,1)S(1)}, bf16[1360,256]{1,0:T(8,128)(2,1)S(1)}, u32[]{:S(2)}, u32[]{:S(2)}) collective-permute-start(bf16[1360,256]{1,0:T(8,128)(2,1)S(1)} %add_convert_fusion.4), channel_id=1, source_target_pairs={{0,24},{1,25},{2,26},{3,27},{4,28},{5,29},{6,30},{7,31},{8,0},{9,1... | collective-permute-start | bytes 2088968 | tf_op jit(solution)/shard_map/ppermute | solution.py:856
  265.5 13.8 %collective-permute-start.44 = (bf16[1360,256]{1,0:T(8,128)(2,1)S(1)}, bf16[1360,256]{1,0:T(8,128)(2,1)S(1)}, u32[]{:S(2)}, u32[]{:S(2)}) collective-permute-start(bf16[1360,256]{1,0:T(8,128)(2,1)S(1)} %copy-done.72), channel_id=1, source_target_pairs={{0,2},{1,3},{2,0},{3,1},{4,6},{5,7},{6,4},{7,5},{8,10},{9,11},{10,... | collective-permute-start | bytes 2088968 | tf_op jit(solution)/shard_map/ppermute | solution.py:856
  279.2 6.0 %collective-permute-start.45 = (bf16[446,256]{1,0:T(8,128)(2,1)S(1)}, bf16[446,256]{1,0:T(8,128)(2,1)S(1)}, u32[]{:S(2)}, u32[]{:S(2)}) collective-permute-start(bf16[446,256]{1,0:T(8,128)(2,1)S(1)} %pad_maximum_fusion.3), channel_id=1, source_target_pairs={{0,2},{1,3},{2,0},{3,1},{4,6},{5,7},{6,4},{7,5},{8,10},{9,11},{10,... | collective-permute-start | bytes 685064 | tf_op jit(solution)/shard_map/ppermute | solution.py:856
  281.2 11.1 %collective-permute-start.47 = (bf16[1360,256]{1,0:T(8,128)(2,1)S(1)}, bf16[1360,256]{1,0:T(8,128)(2,1)S(1)}, u32[]{:S(2)}, u32[]{:S(2)}) collective-permute-start(bf16[1360,256]{1,0:T(8,128)(2,1)S(1)} %add_convert_fusion.5), channel_id=1, source_target_pairs={{0,4},{1,5},{2,6},{3,7},{4,0},{5,1},{6,2},{7,3},{8,12},{9,13},{10,... | collective-permute-start | bytes 2088968 | tf_op jit(solution)/shard_map/ppermute | solution.py:856
  281.8 12.8 %collective-permute-start.50 = (bf16[1360,256]{1,0:T(8,128)(2,1)S(1)}, bf16[1360,256]{1,0:T(8,128)(2,1)S(1)}, u32[]{:S(2)}, u32[]{:S(2)}) collective-permute-start(bf16[1360,256]{1,0:T(8,128)(2,1)S(1)} %add_convert_fusion.2), channel_id=1, source_target_pairs={{0,8},{1,9},{2,10},{3,11},{4,12},{5,13},{6,14},{7,15},{8,16},{9,17... | collective-permute-start | bytes 2088968 | tf_op jit(solution)/shard_map/ppermute | solution.py:856
  (80 other events, 886.5 us)

commit v5 on v4

--- a/solution.py
+++ b/solution.py
@@ -17,8 +17,8 @@
 HEAD = 401
 HEADP = 512
 CORES = 2
-CHUNKS = 4
-EARLY = 2
+CHUNKS = 8
+EARLY = 4
 GROUP = 32
 KSTEP = 7
 LATE_OUT = 192
@@ -75,7 +75,7 @@
             half[pl.ds(pl.multiple_of(i * POOL * 8, 8), POOL * 8), :] = got[:, h * 128 : (h + 1) * 128]
         return carry
 
-    lax.fori_loop(0, GROUP, one, 0, unroll=4)
+    lax.fori_loop(0, GROUP, one, 0, unroll=8)
     for a in range(POOL):
         for b in range(POOL):
             for h, half in enumerate(halves):
@@ -419,17 +419,28 @@
     return slice(begin - back, end - back), slice(lane, lane + 128)
 
 
-def prepare_kernel(first, second, heads, crowd, mine, low, wide_heads):
+def prepare_kernel(first, second, heads, crowd, mine, low, first_s, second_s, heads_s, crowd_s, wide_heads, low_s, in_sems, out_sems):
     feats = first.shape[0]
     share = second.shape[0]
     rows = heads.shape[0]
     half = mine.shape[0] - feats
-    value = first[...].astype(bf16)
-    mine[:feats, :] = value
-    low[...] = value[: low.shape[0], :]
-    kept = jnp.sum(1 - crowd[...], axis=1, keepdims=True)
+    most = low.shape[0]
+    cuts = [feats * k // 4 // 16 * 16 for k in range(4)] + [feats]
+    loads = [
+        pltpu.make_async_copy(first.at[pl.ds(a, b - a)], first_s.at[pl.ds(a, b - a)], in_sems.at[k])
+        for k, (a, b) in enumerate(zip(cuts, cuts[1:]))
+    ]
+    others = [
+        pltpu.make_async_copy(ref, to, in_sems.at[4 + k])
+        for k, (ref, to) in enumerate(((second, second_s), (heads, heads_s), (crowd, crowd_s)))
+    ]
+    for copy in others + loads:
+        copy.start()
+    for copy in others:
+        copy.wait()
+    kept = jnp.sum(1 - crowd_s[...], axis=1, keepdims=True)
     wide_heads[...] = jnp.zeros_like(wide_heads)
-    wide_heads[:, :HEAD] = heads[...]
+    wide_heads[:, :HEAD] = heads_s[...]
     lane = lax.broadcasted_iota(jnp.int32, (rows, 128), 1)
     row = lax.broadcasted_iota(jnp.int32, (rows, 128), 0)
     marks = jnp.where(lane == 127, kept % 128, jnp.where(lane == 126, kept // 128, 0))
@@ -437,26 +448,47 @@
     for begin, end in ((0, min(share, half)), (half, share)):
         if begin < end:
             at, lanes = small_place(half, begin, end)
-            mine[feats + at.start : feats + at.stop, lanes] = second[begin:end, :].astype(bf16)
+            low_s[feats + at.start : feats + at.stop, lanes] = second_s[begin:end, :].astype(bf16)
     for k in range(HEADP // 128):
         at, lanes = small_place(half, share + k * rows, share + (k + 1) * rows)
-        mine[feats + at.start : feats + at.stop, lanes] = wide_heads[:, k * 128 : (k + 1) * 128].astype(bf16)
+        low_s[feats + at.start : feats + at.stop, lanes] = wide_heads[:, k * 128 : (k + 1) * 128].astype(bf16)
+    stores = []
+    for k, (a, b) in enumerate(zip(cuts, cuts[1:])):
+        loads[k].wait()
+        low_s[a:b, :] = first_s[a:b, :].astype(bf16)
+        end = mine.shape[0] if b == feats else b
+        stores.append(pltpu.make_async_copy(low_s.at[pl.ds(a, end - a)], mine.at[pl.ds(a, end - a)], out_sems.at[k]))
+        stores[-1].start()
+    stores.append(pltpu.make_async_copy(low_s.at[pl.ds(0, most)], low, out_sems.at[4]))
+    stores[-1].start()
+    for copy in stores:
+        copy.wait()
 
 
 def prepare(first, second, heads, crowd, most):
     feats, cols = first.shape
     half = (second.shape[0] + heads.shape[0] * HEADP // 128) // 2
-    vmem = pl.BlockSpec(memory_space=pltpu.VMEM)
+    away = pl.BlockSpec(memory_space=pl.ANY)
+    crowd = crowd[None, :]
     return pl.pallas_call(
         prepare_kernel,
-        in_specs=[vmem] * 4,
-        out_specs=[vmem] * 2,
+        in_specs=[away] * 4,
+        out_specs=[away] * 2,
         out_shape=[jax.ShapeDtypeStruct((feats + half, cols), bf16), jax.ShapeDtypeStruct((most, cols), bf16)],
-        scratch_shapes=[pltpu.VMEM((heads.shape[0], HEADP), f32)],
+        scratch_shapes=[
+            pltpu.VMEM(first.shape, f32),
+            pltpu.VMEM(second.shape, f32),
+            pltpu.VMEM(heads.shape, f32),
+            pltpu.VMEM(crowd.shape, jnp.int32),
+            pltpu.VMEM((heads.shape[0], HEADP), f32),
+            pltpu.VMEM((feats + half, cols), bf16),
+            pltpu.SemaphoreType.DMA((7,)),
+            pltpu.SemaphoreType.DMA((5,)),
+        ],
         cost_estimate=LIGHT,
-        compiler_params=pltpu.CompilerParams(vmem_limit_bytes=16 * MIB),
+        compiler_params=pltpu.CompilerParams(vmem_limit_bytes=WIDE * MIB),
         name="prepare",
-    )(first, second, heads, crowd[None, :])
+    )(first, second, heads, crowd)
 
 
 def pack_kernel(table, *refs):
@@ -572,26 +604,35 @@
     return 128.0 * ends[:, 126:127] + ends[:, 127:128]
 
 
-def losses(out, label, valid, targets, kept):
-    col = lax.broadcasted_iota(jnp.int32, out.shape, 1)
+def losses(out, flags, kept):
+    rows, width = out.shape
+    label = flags[:, 0:1].astype(jnp.int32)
+    valid = 1.0 - flags[:, 1:2]
     fore = jnp.where(label > 0, valid, 0.0)
-    is_logit = col < CLS
-    onehot = jnp.where(col == label, 1.0, 0.0)
-    masked = jnp.where(is_logit, out, -jnp.inf)
+    scale = 1.0 / kept
+    lane = lax.broadcasted_iota(jnp.int32, flags.shape, 1)
+    onehot = jnp.where(lane == label, 1.0, 0.0)
+    logits = out[:, : flags.shape[1]]
+    masked = jnp.where(lane < CLS, logits, -jnp.inf)
     top = jnp.max(masked, axis=1, keepdims=True)
     shifted = jnp.exp(masked - top)
     total = jnp.sum(shifted, axis=1, keepdims=True)
-    row_loss = valid * (jnp.log(total) + top - jnp.sum(onehot * out, axis=1, keepdims=True))
-    scale = 1.0 / kept
-    grad = (shifted / total - onehot) * (valid * scale)
+    cross = jnp.log(total) + top - jnp.sum(onehot * logits, axis=1, keepdims=True)
+    col = lax.broadcasted_iota(jnp.int32, out.shape, 1)
     base = CLS + 4 * (label - 1)
-    for j in range(4):
-        mark = (col == base + j) & (col >= CLS)
-        err = jnp.sum(jnp.where(mark, out, 0.0), axis=1, keepdims=True) - targets[:, j : j + 1]
-        size = jnp.abs(err)
-        row_loss += fore * jnp.where(size < 1.0, 0.5 * err * err, size - 0.5)
-        grad += jnp.where(mark, jnp.clip(err, -1.0, 1.0) * (fore * scale), 0.0)
-    return row_loss, grad
+    row = jnp.where((col >= base) & (col < base + 4) & (col >= CLS), 1.0, 0.0)
+    at = lax.broadcasted_iota(jnp.int32, (width, flags.shape[1]), 0) - CLS
+    to = lax.broadcasted_iota(jnp.int32, (width, flags.shape[1]), 1) - 2
+    bring = jnp.where((at >= 0) & (at < HEAD - CLS) & ((at & 3) == to), 1.0, 0.0)
+    full = functools.partial(lax.dot_general, precision=lax.Precision.HIGHEST, preferred_element_type=f32)
+    boxes = full(out * row, bring, (((1,), (0,)), ((), ())))
+    error = jnp.where((lane >= 2) & (lane < 6), boxes - flags, 0.0)
+    size = jnp.abs(error)
+    smooth = jnp.sum(jnp.where(size < 1.0, 0.5 * error * error, size - 0.5 * jnp.where(size > 0.0, 1.0, 0.0)), axis=1, keepdims=True)
+    back = full(jnp.clip(error, -1.0, 1.0) * (fore * scale), bring, (((1,), (1,)), ((), ())))
+    grad = back * row
+    first = (shifted / total - onehot) * (valid * scale) + grad[:, : flags.shape[1]]
+    return valid * cross + fore * smooth, jnp.concatenate([first, grad[:, flags.shape[1] :]], axis=1)
 
 
 def head_blocks_kernel(share, depth, table, *refs):
@@ -599,7 +640,9 @@
     g_outs, gw2_outs, gwh_outs = refs[2 * depth + 6 : 2 * depth + 8], refs[2 * depth + 8 : 2 * depth + 10], refs[
         2 * depth + 10 : 2 * depth + 12
     ]
-    sums, kept_out, small, w2, wh, pre1, h1, pre2, gpre2, gwh, g, gw2, gwhs, bias, in_sems, out_sems = refs[2 * depth + 12 :]
+    sums, kept_out, small, pres, w2, wh, pre1, h1, pre2, gpre2, gwh, g, gw2, gwhs, bias, in_sems, out_sems = refs[
+        2 * depth + 12 :
+    ]
     rows, units = pre_own.shape
     blocks, xs, half, _ = small.shape[1:]
     count = depth * xs
@@ -608,10 +651,13 @@
         pltpu.make_async_copy(ref.at[:, :, pl.ds(ref.shape[2] - half, half)], small.at[n], in_sems.at[n])
         for n, ref in enumerate(stacks)
     ]
-    for copy in copies:
+    early = [pltpu.make_async_copy(ref, pres.at[n], in_sems.at[2 * depth + n]) for n, ref in enumerate((pre_own, pre_sib))]
+    for copy in early + copies:
         copy.start()
     core = table[2 * count + 1]
-    for side, pre in enumerate((pre_own, pre_sib)):
+    for copy in early:
+        copy.wait()
+    for side, pre in enumerate((pres.at[0], pres.at[1])):
         for k in range(blocks):
             unit = table[2 * count + 2 + side * blocks + k]
             lanes = slice(side * units + k * share, side * units + (k + 1) * share)
@@ -649,11 +695,11 @@
     h2 = gelu(pre2[...]).astype(bf16)
     out = dot(h2, wh[...]) + bias[...]
     flags = jnp.concatenate([labels[...], crowd[...]], axis=0).astype(f32)
-    flags = jnp.concatenate([flags, targets[...].astype(f32), jnp.zeros((2, rows), f32)], axis=0)
+    flags = jnp.concatenate([flags, targets[...].astype(f32), jnp.zeros((122, rows), f32)], axis=0)
     flags = jnp.transpose(flags)
     kept = kept_count(wh)
     kept_out[...] = kept
-    row_loss, grad = losses(out, flags[:, 0:1].astype(jnp.int32), 1.0 - flags[:, 1:2], flags[:, 2:6], kept)
+    row_loss, grad = losses(out, flags, kept)
     g_out = grad.astype(bf16)
     g_h2 = dot(g_out, wh[...], ((1,), (1,)))
     g2 = (g_h2 * gelu_slope(pre2[...])).astype(bf16)
@@ -703,7 +749,7 @@
     shape = jax.ShapeDtypeStruct
     return pl.pallas_call(
         functools.partial(head_blocks_kernel, share, depth),
-        in_specs=[smem] + [away] * (2 * depth) + [vmem] * 6,
+        in_specs=[smem] + [away] * (2 * depth + 2) + [vmem] * 4,
         out_specs=[away] * 6 + [vmem] * 2,
         out_shape=[shape((rows, units), bf16)] * 2
         + [shape((units, HID), bf16)] * 2
@@ -711,6 +757,7 @@
         + [shape((1, 2 * HID + HEADP), f32), shape((1, 1), f32)],
         scratch_shapes=[
             pltpu.VMEM((2 * depth, blocks, xs, half, cols), bf16),
+            pltpu.VMEM((CORES, rows, units), f32),
             pltpu.VMEM((CORES, units, HID), bf16),
             pltpu.VMEM((HID, HEADP), bf16),
             pltpu.VMEM((rows, HID), f32),
@@ -722,7 +769,7 @@
             pltpu.VMEM((CORES, units, HID), bf16),
             pltpu.VMEM((CORES, HID // CORES, HEADP), bf16),
             pltpu.VMEM((1, HEADP), f32),
-            pltpu.SemaphoreType.DMA((2 * depth,)),
+            pltpu.SemaphoreType.DMA((2 * depth + 2,)),
             pltpu.SemaphoreType.DMA((3 * CORES,)),
         ],
         compiler_params=pltpu.CompilerParams(vmem_limit_bytes=WIDE * MIB),
@@ -767,10 +814,9 @@
             pre2[...] += part.astype(bf16).astype(f32)
     h2 = gelu(pre2[...]).astype(bf16)
     out = dot(h2, wh[...]) + bh[...]
-    label = tags[:, 4:5].astype(jnp.int32)
     kept = kept_count(wh)
     count[...] = kept
-    row_loss, grad = losses(out, label, 1.0 - tags[:, 5:6], tags[:, :4], kept)
+    row_loss, grad = losses(out, tags[...], kept)
     g_out = grad.astype(bf16)
     head_sums = jnp.sum(g_out.astype(f32), axis=0, keepdims=True)
     lane = lax.broadcasted_iota(jnp.int32, head_sums.shape, 1)
@@ -1150,9 +1196,8 @@
 
 
 def stacked_step(grid, make_crops, w_first, w_second, w_heads, biases, labels, crowd, targets):
-    tags = jnp.concatenate(
-        [targets.astype(f32), labels[:, None].astype(f32), crowd[:, None].astype(f32)], axis=1
-    )
+    tags = jnp.concatenate([labels[:, None].astype(f32), crowd[:, None].astype(f32), targets.astype(f32)], axis=1)
+    tags = jnp.pad(tags, ((0, 0), (0, 122)))
     feats, cols = w_first.shape
     share, second_cols = w_second.shape
     head_rows = w_heads.shape[0]

time: 301 us -> 291 us (0.967)
  local copies, waits for them, and re-layouts: 21.6 us -> 14.6 us
  Pallas kernels: 91.8 us -> 88.2 us
    unnamed x153 -> x157, local copies, waits for them, and re-layouts: 15.8 us -> 9.08 us
    pallas_call x4 -> x8, Pallas kernels: 29.6 us -> 25 us  [window_crops(): pl.pallas_call(functools.partial(crop_kernel, first), grid_spec=pltpu.Pre...]
    ppermute x51 -> x55, starting transfers between devices: 36.5 us -> 36.8 us  [move(): return lax.ppermute(value, AXES, pairs)]
    ppermute x51 -> x55, waiting for transfers between devices: 140 us -> 140 us  [move(): return lax.ppermute(value, AXES, pairs)]
  transfers between devices with their start and end apart: 51 -> 55, of which waited for: 24 -> 29; matrix products, arithmetic and copies ran while one was open for 4% -> 4% of each run, Pallas kernels for 25% -> 24%
where the time goes in v5:
time: 291 us; the launch traced here: 290 us
  waiting for transfers between devices  140 us (48%)
  Pallas kernels  88.2 us (30%)
  starting transfers between devices  36.8 us (13%)
  local copies, waits for them, and re-layouts  14.6 us (5%)
  other arithmetic  8.5 us (3%)
    ppermute x55, waiting for transfers between devices, move(): return lax.ppermute(value, AXES, pairs)  140 us
    ppermute x55, starting transfers between devices, move(): return lax.ppermute(value, AXES, pairs)  36.8 us
    pallas_call x8, Pallas kernels, window_crops(): pl.pallas_call(functools.partial(crop_kernel, first), grid_spec=pltpu.Pre...  25 us
    pallas_call x2, Pallas kernels, first_blocks(): pl.pallas_call(functools.partial(block_kernel, items, feats, most, wide,...  23.8 us
    pallas_call x2, Pallas kernels, first_grad_blocks(): pl.pallas_call(functools.partial(block_grad_kernel, span, numbers, feats,...  21.5 us
    pallas_call x1, Pallas kernels, heads_blocks(): pl.pallas_call(functools.partial(head_blocks_kernel, share, depth), in_sp...  10.6 us
    unnamed x157, local copies, waits for them, and re-layouts  9.08 us
  transfers between devices with their start and end apart: 55, of which 29 were waited for; matrix products, arithmetic and copies ran while one was open for 4% of the time, Pallas kernels for 24%

profile of v5, /device:TPU:0, one launch (start us, length us, event | category | flops | bytes accessed | tf_op | source)
XLA Modules:
  0.0 289.7 jit_solution(1816498089090968416)
XLA Ops:
  0.7 2.6 prepare.1
  3.3 3.0 %collective-permute-start.1 = (bf16[1760,256]{1,0:T(8,128)(2,1)}, bf16[1760,256]{1,0:T(8,128)(2,1)}, u32[]{:S(2)}, u32[]{:S(2)}) collective-permute-start(bf16[1760,256]{1,0:T(8,128)(2,1)} %get-tuple-element.112.refs_16_), channel_id=1, source_target_pairs={{0,2},{1,3},{2,0},{3,1},{4,6},{5,7},{6,4},{7,5},{8,10},{9,11},{10,... | collective-permute-start | bytes 2703368 | tf_op jit(solution)/shard_map/ppermute | solution.py:902
  6.4 1.5 collective-permute-start
  7.9 1.6 collective-permute-start.2
  10.2 2.2 copy-done
  12.4 3.1 %crops.11.refs_3_ = bf16[49,32,256]{2,1,0:T(8,128)(2,1)S(1)} custom-call(s32[256]{0:T(256)S(1)} %multiply_add_fusion.4.base_ref, s32[256]{0:T(256)S(1)} %bitcast.109, bf16[256,32,256]{2,1,0:T(8,128)(2,1)S(1)} %bitcast.85, bf16[2048,16]{1,0:T(8,128)(2,1)S(1)} %bitcast.101, bf16[2048,16]{1,0:T(8,128)(2,1)S(1)} %bitcast.93, bf16[16,512]{1,0:T(8,128)(2,1)S(1)} %copy-done.10, ...), custom_call_target="tpu_custom_call" | custom-call | bytes 1024 | tf_op jit(solution)/shard_map/crops/pallas_call | solution.py:94
  15.5 3.1 %crops.10.refs_2_ = bf16[49,32,256]{2,1,0:T(8,128)(2,1)S(1)} custom-call(s32[256]{0:T(256)S(1)} %multiply_add_fusion.4.base_ref, s32[256]{0:T(256)S(1)} %bitcast.110, bf16[256,32,256]{2,1,0:T(8,128)(2,1)S(1)} %bitcast.86, bf16[2048,16]{1,0:T(8,128)(2,1)S(1)} %bitcast.102, bf16[2048,16]{1,0:T(8,128)(2,1)S(1)} %bitcast.94, bf16[16,512]{1,0:T(8,128)(2,1)S(1)} %copy-done.10, ...), custom_call_target="tpu_custom_call" | custom-call | bytes 1024 | tf_op jit(solution)/shard_map/crops/pallas_call | solution.py:94
  18.6 3.1 %crops.9.refs_1_ = bf16[49,32,256]{2,1,0:T(8,128)(2,1)S(1)} custom-call(s32[256]{0:T(256)S(1)} %multiply_add_fusion.4.base_ref, s32[256]{0:T(256)S(1)} %bitcast.111, bf16[256,32,256]{2,1,0:T(8,128)(2,1)S(1)} %bitcast.87, bf16[2048,16]{1,0:T(8,128)(2,1)S(1)} %bitcast.103, bf16[2048,16]{1,0:T(8,128)(2,1)S(1)} %bitcast.95, bf16[16,512]{1,0:T(8,128)(2,1)S(1)} %copy-done.10, ...), custom_call_target="tpu_custom_call" | custom-call | bytes 1024 | tf_op jit(solution)/shard_map/crops/pallas_call | solution.py:94
  21.8 3.1 %crops.8.refs_0_ = bf16[49,32,256]{2,1,0:T(8,128)(2,1)S(1)} custom-call(s32[256]{0:T(256)S(1)} %multiply_add_fusion.4.base_ref, s32[256]{0:T(256)S(1)} %bitcast.112, bf16[256,32,256]{2,1,0:T(8,128)(2,1)S(1)} %bitcast.88, bf16[2048,16]{1,0:T(8,128)(2,1)S(1)} %bitcast.104, bf16[2048,16]{1,0:T(8,128)(2,1)S(1)} %bitcast.96, bf16[16,512]{1,0:T(8,128)(2,1)S(1)} %copy-done.10, ...), custom_call_target="tpu_custom_call" | custom-call | bytes 1024 | tf_op jit(solution)/shard_map/crops/pallas_call | solution.py:94
  24.9 2.1 collective-permute-done.2.refs_22_
  28.1 3.6 %collective-permute-start.4 = (bf16[1376,256]{1,0:T(8,128)(2,1)S(1)}, bf16[1376,256]{1,0:T(8,128)(2,1)S(1)}, u32[]{:S(2)}, u32[]{:S(2)}) collective-permute-start(bf16[1376,256]{1,0:T(8,128)(2,1)S(1)} %copy-done.73), channel_id=1, source_target_pairs={{0,24},{1,25},{2,26},{3,27},{4,28},{5,29},{6,30},{7,31},{8,0},{9,1... | collective-permute-start | bytes 2113544 | tf_op jit(solution)/shard_map/ppermute | solution.py:902
  36.3 9.3 %collective-permute-done.4.refs_25_ = bf16[1376,256]{1,0:T(8,128)(2,1)S(1)} collective-permute-done((bf16[1376,256]{1,0:T(8,128)(2,1)S(1)}, bf16[1376,256]{1,0:T(8,128)(2,1)S(1)}, u32[]{:S(2)}, u32[]{:S(2)}) %collective-permute-start.4) | collective-permute-done | bytes 704544 | tf_op jit(solution)/shard_map/ppermute | solution.py:902
  45.6 2.4 collective-permute-done.5.refs_28_
  50.5 3.0 %collective-permute-done.3.refs_20_ = bf16[1760,256]{1,0:T(8,128)(2,1)S(1)} collective-permute-done((bf16[1760,256]{1,0:T(8,128)(2,1)}, bf16[1760,256]{1,0:T(8,128)(2,1)S(1)}, u32[]{:S(2)}, u32[]{:S(2)}) %collective-permute-start.3) | collective-permute-done | bytes 901152 | tf_op jit(solution)/shard_map/ppermute | solution.py:902
  54.5 8.6 %collective-permute-done.6.refs_31_ = bf16[1376,256]{1,0:T(8,128)(2,1)S(1)} collective-permute-done((bf16[1376,256]{1,0:T(8,128)(2,1)S(1)}, bf16[1376,256]{1,0:T(8,128)(2,1)S(1)}, u32[]{:S(2)}, u32[]{:S(2)}) %collective-permute-start.6) | collective-permute-done | bytes 704544 | tf_op jit(solution)/shard_map/ppermute | solution.py:902
  63.2 3.2 %collective-permute-done.7.refs_33_ = bf16[1376,256]{1,0:T(8,128)(2,1)S(1)} collective-permute-done((bf16[1376,256]{1,0:T(8,128)(2,1)}, bf16[1376,256]{1,0:T(8,128)(2,1)S(1)}, u32[]{:S(2)}, u32[]{:S(2)}) %collective-permute-start.7) | collective-permute-done | bytes 704544 | tf_op jit(solution)/shard_map/ppermute | solution.py:902
  67.0 1.5 collective-permute-done.9.refs_23_
  70.3 3.1 %crops.12.refs_4_ = bf16[49,32,256]{2,1,0:T(8,128)(2,1)S(1)} custom-call(s32[256]{0:T(256)S(1)} %multiply_add_fusion.4.base_ref, s32[256]{0:T(256)S(1)} %bitcast.113, bf16[256,32,256]{2,1,0:T(8,128)(2,1)S(1)} %bitcast.89, bf16[2048,16]{1,0:T(8,128)(2,1)S(1)} %bitcast.105, bf16[2048,16]{1,0:T(8,128)(2,1)S(1)} %bitcast.97, bf16[16,512]{1,0:T(8,128)(2,1)S(1)} %copy-done.10, ...), custom_call_target="tpu_custom_call" | custom-call | bytes 1024 | tf_op jit(solution)/shard_map/crops/pallas_call | solution.py:94
  73.4 7.0 %collective-permute-done.10.refs_35_ = bf16[1376,256]{1,0:T(8,128)(2,1)} collective-permute-done((bf16[1376,256]{1,0:T(8,128)(2,1)S(1)}, bf16[1376,256]{1,0:T(8,128)(2,1)}, u32[]{:S(2)}, u32[]{:S(2)}) %collective-permute-start.10) | collective-permute-done | bytes 704544 | tf_op jit(solution)/shard_map/ppermute | solution.py:902
  80.4 3.5 %collective-permute-done.8.refs_24_.refs_30_.refs_1_ = bf16[2,2,384,256]{3,2,1,0:T(8,128)(2,1)} collective-permute-done((bf16[2,2,384,256]{3,2,1,0:T(8,128)(2,1)S(1)}, bf16[2,2,384,256]{3,2,1,0:T(8,128)(2,1)}, u32[]{:S(2)}, u32[]{:S(2)}) %collective-permute-start.8) | collective-permute-done | bytes 786464 | tf_op jit(solution)/shard_map/ppermute | solution.py:902
  84.5 3.3 %collective-permute-done.24.refs_26_ = bf16[1376,256]{1,0:T(8,128)(2,1)} collective-permute-done((bf16[1376,256]{1,0:T(8,128)(2,1)S(1)}, bf16[1376,256]{1,0:T(8,128)(2,1)}, u32[]{:S(2)}, u32[]{:S(2)}) %collective-permute-start.24) | collective-permute-done | bytes 704544 | tf_op jit(solution)/shard_map/ppermute | solution.py:902
  89.0 3.1 %crops.14.refs_6_ = bf16[49,32,256]{2,1,0:T(8,128)(2,1)S(1)} custom-call(s32[256]{0:T(256)S(1)} %multiply_add_fusion.4.base_ref, s32[256]{0:T(256)S(1)} %bitcast.114, bf16[256,32,256]{2,1,0:T(8,128)(2,1)S(1)} %bitcast.90, bf16[2048,16]{1,0:T(8,128)(2,1)S(1)} %bitcast.106, bf16[2048,16]{1,0:T(8,128)(2,1)S(1)} %bitcast.98, bf16[16,512]{1,0:T(8,128)(2,1)S(1)} %copy-done.10, ...), custom_call_target="tpu_custom_call" | custom-call | bytes 1024 | tf_op jit(solution)/shard_map/crops/pallas_call | solution.py:94
  92.2 3.1 %crops.13.refs_5_ = bf16[49,32,256]{2,1,0:T(8,128)(2,1)S(1)} custom-call(s32[256]{0:T(256)S(1)} %multiply_add_fusion.4.base_ref, s32[256]{0:T(256)S(1)} %bitcast.115, bf16[256,32,256]{2,1,0:T(8,128)(2,1)S(1)} %bitcast.91, bf16[2048,16]{1,0:T(8,128)(2,1)S(1)} %bitcast.107, bf16[2048,16]{1,0:T(8,128)(2,1)S(1)} %bitcast.99, bf16[16,512]{1,0:T(8,128)(2,1)S(1)} %copy-done.10, ...), custom_call_target="tpu_custom_call" | custom-call | bytes 1024 | tf_op jit(solution)/shard_map/crops/pallas_call | solution.py:94
  96.1 3.1 %crops.15.refs_7_ = bf16[49,32,256]{2,1,0:T(8,128)(2,1)S(1)} custom-call(s32[256]{0:T(256)S(1)} %multiply_add_fusion.4.base_ref, s32[256]{0:T(256)S(1)} %bitcast.116, bf16[256,32,256]{2,1,0:T(8,128)(2,1)S(1)} %bitcast.92, bf16[2048,16]{1,0:T(8,128)(2,1)S(1)} %bitcast.108, bf16[2048,16]{1,0:T(8,128)(2,1)S(1)} %bitcast.100, bf16[16,512]{1,0:T(8,128)(2,1)S(1)} %copy-done.10, ...), custom_call_target="tpu_custom_call" | custom-call | bytes 1024 | tf_op jit(solution)/shard_map/crops/pallas_call | solution.py:94
  99.2 6.0 %collective-permute-done.11.refs_29_ = bf16[1376,256]{1,0:T(8,128)(2,1)S(1)} collective-permute-done((bf16[1376,256]{1,0:T(8,128)(2,1)S(1)}, bf16[1376,256]{1,0:T(8,128)(2,1)S(1)}, u32[]{:S(2)}, u32[]{:S(2)}) %collective-permute-start.11) | collective-permute-done | bytes 704544 | tf_op jit(solution)/shard_map/ppermute | solution.py:902
  109.5 15.4 %first_blocks.2 = (f32[256,512]{1,0:T(8,128)}, f32[256,512]{1,0:T(8,128)}) custom-call(s32[22]{0:T(128)} %stack.169.table, bf16[49,32,256]{2,1,0:T(8,128)(2,1)} %copy-done.4, bf16[49,32,256]{2,1,0:T(8,128)(2,1)} %copy-done.3, bf16[49,32,256]{2,1,0:T(8,128)(2,1)} %copy-done.2, bf16[49,32,256]{2,1,0:T(8,128)(2,1)} %copy-done.1, ...), custom_call_target="tpu_custom_call" | custom-call | bytes 1024 | tf_op jit(solution)/shard_map/first_blocks/pallas_call | solution.py:303
  125.1 2.3 collective-permute-done.13.refs_18_.refs_19_.refs_2_
  127.4 8.3 %first_blocks.3 = (f32[256,512]{1,0:T(8,128)}, f32[256,512]{1,0:T(8,128)}) custom-call(s32[22]{0:T(128)} %stack.169.table, bf16[49,32,256]{2,1,0:T(8,128)(2,1)} %copy-done.4, bf16[49,32,256]{2,1,0:T(8,128)(2,1)} %copy-done.3, bf16[49,32,256]{2,1,0:T(8,128)(2,1)} %copy-done.2, ...), custom_call_target="tpu_custom_call", output_to_operand_aliasing={{0}: (17, {}), {1}: (18, {})} | custom-call | bytes 1024 | tf_op jit(solution)/shard_map/first_blocks/pallas_call | solution.py:303
  139.0 10.6 %heads.3 = (bf16[256,512]{1,0:T(8,128)(2,1)}, bf16[256,512]{1,0:T(8,128)(2,1)}, bf16[512,1024]{1,0:T(8,128)(2,1)}, bf16[512,1024]{1,0:T(8,128)(2,1)}, bf16[512,5...) custom-call(s32[22]{0:T(128)} %stack.169.table, ...), custom_call_target="tpu_custom_call" | custom-call | bytes 1024 | tf_op jit(solution)/shard_map/heads/pallas_call | solution.py:750
  152.2 10.5 %first_grad.2 = (bf16[1360,256]{1,0:T(8,128)(2,1)}, bf16[208,256]{1,0:T(8,128)(2,1)}, bf16[1360,256]{1,0:T(8,128)(2,1)}, bf16[208,256]{1,0:T(8,128)(2,1)}, bf16[...) custom-call(s32[22]{0:T(128)} %stack.169.table, ...), custom_call_target="tpu_custom_call" | custom-call | bytes 1024 | tf_op jit(solution)/shard_map/first_grad/pallas_call | solution.py:395
  163.8 4.7 %pack.1 = (bf16[2,2,416,256]{3,2,1,0:T(8,128)(2,1)}, bf16[2,2,416,256]{3,2,1,0:T(8,128)(2,1)}, bf16[2,2,2,208,256]{4,3,2,1,0:T(8,128)(2,1)}) custom-call(s32[22]{0:T(128)} %stack.169.table, bf16[208,256]{1,0:T(8,128)(2,1)} %get-tuple-element.147.refs_0_, bf16[208,256]{1,0:T(8,128)(2,1)} %get-tuple-element.148.refs_1_, ...), custom_call_target="tpu_custom_call" | custom-call | bytes 1024 | tf_op jit(solution)/shard_map/pack/pallas_call | solution.py:573
  170.1 11.0 %first_grad.3 = (bf16[1360,256]{1,0:T(8,128)(2,1)}, bf16[208,256]{1,0:T(8,128)(2,1)}, bf16[1360,256]{1,0:T(8,128)(2,1)}, bf16[208,256]{1,0:T(8,128)(2,1)}, bf16[...) custom-call(s32[22]{0:T(128)} %stack.169.table, ...), custom_call_target="tpu_custom_call" | custom-call | bytes 1024 | tf_op jit(solution)/shard_map/first_grad/pallas_call | solution.py:395
  181.1 5.6 %collective-permute-done.37 = bf16[1360,256]{1,0:T(8,128)(2,1)S(1)} collective-permute-done((bf16[1360,256]{1,0:T(8,128)(2,1)}, bf16[1360,256]{1,0:T(8,128)(2,1)S(1)}, u32[]{:S(2)}, u32[]{:S(2)}) %collective-permute-start.37) | collective-permute-done | bytes 696352 | tf_op jit(solution)/shard_map/ppermute | solution.py:902
  188.0 4.3 %collective-permute-done.34 = bf16[2,2,416,256]{3,2,1,0:T(8,128)(2,1)S(1)} collective-permute-done((bf16[2,2,416,256]{3,2,1,0:T(8,128)(2,1)}, bf16[2,2,416,256]{3,2,1,0:T(8,128)(2,1)S(1)}, u32[]{:S(2)}, u32[]{:S(2)}) %collective-permute-start.34) | collective-permute-done | bytes 852000 | tf_op jit(solution)/shard_map/ppermute | solution.py:902
  193.5 10.5 %collective-permute-done.44 = bf16[1360,256]{1,0:T(8,128)(2,1)S(1)} collective-permute-done((bf16[1360,256]{1,0:T(8,128)(2,1)}, bf16[1360,256]{1,0:T(8,128)(2,1)S(1)}, u32[]{:S(2)}, u32[]{:S(2)}) %collective-permute-start.44) | collective-permute-done | bytes 696352 | tf_op jit(solution)/shard_map/ppermute | solution.py:902
  206.6 5.5 %collective-permute-done.35 = bf16[2,2,416,256]{3,2,1,0:T(8,128)(2,1)S(1)} collective-permute-done((bf16[2,2,416,256]{3,2,1,0:T(8,128)(2,1)S(1)}, bf16[2,2,416,256]{3,2,1,0:T(8,128)(2,1)S(1)}, u32[]{:S(2)}, u32[]{:S(2)}) %collective-permute-start.35) | collective-permute-done | bytes 852000 | tf_op jit(solution)/shard_map/ppermute | solution.py:902
  212.1 8.2 %collective-permute-done.40 = bf16[1360,256]{1,0:T(8,128)(2,1)S(1)} collective-permute-done((bf16[1360,256]{1,0:T(8,128)(2,1)S(1)}, bf16[1360,256]{1,0:T(8,128)(2,1)S(1)}, u32[]{:S(2)}, u32[]{:S(2)}) %collective-permute-start.40) | collective-permute-done | bytes 696352 | tf_op jit(solution)/shard_map/ppermute | solution.py:902
  222.6 10.1 %collective-permute-done.36 = bf16[2,2,416,256]{3,2,1,0:T(8,128)(2,1)S(1)} collective-permute-done((bf16[2,2,416,256]{3,2,1,0:T(8,128)(2,1)S(1)}, bf16[2,2,416,256]{3,2,1,0:T(8,128)(2,1)S(1)}, u32[]{:S(2)}, u32[]{:S(2)}) %collective-permute-start.36) | collective-permute-done | bytes 852000 | tf_op jit(solution)/shard_map/ppermute | solution.py:902
  233.2 2.8 collective-permute-done.41
  236.3 1.8 collective-permute-start.47
  238.2 13.7 %collective-permute-done.42 = bf16[1360,256]{1,0:T(8,128)(2,1)S(1)} collective-permute-done((bf16[1360,256]{1,0:T(8,128)(2,1)S(1)}, bf16[1360,256]{1,0:T(8,128)(2,1)S(1)}, u32[]{:S(2)}, u32[]{:S(2)}) %collective-permute-start.42) | collective-permute-done | bytes 696352 | tf_op jit(solution)/shard_map/ppermute | solution.py:902
  252.0 3.4 %collective-permute-start.53 = (bf16[1360,256]{1,0:T(8,128)(2,1)S(1)}, bf16[1360,256]{1,0:T(8,128)(2,1)S(1)}, u32[]{:S(2)}, u32[]{:S(2)}) collective-permute-start(bf16[1360,256]{1,0:T(8,128)(2,1)S(1)} %add_convert_fusion.4), channel_id=1, source_target_pairs={{0,24},{1,25},{2,26},{3,27},{4,28},{5,29},{6,30},{7,31},{8,0},{9,1... | collective-permute-start | bytes 2088968 | tf_op jit(solution)/shard_map/ppermute | solution.py:902
  256.2 3.9 %collective-permute-done.43 = bf16[862,256]{1,0:T(8,128)(2,1)S(1)} collective-permute-done((bf16[862,256]{1,0:T(8,128)(2,1)S(1)}, bf16[862,256]{1,0:T(8,128)(2,1)S(1)}, u32[]{:S(2)}, u32[]{:S(2)}) %collective-permute-start.43) | collective-permute-done | bytes 441376 | tf_op jit(solution)/shard_map/ppermute | solution.py:902
  260.4 8.9 %collective-permute-done.48 = bf16[1360,256]{1,0:T(8,128)(2,1)S(1)} collective-permute-done((bf16[1360,256]{1,0:T(8,128)(2,1)S(1)}, bf16[1360,256]{1,0:T(8,128)(2,1)S(1)}, u32[]{:S(2)}, u32[]{:S(2)}) %collective-permute-start.48) | collective-permute-done | bytes 696352 | tf_op jit(solution)/shard_map/ppermute | solution.py:902
  271.5 3.8 %collective-permute-done.49 = bf16[446,256]{1,0:T(8,128)(2,1)S(1)} collective-permute-done((bf16[446,256]{1,0:T(8,128)(2,1)S(1)}, bf16[446,256]{1,0:T(8,128)(2,1)S(1)}, u32[]{:S(2)}, u32[]{:S(2)}) %collective-permute-start.49) | collective-permute-done | bytes 228384 | tf_op jit(solution)/shard_map/ppermute | solution.py:902
  278.3 2.9 %collective-permute-done.51 = bf16[1360,256]{1,0:T(8,128)(2,1)S(1)} collective-permute-done((bf16[1360,256]{1,0:T(8,128)(2,1)S(1)}, bf16[1360,256]{1,0:T(8,128)(2,1)S(1)}, u32[]{:S(2)}, u32[]{:S(2)}) %collective-permute-start.51) | collective-permute-done | bytes 696352 | tf_op jit(solution)/shard_map/ppermute | solution.py:902
  281.2 3.1 %collective-permute-done.54 = bf16[1360,256]{1,0:T(8,128)(2,1)S(1)} collective-permute-done((bf16[1360,256]{1,0:T(8,128)(2,1)S(1)}, bf16[1360,256]{1,0:T(8,128)(2,1)S(1)}, u32[]{:S(2)}, u32[]{:S(2)}) %collective-permute-start.54) | collective-permute-done | bytes 696352 | tf_op jit(solution)/shard_map/ppermute | solution.py:902
  286.7 3.0 %multiply_subtract_fusion = (f32[1568,256]{1,0:T(8,128)}, f32[1568,256]{1,0:T(8,128)}, f32[1568,256]{1,0:T(8,128)}) fusion(f32[1568,256]{1,0:T(8,128)S(1)} %copy-done.22, f32[208,256]{1,0:T(8,128)S(1)} %slice.235, f32[1360,256]{1,0:T(8,128)S(1)} %convert_add_fusion, f32[1568,256]{1,0:T(8,128)S(1)} %copy-done.23, f32[1568,256]{1,0:T(8,128)S(1)} %copy-done.24), kind=kLoop, calls=%fused_computation.5 | loop fusion | flops 6422528 | bytes 11239424 | tf_op jit(solution)/shard_map/sub | solution.py:986
  (291 shorter events, 43.9 us)
Async XLA Ops:
  3.3 23.7 %collective-permute-start.1 = (bf16[1760,256]{1,0:T(8,128)(2,1)}, bf16[1760,256]{1,0:T(8,128)(2,1)}, u32[]{:S(2)}, u32[]{:S(2)}) collective-permute-start(bf16[1760,256]{1,0:T(8,128)(2,1)} %get-tuple-element.112.refs_16_), channel_id=1, source_target_pairs={{0,2},{1,3},{2,0},{3,1},{4,6},{5,7},{6,4},{7,5},{8,10},{9,11},{10,... | collective-permute-start | bytes 2703368 | tf_op jit(solution)/shard_map/ppermute | solution.py:902
  6.4 21.8 %collective-permute-start = (bf16[1760,256]{1,0:T(8,128)(2,1)}, bf16[1760,256]{1,0:T(8,128)(2,1)}, u32[]{:S(2)}, u32[]{:S(2)}) collective-permute-start(bf16[1760,256]{1,0:T(8,128)(2,1)} %get-tuple-element.112.refs_16_), channel_id=1, source_target_pairs={{0,4},{1,5},{2,6},{3,7},{4,0},{5,1},{6,2},{7,3},{8,12},{9,13},{10,... | collective-permute-start | bytes 2703368 | tf_op jit(solution)/shard_map/ppermute | solution.py:902
  7.9 19.1 %collective-permute-start.2 = (bf16[1376,256]{1,0:T(8,128)(2,1)}, bf16[1376,256]{1,0:T(8,128)(2,1)}, u32[]{:S(2)}, u32[]{:S(2)}) collective-permute-start(bf16[1376,256]{1,0:T(8,128)(2,1)} %get-tuple-element.115), channel_id=1, source_target_pairs={{0,8},{1,9},{2,10},{3,11},{4,12},{5,13},{6,14},{7,15},{8,16},{9,17... | collective-permute-start | bytes 2113544 | tf_op jit(solution)/shard_map/ppermute | solution.py:902
  28.1 17.5 %collective-permute-start.4 = (bf16[1376,256]{1,0:T(8,128)(2,1)S(1)}, bf16[1376,256]{1,0:T(8,128)(2,1)S(1)}, u32[]{:S(2)}, u32[]{:S(2)}) collective-permute-start(bf16[1376,256]{1,0:T(8,128)(2,1)S(1)} %copy-done.73), channel_id=1, source_target_pairs={{0,24},{1,25},{2,26},{3,27},{4,28},{5,29},{6,30},{7,31},{8,0},{9,1... | collective-permute-start | bytes 2113544 | tf_op jit(solution)/shard_map/ppermute | solution.py:902
  31.7 16.3 %collective-permute-start.5 = (bf16[1376,256]{1,0:T(8,128)(2,1)}, bf16[1376,256]{1,0:T(8,128)(2,1)S(1)}, u32[]{:S(2)}, u32[]{:S(2)}) collective-permute-start(bf16[1376,256]{1,0:T(8,128)(2,1)} %collective-permute-done.2.refs_22_), channel_id=1, source_target_pairs={{0,4},{1,5},{2,6},{3,7},{4,0},{5,1},{6,2},{7,3},{8,12},{9,13},{10,... | collective-permute-start | bytes 2113544 | tf_op jit(solution)/shard_map/ppermute | solution.py:902
  33.2 20.2 %collective-permute-start.3 = (bf16[1760,256]{1,0:T(8,128)(2,1)}, bf16[1760,256]{1,0:T(8,128)(2,1)S(1)}, u32[]{:S(2)}, u32[]{:S(2)}) collective-permute-start(bf16[1760,256]{1,0:T(8,128)(2,1)} %collective-permute-done.refs_19_), channel_id=1, source_target_pairs={{0,2},{1,3},{2,0},{3,1},{4,6},{5,7},{6,4},{7,5},{8,10},{9,11},{10,... | collective-permute-start | bytes 2703368 | tf_op jit(solution)/shard_map/ppermute | solution.py:902
  34.7 32.2 %collective-permute-start.16 = (bf16[49,32,256]{2,1,0:T(8,128)(2,1)S(1)}, bf16[49,32,256]{2,1,0:T(8,128)(2,1)S(1)}, u32[]{:S(2)}, u32[]{:S(2)}) collective-permute-start(bf16[49,32,256]{2,1,0:T(8,128)(2,1)S(1)} %crops.8.refs_0_), channel_id=1, source_target_pairs={{0,1},{1,0},{2,3},{3,2},{4,5},{5,4},{6,7},{7,6},{8,9},{9,8},{10,11... | collective-permute-start | bytes 2408456 | tf_op jit(solution)/shard_map/ppermute | solution.py:902
  34.8 33.8 %collective-permute-start.17 = (bf16[49,32,256]{2,1,0:T(8,128)(2,1)S(1)}, bf16[49,32,256]{2,1,0:T(8,128)(2,1)S(1)}, u32[]{:S(2)}, u32[]{:S(2)}) collective-permute-start(bf16[49,32,256]{2,1,0:T(8,128)(2,1)S(1)} %crops.9.refs_1_), channel_id=1, source_target_pairs={{0,1},{1,0},{2,3},{3,2},{4,5},{5,4},{6,7},{7,6},{8,9},{9,8},{10,11... | collective-permute-start | bytes 2408456 | tf_op jit(solution)/shard_map/ppermute | solution.py:902
  48.0 15.1 %collective-permute-start.6 = (bf16[1376,256]{1,0:T(8,128)(2,1)S(1)}, bf16[1376,256]{1,0:T(8,128)(2,1)S(1)}, u32[]{:S(2)}, u32[]{:S(2)}) collective-permute-start(bf16[1376,256]{1,0:T(8,128)(2,1)S(1)} %collective-permute-done.4.refs_25_), channel_id=1, source_target_pairs={{0,4},{1,5},{2,6},{3,7},{4,0},{5,1},{6,2},{7,3},{8,12},{9,13},{10,... | collective-permute-start | bytes 2113544 | tf_op jit(solution)/shard_map/ppermute | solution.py:902
  49.5 16.9 %collective-permute-start.7 = (bf16[1376,256]{1,0:T(8,128)(2,1)}, bf16[1376,256]{1,0:T(8,128)(2,1)S(1)}, u32[]{:S(2)}, u32[]{:S(2)}) collective-permute-start(bf16[1376,256]{1,0:T(8,128)(2,1)} %collective-permute-done.2.refs_22_), channel_id=1, source_target_pairs={{0,8},{1,9},{2,10},{3,11},{4,12},{5,13},{6,14},{7,15},{8,16},{9,17... | collective-permute-start | bytes 2113544 | tf_op jit(solution)/shard_map/ppermute | solution.py:902
  53.4 15.1 %collective-permute-start.9 = (bf16[1376,256]{1,0:T(8,128)(2,1)}, bf16[1376,256]{1,0:T(8,128)(2,1)S(1)}, u32[]{:S(2)}, u32[]{:S(2)}) collective-permute-start(bf16[1376,256]{1,0:T(8,128)(2,1)} %collective-permute-done.2.refs_22_), channel_id=1, source_target_pairs={{0,2},{1,3},{2,0},{3,1},{4,6},{5,7},{6,4},{7,5},{8,10},{9,11},{10,... | collective-permute-start | bytes 2113544 | tf_op jit(solution)/shard_map/ppermute | solution.py:902
  66.4 17.6 %collective-permute-start.8 = (bf16[2,2,384,256]{3,2,1,0:T(8,128)(2,1)S(1)}, bf16[2,2,384,256]{3,2,1,0:T(8,128)(2,1)}, u32[]{:S(2)}, u32[]{:S(2)}) collective-permute-start(bf16[2,2,384,256]{3,2,1,0:T(8,128)(2,1)S(1)} %pad_maximum_fusion.1.refs_18_.refs_21_.refs_0_), channel_id=1, source_target_pairs={{0,8},{1,9},{2,10},{3,11},{4,12},{5,13},{6,14},{7,15},{8,16},{9,17... | collective-permute-start | bytes 2359304 | tf_op jit(solution)/shard_map/ppermute | solution.py:902
  66.4 14.0 %collective-permute-start.10 = (bf16[1376,256]{1,0:T(8,128)(2,1)S(1)}, bf16[1376,256]{1,0:T(8,128)(2,1)}, u32[]{:S(2)}, u32[]{:S(2)}) collective-permute-start(bf16[1376,256]{1,0:T(8,128)(2,1)S(1)} %collective-permute-done.7.refs_33_), channel_id=1, source_target_pairs={{0,4},{1,5},{2,6},{3,7},{4,0},{5,1},{6,2},{7,3},{8,12},{9,13},{10,... | collective-permute-start | bytes 2113544 | tf_op jit(solution)/shard_map/ppermute | solution.py:902
  66.9 17.1 %collective-permute-start.18 = (bf16[49,32,256]{2,1,0:T(8,128)(2,1)S(1)}, bf16[49,32,256]{2,1,0:T(8,128)(2,1)S(1)}, u32[]{:S(2)}, u32[]{:S(2)}) collective-permute-start(bf16[49,32,256]{2,1,0:T(8,128)(2,1)S(1)} %crops.10.refs_2_), channel_id=1, source_target_pairs={{0,1},{1,0},{2,3},{3,2},{4,5},{5,4},{6,7},{7,6},{8,9},{9,8},{10,11... | collective-permute-start | bytes 2408456 | tf_op jit(solution)/shard_map/ppermute | solution.py:902
  68.5 19.8 %collective-permute-start.19 = (bf16[49,32,256]{2,1,0:T(8,128)(2,1)S(1)}, bf16[49,32,256]{2,1,0:T(8,128)(2,1)S(1)}, u32[]{:S(2)}, u32[]{:S(2)}) collective-permute-start(bf16[49,32,256]{2,1,0:T(8,128)(2,1)S(1)} %crops.11.refs_3_), channel_id=1, source_target_pairs={{0,1},{1,0},{2,3},{3,2},{4,5},{5,4},{6,7},{7,6},{8,9},{9,8},{10,11... | collective-permute-start | bytes 2408456 | tf_op jit(solution)/shard_map/ppermute | solution.py:902
  69.6 18.2 %collective-permute-start.24 = (bf16[1376,256]{1,0:T(8,128)(2,1)S(1)}, bf16[1376,256]{1,0:T(8,128)(2,1)}, u32[]{:S(2)}, u32[]{:S(2)}) collective-permute-start(bf16[1376,256]{1,0:T(8,128)(2,1)S(1)} %collective-permute-done.4.refs_25_), channel_id=1, source_target_pairs={{0,2},{1,3},{2,0},{3,1},{4,6},{5,7},{6,4},{7,5},{8,10},{9,11},{10,... | collective-permute-start | bytes 2113544 | tf_op jit(solution)/shard_map/ppermute | solution.py:902
  80.4 15.0 %collective-permute-start.20 = (bf16[49,32,256]{2,1,0:T(8,128)(2,1)S(1)}, bf16[49,32,256]{2,1,0:T(8,128)(2,1)S(1)}, u32[]{:S(2)}, u32[]{:S(2)}) collective-permute-start(bf16[49,32,256]{2,1,0:T(8,128)(2,1)S(1)} %crops.12.refs_4_), channel_id=1, source_target_pairs={{0,1},{1,0},{2,3},{3,2},{4,5},{5,4},{6,7},{7,6},{8,9},{9,8},{10,11... | collective-permute-start | bytes 2408456 | tf_op jit(solution)/shard_map/ppermute | solution.py:902
  84.0 11.5 %collective-permute-start.14 = (bf16[2,2,384,256]{3,2,1,0:T(8,128)(2,1)S(1)}, bf16[2,2,384,256]{3,2,1,0:T(8,128)(2,1)S(1)}, u32[]{:S(2)}, u32[]{:S(2)}) collective-permute-start(bf16[2,2,384,256]{3,2,1,0:T(8,128)(2,1)S(1)} %pad_maximum_fusion.1.refs_18_.refs_21_.refs_0_), channel_id=1, source_target_pairs={{0,1},{1,0},{2,3},{3,2},{4,5},{5,4},{6,7},{7,6},{8,9},{9,8},{10,11... | collective-permute-start | bytes 2359304 | tf_op jit(solution)/shard_map/ppermute | solution.py:902
  84.0 21.2 %collective-permute-start.12 = (bf16[2,2,384,256]{3,2,1,0:T(8,128)(2,1)S(1)}, bf16[2,2,384,256]{3,2,1,0:T(8,128)(2,1)S(1)}, u32[]{:S(2)}, u32[]{:S(2)}) collective-permute-start(bf16[2,2,384,256]{3,2,1,0:T(8,128)(2,1)S(1)} %pad_maximum_fusion.1.refs_18_.refs_21_.refs_0_), channel_id=1, source_target_pairs={{0,24},{1,25},{2,26},{3,27},{4,28},{5,29},{6,30},{7,31},{8,0},{9,1... | collective-permute-start | bytes 2359304 | tf_op jit(solution)/shard_map/ppermute | solution.py:902
  87.8 17.4 %collective-permute-start.11 = (bf16[1376,256]{1,0:T(8,128)(2,1)S(1)}, bf16[1376,256]{1,0:T(8,128)(2,1)S(1)}, u32[]{:S(2)}, u32[]{:S(2)}) collective-permute-start(bf16[1376,256]{1,0:T(8,128)(2,1)S(1)} %collective-permute-done.9.refs_23_), channel_id=1, source_target_pairs={{0,4},{1,5},{2,6},{3,7},{4,0},{5,1},{6,2},{7,3},{8,12},{9,13},{10,... | collective-permute-start | bytes 2113544 | tf_op jit(solution)/shard_map/ppermute | solution.py:902
  88.4 17.3 %collective-permute-start.25 = (bf16[1376,256]{1,0:T(8,128)(2,1)S(1)}, bf16[1376,256]{1,0:T(8,128)(2,1)S(1)}, u32[]{:S(2)}, u32[]{:S(2)}) collective-permute-start(bf16[1376,256]{1,0:T(8,128)(2,1)S(1)} %collective-permute-done.7.refs_33_), channel_id=1, source_target_pairs={{0,2},{1,3},{2,0},{3,1},{4,6},{5,7},{6,4},{7,5},{8,10},{9,11},{10,... | collective-permute-start | bytes 2113544 | tf_op jit(solution)/shard_map/ppermute | solution.py:902
  95.5 11.5 %collective-permute-start.22 = (bf16[49,32,256]{2,1,0:T(8,128)(2,1)S(1)}, bf16[49,32,256]{2,1,0:T(8,128)(2,1)S(1)}, u32[]{:S(2)}, u32[]{:S(2)}) collective-permute-start(bf16[49,32,256]{2,1,0:T(8,128)(2,1)S(1)} %crops.14.refs_6_), channel_id=1, source_target_pairs={{0,1},{1,0},{2,3},{3,2},{4,5},{5,4},{6,7},{7,6},{8,9},{9,8},{10,11... | collective-permute-start | bytes 2408456 | tf_op jit(solution)/shard_map/ppermute | solution.py:902
  105.2 19.8 %collective-permute-start.15 = (bf16[2,2,384,256]{3,2,1,0:T(8,128)(2,1)}, bf16[2,2,384,256]{3,2,1,0:T(8,128)(2,1)}, u32[]{:S(2)}, u32[]{:S(2)}) collective-permute-start(bf16[2,2,384,256]{3,2,1,0:T(8,128)(2,1)} %collective-permute-done.8.refs_24_.refs_30_.refs_1_), channel_id=1, source_target_pairs={{0,1},{1,0},{2,3},{3,2},{4,5},{5,4},{6,7},{7,6},{8,9},{9,8},{10,11... | collective-permute-start | bytes 2359304 | tf_op jit(solution)/shard_map/ppermute | solution.py:902
  105.7 21.6 %collective-permute-start.13 = (bf16[2,2,384,256]{3,2,1,0:T(8,128)(2,1)}, bf16[2,2,384,256]{3,2,1,0:T(8,128)(2,1)}, u32[]{:S(2)}, u32[]{:S(2)}) collective-permute-start(bf16[2,2,384,256]{3,2,1,0:T(8,128)(2,1)} %collective-permute-done.8.refs_24_.refs_30_.refs_1_), channel_id=1, source_target_pairs={{0,8},{1,9},{2,10},{3,11},{4,12},{5,13},{6,14},{7,15},{8,16},{9,17... | collective-permute-start | bytes 2359304 | tf_op jit(solution)/shard_map/ppermute | solution.py:902
  105.7 21.6 %collective-permute-start.29 = (bf16[1376,256]{1,0:T(8,128)(2,1)}, bf16[1376,256]{1,0:T(8,128)(2,1)}, u32[]{:S(2)}, u32[]{:S(2)}) collective-permute-start(bf16[1376,256]{1,0:T(8,128)(2,1)} %collective-permute-done.24.refs_26_), channel_id=1, source_target_pairs={{0,4},{1,5},{2,6},{3,7},{4,0},{5,1},{6,2},{7,3},{8,12},{9,13},{10,... | collective-permute-start | bytes 2113544 | tf_op jit(solution)/shard_map/ppermute | solution.py:902
  107.0 20.3 %collective-permute-start.28 = (bf16[1376,256]{1,0:T(8,128)(2,1)}, bf16[1376,256]{1,0:T(8,128)(2,1)}, u32[]{:S(2)}, u32[]{:S(2)}) collective-permute-start(bf16[1376,256]{1,0:T(8,128)(2,1)} %collective-permute-done.10.refs_35_), channel_id=1, source_target_pairs={{0,2},{1,3},{2,0},{3,1},{4,6},{5,7},{6,4},{7,5},{8,10},{9,11},{10,... | collective-permute-start | bytes 2113544 | tf_op jit(solution)/shard_map/ppermute | solution.py:902
  125.0 11.9 %collective-permute-start.27 = (bf16[2,2,384,256]{3,2,1,0:T(8,128)(2,1)S(1)}, bf16[2,2,384,256]{3,2,1,0:T(8,128)(2,1)S(1)}, u32[]{:S(2)}, u32[]{:S(2)}) collective-permute-start(bf16[2,2,384,256]{3,2,1,0:T(8,128)(2,1)S(1)} %copy-done.20), channel_id=1, source_target_pairs={{0,1},{1,0},{2,3},{3,2},{4,5},{5,4},{6,7},{7,6},{8,9},{9,8},{10,11... | collective-permute-start | bytes 2359304 | tf_op jit(solution)/shard_map/ppermute | solution.py:902
  127.3 10.7 %collective-permute-start.26 = (bf16[2,2,384,256]{3,2,1,0:T(8,128)(2,1)}, bf16[2,2,384,256]{3,2,1,0:T(8,128)(2,1)S(1)}, u32[]{:S(2)}, u32[]{:S(2)}) collective-permute-start(bf16[2,2,384,256]{3,2,1,0:T(8,128)(2,1)} %collective-permute-done.13.refs_18_.refs_19_.refs_2_), channel_id=1, source_target_pairs={{0,1},{1,0},{2,3},{3,2},{4,5},{5,4},{6,7},{7,6},{8,9},{9,8},{10,11... | collective-permute-start | bytes 2359304 | tf_op jit(solution)/shard_map/ppermute | solution.py:902
  151.5 11.2 %collective-permute-start.32 = (bf16[512,1024]{1,0:T(8,128)(2,1)}, bf16[512,1024]{1,0:T(8,128)(2,1)S(1)}, u32[]{:S(2)}, u32[]{:S(2)}) collective-permute-start(bf16[512,1024]{1,0:T(8,128)(2,1)} %get-tuple-element.157), channel_id=1, source_target_pairs={{0,1},{1,0},{2,3},{3,2},{4,5},{5,4},{6,7},{7,6},{8,9},{9,8},{10,11... | collective-permute-start | bytes 3145736 | tf_op jit(solution)/shard_map/ppermute | solution.py:902
  151.8 10.8 %collective-permute-start.33 = (bf16[512,512]{1,0:T(8,128)(2,1)}, bf16[512,512]{1,0:T(8,128)(2,1)S(1)}, u32[]{:S(2)}, u32[]{:S(2)}) collective-permute-start(bf16[512,512]{1,0:T(8,128)(2,1)} %get-tuple-element.160), channel_id=1, source_target_pairs={{0,1},{1,0},{2,3},{3,2},{4,5},{5,4},{6,7},{7,6},{8,9},{9,8},{10,11... | collective-permute-start | bytes 1572872 | tf_op jit(solution)/shard_map/ppermute | solution.py:902
  168.6 18.2 %collective-permute-start.37 = (bf16[1360,256]{1,0:T(8,128)(2,1)}, bf16[1360,256]{1,0:T(8,128)(2,1)S(1)}, u32[]{:S(2)}, u32[]{:S(2)}) collective-permute-start(bf16[1360,256]{1,0:T(8,128)(2,1)} %get-tuple-element.181), channel_id=1, source_target_pairs={{0,2},{1,3},{2,0},{3,1},{4,6},{5,7},{6,4},{7,5},{8,10},{9,11},{10,... | collective-permute-start | bytes 2088968 | tf_op jit(solution)/shard_map/ppermute | solution.py:902
  169.3 18.1 %collective-permute-start.38 = (bf16[1360,256]{1,0:T(8,128)(2,1)}, bf16[1360,256]{1,0:T(8,128)(2,1)S(1)}, u32[]{:S(2)}, u32[]{:S(2)}) collective-permute-start(bf16[1360,256]{1,0:T(8,128)(2,1)} %get-tuple-element.183), channel_id=1, source_target_pairs={{0,4},{1,5},{2,6},{3,7},{4,0},{5,1},{6,2},{7,3},{8,12},{9,13},{10,... | collective-permute-start | bytes 2088968 | tf_op jit(solution)/shard_map/ppermute | solution.py:902
  169.6 22.7 %collective-permute-start.34 = (bf16[2,2,416,256]{3,2,1,0:T(8,128)(2,1)}, bf16[2,2,416,256]{3,2,1,0:T(8,128)(2,1)S(1)}, u32[]{:S(2)}, u32[]{:S(2)}) collective-permute-start(bf16[2,2,416,256]{3,2,1,0:T(8,128)(2,1)} %get-tuple-element.163), channel_id=1, source_target_pairs={{0,8},{1,9},{2,10},{3,11},{4,12},{5,13},{6,14},{7,15},{8,16},{9,17... | collective-permute-start | bytes 2555912 | tf_op jit(solution)/shard_map/ppermute | solution.py:902
  186.7 17.3 %collective-permute-start.44 = (bf16[1360,256]{1,0:T(8,128)(2,1)}, bf16[1360,256]{1,0:T(8,128)(2,1)S(1)}, u32[]{:S(2)}, u32[]{:S(2)}) collective-permute-start(bf16[1360,256]{1,0:T(8,128)(2,1)} %get-tuple-element.194), channel_id=1, source_target_pairs={{0,2},{1,3},{2,0},{3,1},{4,6},{5,7},{6,4},{7,5},{8,10},{9,11},{10,... | collective-permute-start | bytes 2088968 | tf_op jit(solution)/shard_map/ppermute | solution.py:902
  187.4 17.0 %collective-permute-start.39 = (bf16[1360,256]{1,0:T(8,128)(2,1)}, bf16[1360,256]{1,0:T(8,128)(2,1)S(1)}, u32[]{:S(2)}, u32[]{:S(2)}) collective-permute-start(bf16[1360,256]{1,0:T(8,128)(2,1)} %get-tuple-element.184), channel_id=1, source_target_pairs={{0,4},{1,5},{2,6},{3,7},{4,0},{5,1},{6,2},{7,3},{8,12},{9,13},{10,... | collective-permute-start | bytes 2088968 | tf_op jit(solution)/shard_map/ppermute | solution.py:902
  192.3 19.8 %collective-permute-start.35 = (bf16[2,2,416,256]{3,2,1,0:T(8,128)(2,1)S(1)}, bf16[2,2,416,256]{3,2,1,0:T(8,128)(2,1)S(1)}, u32[]{:S(2)}, u32[]{:S(2)}) collective-permute-start(bf16[2,2,416,256]{3,2,1,0:T(8,128)(2,1)S(1)} %copy-done.72), channel_id=1, source_target_pairs={{0,24},{1,25},{2,26},{3,27},{4,28},{5,29},{6,30},{7,31},{8,0},{9,1... | collective-permute-start | bytes 2555912 | tf_op jit(solution)/shard_map/ppermute | solution.py:902
  204.4 15.9 %collective-permute-start.40 = (bf16[1360,256]{1,0:T(8,128)(2,1)S(1)}, bf16[1360,256]{1,0:T(8,128)(2,1)S(1)}, u32[]{:S(2)}, u32[]{:S(2)}) collective-permute-start(bf16[1360,256]{1,0:T(8,128)(2,1)S(1)} %add_convert_fusion.8), channel_id=1, source_target_pairs={{0,4},{1,5},{2,6},{3,7},{4,0},{5,1},{6,2},{7,3},{8,12},{9,13},{10,... | collective-permute-start | bytes 2088968 | tf_op jit(solution)/shard_map/ppermute | solution.py:902
  204.7 15.9 %collective-permute-start.45 = (bf16[1360,256]{1,0:T(8,128)(2,1)S(1)}, bf16[1360,256]{1,0:T(8,128)(2,1)S(1)}, u32[]{:S(2)}, u32[]{:S(2)}) collective-permute-start(bf16[1360,256]{1,0:T(8,128)(2,1)S(1)} %add_convert_fusion.6), channel_id=1, source_target_pairs={{0,2},{1,3},{2,0},{3,1},{4,6},{5,7},{6,4},{7,5},{8,10},{9,11},{10,... | collective-permute-start | bytes 2088968 | tf_op jit(solution)/shard_map/ppermute | solution.py:902
  212.1 20.6 %collective-permute-start.36 = (bf16[2,2,416,256]{3,2,1,0:T(8,128)(2,1)S(1)}, bf16[2,2,416,256]{3,2,1,0:T(8,128)(2,1)S(1)}, u32[]{:S(2)}, u32[]{:S(2)}) collective-permute-start(bf16[2,2,416,256]{3,2,1,0:T(8,128)(2,1)S(1)} %add_convert_fusion.1), channel_id=1, source_target_pairs={{0,8},{1,9},{2,10},{3,11},{4,12},{5,13},{6,14},{7,15},{8,16},{9,17... | collective-permute-start | bytes 2555912 | tf_op jit(solution)/shard_map/ppermute | solution.py:902
  220.3 15.8 %collective-permute-start.41 = (bf16[1360,256]{1,0:T(8,128)(2,1)S(1)}, bf16[1360,256]{1,0:T(8,128)(2,1)S(1)}, u32[]{:S(2)}, u32[]{:S(2)}) collective-permute-start(bf16[1360,256]{1,0:T(8,128)(2,1)S(1)} %copy-done.77), channel_id=1, source_target_pairs={{0,4},{1,5},{2,6},{3,7},{4,0},{5,1},{6,2},{7,3},{8,12},{9,13},{10,... | collective-permute-start | bytes 2088968 | tf_op jit(solution)/shard_map/ppermute | solution.py:902
  220.6 15.7 %collective-permute-start.46 = (bf16[1360,256]{1,0:T(8,128)(2,1)S(1)}, bf16[1360,256]{1,0:T(8,128)(2,1)S(1)}, u32[]{:S(2)}, u32[]{:S(2)}) collective-permute-start(bf16[1360,256]{1,0:T(8,128)(2,1)S(1)} %copy-done.76), channel_id=1, source_target_pairs={{0,2},{1,3},{2,0},{3,1},{4,6},{5,7},{6,4},{7,5},{8,10},{9,11},{10,... | collective-permute-start | bytes 2088968 | tf_op jit(solution)/shard_map/ppermute | solution.py:902
  232.7 19.3 %collective-permute-start.52 = (bf16[1360,256]{1,0:T(8,128)(2,1)S(1)}, bf16[1360,256]{1,0:T(8,128)(2,1)S(1)}, u32[]{:S(2)}, u32[]{:S(2)}) collective-permute-start(bf16[1360,256]{1,0:T(8,128)(2,1)S(1)} %add_convert_fusion.3), channel_id=1, source_target_pairs={{0,8},{1,9},{2,10},{3,11},{4,12},{5,13},{6,14},{7,15},{8,16},{9,17... | collective-permute-start | bytes 2088968 | tf_op jit(solution)/shard_map/ppermute | solution.py:902
  236.0 15.8 %collective-permute-start.42 = (bf16[1360,256]{1,0:T(8,128)(2,1)S(1)}, bf16[1360,256]{1,0:T(8,128)(2,1)S(1)}, u32[]{:S(2)}, u32[]{:S(2)}) collective-permute-start(bf16[1360,256]{1,0:T(8,128)(2,1)S(1)} %copy-done.75), channel_id=1, source_target_pairs={{0,4},{1,5},{2,6},{3,7},{4,0},{5,1},{6,2},{7,3},{8,12},{9,13},{10,... | collective-permute-start | bytes 2088968 | tf_op jit(solution)/shard_map/ppermute | solution.py:902
  236.3 19.1 %collective-permute-start.47 = (bf16[1360,256]{1,0:T(8,128)(2,1)S(1)}, bf16[1360,256]{1,0:T(8,128)(2,1)S(1)}, u32[]{:S(2)}, u32[]{:S(2)}) collective-permute-start(bf16[1360,256]{1,0:T(8,128)(2,1)S(1)} %add_convert_fusion.7), channel_id=1, source_target_pairs={{0,2},{1,3},{2,0},{3,1},{4,6},{5,7},{6,4},{7,5},{8,10},{9,11},{10,... | collective-permute-start | bytes 2088968 | tf_op jit(solution)/shard_map/ppermute | solution.py:902
  252.0 19.5 %collective-permute-start.53 = (bf16[1360,256]{1,0:T(8,128)(2,1)S(1)}, bf16[1360,256]{1,0:T(8,128)(2,1)S(1)}, u32[]{:S(2)}, u32[]{:S(2)}) collective-permute-start(bf16[1360,256]{1,0:T(8,128)(2,1)S(1)} %add_convert_fusion.4), channel_id=1, source_target_pairs={{0,24},{1,25},{2,26},{3,27},{4,28},{5,29},{6,30},{7,31},{8,0},{9,1... | collective-permute-start | bytes 2088968 | tf_op jit(solution)/shard_map/ppermute | solution.py:902
  255.5 13.8 %collective-permute-start.48 = (bf16[1360,256]{1,0:T(8,128)(2,1)S(1)}, bf16[1360,256]{1,0:T(8,128)(2,1)S(1)}, u32[]{:S(2)}, u32[]{:S(2)}) collective-permute-start(bf16[1360,256]{1,0:T(8,128)(2,1)S(1)} %copy-done.74), channel_id=1, source_target_pairs={{0,2},{1,3},{2,0},{3,1},{4,6},{5,7},{6,4},{7,5},{8,10},{9,11},{10,... | collective-permute-start | bytes 2088968 | tf_op jit(solution)/shard_map/ppermute | solution.py:902
  270.1 11.1 %collective-permute-start.51 = (bf16[1360,256]{1,0:T(8,128)(2,1)S(1)}, bf16[1360,256]{1,0:T(8,128)(2,1)S(1)}, u32[]{:S(2)}, u32[]{:S(2)}) collective-permute-start(bf16[1360,256]{1,0:T(8,128)(2,1)S(1)} %add_convert_fusion.5), channel_id=1, source_target_pairs={{0,4},{1,5},{2,6},{3,7},{4,0},{5,1},{6,2},{7,3},{8,12},{9,13},{10,... | collective-permute-start | bytes 2088968 | tf_op jit(solution)/shard_map/ppermute | solution.py:902
  271.5 12.8 %collective-permute-start.54 = (bf16[1360,256]{1,0:T(8,128)(2,1)S(1)}, bf16[1360,256]{1,0:T(8,128)(2,1)S(1)}, u32[]{:S(2)}, u32[]{:S(2)}) collective-permute-start(bf16[1360,256]{1,0:T(8,128)(2,1)S(1)} %add_convert_fusion.2), channel_id=1, source_target_pairs={{0,8},{1,9},{2,10},{3,11},{4,12},{5,13},{6,14},{7,15},{8,16},{9,17... | collective-permute-start | bytes 2088968 | tf_op jit(solution)/shard_map/ppermute | solution.py:902
  (86 other events, 913.8 us)

commit v6 on v5

--- a/solution.py
+++ b/solution.py
@@ -1055,7 +1055,7 @@
     m[1, 0, 0] = grid.move(first_low, "z", 1)
     own_crops = [make_crops(i) for i in range(CHUNKS)]
     made = own_crops[:EARLY] + [m[key] for key in ((0, 1, 0), (0, 0, 1), (1, 0, 0))]
-    m[3, 0, 0] = links.send(after(first_low, *made), "z", 3)
+    m[3, 0, 0] = links.send(after(first_low, m[1, 0, 0]), "z", 3)
     m[1, 1, 0] = links.send(after(m[1, 0, 0], *made), "x")
     m[0, 1, 1] = links.send(after(m[0, 1, 0], *made), "y")
     stacks[0] = jnp.stack([jnp.stack([m[0, x, y][most:] for x in range(grid.x)]) for y in range(grid.y)])

time: 291 us -> 288 us (0.990)
  waiting for transfers between devices: 140 us -> 133 us
  starting transfers between devices: 36.8 us -> 40.7 us
    ppermute x55, waiting for transfers between devices: 140 us -> 133 us  [move(): return lax.ppermute(value, AXES, pairs)]
    ppermute x55, starting transfers between devices: 36.8 us -> 40.7 us  [move(): return lax.ppermute(value, AXES, pairs)]
  transfers between devices with their start and end apart: 55 -> 55, of which waited for: 29 -> 28; matrix products, arithmetic and copies ran while one was open for 4% -> 4% of each run, Pallas kernels for 24% -> 24%
where the time goes in v6:
time: 288 us; the launch traced here: 287 us
  waiting for transfers between devices  133 us (46%)
  Pallas kernels  88.2 us (31%)
  starting transfers between devices  40.7 us (14%)
  local copies, waits for them, and re-layouts  14.6 us (5%)
  other arithmetic  8.5 us (3%)
    ppermute x55, waiting for transfers between devices, move(): return lax.ppermute(value, AXES, pairs)  133 us
    ppermute x55, starting transfers between devices, move(): return lax.ppermute(value, AXES, pairs)  40.7 us
    pallas_call x8, Pallas kernels, window_crops(): pl.pallas_call(functools.partial(crop_kernel, first), grid_spec=pltpu.Pre...  25 us
    pallas_call x2, Pallas kernels, first_blocks(): pl.pallas_call(functools.partial(block_kernel, items, feats, most, wide,...  23.8 us
    pallas_call x2, Pallas kernels, first_grad_blocks(): pl.pallas_call(functools.partial(block_grad_kernel, span, numbers, feats,...  21.5 us
    pallas_call x1, Pallas kernels, heads_blocks(): pl.pallas_call(functools.partial(head_blocks_kernel, share, depth), in_sp...  10.6 us
    unnamed x157, local copies, waits for them, and re-layouts  9.05 us
  transfers between devices with their start and end apart: 55, of which 28 were waited for; matrix products, arithmetic and copies ran while one was open for 4% of the time, Pallas kernels for 24%

profile of v6, /device:TPU:0, one launch (start us, length us, event | category | flops | bytes accessed | tf_op | source)
XLA Modules:
  0.0 286.8 jit_solution(17423069071162657605)
XLA Ops:
  0.7 2.6 prepare.1
  3.3 3.0 %collective-permute-start.1 = (bf16[1760,256]{1,0:T(8,128)(2,1)}, bf16[1760,256]{1,0:T(8,128)(2,1)}, u32[]{:S(2)}, u32[]{:S(2)}) collective-permute-start(bf16[1760,256]{1,0:T(8,128)(2,1)} %get-tuple-element.112.refs_16_), channel_id=1, source_target_pairs={{0,2},{1,3},{2,0},{3,1},{4,6},{5,7},{6,4},{7,5},{8,10},{9,11},{10,... | collective-permute-start | bytes 2703368 | tf_op jit(solution)/shard_map/ppermute | solution.py:902
  7.9 1.6 collective-permute-start.2
  10.2 2.2 copy-done
  12.4 3.1 %crops.11.refs_3_ = bf16[49,32,256]{2,1,0:T(8,128)(2,1)S(1)} custom-call(s32[256]{0:T(256)S(1)} %multiply_add_fusion.4.base_ref, s32[256]{0:T(256)S(1)} %bitcast.109, bf16[256,32,256]{2,1,0:T(8,128)(2,1)S(1)} %bitcast.85, bf16[2048,16]{1,0:T(8,128)(2,1)S(1)} %bitcast.101, bf16[2048,16]{1,0:T(8,128)(2,1)S(1)} %bitcast.93, bf16[16,512]{1,0:T(8,128)(2,1)S(1)} %copy-done.10, ...), custom_call_target="tpu_custom_call" | custom-call | bytes 1024 | tf_op jit(solution)/shard_map/crops/pallas_call | solution.py:94
  15.5 3.1 %crops.10.refs_2_ = bf16[49,32,256]{2,1,0:T(8,128)(2,1)S(1)} custom-call(s32[256]{0:T(256)S(1)} %multiply_add_fusion.4.base_ref, s32[256]{0:T(256)S(1)} %bitcast.110, bf16[256,32,256]{2,1,0:T(8,128)(2,1)S(1)} %bitcast.86, bf16[2048,16]{1,0:T(8,128)(2,1)S(1)} %bitcast.102, bf16[2048,16]{1,0:T(8,128)(2,1)S(1)} %bitcast.94, bf16[16,512]{1,0:T(8,128)(2,1)S(1)} %copy-done.10, ...), custom_call_target="tpu_custom_call" | custom-call | bytes 1024 | tf_op jit(solution)/shard_map/crops/pallas_call | solution.py:94
  18.6 3.1 %crops.9.refs_1_ = bf16[49,32,256]{2,1,0:T(8,128)(2,1)S(1)} custom-call(s32[256]{0:T(256)S(1)} %multiply_add_fusion.4.base_ref, s32[256]{0:T(256)S(1)} %bitcast.111, bf16[256,32,256]{2,1,0:T(8,128)(2,1)S(1)} %bitcast.87, bf16[2048,16]{1,0:T(8,128)(2,1)S(1)} %bitcast.103, bf16[2048,16]{1,0:T(8,128)(2,1)S(1)} %bitcast.95, bf16[16,512]{1,0:T(8,128)(2,1)S(1)} %copy-done.10, ...), custom_call_target="tpu_custom_call" | custom-call | bytes 1024 | tf_op jit(solution)/shard_map/crops/pallas_call | solution.py:94
  21.8 3.1 %crops.8.refs_0_ = bf16[49,32,256]{2,1,0:T(8,128)(2,1)S(1)} custom-call(s32[256]{0:T(256)S(1)} %multiply_add_fusion.4.base_ref, s32[256]{0:T(256)S(1)} %bitcast.112, bf16[256,32,256]{2,1,0:T(8,128)(2,1)S(1)} %bitcast.88, bf16[2048,16]{1,0:T(8,128)(2,1)S(1)} %bitcast.104, bf16[2048,16]{1,0:T(8,128)(2,1)S(1)} %bitcast.96, bf16[16,512]{1,0:T(8,128)(2,1)S(1)} %copy-done.10, ...), custom_call_target="tpu_custom_call" | custom-call | bytes 1024 | tf_op jit(solution)/shard_map/crops/pallas_call | solution.py:94
  24.9 2.1 collective-permute-done.2.refs_22_
  27.0 1.7 collective-permute-start.4
  32.7 10.5 %collective-permute-done.4.refs_25_ = bf16[1376,256]{1,0:T(8,128)(2,1)S(1)} collective-permute-done((bf16[1376,256]{1,0:T(8,128)(2,1)S(1)}, bf16[1376,256]{1,0:T(8,128)(2,1)S(1)}, u32[]{:S(2)}, u32[]{:S(2)}) %collective-permute-start.4) | collective-permute-done | bytes 704544 | tf_op jit(solution)/shard_map/ppermute | solution.py:902
  43.1 1.6 collective-permute-done.5.refs_28_
  46.2 1.6 collective-permute-start.7
  51.2 8.7 %collective-permute-done.6.refs_31_ = bf16[1376,256]{1,0:T(8,128)(2,1)S(1)} collective-permute-done((bf16[1376,256]{1,0:T(8,128)(2,1)S(1)}, bf16[1376,256]{1,0:T(8,128)(2,1)S(1)}, u32[]{:S(2)}, u32[]{:S(2)}) %collective-permute-start.6) | collective-permute-done | bytes 704544 | tf_op jit(solution)/shard_map/ppermute | solution.py:902
  59.9 3.5 %collective-permute-done.7.refs_33_ = bf16[1376,256]{1,0:T(8,128)(2,1)S(1)} collective-permute-done((bf16[1376,256]{1,0:T(8,128)(2,1)}, bf16[1376,256]{1,0:T(8,128)(2,1)S(1)}, u32[]{:S(2)}, u32[]{:S(2)}) %collective-permute-start.7) | collective-permute-done | bytes 704544 | tf_op jit(solution)/shard_map/ppermute | solution.py:902
  67.2 3.1 %crops.12.refs_4_ = bf16[49,32,256]{2,1,0:T(8,128)(2,1)S(1)} custom-call(s32[256]{0:T(256)S(1)} %multiply_add_fusion.4.base_ref, s32[256]{0:T(256)S(1)} %bitcast.113, bf16[256,32,256]{2,1,0:T(8,128)(2,1)S(1)} %bitcast.89, bf16[2048,16]{1,0:T(8,128)(2,1)S(1)} %bitcast.105, bf16[2048,16]{1,0:T(8,128)(2,1)S(1)} %bitcast.97, bf16[16,512]{1,0:T(8,128)(2,1)S(1)} %copy-done.10, ...), custom_call_target="tpu_custom_call" | custom-call | bytes 1024 | tf_op jit(solution)/shard_map/crops/pallas_call | solution.py:94
  70.4 7.4 %collective-permute-done.10.refs_35_ = bf16[1376,256]{1,0:T(8,128)(2,1)} collective-permute-done((bf16[1376,256]{1,0:T(8,128)(2,1)S(1)}, bf16[1376,256]{1,0:T(8,128)(2,1)}, u32[]{:S(2)}, u32[]{:S(2)}) %collective-permute-start.10) | collective-permute-done | bytes 704544 | tf_op jit(solution)/shard_map/ppermute | solution.py:902
  77.8 3.5 %collective-permute-done.8.refs_24_.refs_30_.refs_1_ = bf16[2,2,384,256]{3,2,1,0:T(8,128)(2,1)} collective-permute-done((bf16[2,2,384,256]{3,2,1,0:T(8,128)(2,1)S(1)}, bf16[2,2,384,256]{3,2,1,0:T(8,128)(2,1)}, u32[]{:S(2)}, u32[]{:S(2)}) %collective-permute-start.8) | collective-permute-done | bytes 786464 | tf_op jit(solution)/shard_map/ppermute | solution.py:902
  82.2 2.6 collective-permute-done.24.refs_26_
  85.7 3.1 %crops.14.refs_6_ = bf16[49,32,256]{2,1,0:T(8,128)(2,1)S(1)} custom-call(s32[256]{0:T(256)S(1)} %multiply_add_fusion.4.base_ref, s32[256]{0:T(256)S(1)} %bitcast.114, bf16[256,32,256]{2,1,0:T(8,128)(2,1)S(1)} %bitcast.90, bf16[2048,16]{1,0:T(8,128)(2,1)S(1)} %bitcast.106, bf16[2048,16]{1,0:T(8,128)(2,1)S(1)} %bitcast.98, bf16[16,512]{1,0:T(8,128)(2,1)S(1)} %copy-done.10, ...), custom_call_target="tpu_custom_call" | custom-call | bytes 1024 | tf_op jit(solution)/shard_map/crops/pallas_call | solution.py:94
  88.9 3.1 %crops.13.refs_5_ = bf16[49,32,256]{2,1,0:T(8,128)(2,1)S(1)} custom-call(s32[256]{0:T(256)S(1)} %multiply_add_fusion.4.base_ref, s32[256]{0:T(256)S(1)} %bitcast.115, bf16[256,32,256]{2,1,0:T(8,128)(2,1)S(1)} %bitcast.91, bf16[2048,16]{1,0:T(8,128)(2,1)S(1)} %bitcast.107, bf16[2048,16]{1,0:T(8,128)(2,1)S(1)} %bitcast.99, bf16[16,512]{1,0:T(8,128)(2,1)S(1)} %copy-done.10, ...), custom_call_target="tpu_custom_call" | custom-call | bytes 1024 | tf_op jit(solution)/shard_map/crops/pallas_call | solution.py:94
  92.7 3.1 %crops.15.refs_7_ = bf16[49,32,256]{2,1,0:T(8,128)(2,1)S(1)} custom-call(s32[256]{0:T(256)S(1)} %multiply_add_fusion.4.base_ref, s32[256]{0:T(256)S(1)} %bitcast.116, bf16[256,32,256]{2,1,0:T(8,128)(2,1)S(1)} %bitcast.92, bf16[2048,16]{1,0:T(8,128)(2,1)S(1)} %bitcast.108, bf16[2048,16]{1,0:T(8,128)(2,1)S(1)} %bitcast.100, bf16[16,512]{1,0:T(8,128)(2,1)S(1)} %copy-done.10, ...), custom_call_target="tpu_custom_call" | custom-call | bytes 1024 | tf_op jit(solution)/shard_map/crops/pallas_call | solution.py:94
  95.9 6.2 %collective-permute-done.11.refs_29_ = bf16[1376,256]{1,0:T(8,128)(2,1)S(1)} collective-permute-done((bf16[1376,256]{1,0:T(8,128)(2,1)S(1)}, bf16[1376,256]{1,0:T(8,128)(2,1)S(1)}, u32[]{:S(2)}, u32[]{:S(2)}) %collective-permute-start.11) | collective-permute-done | bytes 704544 | tf_op jit(solution)/shard_map/ppermute | solution.py:902
  102.6 1.6 collective-permute-start.13
  108.0 15.4 %first_blocks.2 = (f32[256,512]{1,0:T(8,128)}, f32[256,512]{1,0:T(8,128)}) custom-call(s32[22]{0:T(128)} %stack.169.table, bf16[49,32,256]{2,1,0:T(8,128)(2,1)} %copy-done.4, bf16[49,32,256]{2,1,0:T(8,128)(2,1)} %copy-done.3, bf16[49,32,256]{2,1,0:T(8,128)(2,1)} %copy-done.2, bf16[49,32,256]{2,1,0:T(8,128)(2,1)} %copy-done.1, ...), custom_call_target="tpu_custom_call" | custom-call | bytes 1024 | tf_op jit(solution)/shard_map/first_blocks/pallas_call | solution.py:303
  124.4 8.3 %first_blocks.3 = (f32[256,512]{1,0:T(8,128)}, f32[256,512]{1,0:T(8,128)}) custom-call(s32[22]{0:T(128)} %stack.169.table, bf16[49,32,256]{2,1,0:T(8,128)(2,1)} %copy-done.4, bf16[49,32,256]{2,1,0:T(8,128)(2,1)} %copy-done.3, bf16[49,32,256]{2,1,0:T(8,128)(2,1)} %copy-done.2, ...), custom_call_target="tpu_custom_call", output_to_operand_aliasing={{0}: (17, {}), {1}: (18, {})} | custom-call | bytes 1024 | tf_op jit(solution)/shard_map/first_blocks/pallas_call | solution.py:303
  136.0 10.6 %heads.3 = (bf16[256,512]{1,0:T(8,128)(2,1)}, bf16[256,512]{1,0:T(8,128)(2,1)}, bf16[512,1024]{1,0:T(8,128)(2,1)}, bf16[512,1024]{1,0:T(8,128)(2,1)}, bf16[512,5...) custom-call(s32[22]{0:T(128)} %stack.169.table, ...), custom_call_target="tpu_custom_call" | custom-call | bytes 1024 | tf_op jit(solution)/shard_map/heads/pallas_call | solution.py:750
  149.2 10.5 %first_grad.2 = (bf16[1360,256]{1,0:T(8,128)(2,1)}, bf16[208,256]{1,0:T(8,128)(2,1)}, bf16[1360,256]{1,0:T(8,128)(2,1)}, bf16[208,256]{1,0:T(8,128)(2,1)}, bf16[...) custom-call(s32[22]{0:T(128)} %stack.169.table, ...), custom_call_target="tpu_custom_call" | custom-call | bytes 1024 | tf_op jit(solution)/shard_map/first_grad/pallas_call | solution.py:395
  160.8 4.7 %pack.1 = (bf16[2,2,416,256]{3,2,1,0:T(8,128)(2,1)}, bf16[2,2,416,256]{3,2,1,0:T(8,128)(2,1)}, bf16[2,2,2,208,256]{4,3,2,1,0:T(8,128)(2,1)}) custom-call(s32[22]{0:T(128)} %stack.169.table, bf16[208,256]{1,0:T(8,128)(2,1)} %get-tuple-element.147.refs_0_, bf16[208,256]{1,0:T(8,128)(2,1)} %get-tuple-element.148.refs_1_, ...), custom_call_target="tpu_custom_call" | custom-call | bytes 1024 | tf_op jit(solution)/shard_map/pack/pallas_call | solution.py:573
  167.3 1.7 collective-permute-start.34
  169.1 11.0 %first_grad.3 = (bf16[1360,256]{1,0:T(8,128)(2,1)}, bf16[208,256]{1,0:T(8,128)(2,1)}, bf16[1360,256]{1,0:T(8,128)(2,1)}, bf16[208,256]{1,0:T(8,128)(2,1)}, bf16[...) custom-call(s32[22]{0:T(128)} %stack.169.table, ...), custom_call_target="tpu_custom_call" | custom-call | bytes 1024 | tf_op jit(solution)/shard_map/first_grad/pallas_call | solution.py:395
  180.1 3.6 %collective-permute-done.37 = bf16[1360,256]{1,0:T(8,128)(2,1)S(1)} collective-permute-done((bf16[1360,256]{1,0:T(8,128)(2,1)}, bf16[1360,256]{1,0:T(8,128)(2,1)S(1)}, u32[]{:S(2)}, u32[]{:S(2)}) %collective-permute-start.37) | collective-permute-done | bytes 696352 | tf_op jit(solution)/shard_map/ppermute | solution.py:902
  185.5 4.3 %collective-permute-done.34 = bf16[2,2,416,256]{3,2,1,0:T(8,128)(2,1)S(1)} collective-permute-done((bf16[2,2,416,256]{3,2,1,0:T(8,128)(2,1)}, bf16[2,2,416,256]{3,2,1,0:T(8,128)(2,1)S(1)}, u32[]{:S(2)}, u32[]{:S(2)}) %collective-permute-start.34) | collective-permute-done | bytes 852000 | tf_op jit(solution)/shard_map/ppermute | solution.py:902
  190.5 10.5 %collective-permute-done.44 = bf16[1360,256]{1,0:T(8,128)(2,1)S(1)} collective-permute-done((bf16[1360,256]{1,0:T(8,128)(2,1)}, bf16[1360,256]{1,0:T(8,128)(2,1)S(1)}, u32[]{:S(2)}, u32[]{:S(2)}) %collective-permute-start.44) | collective-permute-done | bytes 696352 | tf_op jit(solution)/shard_map/ppermute | solution.py:902
  203.5 5.8 %collective-permute-done.35 = bf16[2,2,416,256]{3,2,1,0:T(8,128)(2,1)S(1)} collective-permute-done((bf16[2,2,416,256]{3,2,1,0:T(8,128)(2,1)S(1)}, bf16[2,2,416,256]{3,2,1,0:T(8,128)(2,1)S(1)}, u32[]{:S(2)}, u32[]{:S(2)}) %collective-permute-start.35) | collective-permute-done | bytes 852000 | tf_op jit(solution)/shard_map/ppermute | solution.py:902
  209.3 7.8 %collective-permute-done.40 = bf16[1360,256]{1,0:T(8,128)(2,1)S(1)} collective-permute-done((bf16[1360,256]{1,0:T(8,128)(2,1)S(1)}, bf16[1360,256]{1,0:T(8,128)(2,1)S(1)}, u32[]{:S(2)}, u32[]{:S(2)}) %collective-permute-start.40) | collective-permute-done | bytes 696352 | tf_op jit(solution)/shard_map/ppermute | solution.py:902
  219.5 10.2 %collective-permute-done.36 = bf16[2,2,416,256]{3,2,1,0:T(8,128)(2,1)S(1)} collective-permute-done((bf16[2,2,416,256]{3,2,1,0:T(8,128)(2,1)S(1)}, bf16[2,2,416,256]{3,2,1,0:T(8,128)(2,1)S(1)}, u32[]{:S(2)}, u32[]{:S(2)}) %collective-permute-start.36) | collective-permute-done | bytes 852000 | tf_op jit(solution)/shard_map/ppermute | solution.py:902
  230.2 2.7 collective-permute-done.41
  234.8 13.9 %collective-permute-done.42 = bf16[1360,256]{1,0:T(8,128)(2,1)S(1)} collective-permute-done((bf16[1360,256]{1,0:T(8,128)(2,1)S(1)}, bf16[1360,256]{1,0:T(8,128)(2,1)S(1)}, u32[]{:S(2)}, u32[]{:S(2)}) %collective-permute-start.42) | collective-permute-done | bytes 696352 | tf_op jit(solution)/shard_map/ppermute | solution.py:902
  249.2 2.8 collective-permute-start.53
  252.0 1.8 collective-permute-start.48
  253.8 3.2 %collective-permute-done.43 = bf16[862,256]{1,0:T(8,128)(2,1)S(1)} collective-permute-done((bf16[862,256]{1,0:T(8,128)(2,1)S(1)}, bf16[862,256]{1,0:T(8,128)(2,1)S(1)}, u32[]{:S(2)}, u32[]{:S(2)}) %collective-permute-start.43) | collective-permute-done | bytes 441376 | tf_op jit(solution)/shard_map/ppermute | solution.py:902
  257.3 8.6 %collective-permute-done.48 = bf16[1360,256]{1,0:T(8,128)(2,1)S(1)} collective-permute-done((bf16[1360,256]{1,0:T(8,128)(2,1)S(1)}, bf16[1360,256]{1,0:T(8,128)(2,1)S(1)}, u32[]{:S(2)}, u32[]{:S(2)}) %collective-permute-start.48) | collective-permute-done | bytes 696352 | tf_op jit(solution)/shard_map/ppermute | solution.py:902
  265.8 1.7 collective-permute-start.49
  268.6 3.2 %collective-permute-done.49 = bf16[446,256]{1,0:T(8,128)(2,1)S(1)} collective-permute-done((bf16[446,256]{1,0:T(8,128)(2,1)S(1)}, bf16[446,256]{1,0:T(8,128)(2,1)S(1)}, u32[]{:S(2)}, u32[]{:S(2)}) %collective-permute-start.49) | collective-permute-done | bytes 228384 | tf_op jit(solution)/shard_map/ppermute | solution.py:902
  274.9 4.2 %collective-permute-done.51 = bf16[1360,256]{1,0:T(8,128)(2,1)S(1)} collective-permute-done((bf16[1360,256]{1,0:T(8,128)(2,1)S(1)}, bf16[1360,256]{1,0:T(8,128)(2,1)S(1)}, u32[]{:S(2)}, u32[]{:S(2)}) %collective-permute-start.51) | collective-permute-done | bytes 696352 | tf_op jit(solution)/shard_map/ppermute | solution.py:902
  279.1 2.3 collective-permute-done.54
  283.8 3.0 %multiply_subtract_fusion = (f32[1568,256]{1,0:T(8,128)}, f32[1568,256]{1,0:T(8,128)}, f32[1568,256]{1,0:T(8,128)}) fusion(f32[1568,256]{1,0:T(8,128)S(1)} %copy-done.22, f32[208,256]{1,0:T(8,128)S(1)} %slice.235, f32[1360,256]{1,0:T(8,128)S(1)} %convert_add_fusion, f32[1568,256]{1,0:T(8,128)S(1)} %copy-done.23, f32[1568,256]{1,0:T(8,128)S(1)} %copy-done.24), kind=kLoop, calls=%fused_computation.5 | loop fusion | flops 6422528 | bytes 11239424 | tf_op jit(solution)/shard_map/sub | solution.py:986
  (291 shorter events, 47.5 us)
Async XLA Ops:
  3.3 25.4 %collective-permute-start.1 = (bf16[1760,256]{1,0:T(8,128)(2,1)}, bf16[1760,256]{1,0:T(8,128)(2,1)}, u32[]{:S(2)}, u32[]{:S(2)}) collective-permute-start(bf16[1760,256]{1,0:T(8,128)(2,1)} %get-tuple-element.112.refs_16_), channel_id=1, source_target_pairs={{0,2},{1,3},{2,0},{3,1},{4,6},{5,7},{6,4},{7,5},{8,10},{9,11},{10,... | collective-permute-start | bytes 2703368 | tf_op jit(solution)/shard_map/ppermute | solution.py:902
  6.4 22.4 %collective-permute-start = (bf16[1760,256]{1,0:T(8,128)(2,1)}, bf16[1760,256]{1,0:T(8,128)(2,1)}, u32[]{:S(2)}, u32[]{:S(2)}) collective-permute-start(bf16[1760,256]{1,0:T(8,128)(2,1)} %get-tuple-element.112.refs_16_), channel_id=1, source_target_pairs={{0,4},{1,5},{2,6},{3,7},{4,0},{5,1},{6,2},{7,3},{8,12},{9,13},{10,... | collective-permute-start | bytes 2703368 | tf_op jit(solution)/shard_map/ppermute | solution.py:902
  7.9 19.1 %collective-permute-start.2 = (bf16[1376,256]{1,0:T(8,128)(2,1)}, bf16[1376,256]{1,0:T(8,128)(2,1)}, u32[]{:S(2)}, u32[]{:S(2)}) collective-permute-start(bf16[1376,256]{1,0:T(8,128)(2,1)} %get-tuple-element.115), channel_id=1, source_target_pairs={{0,8},{1,9},{2,10},{3,11},{4,12},{5,13},{6,14},{7,15},{8,16},{9,17... | collective-permute-start | bytes 2113544 | tf_op jit(solution)/shard_map/ppermute | solution.py:902
  27.0 16.1 %collective-permute-start.4 = (bf16[1376,256]{1,0:T(8,128)(2,1)S(1)}, bf16[1376,256]{1,0:T(8,128)(2,1)S(1)}, u32[]{:S(2)}, u32[]{:S(2)}) collective-permute-start(bf16[1376,256]{1,0:T(8,128)(2,1)S(1)} %copy-done.73), channel_id=1, source_target_pairs={{0,24},{1,25},{2,26},{3,27},{4,28},{5,29},{6,30},{7,31},{8,0},{9,1... | collective-permute-start | bytes 2113544 | tf_op jit(solution)/shard_map/ppermute | solution.py:902
  28.8 16.0 %collective-permute-start.5 = (bf16[1376,256]{1,0:T(8,128)(2,1)}, bf16[1376,256]{1,0:T(8,128)(2,1)S(1)}, u32[]{:S(2)}, u32[]{:S(2)}) collective-permute-start(bf16[1376,256]{1,0:T(8,128)(2,1)} %collective-permute-done.2.refs_22_), channel_id=1, source_target_pairs={{0,4},{1,5},{2,6},{3,7},{4,0},{5,1},{6,2},{7,3},{8,12},{9,13},{10,... | collective-permute-start | bytes 2113544 | tf_op jit(solution)/shard_map/ppermute | solution.py:902
  29.6 20.5 %collective-permute-start.3 = (bf16[1760,256]{1,0:T(8,128)(2,1)}, bf16[1760,256]{1,0:T(8,128)(2,1)S(1)}, u32[]{:S(2)}, u32[]{:S(2)}) collective-permute-start(bf16[1760,256]{1,0:T(8,128)(2,1)} %collective-permute-done.refs_19_), channel_id=1, source_target_pairs={{0,2},{1,3},{2,0},{3,1},{4,6},{5,7},{6,4},{7,5},{8,10},{9,11},{10,... | collective-permute-start | bytes 2703368 | tf_op jit(solution)/shard_map/ppermute | solution.py:902
  31.1 32.8 %collective-permute-start.16 = (bf16[49,32,256]{2,1,0:T(8,128)(2,1)S(1)}, bf16[49,32,256]{2,1,0:T(8,128)(2,1)S(1)}, u32[]{:S(2)}, u32[]{:S(2)}) collective-permute-start(bf16[49,32,256]{2,1,0:T(8,128)(2,1)S(1)} %crops.8.refs_0_), channel_id=1, source_target_pairs={{0,1},{1,0},{2,3},{3,2},{4,5},{5,4},{6,7},{7,6},{8,9},{9,8},{10,11... | collective-permute-start | bytes 2408456 | tf_op jit(solution)/shard_map/ppermute | solution.py:902
  31.2 34.3 %collective-permute-start.17 = (bf16[49,32,256]{2,1,0:T(8,128)(2,1)S(1)}, bf16[49,32,256]{2,1,0:T(8,128)(2,1)S(1)}, u32[]{:S(2)}, u32[]{:S(2)}) collective-permute-start(bf16[49,32,256]{2,1,0:T(8,128)(2,1)S(1)} %crops.9.refs_1_), channel_id=1, source_target_pairs={{0,1},{1,0},{2,3},{3,2},{4,5},{5,4},{6,7},{7,6},{8,9},{9,8},{10,11... | collective-permute-start | bytes 2408456 | tf_op jit(solution)/shard_map/ppermute | solution.py:902
  44.7 15.1 %collective-permute-start.6 = (bf16[1376,256]{1,0:T(8,128)(2,1)S(1)}, bf16[1376,256]{1,0:T(8,128)(2,1)S(1)}, u32[]{:S(2)}, u32[]{:S(2)}) collective-permute-start(bf16[1376,256]{1,0:T(8,128)(2,1)S(1)} %collective-permute-done.4.refs_25_), channel_id=1, source_target_pairs={{0,4},{1,5},{2,6},{3,7},{4,0},{5,1},{6,2},{7,3},{8,12},{9,13},{10,... | collective-permute-start | bytes 2113544 | tf_op jit(solution)/shard_map/ppermute | solution.py:902
  46.2 17.2 %collective-permute-start.7 = (bf16[1376,256]{1,0:T(8,128)(2,1)}, bf16[1376,256]{1,0:T(8,128)(2,1)S(1)}, u32[]{:S(2)}, u32[]{:S(2)}) collective-permute-start(bf16[1376,256]{1,0:T(8,128)(2,1)} %collective-permute-done.2.refs_22_), channel_id=1, source_target_pairs={{0,8},{1,9},{2,10},{3,11},{4,12},{5,13},{6,14},{7,15},{8,16},{9,17... | collective-permute-start | bytes 2113544 | tf_op jit(solution)/shard_map/ppermute | solution.py:902
  50.1 15.3 %collective-permute-start.9 = (bf16[1376,256]{1,0:T(8,128)(2,1)}, bf16[1376,256]{1,0:T(8,128)(2,1)S(1)}, u32[]{:S(2)}, u32[]{:S(2)}) collective-permute-start(bf16[1376,256]{1,0:T(8,128)(2,1)} %collective-permute-done.2.refs_22_), channel_id=1, source_target_pairs={{0,2},{1,3},{2,0},{3,1},{4,6},{5,7},{6,4},{7,5},{8,10},{9,11},{10,... | collective-permute-start | bytes 2113544 | tf_op jit(solution)/shard_map/ppermute | solution.py:902
  63.4 17.9 %collective-permute-start.8 = (bf16[2,2,384,256]{3,2,1,0:T(8,128)(2,1)S(1)}, bf16[2,2,384,256]{3,2,1,0:T(8,128)(2,1)}, u32[]{:S(2)}, u32[]{:S(2)}) collective-permute-start(bf16[2,2,384,256]{3,2,1,0:T(8,128)(2,1)S(1)} %pad_maximum_fusion.1.refs_18_.refs_21_.refs_0_), channel_id=1, source_target_pairs={{0,8},{1,9},{2,10},{3,11},{4,12},{5,13},{6,14},{7,15},{8,16},{9,17... | collective-permute-start | bytes 2359304 | tf_op jit(solution)/shard_map/ppermute | solution.py:902
  63.4 14.4 %collective-permute-start.10 = (bf16[1376,256]{1,0:T(8,128)(2,1)S(1)}, bf16[1376,256]{1,0:T(8,128)(2,1)}, u32[]{:S(2)}, u32[]{:S(2)}) collective-permute-start(bf16[1376,256]{1,0:T(8,128)(2,1)S(1)} %collective-permute-done.7.refs_33_), channel_id=1, source_target_pairs={{0,4},{1,5},{2,6},{3,7},{4,0},{5,1},{6,2},{7,3},{8,12},{9,13},{10,... | collective-permute-start | bytes 2113544 | tf_op jit(solution)/shard_map/ppermute | solution.py:902
  63.9 17.4 %collective-permute-start.18 = (bf16[49,32,256]{2,1,0:T(8,128)(2,1)S(1)}, bf16[49,32,256]{2,1,0:T(8,128)(2,1)S(1)}, u32[]{:S(2)}, u32[]{:S(2)}) collective-permute-start(bf16[49,32,256]{2,1,0:T(8,128)(2,1)S(1)} %crops.10.refs_2_), channel_id=1, source_target_pairs={{0,1},{1,0},{2,3},{3,2},{4,5},{5,4},{6,7},{7,6},{8,9},{9,8},{10,11... | collective-permute-start | bytes 2408456 | tf_op jit(solution)/shard_map/ppermute | solution.py:902
  65.5 19.6 %collective-permute-start.19 = (bf16[49,32,256]{2,1,0:T(8,128)(2,1)S(1)}, bf16[49,32,256]{2,1,0:T(8,128)(2,1)S(1)}, u32[]{:S(2)}, u32[]{:S(2)}) collective-permute-start(bf16[49,32,256]{2,1,0:T(8,128)(2,1)S(1)} %crops.11.refs_3_), channel_id=1, source_target_pairs={{0,1},{1,0},{2,3},{3,2},{4,5},{5,4},{6,7},{7,6},{8,9},{9,8},{10,11... | collective-permute-start | bytes 2408456 | tf_op jit(solution)/shard_map/ppermute | solution.py:902
  66.5 18.2 %collective-permute-start.24 = (bf16[1376,256]{1,0:T(8,128)(2,1)S(1)}, bf16[1376,256]{1,0:T(8,128)(2,1)}, u32[]{:S(2)}, u32[]{:S(2)}) collective-permute-start(bf16[1376,256]{1,0:T(8,128)(2,1)S(1)} %collective-permute-done.4.refs_25_), channel_id=1, source_target_pairs={{0,2},{1,3},{2,0},{3,1},{4,6},{5,7},{6,4},{7,5},{8,10},{9,11},{10,... | collective-permute-start | bytes 2113544 | tf_op jit(solution)/shard_map/ppermute | solution.py:902
  77.8 14.3 %collective-permute-start.20 = (bf16[49,32,256]{2,1,0:T(8,128)(2,1)S(1)}, bf16[49,32,256]{2,1,0:T(8,128)(2,1)S(1)}, u32[]{:S(2)}, u32[]{:S(2)}) collective-permute-start(bf16[49,32,256]{2,1,0:T(8,128)(2,1)S(1)} %crops.12.refs_4_), channel_id=1, source_target_pairs={{0,1},{1,0},{2,3},{3,2},{4,5},{5,4},{6,7},{7,6},{8,9},{9,8},{10,11... | collective-permute-start | bytes 2408456 | tf_op jit(solution)/shard_map/ppermute | solution.py:902
  81.3 10.8 %collective-permute-start.14 = (bf16[2,2,384,256]{3,2,1,0:T(8,128)(2,1)S(1)}, bf16[2,2,384,256]{3,2,1,0:T(8,128)(2,1)S(1)}, u32[]{:S(2)}, u32[]{:S(2)}) collective-permute-start(bf16[2,2,384,256]{3,2,1,0:T(8,128)(2,1)S(1)} %pad_maximum_fusion.1.refs_18_.refs_21_.refs_0_), channel_id=1, source_target_pairs={{0,1},{1,0},{2,3},{3,2},{4,5},{5,4},{6,7},{7,6},{8,9},{9,8},{10,11... | collective-permute-start | bytes 2359304 | tf_op jit(solution)/shard_map/ppermute | solution.py:902
  81.3 20.8 %collective-permute-start.12 = (bf16[2,2,384,256]{3,2,1,0:T(8,128)(2,1)S(1)}, bf16[2,2,384,256]{3,2,1,0:T(8,128)(2,1)S(1)}, u32[]{:S(2)}, u32[]{:S(2)}) collective-permute-start(bf16[2,2,384,256]{3,2,1,0:T(8,128)(2,1)S(1)} %pad_maximum_fusion.1.refs_18_.refs_21_.refs_0_), channel_id=1, source_target_pairs={{0,24},{1,25},{2,26},{3,27},{4,28},{5,29},{6,30},{7,31},{8,0},{9,1... | collective-permute-start | bytes 2359304 | tf_op jit(solution)/shard_map/ppermute | solution.py:902
  84.8 17.4 %collective-permute-start.11 = (bf16[1376,256]{1,0:T(8,128)(2,1)S(1)}, bf16[1376,256]{1,0:T(8,128)(2,1)S(1)}, u32[]{:S(2)}, u32[]{:S(2)}) collective-permute-start(bf16[1376,256]{1,0:T(8,128)(2,1)S(1)} %collective-permute-done.9.refs_23_), channel_id=1, source_target_pairs={{0,4},{1,5},{2,6},{3,7},{4,0},{5,1},{6,2},{7,3},{8,12},{9,13},{10,... | collective-permute-start | bytes 2113544 | tf_op jit(solution)/shard_map/ppermute | solution.py:902
  85.1 17.5 %collective-permute-start.25 = (bf16[1376,256]{1,0:T(8,128)(2,1)S(1)}, bf16[1376,256]{1,0:T(8,128)(2,1)S(1)}, u32[]{:S(2)}, u32[]{:S(2)}) collective-permute-start(bf16[1376,256]{1,0:T(8,128)(2,1)S(1)} %collective-permute-done.7.refs_33_), channel_id=1, source_target_pairs={{0,2},{1,3},{2,0},{3,1},{4,6},{5,7},{6,4},{7,5},{8,10},{9,11},{10,... | collective-permute-start | bytes 2113544 | tf_op jit(solution)/shard_map/ppermute | solution.py:902
  92.1 12.1 %collective-permute-start.21 = (bf16[49,32,256]{2,1,0:T(8,128)(2,1)S(1)}, bf16[49,32,256]{2,1,0:T(8,128)(2,1)S(1)}, u32[]{:S(2)}, u32[]{:S(2)}) collective-permute-start(bf16[49,32,256]{2,1,0:T(8,128)(2,1)S(1)} %crops.13.refs_5_), channel_id=1, source_target_pairs={{0,1},{1,0},{2,3},{3,2},{4,5},{5,4},{6,7},{7,6},{8,9},{9,8},{10,11... | collective-permute-start | bytes 2408456 | tf_op jit(solution)/shard_map/ppermute | solution.py:902
  92.2 13.2 %collective-permute-start.22 = (bf16[49,32,256]{2,1,0:T(8,128)(2,1)S(1)}, bf16[49,32,256]{2,1,0:T(8,128)(2,1)S(1)}, u32[]{:S(2)}, u32[]{:S(2)}) collective-permute-start(bf16[49,32,256]{2,1,0:T(8,128)(2,1)S(1)} %crops.14.refs_6_), channel_id=1, source_target_pairs={{0,1},{1,0},{2,3},{3,2},{4,5},{5,4},{6,7},{7,6},{8,9},{9,8},{10,11... | collective-permute-start | bytes 2408456 | tf_op jit(solution)/shard_map/ppermute | solution.py:902
  102.1 21.3 %collective-permute-start.15 = (bf16[2,2,384,256]{3,2,1,0:T(8,128)(2,1)}, bf16[2,2,384,256]{3,2,1,0:T(8,128)(2,1)}, u32[]{:S(2)}, u32[]{:S(2)}) collective-permute-start(bf16[2,2,384,256]{3,2,1,0:T(8,128)(2,1)} %collective-permute-done.8.refs_24_.refs_30_.refs_1_), channel_id=1, source_target_pairs={{0,1},{1,0},{2,3},{3,2},{4,5},{5,4},{6,7},{7,6},{8,9},{9,8},{10,11... | collective-permute-start | bytes 2359304 | tf_op jit(solution)/shard_map/ppermute | solution.py:902
  102.6 21.7 %collective-permute-start.13 = (bf16[2,2,384,256]{3,2,1,0:T(8,128)(2,1)}, bf16[2,2,384,256]{3,2,1,0:T(8,128)(2,1)}, u32[]{:S(2)}, u32[]{:S(2)}) collective-permute-start(bf16[2,2,384,256]{3,2,1,0:T(8,128)(2,1)} %collective-permute-done.8.refs_24_.refs_30_.refs_1_), channel_id=1, source_target_pairs={{0,8},{1,9},{2,10},{3,11},{4,12},{5,13},{6,14},{7,15},{8,16},{9,17... | collective-permute-start | bytes 2359304 | tf_op jit(solution)/shard_map/ppermute | solution.py:902
  104.2 20.1 %collective-permute-start.29 = (bf16[1376,256]{1,0:T(8,128)(2,1)}, bf16[1376,256]{1,0:T(8,128)(2,1)}, u32[]{:S(2)}, u32[]{:S(2)}) collective-permute-start(bf16[1376,256]{1,0:T(8,128)(2,1)} %collective-permute-done.24.refs_26_), channel_id=1, source_target_pairs={{0,4},{1,5},{2,6},{3,7},{4,0},{5,1},{6,2},{7,3},{8,12},{9,13},{10,... | collective-permute-start | bytes 2113544 | tf_op jit(solution)/shard_map/ppermute | solution.py:902
  105.5 18.9 %collective-permute-start.28 = (bf16[1376,256]{1,0:T(8,128)(2,1)}, bf16[1376,256]{1,0:T(8,128)(2,1)}, u32[]{:S(2)}, u32[]{:S(2)}) collective-permute-start(bf16[1376,256]{1,0:T(8,128)(2,1)} %collective-permute-done.10.refs_35_), channel_id=1, source_target_pairs={{0,2},{1,3},{2,0},{3,1},{4,6},{5,7},{6,4},{7,5},{8,10},{9,11},{10,... | collective-permute-start | bytes 2113544 | tf_op jit(solution)/shard_map/ppermute | solution.py:902
  124.3 10.7 %collective-permute-start.26 = (bf16[2,2,384,256]{3,2,1,0:T(8,128)(2,1)}, bf16[2,2,384,256]{3,2,1,0:T(8,128)(2,1)S(1)}, u32[]{:S(2)}, u32[]{:S(2)}) collective-permute-start(bf16[2,2,384,256]{3,2,1,0:T(8,128)(2,1)} %collective-permute-done.13.refs_18_.refs_19_.refs_2_), channel_id=1, source_target_pairs={{0,1},{1,0},{2,3},{3,2},{4,5},{5,4},{6,7},{7,6},{8,9},{9,8},{10,11... | collective-permute-start | bytes 2359304 | tf_op jit(solution)/shard_map/ppermute | solution.py:902
  148.5 11.2 %collective-permute-start.32 = (bf16[512,1024]{1,0:T(8,128)(2,1)}, bf16[512,1024]{1,0:T(8,128)(2,1)S(1)}, u32[]{:S(2)}, u32[]{:S(2)}) collective-permute-start(bf16[512,1024]{1,0:T(8,128)(2,1)} %get-tuple-element.157), channel_id=1, source_target_pairs={{0,1},{1,0},{2,3},{3,2},{4,5},{5,4},{6,7},{7,6},{8,9},{9,8},{10,11... | collective-permute-start | bytes 3145736 | tf_op jit(solution)/shard_map/ppermute | solution.py:902
  148.8 10.8 %collective-permute-start.33 = (bf16[512,512]{1,0:T(8,128)(2,1)}, bf16[512,512]{1,0:T(8,128)(2,1)S(1)}, u32[]{:S(2)}, u32[]{:S(2)}) collective-permute-start(bf16[512,512]{1,0:T(8,128)(2,1)} %get-tuple-element.160), channel_id=1, source_target_pairs={{0,1},{1,0},{2,3},{3,2},{4,5},{5,4},{6,7},{7,6},{8,9},{9,8},{10,11... | collective-permute-start | bytes 1572872 | tf_op jit(solution)/shard_map/ppermute | solution.py:902
  165.5 18.2 %collective-permute-start.37 = (bf16[1360,256]{1,0:T(8,128)(2,1)}, bf16[1360,256]{1,0:T(8,128)(2,1)S(1)}, u32[]{:S(2)}, u32[]{:S(2)}) collective-permute-start(bf16[1360,256]{1,0:T(8,128)(2,1)} %get-tuple-element.181), channel_id=1, source_target_pairs={{0,2},{1,3},{2,0},{3,1},{4,6},{5,7},{6,4},{7,5},{8,10},{9,11},{10,... | collective-permute-start | bytes 2088968 | tf_op jit(solution)/shard_map/ppermute | solution.py:902
  166.5 17.9 %collective-permute-start.38 = (bf16[1360,256]{1,0:T(8,128)(2,1)}, bf16[1360,256]{1,0:T(8,128)(2,1)S(1)}, u32[]{:S(2)}, u32[]{:S(2)}) collective-permute-start(bf16[1360,256]{1,0:T(8,128)(2,1)} %get-tuple-element.183), channel_id=1, source_target_pairs={{0,4},{1,5},{2,6},{3,7},{4,0},{5,1},{6,2},{7,3},{8,12},{9,13},{10,... | collective-permute-start | bytes 2088968 | tf_op jit(solution)/shard_map/ppermute | solution.py:902
  167.3 22.4 %collective-permute-start.34 = (bf16[2,2,416,256]{3,2,1,0:T(8,128)(2,1)}, bf16[2,2,416,256]{3,2,1,0:T(8,128)(2,1)S(1)}, u32[]{:S(2)}, u32[]{:S(2)}) collective-permute-start(bf16[2,2,416,256]{3,2,1,0:T(8,128)(2,1)} %get-tuple-element.163), channel_id=1, source_target_pairs={{0,8},{1,9},{2,10},{3,11},{4,12},{5,13},{6,14},{7,15},{8,16},{9,17... | collective-permute-start | bytes 2555912 | tf_op jit(solution)/shard_map/ppermute | solution.py:902
  183.7 17.3 %collective-permute-start.44 = (bf16[1360,256]{1,0:T(8,128)(2,1)}, bf16[1360,256]{1,0:T(8,128)(2,1)S(1)}, u32[]{:S(2)}, u32[]{:S(2)}) collective-permute-start(bf16[1360,256]{1,0:T(8,128)(2,1)} %get-tuple-element.194), channel_id=1, source_target_pairs={{0,2},{1,3},{2,0},{3,1},{4,6},{5,7},{6,4},{7,5},{8,10},{9,11},{10,... | collective-permute-start | bytes 2088968 | tf_op jit(solution)/shard_map/ppermute | solution.py:902
  184.4 16.8 %collective-permute-start.39 = (bf16[1360,256]{1,0:T(8,128)(2,1)}, bf16[1360,256]{1,0:T(8,128)(2,1)S(1)}, u32[]{:S(2)}, u32[]{:S(2)}) collective-permute-start(bf16[1360,256]{1,0:T(8,128)(2,1)} %get-tuple-element.184), channel_id=1, source_target_pairs={{0,4},{1,5},{2,6},{3,7},{4,0},{5,1},{6,2},{7,3},{8,12},{9,13},{10,... | collective-permute-start | bytes 2088968 | tf_op jit(solution)/shard_map/ppermute | solution.py:902
  189.8 19.5 %collective-permute-start.35 = (bf16[2,2,416,256]{3,2,1,0:T(8,128)(2,1)S(1)}, bf16[2,2,416,256]{3,2,1,0:T(8,128)(2,1)S(1)}, u32[]{:S(2)}, u32[]{:S(2)}) collective-permute-start(bf16[2,2,416,256]{3,2,1,0:T(8,128)(2,1)S(1)} %copy-done.72), channel_id=1, source_target_pairs={{0,24},{1,25},{2,26},{3,27},{4,28},{5,29},{6,30},{7,31},{8,0},{9,1... | collective-permute-start | bytes 2555912 | tf_op jit(solution)/shard_map/ppermute | solution.py:902
  201.2 16.0 %collective-permute-start.40 = (bf16[1360,256]{1,0:T(8,128)(2,1)S(1)}, bf16[1360,256]{1,0:T(8,128)(2,1)S(1)}, u32[]{:S(2)}, u32[]{:S(2)}) collective-permute-start(bf16[1360,256]{1,0:T(8,128)(2,1)S(1)} %add_convert_fusion.8), channel_id=1, source_target_pairs={{0,4},{1,5},{2,6},{3,7},{4,0},{5,1},{6,2},{7,3},{8,12},{9,13},{10,... | collective-permute-start | bytes 2088968 | tf_op jit(solution)/shard_map/ppermute | solution.py:902
  202.0 15.6 %collective-permute-start.45 = (bf16[1360,256]{1,0:T(8,128)(2,1)S(1)}, bf16[1360,256]{1,0:T(8,128)(2,1)S(1)}, u32[]{:S(2)}, u32[]{:S(2)}) collective-permute-start(bf16[1360,256]{1,0:T(8,128)(2,1)S(1)} %add_convert_fusion.6), channel_id=1, source_target_pairs={{0,2},{1,3},{2,0},{3,1},{4,6},{5,7},{6,4},{7,5},{8,10},{9,11},{10,... | collective-permute-start | bytes 2088968 | tf_op jit(solution)/shard_map/ppermute | solution.py:902
  209.3 20.4 %collective-permute-start.36 = (bf16[2,2,416,256]{3,2,1,0:T(8,128)(2,1)S(1)}, bf16[2,2,416,256]{3,2,1,0:T(8,128)(2,1)S(1)}, u32[]{:S(2)}, u32[]{:S(2)}) collective-permute-start(bf16[2,2,416,256]{3,2,1,0:T(8,128)(2,1)S(1)} %add_convert_fusion.1), channel_id=1, source_target_pairs={{0,8},{1,9},{2,10},{3,11},{4,12},{5,13},{6,14},{7,15},{8,16},{9,17... | collective-permute-start | bytes 2555912 | tf_op jit(solution)/shard_map/ppermute | solution.py:902
  217.2 15.8 %collective-permute-start.41 = (bf16[1360,256]{1,0:T(8,128)(2,1)S(1)}, bf16[1360,256]{1,0:T(8,128)(2,1)S(1)}, u32[]{:S(2)}, u32[]{:S(2)}) collective-permute-start(bf16[1360,256]{1,0:T(8,128)(2,1)S(1)} %copy-done.77), channel_id=1, source_target_pairs={{0,4},{1,5},{2,6},{3,7},{4,0},{5,1},{6,2},{7,3},{8,12},{9,13},{10,... | collective-permute-start | bytes 2088968 | tf_op jit(solution)/shard_map/ppermute | solution.py:902
  217.6 15.9 %collective-permute-start.46 = (bf16[1360,256]{1,0:T(8,128)(2,1)S(1)}, bf16[1360,256]{1,0:T(8,128)(2,1)S(1)}, u32[]{:S(2)}, u32[]{:S(2)}) collective-permute-start(bf16[1360,256]{1,0:T(8,128)(2,1)S(1)} %copy-done.76), channel_id=1, source_target_pairs={{0,2},{1,3},{2,0},{3,1},{4,6},{5,7},{6,4},{7,5},{8,10},{9,11},{10,... | collective-permute-start | bytes 2088968 | tf_op jit(solution)/shard_map/ppermute | solution.py:902
  229.7 19.5 %collective-permute-start.52 = (bf16[1360,256]{1,0:T(8,128)(2,1)S(1)}, bf16[1360,256]{1,0:T(8,128)(2,1)S(1)}, u32[]{:S(2)}, u32[]{:S(2)}) collective-permute-start(bf16[1360,256]{1,0:T(8,128)(2,1)S(1)} %add_convert_fusion.3), channel_id=1, source_target_pairs={{0,8},{1,9},{2,10},{3,11},{4,12},{5,13},{6,14},{7,15},{8,16},{9,17... | collective-permute-start | bytes 2088968 | tf_op jit(solution)/shard_map/ppermute | solution.py:902
  232.9 15.8 %collective-permute-start.42 = (bf16[1360,256]{1,0:T(8,128)(2,1)S(1)}, bf16[1360,256]{1,0:T(8,128)(2,1)S(1)}, u32[]{:S(2)}, u32[]{:S(2)}) collective-permute-start(bf16[1360,256]{1,0:T(8,128)(2,1)S(1)} %copy-done.75), channel_id=1, source_target_pairs={{0,4},{1,5},{2,6},{3,7},{4,0},{5,1},{6,2},{7,3},{8,12},{9,13},{10,... | collective-permute-start | bytes 2088968 | tf_op jit(solution)/shard_map/ppermute | solution.py:902
  233.5 18.5 %collective-permute-start.47 = (bf16[1360,256]{1,0:T(8,128)(2,1)S(1)}, bf16[1360,256]{1,0:T(8,128)(2,1)S(1)}, u32[]{:S(2)}, u32[]{:S(2)}) collective-permute-start(bf16[1360,256]{1,0:T(8,128)(2,1)S(1)} %add_convert_fusion.7), channel_id=1, source_target_pairs={{0,2},{1,3},{2,0},{3,1},{4,6},{5,7},{6,4},{7,5},{8,10},{9,11},{10,... | collective-permute-start | bytes 2088968 | tf_op jit(solution)/shard_map/ppermute | solution.py:902
  249.2 19.4 %collective-permute-start.53 = (bf16[1360,256]{1,0:T(8,128)(2,1)S(1)}, bf16[1360,256]{1,0:T(8,128)(2,1)S(1)}, u32[]{:S(2)}, u32[]{:S(2)}) collective-permute-start(bf16[1360,256]{1,0:T(8,128)(2,1)S(1)} %add_convert_fusion.4), channel_id=1, source_target_pairs={{0,24},{1,25},{2,26},{3,27},{4,28},{5,29},{6,30},{7,31},{8,0},{9,1... | collective-permute-start | bytes 2088968 | tf_op jit(solution)/shard_map/ppermute | solution.py:902
  252.0 13.8 %collective-permute-start.48 = (bf16[1360,256]{1,0:T(8,128)(2,1)S(1)}, bf16[1360,256]{1,0:T(8,128)(2,1)S(1)}, u32[]{:S(2)}, u32[]{:S(2)}) collective-permute-start(bf16[1360,256]{1,0:T(8,128)(2,1)S(1)} %copy-done.74), channel_id=1, source_target_pairs={{0,2},{1,3},{2,0},{3,1},{4,6},{5,7},{6,4},{7,5},{8,10},{9,11},{10,... | collective-permute-start | bytes 2088968 | tf_op jit(solution)/shard_map/ppermute | solution.py:902
  268.1 11.1 %collective-permute-start.51 = (bf16[1360,256]{1,0:T(8,128)(2,1)S(1)}, bf16[1360,256]{1,0:T(8,128)(2,1)S(1)}, u32[]{:S(2)}, u32[]{:S(2)}) collective-permute-start(bf16[1360,256]{1,0:T(8,128)(2,1)S(1)} %add_convert_fusion.5), channel_id=1, source_target_pairs={{0,4},{1,5},{2,6},{3,7},{4,0},{5,1},{6,2},{7,3},{8,12},{9,13},{10,... | collective-permute-start | bytes 2088968 | tf_op jit(solution)/shard_map/ppermute | solution.py:902
  268.6 12.8 %collective-permute-start.54 = (bf16[1360,256]{1,0:T(8,128)(2,1)S(1)}, bf16[1360,256]{1,0:T(8,128)(2,1)S(1)}, u32[]{:S(2)}, u32[]{:S(2)}) collective-permute-start(bf16[1360,256]{1,0:T(8,128)(2,1)S(1)} %add_convert_fusion.2), channel_id=1, source_target_pairs={{0,8},{1,9},{2,10},{3,11},{4,12},{5,13},{6,14},{7,15},{8,16},{9,17... | collective-permute-start | bytes 2088968 | tf_op jit(solution)/shard_map/ppermute | solution.py:902
  (86 other events, 887.5 us)

commit v7 on v6

--- a/solution.py
+++ b/solution.py
@@ -1057,7 +1057,7 @@
     made = own_crops[:EARLY] + [m[key] for key in ((0, 1, 0), (0, 0, 1), (1, 0, 0))]
     m[3, 0, 0] = links.send(after(first_low, m[1, 0, 0]), "z", 3)
     m[1, 1, 0] = links.send(after(m[1, 0, 0], *made), "x")
-    m[0, 1, 1] = links.send(after(m[0, 1, 0], *made), "y")
+    m[0, 1, 1] = links.send(after(m[0, 1, 0], m[0, 0, 1]), "y")
     stacks[0] = jnp.stack([jnp.stack([m[0, x, y][most:] for x in range(grid.x)]) for y in range(grid.y)])
     links.next()
     m[2, 0, 0] = links.send(m[1, 0, 0], "z", 1)

time: 288 us -> 288 us (level)
  no operation moved by 1% of the time
where the time goes in v7:
time: 288 us; the launch traced here: 287 us
  waiting for transfers between devices  133 us (46%)
  Pallas kernels  88.2 us (31%)
  starting transfers between devices  40.7 us (14%)
  local copies, waits for them, and re-layouts  14.6 us (5%)
  other arithmetic  8.5 us (3%)
    ppermute x55, waiting for transfers between devices, move(): return lax.ppermute(value, AXES, pairs)  133 us
    ppermute x55, starting transfers between devices, move(): return lax.ppermute(value, AXES, pairs)  40.7 us
    pallas_call x8, Pallas kernels, window_crops(): pl.pallas_call(functools.partial(crop_kernel, first), grid_spec=pltpu.Pre...  25 us
    pallas_call x2, Pallas kernels, first_blocks(): pl.pallas_call(functools.partial(block_kernel, items, feats, most, wide,...  23.8 us
    pallas_call x2, Pallas kernels, first_grad_blocks(): pl.pallas_call(functools.partial(block_grad_kernel, span, numbers, feats,...  21.5 us
    pallas_call x1, Pallas kernels, heads_blocks(): pl.pallas_call(functools.partial(head_blocks_kernel, share, depth), in_sp...  10.6 us
    unnamed x157, local copies, waits for them, and re-layouts  9.05 us
  transfers between devices with their start and end apart: 55, of which 28 were waited for; matrix products, arithmetic and copies ran while one was open for 4% of the time, Pallas kernels for 24%

profile of v7, /device:TPU:0, one launch (start us, length us, event | category | flops | bytes accessed | tf_op | source)
XLA Modules:
  0.0 286.8 jit_solution(17423069071162657605)
XLA Ops:
  0.7 2.6 prepare.1
  3.3 3.0 %collective-permute-start.1 = (bf16[1760,256]{1,0:T(8,128)(2,1)}, bf16[1760,256]{1,0:T(8,128)(2,1)}, u32[]{:S(2)}, u32[]{:S(2)}) collective-permute-start(bf16[1760,256]{1,0:T(8,128)(2,1)} %get-tuple-element.112.refs_16_), channel_id=1, source_target_pairs={{0,2},{1,3},{2,0},{3,1},{4,6},{5,7},{6,4},{7,5},{8,10},{9,11},{10,... | collective-permute-start | bytes 2703368 | tf_op jit(solution)/shard_map/ppermute | solution.py:902
  7.9 1.6 collective-permute-start.3
  10.2 2.2 copy-done
  12.4 3.1 %crops.11.refs_3_ = bf16[49,32,256]{2,1,0:T(8,128)(2,1)S(1)} custom-call(s32[256]{0:T(256)S(1)} %multiply_add_fusion.4.base_ref, s32[256]{0:T(256)S(1)} %bitcast.109, bf16[256,32,256]{2,1,0:T(8,128)(2,1)S(1)} %bitcast.85, bf16[2048,16]{1,0:T(8,128)(2,1)S(1)} %bitcast.101, bf16[2048,16]{1,0:T(8,128)(2,1)S(1)} %bitcast.93, bf16[16,512]{1,0:T(8,128)(2,1)S(1)} %copy-done.10, ...), custom_call_target="tpu_custom_call" | custom-call | bytes 1024 | tf_op jit(solution)/shard_map/crops/pallas_call | solution.py:94
  15.5 3.1 %crops.10.refs_2_ = bf16[49,32,256]{2,1,0:T(8,128)(2,1)S(1)} custom-call(s32[256]{0:T(256)S(1)} %multiply_add_fusion.4.base_ref, s32[256]{0:T(256)S(1)} %bitcast.110, bf16[256,32,256]{2,1,0:T(8,128)(2,1)S(1)} %bitcast.86, bf16[2048,16]{1,0:T(8,128)(2,1)S(1)} %bitcast.102, bf16[2048,16]{1,0:T(8,128)(2,1)S(1)} %bitcast.94, bf16[16,512]{1,0:T(8,128)(2,1)S(1)} %copy-done.10, ...), custom_call_target="tpu_custom_call" | custom-call | bytes 1024 | tf_op jit(solution)/shard_map/crops/pallas_call | solution.py:94
  18.6 3.1 %crops.9.refs_1_ = bf16[49,32,256]{2,1,0:T(8,128)(2,1)S(1)} custom-call(s32[256]{0:T(256)S(1)} %multiply_add_fusion.4.base_ref, s32[256]{0:T(256)S(1)} %bitcast.111, bf16[256,32,256]{2,1,0:T(8,128)(2,1)S(1)} %bitcast.87, bf16[2048,16]{1,0:T(8,128)(2,1)S(1)} %bitcast.103, bf16[2048,16]{1,0:T(8,128)(2,1)S(1)} %bitcast.95, bf16[16,512]{1,0:T(8,128)(2,1)S(1)} %copy-done.10, ...), custom_call_target="tpu_custom_call" | custom-call | bytes 1024 | tf_op jit(solution)/shard_map/crops/pallas_call | solution.py:94
  21.8 3.1 %crops.8.refs_0_ = bf16[49,32,256]{2,1,0:T(8,128)(2,1)S(1)} custom-call(s32[256]{0:T(256)S(1)} %multiply_add_fusion.4.base_ref, s32[256]{0:T(256)S(1)} %bitcast.112, bf16[256,32,256]{2,1,0:T(8,128)(2,1)S(1)} %bitcast.88, bf16[2048,16]{1,0:T(8,128)(2,1)S(1)} %bitcast.104, bf16[2048,16]{1,0:T(8,128)(2,1)S(1)} %bitcast.96, bf16[16,512]{1,0:T(8,128)(2,1)S(1)} %copy-done.10, ...), custom_call_target="tpu_custom_call" | custom-call | bytes 1024 | tf_op jit(solution)/shard_map/crops/pallas_call | solution.py:94
  24.9 2.1 collective-permute-done.3.refs_22_
  27.0 1.7 collective-permute-start.4
  32.7 10.5 %collective-permute-done.4.refs_25_ = bf16[1376,256]{1,0:T(8,128)(2,1)S(1)} collective-permute-done((bf16[1376,256]{1,0:T(8,128)(2,1)S(1)}, bf16[1376,256]{1,0:T(8,128)(2,1)S(1)}, u32[]{:S(2)}, u32[]{:S(2)}) %collective-permute-start.4) | collective-permute-done | bytes 704544 | tf_op jit(solution)/shard_map/ppermute | solution.py:902
  43.1 1.6 collective-permute-done.5.refs_28_
  46.2 1.6 collective-permute-start.7
  51.2 8.7 %collective-permute-done.6.refs_31_ = bf16[1376,256]{1,0:T(8,128)(2,1)S(1)} collective-permute-done((bf16[1376,256]{1,0:T(8,128)(2,1)S(1)}, bf16[1376,256]{1,0:T(8,128)(2,1)S(1)}, u32[]{:S(2)}, u32[]{:S(2)}) %collective-permute-start.6) | collective-permute-done | bytes 704544 | tf_op jit(solution)/shard_map/ppermute | solution.py:902
  59.9 3.5 %collective-permute-done.7.refs_33_ = bf16[1376,256]{1,0:T(8,128)(2,1)S(1)} collective-permute-done((bf16[1376,256]{1,0:T(8,128)(2,1)}, bf16[1376,256]{1,0:T(8,128)(2,1)S(1)}, u32[]{:S(2)}, u32[]{:S(2)}) %collective-permute-start.7) | collective-permute-done | bytes 704544 | tf_op jit(solution)/shard_map/ppermute | solution.py:902
  67.2 3.1 %crops.12.refs_4_ = bf16[49,32,256]{2,1,0:T(8,128)(2,1)S(1)} custom-call(s32[256]{0:T(256)S(1)} %multiply_add_fusion.4.base_ref, s32[256]{0:T(256)S(1)} %bitcast.113, bf16[256,32,256]{2,1,0:T(8,128)(2,1)S(1)} %bitcast.89, bf16[2048,16]{1,0:T(8,128)(2,1)S(1)} %bitcast.105, bf16[2048,16]{1,0:T(8,128)(2,1)S(1)} %bitcast.97, bf16[16,512]{1,0:T(8,128)(2,1)S(1)} %copy-done.10, ...), custom_call_target="tpu_custom_call" | custom-call | bytes 1024 | tf_op jit(solution)/shard_map/crops/pallas_call | solution.py:94
  70.4 7.4 %collective-permute-done.10.refs_35_ = bf16[1376,256]{1,0:T(8,128)(2,1)} collective-permute-done((bf16[1376,256]{1,0:T(8,128)(2,1)S(1)}, bf16[1376,256]{1,0:T(8,128)(2,1)}, u32[]{:S(2)}, u32[]{:S(2)}) %collective-permute-start.10) | collective-permute-done | bytes 704544 | tf_op jit(solution)/shard_map/ppermute | solution.py:902
  77.8 3.5 %collective-permute-done.8.refs_24_.refs_30_.refs_1_ = bf16[2,2,384,256]{3,2,1,0:T(8,128)(2,1)} collective-permute-done((bf16[2,2,384,256]{3,2,1,0:T(8,128)(2,1)S(1)}, bf16[2,2,384,256]{3,2,1,0:T(8,128)(2,1)}, u32[]{:S(2)}, u32[]{:S(2)}) %collective-permute-start.8) | collective-permute-done | bytes 786464 | tf_op jit(solution)/shard_map/ppermute | solution.py:902
  82.2 2.6 collective-permute-done.24.refs_26_
  85.7 3.1 %crops.14.refs_6_ = bf16[49,32,256]{2,1,0:T(8,128)(2,1)S(1)} custom-call(s32[256]{0:T(256)S(1)} %multiply_add_fusion.4.base_ref, s32[256]{0:T(256)S(1)} %bitcast.114, bf16[256,32,256]{2,1,0:T(8,128)(2,1)S(1)} %bitcast.90, bf16[2048,16]{1,0:T(8,128)(2,1)S(1)} %bitcast.106, bf16[2048,16]{1,0:T(8,128)(2,1)S(1)} %bitcast.98, bf16[16,512]{1,0:T(8,128)(2,1)S(1)} %copy-done.10, ...), custom_call_target="tpu_custom_call" | custom-call | bytes 1024 | tf_op jit(solution)/shard_map/crops/pallas_call | solution.py:94
  88.9 3.1 %crops.13.refs_5_ = bf16[49,32,256]{2,1,0:T(8,128)(2,1)S(1)} custom-call(s32[256]{0:T(256)S(1)} %multiply_add_fusion.4.base_ref, s32[256]{0:T(256)S(1)} %bitcast.115, bf16[256,32,256]{2,1,0:T(8,128)(2,1)S(1)} %bitcast.91, bf16[2048,16]{1,0:T(8,128)(2,1)S(1)} %bitcast.107, bf16[2048,16]{1,0:T(8,128)(2,1)S(1)} %bitcast.99, bf16[16,512]{1,0:T(8,128)(2,1)S(1)} %copy-done.10, ...), custom_call_target="tpu_custom_call" | custom-call | bytes 1024 | tf_op jit(solution)/shard_map/crops/pallas_call | solution.py:94
  92.7 3.1 %crops.15.refs_7_ = bf16[49,32,256]{2,1,0:T(8,128)(2,1)S(1)} custom-call(s32[256]{0:T(256)S(1)} %multiply_add_fusion.4.base_ref, s32[256]{0:T(256)S(1)} %bitcast.116, bf16[256,32,256]{2,1,0:T(8,128)(2,1)S(1)} %bitcast.92, bf16[2048,16]{1,0:T(8,128)(2,1)S(1)} %bitcast.108, bf16[2048,16]{1,0:T(8,128)(2,1)S(1)} %bitcast.100, bf16[16,512]{1,0:T(8,128)(2,1)S(1)} %copy-done.10, ...), custom_call_target="tpu_custom_call" | custom-call | bytes 1024 | tf_op jit(solution)/shard_map/crops/pallas_call | solution.py:94
  95.9 6.2 %collective-permute-done.11.refs_29_ = bf16[1376,256]{1,0:T(8,128)(2,1)S(1)} collective-permute-done((bf16[1376,256]{1,0:T(8,128)(2,1)S(1)}, bf16[1376,256]{1,0:T(8,128)(2,1)S(1)}, u32[]{:S(2)}, u32[]{:S(2)}) %collective-permute-start.11) | collective-permute-done | bytes 704544 | tf_op jit(solution)/shard_map/ppermute | solution.py:902
  102.6 1.6 collective-permute-start.13
  108.0 15.4 %first_blocks.2 = (f32[256,512]{1,0:T(8,128)}, f32[256,512]{1,0:T(8,128)}) custom-call(s32[22]{0:T(128)} %stack.169.table, bf16[49,32,256]{2,1,0:T(8,128)(2,1)} %copy-done.4, bf16[49,32,256]{2,1,0:T(8,128)(2,1)} %copy-done.3, bf16[49,32,256]{2,1,0:T(8,128)(2,1)} %copy-done.2, bf16[49,32,256]{2,1,0:T(8,128)(2,1)} %copy-done.1, ...), custom_call_target="tpu_custom_call" | custom-call | bytes 1024 | tf_op jit(solution)/shard_map/first_blocks/pallas_call | solution.py:303
  124.4 8.3 %first_blocks.3 = (f32[256,512]{1,0:T(8,128)}, f32[256,512]{1,0:T(8,128)}) custom-call(s32[22]{0:T(128)} %stack.169.table, bf16[49,32,256]{2,1,0:T(8,128)(2,1)} %copy-done.4, bf16[49,32,256]{2,1,0:T(8,128)(2,1)} %copy-done.3, bf16[49,32,256]{2,1,0:T(8,128)(2,1)} %copy-done.2, ...), custom_call_target="tpu_custom_call", output_to_operand_aliasing={{0}: (17, {}), {1}: (18, {})} | custom-call | bytes 1024 | tf_op jit(solution)/shard_map/first_blocks/pallas_call | solution.py:303
  136.0 10.6 %heads.3 = (bf16[256,512]{1,0:T(8,128)(2,1)}, bf16[256,512]{1,0:T(8,128)(2,1)}, bf16[512,1024]{1,0:T(8,128)(2,1)}, bf16[512,1024]{1,0:T(8,128)(2,1)}, bf16[512,5...) custom-call(s32[22]{0:T(128)} %stack.169.table, ...), custom_call_target="tpu_custom_call" | custom-call | bytes 1024 | tf_op jit(solution)/shard_map/heads/pallas_call | solution.py:750
  149.2 10.5 %first_grad.2 = (bf16[1360,256]{1,0:T(8,128)(2,1)}, bf16[208,256]{1,0:T(8,128)(2,1)}, bf16[1360,256]{1,0:T(8,128)(2,1)}, bf16[208,256]{1,0:T(8,128)(2,1)}, bf16[...) custom-call(s32[22]{0:T(128)} %stack.169.table, ...), custom_call_target="tpu_custom_call" | custom-call | bytes 1024 | tf_op jit(solution)/shard_map/first_grad/pallas_call | solution.py:395
  160.8 4.7 %pack.1 = (bf16[2,2,416,256]{3,2,1,0:T(8,128)(2,1)}, bf16[2,2,416,256]{3,2,1,0:T(8,128)(2,1)}, bf16[2,2,2,208,256]{4,3,2,1,0:T(8,128)(2,1)}) custom-call(s32[22]{0:T(128)} %stack.169.table, bf16[208,256]{1,0:T(8,128)(2,1)} %get-tuple-element.147.refs_0_, bf16[208,256]{1,0:T(8,128)(2,1)} %get-tuple-element.148.refs_1_, ...), custom_call_target="tpu_custom_call" | custom-call | bytes 1024 | tf_op jit(solution)/shard_map/pack/pallas_call | solution.py:573
  167.3 1.7 collective-permute-start.34
  169.1 11.0 %first_grad.3 = (bf16[1360,256]{1,0:T(8,128)(2,1)}, bf16[208,256]{1,0:T(8,128)(2,1)}, bf16[1360,256]{1,0:T(8,128)(2,1)}, bf16[208,256]{1,0:T(8,128)(2,1)}, bf16[...) custom-call(s32[22]{0:T(128)} %stack.169.table, ...), custom_call_target="tpu_custom_call" | custom-call | bytes 1024 | tf_op jit(solution)/shard_map/first_grad/pallas_call | solution.py:395
  180.1 3.6 %collective-permute-done.37 = bf16[1360,256]{1,0:T(8,128)(2,1)S(1)} collective-permute-done((bf16[1360,256]{1,0:T(8,128)(2,1)}, bf16[1360,256]{1,0:T(8,128)(2,1)S(1)}, u32[]{:S(2)}, u32[]{:S(2)}) %collective-permute-start.37) | collective-permute-done | bytes 696352 | tf_op jit(solution)/shard_map/ppermute | solution.py:902
  185.5 4.3 %collective-permute-done.34 = bf16[2,2,416,256]{3,2,1,0:T(8,128)(2,1)S(1)} collective-permute-done((bf16[2,2,416,256]{3,2,1,0:T(8,128)(2,1)}, bf16[2,2,416,256]{3,2,1,0:T(8,128)(2,1)S(1)}, u32[]{:S(2)}, u32[]{:S(2)}) %collective-permute-start.34) | collective-permute-done | bytes 852000 | tf_op jit(solution)/shard_map/ppermute | solution.py:902
  190.5 10.5 %collective-permute-done.44 = bf16[1360,256]{1,0:T(8,128)(2,1)S(1)} collective-permute-done((bf16[1360,256]{1,0:T(8,128)(2,1)}, bf16[1360,256]{1,0:T(8,128)(2,1)S(1)}, u32[]{:S(2)}, u32[]{:S(2)}) %collective-permute-start.44) | collective-permute-done | bytes 696352 | tf_op jit(solution)/shard_map/ppermute | solution.py:902
  203.5 5.8 %collective-permute-done.35 = bf16[2,2,416,256]{3,2,1,0:T(8,128)(2,1)S(1)} collective-permute-done((bf16[2,2,416,256]{3,2,1,0:T(8,128)(2,1)S(1)}, bf16[2,2,416,256]{3,2,1,0:T(8,128)(2,1)S(1)}, u32[]{:S(2)}, u32[]{:S(2)}) %collective-permute-start.35) | collective-permute-done | bytes 852000 | tf_op jit(solution)/shard_map/ppermute | solution.py:902
  209.3 7.8 %collective-permute-done.40 = bf16[1360,256]{1,0:T(8,128)(2,1)S(1)} collective-permute-done((bf16[1360,256]{1,0:T(8,128)(2,1)S(1)}, bf16[1360,256]{1,0:T(8,128)(2,1)S(1)}, u32[]{:S(2)}, u32[]{:S(2)}) %collective-permute-start.40) | collective-permute-done | bytes 696352 | tf_op jit(solution)/shard_map/ppermute | solution.py:902
  219.5 10.2 %collective-permute-done.36 = bf16[2,2,416,256]{3,2,1,0:T(8,128)(2,1)S(1)} collective-permute-done((bf16[2,2,416,256]{3,2,1,0:T(8,128)(2,1)S(1)}, bf16[2,2,416,256]{3,2,1,0:T(8,128)(2,1)S(1)}, u32[]{:S(2)}, u32[]{:S(2)}) %collective-permute-start.36) | collective-permute-done | bytes 852000 | tf_op jit(solution)/shard_map/ppermute | solution.py:902
  230.2 2.7 collective-permute-done.41
  234.8 13.9 %collective-permute-done.42 = bf16[1360,256]{1,0:T(8,128)(2,1)S(1)} collective-permute-done((bf16[1360,256]{1,0:T(8,128)(2,1)S(1)}, bf16[1360,256]{1,0:T(8,128)(2,1)S(1)}, u32[]{:S(2)}, u32[]{:S(2)}) %collective-permute-start.42) | collective-permute-done | bytes 696352 | tf_op jit(solution)/shard_map/ppermute | solution.py:902
  249.2 2.8 collective-permute-start.53
  252.0 1.8 collective-permute-start.48
  253.8 3.2 %collective-permute-done.43 = bf16[862,256]{1,0:T(8,128)(2,1)S(1)} collective-permute-done((bf16[862,256]{1,0:T(8,128)(2,1)S(1)}, bf16[862,256]{1,0:T(8,128)(2,1)S(1)}, u32[]{:S(2)}, u32[]{:S(2)}) %collective-permute-start.43) | collective-permute-done | bytes 441376 | tf_op jit(solution)/shard_map/ppermute | solution.py:902
  257.3 8.6 %collective-permute-done.48 = bf16[1360,256]{1,0:T(8,128)(2,1)S(1)} collective-permute-done((bf16[1360,256]{1,0:T(8,128)(2,1)S(1)}, bf16[1360,256]{1,0:T(8,128)(2,1)S(1)}, u32[]{:S(2)}, u32[]{:S(2)}) %collective-permute-start.48) | collective-permute-done | bytes 696352 | tf_op jit(solution)/shard_map/ppermute | solution.py:902
  265.8 1.7 collective-permute-start.49
  268.6 3.2 %collective-permute-done.49 = bf16[446,256]{1,0:T(8,128)(2,1)S(1)} collective-permute-done((bf16[446,256]{1,0:T(8,128)(2,1)S(1)}, bf16[446,256]{1,0:T(8,128)(2,1)S(1)}, u32[]{:S(2)}, u32[]{:S(2)}) %collective-permute-start.49) | collective-permute-done | bytes 228384 | tf_op jit(solution)/shard_map/ppermute | solution.py:902
  274.9 4.2 %collective-permute-done.51 = bf16[1360,256]{1,0:T(8,128)(2,1)S(1)} collective-permute-done((bf16[1360,256]{1,0:T(8,128)(2,1)S(1)}, bf16[1360,256]{1,0:T(8,128)(2,1)S(1)}, u32[]{:S(2)}, u32[]{:S(2)}) %collective-permute-start.51) | collective-permute-done | bytes 696352 | tf_op jit(solution)/shard_map/ppermute | solution.py:902
  279.1 2.3 collective-permute-done.54
  283.8 3.0 %multiply_subtract_fusion = (f32[1568,256]{1,0:T(8,128)}, f32[1568,256]{1,0:T(8,128)}, f32[1568,256]{1,0:T(8,128)}) fusion(f32[1568,256]{1,0:T(8,128)S(1)} %copy-done.22, f32[208,256]{1,0:T(8,128)S(1)} %slice.235, f32[1360,256]{1,0:T(8,128)S(1)} %convert_add_fusion, f32[1568,256]{1,0:T(8,128)S(1)} %copy-done.23, f32[1568,256]{1,0:T(8,128)S(1)} %copy-done.24), kind=kLoop, calls=%fused_computation.5 | loop fusion | flops 6422528 | bytes 11239424 | tf_op jit(solution)/shard_map/sub | solution.py:986
  (291 shorter events, 47.5 us)
Async XLA Ops:
  3.3 25.4 %collective-permute-start.1 = (bf16[1760,256]{1,0:T(8,128)(2,1)}, bf16[1760,256]{1,0:T(8,128)(2,1)}, u32[]{:S(2)}, u32[]{:S(2)}) collective-permute-start(bf16[1760,256]{1,0:T(8,128)(2,1)} %get-tuple-element.112.refs_16_), channel_id=1, source_target_pairs={{0,2},{1,3},{2,0},{3,1},{4,6},{5,7},{6,4},{7,5},{8,10},{9,11},{10,... | collective-permute-start | bytes 2703368 | tf_op jit(solution)/shard_map/ppermute | solution.py:902
  6.4 22.4 %collective-permute-start = (bf16[1760,256]{1,0:T(8,128)(2,1)}, bf16[1760,256]{1,0:T(8,128)(2,1)}, u32[]{:S(2)}, u32[]{:S(2)}) collective-permute-start(bf16[1760,256]{1,0:T(8,128)(2,1)} %get-tuple-element.112.refs_16_), channel_id=1, source_target_pairs={{0,4},{1,5},{2,6},{3,7},{4,0},{5,1},{6,2},{7,3},{8,12},{9,13},{10,... | collective-permute-start | bytes 2703368 | tf_op jit(solution)/shard_map/ppermute | solution.py:902
  7.9 19.1 %collective-permute-start.3 = (bf16[1376,256]{1,0:T(8,128)(2,1)}, bf16[1376,256]{1,0:T(8,128)(2,1)}, u32[]{:S(2)}, u32[]{:S(2)}) collective-permute-start(bf16[1376,256]{1,0:T(8,128)(2,1)} %get-tuple-element.115), channel_id=1, source_target_pairs={{0,8},{1,9},{2,10},{3,11},{4,12},{5,13},{6,14},{7,15},{8,16},{9,17... | collective-permute-start | bytes 2113544 | tf_op jit(solution)/shard_map/ppermute | solution.py:902
  27.0 16.1 %collective-permute-start.4 = (bf16[1376,256]{1,0:T(8,128)(2,1)S(1)}, bf16[1376,256]{1,0:T(8,128)(2,1)S(1)}, u32[]{:S(2)}, u32[]{:S(2)}) collective-permute-start(bf16[1376,256]{1,0:T(8,128)(2,1)S(1)} %copy-done.73), channel_id=1, source_target_pairs={{0,24},{1,25},{2,26},{3,27},{4,28},{5,29},{6,30},{7,31},{8,0},{9,1... | collective-permute-start | bytes 2113544 | tf_op jit(solution)/shard_map/ppermute | solution.py:902
  28.8 16.0 %collective-permute-start.5 = (bf16[1376,256]{1,0:T(8,128)(2,1)}, bf16[1376,256]{1,0:T(8,128)(2,1)S(1)}, u32[]{:S(2)}, u32[]{:S(2)}) collective-permute-start(bf16[1376,256]{1,0:T(8,128)(2,1)} %collective-permute-done.3.refs_22_), channel_id=1, source_target_pairs={{0,4},{1,5},{2,6},{3,7},{4,0},{5,1},{6,2},{7,3},{8,12},{9,13},{10,... | collective-permute-start | bytes 2113544 | tf_op jit(solution)/shard_map/ppermute | solution.py:902
  29.6 20.5 %collective-permute-start.2 = (bf16[1760,256]{1,0:T(8,128)(2,1)}, bf16[1760,256]{1,0:T(8,128)(2,1)S(1)}, u32[]{:S(2)}, u32[]{:S(2)}) collective-permute-start(bf16[1760,256]{1,0:T(8,128)(2,1)} %collective-permute-done.refs_19_), channel_id=1, source_target_pairs={{0,2},{1,3},{2,0},{3,1},{4,6},{5,7},{6,4},{7,5},{8,10},{9,11},{10,... | collective-permute-start | bytes 2703368 | tf_op jit(solution)/shard_map/ppermute | solution.py:902
  31.1 32.8 %collective-permute-start.16 = (bf16[49,32,256]{2,1,0:T(8,128)(2,1)S(1)}, bf16[49,32,256]{2,1,0:T(8,128)(2,1)S(1)}, u32[]{:S(2)}, u32[]{:S(2)}) collective-permute-start(bf16[49,32,256]{2,1,0:T(8,128)(2,1)S(1)} %crops.8.refs_0_), channel_id=1, source_target_pairs={{0,1},{1,0},{2,3},{3,2},{4,5},{5,4},{6,7},{7,6},{8,9},{9,8},{10,11... | collective-permute-start | bytes 2408456 | tf_op jit(solution)/shard_map/ppermute | solution.py:902
  31.2 34.3 %collective-permute-start.17 = (bf16[49,32,256]{2,1,0:T(8,128)(2,1)S(1)}, bf16[49,32,256]{2,1,0:T(8,128)(2,1)S(1)}, u32[]{:S(2)}, u32[]{:S(2)}) collective-permute-start(bf16[49,32,256]{2,1,0:T(8,128)(2,1)S(1)} %crops.9.refs_1_), channel_id=1, source_target_pairs={{0,1},{1,0},{2,3},{3,2},{4,5},{5,4},{6,7},{7,6},{8,9},{9,8},{10,11... | collective-permute-start | bytes 2408456 | tf_op jit(solution)/shard_map/ppermute | solution.py:902
  44.7 15.1 %collective-permute-start.6 = (bf16[1376,256]{1,0:T(8,128)(2,1)S(1)}, bf16[1376,256]{1,0:T(8,128)(2,1)S(1)}, u32[]{:S(2)}, u32[]{:S(2)}) collective-permute-start(bf16[1376,256]{1,0:T(8,128)(2,1)S(1)} %collective-permute-done.4.refs_25_), channel_id=1, source_target_pairs={{0,4},{1,5},{2,6},{3,7},{4,0},{5,1},{6,2},{7,3},{8,12},{9,13},{10,... | collective-permute-start | bytes 2113544 | tf_op jit(solution)/shard_map/ppermute | solution.py:902
  46.2 17.2 %collective-permute-start.7 = (bf16[1376,256]{1,0:T(8,128)(2,1)}, bf16[1376,256]{1,0:T(8,128)(2,1)S(1)}, u32[]{:S(2)}, u32[]{:S(2)}) collective-permute-start(bf16[1376,256]{1,0:T(8,128)(2,1)} %collective-permute-done.3.refs_22_), channel_id=1, source_target_pairs={{0,8},{1,9},{2,10},{3,11},{4,12},{5,13},{6,14},{7,15},{8,16},{9,17... | collective-permute-start | bytes 2113544 | tf_op jit(solution)/shard_map/ppermute | solution.py:902
  50.1 15.3 %collective-permute-start.9 = (bf16[1376,256]{1,0:T(8,128)(2,1)}, bf16[1376,256]{1,0:T(8,128)(2,1)S(1)}, u32[]{:S(2)}, u32[]{:S(2)}) collective-permute-start(bf16[1376,256]{1,0:T(8,128)(2,1)} %collective-permute-done.3.refs_22_), channel_id=1, source_target_pairs={{0,2},{1,3},{2,0},{3,1},{4,6},{5,7},{6,4},{7,5},{8,10},{9,11},{10,... | collective-permute-start | bytes 2113544 | tf_op jit(solution)/shard_map/ppermute | solution.py:902
  63.4 17.9 %collective-permute-start.8 = (bf16[2,2,384,256]{3,2,1,0:T(8,128)(2,1)S(1)}, bf16[2,2,384,256]{3,2,1,0:T(8,128)(2,1)}, u32[]{:S(2)}, u32[]{:S(2)}) collective-permute-start(bf16[2,2,384,256]{3,2,1,0:T(8,128)(2,1)S(1)} %pad_maximum_fusion.1.refs_18_.refs_21_.refs_0_), channel_id=1, source_target_pairs={{0,8},{1,9},{2,10},{3,11},{4,12},{5,13},{6,14},{7,15},{8,16},{9,17... | collective-permute-start | bytes 2359304 | tf_op jit(solution)/shard_map/ppermute | solution.py:902
  63.4 14.4 %collective-permute-start.10 = (bf16[1376,256]{1,0:T(8,128)(2,1)S(1)}, bf16[1376,256]{1,0:T(8,128)(2,1)}, u32[]{:S(2)}, u32[]{:S(2)}) collective-permute-start(bf16[1376,256]{1,0:T(8,128)(2,1)S(1)} %collective-permute-done.7.refs_33_), channel_id=1, source_target_pairs={{0,4},{1,5},{2,6},{3,7},{4,0},{5,1},{6,2},{7,3},{8,12},{9,13},{10,... | collective-permute-start | bytes 2113544 | tf_op jit(solution)/shard_map/ppermute | solution.py:902
  63.9 17.4 %collective-permute-start.18 = (bf16[49,32,256]{2,1,0:T(8,128)(2,1)S(1)}, bf16[49,32,256]{2,1,0:T(8,128)(2,1)S(1)}, u32[]{:S(2)}, u32[]{:S(2)}) collective-permute-start(bf16[49,32,256]{2,1,0:T(8,128)(2,1)S(1)} %crops.10.refs_2_), channel_id=1, source_target_pairs={{0,1},{1,0},{2,3},{3,2},{4,5},{5,4},{6,7},{7,6},{8,9},{9,8},{10,11... | collective-permute-start | bytes 2408456 | tf_op jit(solution)/shard_map/ppermute | solution.py:902
  65.5 19.6 %collective-permute-start.19 = (bf16[49,32,256]{2,1,0:T(8,128)(2,1)S(1)}, bf16[49,32,256]{2,1,0:T(8,128)(2,1)S(1)}, u32[]{:S(2)}, u32[]{:S(2)}) collective-permute-start(bf16[49,32,256]{2,1,0:T(8,128)(2,1)S(1)} %crops.11.refs_3_), channel_id=1, source_target_pairs={{0,1},{1,0},{2,3},{3,2},{4,5},{5,4},{6,7},{7,6},{8,9},{9,8},{10,11... | collective-permute-start | bytes 2408456 | tf_op jit(solution)/shard_map/ppermute | solution.py:902
  66.5 18.2 %collective-permute-start.24 = (bf16[1376,256]{1,0:T(8,128)(2,1)S(1)}, bf16[1376,256]{1,0:T(8,128)(2,1)}, u32[]{:S(2)}, u32[]{:S(2)}) collective-permute-start(bf16[1376,256]{1,0:T(8,128)(2,1)S(1)} %collective-permute-done.4.refs_25_), channel_id=1, source_target_pairs={{0,2},{1,3},{2,0},{3,1},{4,6},{5,7},{6,4},{7,5},{8,10},{9,11},{10,... | collective-permute-start | bytes 2113544 | tf_op jit(solution)/shard_map/ppermute | solution.py:902
  77.8 14.3 %collective-permute-start.20 = (bf16[49,32,256]{2,1,0:T(8,128)(2,1)S(1)}, bf16[49,32,256]{2,1,0:T(8,128)(2,1)S(1)}, u32[]{:S(2)}, u32[]{:S(2)}) collective-permute-start(bf16[49,32,256]{2,1,0:T(8,128)(2,1)S(1)} %crops.12.refs_4_), channel_id=1, source_target_pairs={{0,1},{1,0},{2,3},{3,2},{4,5},{5,4},{6,7},{7,6},{8,9},{9,8},{10,11... | collective-permute-start | bytes 2408456 | tf_op jit(solution)/shard_map/ppermute | solution.py:902
  81.3 10.8 %collective-permute-start.14 = (bf16[2,2,384,256]{3,2,1,0:T(8,128)(2,1)S(1)}, bf16[2,2,384,256]{3,2,1,0:T(8,128)(2,1)S(1)}, u32[]{:S(2)}, u32[]{:S(2)}) collective-permute-start(bf16[2,2,384,256]{3,2,1,0:T(8,128)(2,1)S(1)} %pad_maximum_fusion.1.refs_18_.refs_21_.refs_0_), channel_id=1, source_target_pairs={{0,1},{1,0},{2,3},{3,2},{4,5},{5,4},{6,7},{7,6},{8,9},{9,8},{10,11... | collective-permute-start | bytes 2359304 | tf_op jit(solution)/shard_map/ppermute | solution.py:902
  81.3 20.8 %collective-permute-start.12 = (bf16[2,2,384,256]{3,2,1,0:T(8,128)(2,1)S(1)}, bf16[2,2,384,256]{3,2,1,0:T(8,128)(2,1)S(1)}, u32[]{:S(2)}, u32[]{:S(2)}) collective-permute-start(bf16[2,2,384,256]{3,2,1,0:T(8,128)(2,1)S(1)} %pad_maximum_fusion.1.refs_18_.refs_21_.refs_0_), channel_id=1, source_target_pairs={{0,24},{1,25},{2,26},{3,27},{4,28},{5,29},{6,30},{7,31},{8,0},{9,1... | collective-permute-start | bytes 2359304 | tf_op jit(solution)/shard_map/ppermute | solution.py:902
  84.8 17.4 %collective-permute-start.11 = (bf16[1376,256]{1,0:T(8,128)(2,1)S(1)}, bf16[1376,256]{1,0:T(8,128)(2,1)S(1)}, u32[]{:S(2)}, u32[]{:S(2)}) collective-permute-start(bf16[1376,256]{1,0:T(8,128)(2,1)S(1)} %collective-permute-done.9.refs_23_), channel_id=1, source_target_pairs={{0,4},{1,5},{2,6},{3,7},{4,0},{5,1},{6,2},{7,3},{8,12},{9,13},{10,... | collective-permute-start | bytes 2113544 | tf_op jit(solution)/shard_map/ppermute | solution.py:902
  85.1 17.5 %collective-permute-start.25 = (bf16[1376,256]{1,0:T(8,128)(2,1)S(1)}, bf16[1376,256]{1,0:T(8,128)(2,1)S(1)}, u32[]{:S(2)}, u32[]{:S(2)}) collective-permute-start(bf16[1376,256]{1,0:T(8,128)(2,1)S(1)} %collective-permute-done.7.refs_33_), channel_id=1, source_target_pairs={{0,2},{1,3},{2,0},{3,1},{4,6},{5,7},{6,4},{7,5},{8,10},{9,11},{10,... | collective-permute-start | bytes 2113544 | tf_op jit(solution)/shard_map/ppermute | solution.py:902
  92.1 12.1 %collective-permute-start.21 = (bf16[49,32,256]{2,1,0:T(8,128)(2,1)S(1)}, bf16[49,32,256]{2,1,0:T(8,128)(2,1)S(1)}, u32[]{:S(2)}, u32[]{:S(2)}) collective-permute-start(bf16[49,32,256]{2,1,0:T(8,128)(2,1)S(1)} %crops.13.refs_5_), channel_id=1, source_target_pairs={{0,1},{1,0},{2,3},{3,2},{4,5},{5,4},{6,7},{7,6},{8,9},{9,8},{10,11... | collective-permute-start | bytes 2408456 | tf_op jit(solution)/shard_map/ppermute | solution.py:902
  92.2 13.2 %collective-permute-start.22 = (bf16[49,32,256]{2,1,0:T(8,128)(2,1)S(1)}, bf16[49,32,256]{2,1,0:T(8,128)(2,1)S(1)}, u32[]{:S(2)}, u32[]{:S(2)}) collective-permute-start(bf16[49,32,256]{2,1,0:T(8,128)(2,1)S(1)} %crops.14.refs_6_), channel_id=1, source_target_pairs={{0,1},{1,0},{2,3},{3,2},{4,5},{5,4},{6,7},{7,6},{8,9},{9,8},{10,11... | collective-permute-start | bytes 2408456 | tf_op jit(solution)/shard_map/ppermute | solution.py:902
  102.1 21.3 %collective-permute-start.15 = (bf16[2,2,384,256]{3,2,1,0:T(8,128)(2,1)}, bf16[2,2,384,256]{3,2,1,0:T(8,128)(2,1)}, u32[]{:S(2)}, u32[]{:S(2)}) collective-permute-start(bf16[2,2,384,256]{3,2,1,0:T(8,128)(2,1)} %collective-permute-done.8.refs_24_.refs_30_.refs_1_), channel_id=1, source_target_pairs={{0,1},{1,0},{2,3},{3,2},{4,5},{5,4},{6,7},{7,6},{8,9},{9,8},{10,11... | collective-permute-start | bytes 2359304 | tf_op jit(solution)/shard_map/ppermute | solution.py:902
  102.6 21.7 %collective-permute-start.13 = (bf16[2,2,384,256]{3,2,1,0:T(8,128)(2,1)}, bf16[2,2,384,256]{3,2,1,0:T(8,128)(2,1)}, u32[]{:S(2)}, u32[]{:S(2)}) collective-permute-start(bf16[2,2,384,256]{3,2,1,0:T(8,128)(2,1)} %collective-permute-done.8.refs_24_.refs_30_.refs_1_), channel_id=1, source_target_pairs={{0,8},{1,9},{2,10},{3,11},{4,12},{5,13},{6,14},{7,15},{8,16},{9,17... | collective-permute-start | bytes 2359304 | tf_op jit(solution)/shard_map/ppermute | solution.py:902
  104.2 20.1 %collective-permute-start.29 = (bf16[1376,256]{1,0:T(8,128)(2,1)}, bf16[1376,256]{1,0:T(8,128)(2,1)}, u32[]{:S(2)}, u32[]{:S(2)}) collective-permute-start(bf16[1376,256]{1,0:T(8,128)(2,1)} %collective-permute-done.24.refs_26_), channel_id=1, source_target_pairs={{0,4},{1,5},{2,6},{3,7},{4,0},{5,1},{6,2},{7,3},{8,12},{9,13},{10,... | collective-permute-start | bytes 2113544 | tf_op jit(solution)/shard_map/ppermute | solution.py:902
  105.5 18.9 %collective-permute-start.28 = (bf16[1376,256]{1,0:T(8,128)(2,1)}, bf16[1376,256]{1,0:T(8,128)(2,1)}, u32[]{:S(2)}, u32[]{:S(2)}) collective-permute-start(bf16[1376,256]{1,0:T(8,128)(2,1)} %collective-permute-done.10.refs_35_), channel_id=1, source_target_pairs={{0,2},{1,3},{2,0},{3,1},{4,6},{5,7},{6,4},{7,5},{8,10},{9,11},{10,... | collective-permute-start | bytes 2113544 | tf_op jit(solution)/shard_map/ppermute | solution.py:902
  124.3 10.7 %collective-permute-start.26 = (bf16[2,2,384,256]{3,2,1,0:T(8,128)(2,1)}, bf16[2,2,384,256]{3,2,1,0:T(8,128)(2,1)S(1)}, u32[]{:S(2)}, u32[]{:S(2)}) collective-permute-start(bf16[2,2,384,256]{3,2,1,0:T(8,128)(2,1)} %collective-permute-done.13.refs_18_.refs_19_.refs_2_), channel_id=1, source_target_pairs={{0,1},{1,0},{2,3},{3,2},{4,5},{5,4},{6,7},{7,6},{8,9},{9,8},{10,11... | collective-permute-start | bytes 2359304 | tf_op jit(solution)/shard_map/ppermute | solution.py:902
  148.5 11.2 %collective-permute-start.32 = (bf16[512,1024]{1,0:T(8,128)(2,1)}, bf16[512,1024]{1,0:T(8,128)(2,1)S(1)}, u32[]{:S(2)}, u32[]{:S(2)}) collective-permute-start(bf16[512,1024]{1,0:T(8,128)(2,1)} %get-tuple-element.157), channel_id=1, source_target_pairs={{0,1},{1,0},{2,3},{3,2},{4,5},{5,4},{6,7},{7,6},{8,9},{9,8},{10,11... | collective-permute-start | bytes 3145736 | tf_op jit(solution)/shard_map/ppermute | solution.py:902
  148.8 10.8 %collective-permute-start.33 = (bf16[512,512]{1,0:T(8,128)(2,1)}, bf16[512,512]{1,0:T(8,128)(2,1)S(1)}, u32[]{:S(2)}, u32[]{:S(2)}) collective-permute-start(bf16[512,512]{1,0:T(8,128)(2,1)} %get-tuple-element.160), channel_id=1, source_target_pairs={{0,1},{1,0},{2,3},{3,2},{4,5},{5,4},{6,7},{7,6},{8,9},{9,8},{10,11... | collective-permute-start | bytes 1572872 | tf_op jit(solution)/shard_map/ppermute | solution.py:902
  165.5 18.2 %collective-permute-start.37 = (bf16[1360,256]{1,0:T(8,128)(2,1)}, bf16[1360,256]{1,0:T(8,128)(2,1)S(1)}, u32[]{:S(2)}, u32[]{:S(2)}) collective-permute-start(bf16[1360,256]{1,0:T(8,128)(2,1)} %get-tuple-element.181), channel_id=1, source_target_pairs={{0,2},{1,3},{2,0},{3,1},{4,6},{5,7},{6,4},{7,5},{8,10},{9,11},{10,... | collective-permute-start | bytes 2088968 | tf_op jit(solution)/shard_map/ppermute | solution.py:902
  166.5 17.9 %collective-permute-start.38 = (bf16[1360,256]{1,0:T(8,128)(2,1)}, bf16[1360,256]{1,0:T(8,128)(2,1)S(1)}, u32[]{:S(2)}, u32[]{:S(2)}) collective-permute-start(bf16[1360,256]{1,0:T(8,128)(2,1)} %get-tuple-element.183), channel_id=1, source_target_pairs={{0,4},{1,5},{2,6},{3,7},{4,0},{5,1},{6,2},{7,3},{8,12},{9,13},{10,... | collective-permute-start | bytes 2088968 | tf_op jit(solution)/shard_map/ppermute | solution.py:902
  167.3 22.4 %collective-permute-start.34 = (bf16[2,2,416,256]{3,2,1,0:T(8,128)(2,1)}, bf16[2,2,416,256]{3,2,1,0:T(8,128)(2,1)S(1)}, u32[]{:S(2)}, u32[]{:S(2)}) collective-permute-start(bf16[2,2,416,256]{3,2,1,0:T(8,128)(2,1)} %get-tuple-element.163), channel_id=1, source_target_pairs={{0,8},{1,9},{2,10},{3,11},{4,12},{5,13},{6,14},{7,15},{8,16},{9,17... | collective-permute-start | bytes 2555912 | tf_op jit(solution)/shard_map/ppermute | solution.py:902
  183.7 17.3 %collective-permute-start.44 = (bf16[1360,256]{1,0:T(8,128)(2,1)}, bf16[1360,256]{1,0:T(8,128)(2,1)S(1)}, u32[]{:S(2)}, u32[]{:S(2)}) collective-permute-start(bf16[1360,256]{1,0:T(8,128)(2,1)} %get-tuple-element.194), channel_id=1, source_target_pairs={{0,2},{1,3},{2,0},{3,1},{4,6},{5,7},{6,4},{7,5},{8,10},{9,11},{10,... | collective-permute-start | bytes 2088968 | tf_op jit(solution)/shard_map/ppermute | solution.py:902
  184.4 16.8 %collective-permute-start.39 = (bf16[1360,256]{1,0:T(8,128)(2,1)}, bf16[1360,256]{1,0:T(8,128)(2,1)S(1)}, u32[]{:S(2)}, u32[]{:S(2)}) collective-permute-start(bf16[1360,256]{1,0:T(8,128)(2,1)} %get-tuple-element.184), channel_id=1, source_target_pairs={{0,4},{1,5},{2,6},{3,7},{4,0},{5,1},{6,2},{7,3},{8,12},{9,13},{10,... | collective-permute-start | bytes 2088968 | tf_op jit(solution)/shard_map/ppermute | solution.py:902
  189.8 19.5 %collective-permute-start.35 = (bf16[2,2,416,256]{3,2,1,0:T(8,128)(2,1)S(1)}, bf16[2,2,416,256]{3,2,1,0:T(8,128)(2,1)S(1)}, u32[]{:S(2)}, u32[]{:S(2)}) collective-permute-start(bf16[2,2,416,256]{3,2,1,0:T(8,128)(2,1)S(1)} %copy-done.72), channel_id=1, source_target_pairs={{0,24},{1,25},{2,26},{3,27},{4,28},{5,29},{6,30},{7,31},{8,0},{9,1... | collective-permute-start | bytes 2555912 | tf_op jit(solution)/shard_map/ppermute | solution.py:902
  201.2 16.0 %collective-permute-start.40 = (bf16[1360,256]{1,0:T(8,128)(2,1)S(1)}, bf16[1360,256]{1,0:T(8,128)(2,1)S(1)}, u32[]{:S(2)}, u32[]{:S(2)}) collective-permute-start(bf16[1360,256]{1,0:T(8,128)(2,1)S(1)} %add_convert_fusion.8), channel_id=1, source_target_pairs={{0,4},{1,5},{2,6},{3,7},{4,0},{5,1},{6,2},{7,3},{8,12},{9,13},{10,... | collective-permute-start | bytes 2088968 | tf_op jit(solution)/shard_map/ppermute | solution.py:902
  202.0 15.6 %collective-permute-start.45 = (bf16[1360,256]{1,0:T(8,128)(2,1)S(1)}, bf16[1360,256]{1,0:T(8,128)(2,1)S(1)}, u32[]{:S(2)}, u32[]{:S(2)}) collective-permute-start(bf16[1360,256]{1,0:T(8,128)(2,1)S(1)} %add_convert_fusion.6), channel_id=1, source_target_pairs={{0,2},{1,3},{2,0},{3,1},{4,6},{5,7},{6,4},{7,5},{8,10},{9,11},{10,... | collective-permute-start | bytes 2088968 | tf_op jit(solution)/shard_map/ppermute | solution.py:902
  209.3 20.4 %collective-permute-start.36 = (bf16[2,2,416,256]{3,2,1,0:T(8,128)(2,1)S(1)}, bf16[2,2,416,256]{3,2,1,0:T(8,128)(2,1)S(1)}, u32[]{:S(2)}, u32[]{:S(2)}) collective-permute-start(bf16[2,2,416,256]{3,2,1,0:T(8,128)(2,1)S(1)} %add_convert_fusion.1), channel_id=1, source_target_pairs={{0,8},{1,9},{2,10},{3,11},{4,12},{5,13},{6,14},{7,15},{8,16},{9,17... | collective-permute-start | bytes 2555912 | tf_op jit(solution)/shard_map/ppermute | solution.py:902
  217.2 15.8 %collective-permute-start.41 = (bf16[1360,256]{1,0:T(8,128)(2,1)S(1)}, bf16[1360,256]{1,0:T(8,128)(2,1)S(1)}, u32[]{:S(2)}, u32[]{:S(2)}) collective-permute-start(bf16[1360,256]{1,0:T(8,128)(2,1)S(1)} %copy-done.77), channel_id=1, source_target_pairs={{0,4},{1,5},{2,6},{3,7},{4,0},{5,1},{6,2},{7,3},{8,12},{9,13},{10,... | collective-permute-start | bytes 2088968 | tf_op jit(solution)/shard_map/ppermute | solution.py:902
  217.6 15.9 %collective-permute-start.46 = (bf16[1360,256]{1,0:T(8,128)(2,1)S(1)}, bf16[1360,256]{1,0:T(8,128)(2,1)S(1)}, u32[]{:S(2)}, u32[]{:S(2)}) collective-permute-start(bf16[1360,256]{1,0:T(8,128)(2,1)S(1)} %copy-done.76), channel_id=1, source_target_pairs={{0,2},{1,3},{2,0},{3,1},{4,6},{5,7},{6,4},{7,5},{8,10},{9,11},{10,... | collective-permute-start | bytes 2088968 | tf_op jit(solution)/shard_map/ppermute | solution.py:902
  229.7 19.5 %collective-permute-start.52 = (bf16[1360,256]{1,0:T(8,128)(2,1)S(1)}, bf16[1360,256]{1,0:T(8,128)(2,1)S(1)}, u32[]{:S(2)}, u32[]{:S(2)}) collective-permute-start(bf16[1360,256]{1,0:T(8,128)(2,1)S(1)} %add_convert_fusion.3), channel_id=1, source_target_pairs={{0,8},{1,9},{2,10},{3,11},{4,12},{5,13},{6,14},{7,15},{8,16},{9,17... | collective-permute-start | bytes 2088968 | tf_op jit(solution)/shard_map/ppermute | solution.py:902
  232.9 15.8 %collective-permute-start.42 = (bf16[1360,256]{1,0:T(8,128)(2,1)S(1)}, bf16[1360,256]{1,0:T(8,128)(2,1)S(1)}, u32[]{:S(2)}, u32[]{:S(2)}) collective-permute-start(bf16[1360,256]{1,0:T(8,128)(2,1)S(1)} %copy-done.75), channel_id=1, source_target_pairs={{0,4},{1,5},{2,6},{3,7},{4,0},{5,1},{6,2},{7,3},{8,12},{9,13},{10,... | collective-permute-start | bytes 2088968 | tf_op jit(solution)/shard_map/ppermute | solution.py:902
  233.5 18.5 %collective-permute-start.47 = (bf16[1360,256]{1,0:T(8,128)(2,1)S(1)}, bf16[1360,256]{1,0:T(8,128)(2,1)S(1)}, u32[]{:S(2)}, u32[]{:S(2)}) collective-permute-start(bf16[1360,256]{1,0:T(8,128)(2,1)S(1)} %add_convert_fusion.7), channel_id=1, source_target_pairs={{0,2},{1,3},{2,0},{3,1},{4,6},{5,7},{6,4},{7,5},{8,10},{9,11},{10,... | collective-permute-start | bytes 2088968 | tf_op jit(solution)/shard_map/ppermute | solution.py:902
  249.2 19.4 %collective-permute-start.53 = (bf16[1360,256]{1,0:T(8,128)(2,1)S(1)}, bf16[1360,256]{1,0:T(8,128)(2,1)S(1)}, u32[]{:S(2)}, u32[]{:S(2)}) collective-permute-start(bf16[1360,256]{1,0:T(8,128)(2,1)S(1)} %add_convert_fusion.4), channel_id=1, source_target_pairs={{0,24},{1,25},{2,26},{3,27},{4,28},{5,29},{6,30},{7,31},{8,0},{9,1... | collective-permute-start | bytes 2088968 | tf_op jit(solution)/shard_map/ppermute | solution.py:902
  252.0 13.8 %collective-permute-start.48 = (bf16[1360,256]{1,0:T(8,128)(2,1)S(1)}, bf16[1360,256]{1,0:T(8,128)(2,1)S(1)}, u32[]{:S(2)}, u32[]{:S(2)}) collective-permute-start(bf16[1360,256]{1,0:T(8,128)(2,1)S(1)} %copy-done.74), channel_id=1, source_target_pairs={{0,2},{1,3},{2,0},{3,1},{4,6},{5,7},{6,4},{7,5},{8,10},{9,11},{10,... | collective-permute-start | bytes 2088968 | tf_op jit(solution)/shard_map/ppermute | solution.py:902
  268.1 11.1 %collective-permute-start.51 = (bf16[1360,256]{1,0:T(8,128)(2,1)S(1)}, bf16[1360,256]{1,0:T(8,128)(2,1)S(1)}, u32[]{:S(2)}, u32[]{:S(2)}) collective-permute-start(bf16[1360,256]{1,0:T(8,128)(2,1)S(1)} %add_convert_fusion.5), channel_id=1, source_target_pairs={{0,4},{1,5},{2,6},{3,7},{4,0},{5,1},{6,2},{7,3},{8,12},{9,13},{10,... | collective-permute-start | bytes 2088968 | tf_op jit(solution)/shard_map/ppermute | solution.py:902
  268.6 12.8 %collective-permute-start.54 = (bf16[1360,256]{1,0:T(8,128)(2,1)S(1)}, bf16[1360,256]{1,0:T(8,128)(2,1)S(1)}, u32[]{:S(2)}, u32[]{:S(2)}) collective-permute-start(bf16[1360,256]{1,0:T(8,128)(2,1)S(1)} %add_convert_fusion.2), channel_id=1, source_target_pairs={{0,8},{1,9},{2,10},{3,11},{4,12},{5,13},{6,14},{7,15},{8,16},{9,17... | collective-permute-start | bytes 2088968 | tf_op jit(solution)/shard_map/ppermute | solution.py:902
  (86 other events, 887.5 us)
